TPU v7x, 128 devices: a whole 4x4x4 slice. The times are simulated.
128 devices in a mesh: dp: 8 (over x, core), fsdp: 16 (over z, y).
Axes of the slice: x: 4, y: 4, z: 4, core: 2. Of those that a mesh axis runs over, the one named last changes fastest.
Arguments:
- tokens: bfloat16 [65536, 1024], P(('dp', 'fsdp')), may hold values from -6 to 6
- cotangent: bfloat16 [65536, 1024], P(('dp', 'fsdp')), may hold values from -6 to 6
- lengths: int32 [128], P(('dp', 'fsdp')), may hold values from 85 to 512, as said below
- valid: int32 [65536], P(('dp', 'fsdp')), may hold values from 0 to 1, as said below
- owner_perm: int32 [96], replicated, may hold values from 0 to 95, each once
- w_qkv: float32 [1024, 3072], P(('dp', 'fsdp')), may hold values from -0.1875 to 0.1875
- w_out: float32 [1024, 1024], P(('dp', 'fsdp')), may hold values from -0.1875 to 0.1875
- w_up: float32 [1024, 4096], P(('dp', 'fsdp')), may hold values from -0.1875 to 0.1875
- w_down: float32 [1024, 4096], P(('dp', 'fsdp')), may hold values from -0.09375 to 0.09375
- vectors: float32 [22, 1024], P(None, ('dp', 'fsdp')), may hold values from -1.8 to 1.8
- head_scale: float32 [16], replicated, may hold values from 0.5 to 1.5
- left_stats: float32 [8, 96, 128, 128], P('dp', 'fsdp'), may hold values from 0 to 33554432, as said below
- right_stats: float32 [8, 96, 128, 128], P('dp', 'fsdp'), may hold values from 0 to 33554432, as said below
- left_roots: float32 [8, 96, 128, 128], P('dp', 'fsdp'), may hold values from -1 to 1, as said below
- right_roots: float32 [8, 96, 128, 128], P('dp', 'fsdp'), may hold values from -1 to 1, as said below
- vector_stats: float32 [22, 1024], P(None, ('dp', 'fsdp')), may hold values from 65536 to 262144
- head_stats: float32 [16], replicated, may hold values from 4194304 to 16777216
Outputs:
- output: bfloat16 [65536, 1024], P(('dp', 'fsdp'))
- input_grad: float32 [65536, 1024], P(('dp', 'fsdp'))
- grad_qkv: float32 [1024, 3072], P(('dp', 'fsdp'))
- grad_out: float32 [1024, 1024], P(('dp', 'fsdp'))
- grad_up: float32 [1024, 4096], P(('dp', 'fsdp'))
- grad_down: float32 [1024, 4096], P(('dp', 'fsdp'))
- vector_grads: float32 [22, 1024], P(None, ('dp', 'fsdp'))
- head_grads: float32 [16], replicated
- left_new: float32 [8, 96, 128, 128], P('dp', 'fsdp')
- right_new: float32 [8, 96, 128, 128], P('dp', 'fsdp')
- new_qkv: float32 [1024, 3072], P(('dp', 'fsdp'))
- new_out: float32 [1024, 1024], P(('dp', 'fsdp'))
- new_up: float32 [1024, 4096], P(('dp', 'fsdp'))
- new_down: float32 [1024, 4096], P(('dp', 'fsdp'))
- vector_stats_new: float32 [22, 1024], P(None, ('dp', 'fsdp'))
- vectors_new: float32 [22, 1024], P(None, ('dp', 'fsdp'))
- head_stats_new: float32 [16], replicated
- head_new: float32 [16], replicated
Inputs may be any that keep to these rules, and one draw needn't show every extreme that they name: `lengths`: the last sequence's length is 512. `valid`: 0 at every position at or past its sequence's length. `owner_perm`: each column block once. `left_stats`: symmetric. `right_stats`: symmetric. `left_roots`: symmetric. `right_roots`: symmetric.
All inputs are finite; a program needn't handle non-finite values.
Results may differ from a plain program's by a relative error of at most 0.018.
Values may be sent and summed in bfloat16 or wider, within the bound.
No kernel may reach another device: no remote copies, remote signals or barrier semaphores. Data moves between devices by JAX's collectives and lax.ppermute only.
A program may use at most 256 MiB of HBM per device.

v0:
```python
import math

import jax
import jax.numpy as jnp
from jax import lax
from jax.sharding import PartitionSpec as P

TILE = 128


EPS = 1e-05
DECAY = 0.5
RATE_MATRIX = 0.1
RATE_VECTOR = 0.3
HIGHEST = lax.Precision.HIGHEST


def norm_rows(values, scale_row, shift_row):
    row_mean = jnp.mean(values, axis=-1, keepdims=True)
    centered = values - row_mean
    variance = jnp.mean(centered * centered, axis=-1, keepdims=True)
    return centered * lax.rsqrt(variance + EPS) * scale_row + shift_row


def mlp_middle(hidden_in, gain_in, shift_in):
    return norm_rows(jax.nn.gelu(hidden_in, approximate=False), gain_in, shift_in)


def contract_last(left, right):
    return lax.dot_general(
        left, right, (((1,), (1,)), ((), ())), preferred_element_type=jnp.float32
    )


def contract_first(left, right):
    return lax.dot_general(
        left, right, (((0,), (0,)), ((), ())), preferred_element_type=jnp.float32
    )


def owner_update(grad_owned, weight_owned, left_stats, right_stats, left_roots, right_roots):
    group_rows = grad_owned.shape[0]
    own_slots = grad_owned.shape[1]

    def as_tiles(block_rows):
        return block_rows.reshape(group_rows // TILE, TILE, own_slots, TILE).transpose(0, 2, 1, 3)

    grad_tiles = as_tiles(grad_owned)
    weight_tiles = as_tiles(weight_owned)
    left_new = DECAY * left_stats + (1.0 - DECAY) * jnp.einsum(
        "rsij,rskj->rsik", grad_tiles, grad_tiles, precision=HIGHEST
    )
    right_new = DECAY * right_stats + (1.0 - DECAY) * jnp.einsum(
        "rsji,rsjk->rsik", grad_tiles, grad_tiles, precision=HIGHEST
    )
    right_side = jnp.einsum("rsij,rsjk->rsik", grad_tiles, right_roots, precision=HIGHEST)
    direction = jnp.einsum("rsij,rsjk->rsik", left_roots, right_side, precision=HIGHEST)
    new_tiles = weight_tiles - RATE_MATRIX * direction
    new_block = new_tiles.transpose(0, 2, 1, 3).reshape(group_rows, own_slots, TILE)
    return (left_new, right_new, new_block)


def shards(
    tokens,
    cotangent,
    lengths,
    valid,
    owner_perm,
    w_qkv,
    w_out,
    w_up,
    w_down,
    vectors,
    head_scale,
    left_stats,
    right_stats,
    left_roots,
    right_roots,
    vector_stats,
    head_stats,
):
    row_count, model_width = tokens.shape
    head_count = head_scale.shape[0]
    head_dim = model_width // head_count
    hidden_ratio = w_up.shape[1] // model_width
    root_dim = math.sqrt(head_dim)
    gathered_qkv, gathered_out, gathered_vectors = (
        lax.all_gather(w_qkv.astype(jnp.bfloat16), ("dp", "fsdp"), axis=0, tiled=True),
        lax.all_gather(w_out.astype(jnp.bfloat16), ("dp", "fsdp"), axis=0, tiled=True),
        lax.all_gather(vectors.astype(jnp.bfloat16), ("dp", "fsdp"), axis=1, tiled=True),
    )
    vector_rows = gathered_vectors.astype(jnp.float32)
    up_bias = vector_rows[9 : 9 + hidden_ratio].reshape(-1)
    ffn_gain = vector_rows[9 + hidden_ratio : 9 + 2 * hidden_ratio].reshape(-1)
    ffn_shift = vector_rows[9 + 2 * hidden_ratio : 9 + 3 * hidden_ratio].reshape(-1)
    down_bias = vector_rows[9 + 3 * hidden_ratio]
    inputs = tokens.astype(jnp.float32)
    normed, first_back = jax.vjp(norm_rows, inputs, vector_rows[0], vector_rows[1])
    normed_low = normed.astype(jnp.bfloat16)
    bias_full = jnp.concatenate(
        [vector_rows[2], jnp.zeros((model_width,), jnp.float32), vector_rows[3]]
    )
    projected = (
        jnp.dot(normed_low, gathered_qkv, preferred_element_type=jnp.float32) + bias_full
    ).astype(jnp.bfloat16)
    query_heads = projected[:, :model_width].reshape(row_count, head_count, head_dim)
    key_heads = projected[:, model_width : 2 * model_width].reshape(row_count, head_count, head_dim)
    value_heads = projected[:, 2 * model_width :].reshape(row_count, head_count, head_dim)
    position = jnp.arange(row_count)
    allowed = (position[None, :] <= position[:, None]) & (position[None, :] < lengths[0])

    def masked_softmax(score_block):
        masked = jnp.where(allowed[None], score_block, -1e30)
        largest = jnp.max(masked, axis=-1, keepdims=True)
        exponent = jnp.exp(masked - largest)
        return exponent / jnp.sum(exponent, axis=-1, keepdims=True)

    scores = (
        jnp.einsum("qhd,khd->hqk", query_heads, key_heads, preferred_element_type=jnp.float32)
        / root_dim
    )
    attention, softmax_back = jax.vjp(masked_softmax, scores)
    attention_low = attention.astype(jnp.bfloat16)
    mixed_heads = jnp.einsum(
        "hqk,khd->qhd", attention_low, value_heads, preferred_element_type=jnp.float32
    )
    scaled_low = (
        (mixed_heads * head_scale[None, :, None])
        .astype(jnp.bfloat16)
        .reshape(row_count, model_width)
    )
    branch = jnp.dot(scaled_low, gathered_out, preferred_element_type=jnp.float32) + vector_rows[6]
    post_norm, post_back = jax.vjp(norm_rows, branch, vector_rows[4], vector_rows[5])
    attended = inputs + post_norm
    gathered_up, gathered_down = (
        lax.all_gather(w_up.astype(jnp.bfloat16), ("dp", "fsdp"), axis=0, tiled=True),
        lax.all_gather(w_down.astype(jnp.bfloat16), ("dp", "fsdp"), axis=0, tiled=True),
    )
    normed_mid, middle_back = jax.vjp(norm_rows, attended, vector_rows[7], vector_rows[8])
    normed_mid_low = normed_mid.astype(jnp.bfloat16)
    hidden = jnp.dot(normed_mid_low, gathered_up, preferred_element_type=jnp.float32) + up_bias
    normed_top, upper_back = jax.vjp(mlp_middle, hidden, ffn_gain, ffn_shift)
    normed_top_low = normed_top.astype(jnp.bfloat16)
    output = (attended + contract_last(normed_top_low, gathered_down) + down_bias).astype(
        jnp.bfloat16
    )
    upstream = cotangent.astype(jnp.float32) * valid.astype(jnp.float32)[:, None]
    upstream_low = upstream.astype(jnp.bfloat16)
    back_up, back_down = (
        lax.all_gather(w_up.astype(jnp.bfloat16), ("dp", "fsdp"), axis=0, tiled=True),
        lax.all_gather(w_down.astype(jnp.bfloat16), ("dp", "fsdp"), axis=0, tiled=True),
    )
    grad_down_local = contract_first(upstream_low, normed_top_low)
    grad_top = jnp.dot(upstream_low, back_down, preferred_element_type=jnp.float32)
    grad_hidden, grad_ffn_gain, grad_ffn_shift = upper_back(grad_top)
    grad_hidden_low = grad_hidden.astype(jnp.bfloat16)
    grad_up_local = contract_first(normed_mid_low, grad_hidden_low)
    grad_mid = contract_last(grad_hidden_low, back_up)
    grad_from_mid, grad_mid_gain, grad_mid_shift = middle_back(grad_mid)
    grad_attended = upstream + grad_from_mid
    mlp_vector_grads = jnp.concatenate(
        [
            grad_mid_gain[None],
            grad_mid_shift[None],
            jnp.sum(grad_hidden_low.astype(jnp.float32), axis=0).reshape(hidden_ratio, model_width),
            grad_ffn_gain.reshape(hidden_ratio, model_width),
            grad_ffn_shift.reshape(hidden_ratio, model_width),
            jnp.sum(upstream, axis=0)[None],
        ],
        axis=0,
    )
    summed_up, summed_down, summed_mlp = (
        lax.psum_scatter(grad_up_local, ("dp", "fsdp"), scatter_dimension=0, tiled=True),
        lax.psum_scatter(grad_down_local, ("dp", "fsdp"), scatter_dimension=0, tiled=True),
        lax.psum_scatter(mlp_vector_grads, ("dp", "fsdp"), scatter_dimension=1, tiled=True),
    )
    back_qkv, back_out = (
        lax.all_gather(w_qkv.astype(jnp.bfloat16), ("dp", "fsdp"), axis=0, tiled=True),
        lax.all_gather(w_out.astype(jnp.bfloat16), ("dp", "fsdp"), axis=0, tiled=True),
    )
    grad_branch, grad_post_gain, grad_post_shift = post_back(grad_attended)
    grad_branch_low = grad_branch.astype(jnp.bfloat16)
    grad_out_local = contract_first(scaled_low, grad_branch_low)
    grad_scaled = contract_last(grad_branch_low, back_out).reshape(row_count, head_count, head_dim)
    grad_head = jnp.sum(grad_scaled * mixed_heads, axis=(0, 2))
    grad_mixed_low = (grad_scaled * head_scale[None, :, None]).astype(jnp.bfloat16)
    grad_attention = jnp.einsum(
        "qhd,khd->hqk", grad_mixed_low, value_heads, preferred_element_type=jnp.float32
    )
    grad_value = jnp.einsum(
        "hqk,qhd->khd", attention_low, grad_mixed_low, preferred_element_type=jnp.float32
    )
    grad_scores_low = softmax_back(grad_attention)[0].astype(jnp.bfloat16)
    grad_query = (
        jnp.einsum("hqk,khd->qhd", grad_scores_low, key_heads, preferred_element_type=jnp.float32)
        / root_dim
    )
    grad_key = (
        jnp.einsum("hqk,qhd->khd", grad_scores_low, query_heads, preferred_element_type=jnp.float32)
        / root_dim
    )
    grad_projected_low = jnp.concatenate(
        [
            grad_query.reshape(row_count, model_width),
            grad_key.reshape(row_count, model_width),
            grad_value.reshape(row_count, model_width),
        ],
        axis=1,
    ).astype(jnp.bfloat16)
    grad_qkv_local = contract_first(normed_low, grad_projected_low)
    grad_normed = contract_last(grad_projected_low, back_qkv)
    grad_from_first, grad_first_gain, grad_first_shift = first_back(grad_normed)
    input_grad = grad_attended + grad_from_first
    projected_sums = jnp.sum(grad_projected_low.astype(jnp.float32), axis=0)
    attn_vector_grads = jnp.stack(
        [
            grad_first_gain,
            grad_first_shift,
            projected_sums[:model_width],
            projected_sums[2 * model_width :],
            grad_post_gain,
            grad_post_shift,
            jnp.sum(grad_branch_low.astype(jnp.float32), axis=0),
        ],
        axis=0,
    )
    head_total = lax.psum(grad_head, ("dp", "fsdp"))
    column_weights = jnp.concatenate([w_qkv, w_out, w_up, w_down], axis=1)
    shard_rows = column_weights.shape[0]
    tile_count = column_weights.shape[1] // TILE
    weight_slots = jnp.take(
        column_weights.reshape(shard_rows, tile_count, TILE), owner_perm, axis=1
    )
    inverse = (
        jnp.zeros((tile_count,), jnp.int32)
        .at[owner_perm]
        .set(jnp.arange(tile_count, dtype=jnp.int32))
    )
    summed_qkv, summed_out, summed_attn = (
        lax.psum_scatter(grad_qkv_local, ("dp", "fsdp"), scatter_dimension=0, tiled=True),
        lax.psum_scatter(grad_out_local, ("dp", "fsdp"), scatter_dimension=0, tiled=True),
        lax.psum_scatter(attn_vector_grads, ("dp", "fsdp"), scatter_dimension=1, tiled=True),
    )
    column_grads = jnp.concatenate([summed_qkv, summed_out, summed_up, summed_down], axis=1)
    grad_slots = jnp.take(column_grads.reshape(shard_rows, tile_count, TILE), owner_perm, axis=1)
    grad_owned, weight_owned = (
        lax.all_to_all(
            grad_slots.astype(jnp.bfloat16), "fsdp", split_axis=1, concat_axis=0, tiled=True
        ).astype(grad_slots.dtype),
        lax.all_to_all(
            weight_slots.astype(jnp.bfloat16), "fsdp", split_axis=1, concat_axis=0, tiled=True
        ).astype(weight_slots.dtype),
    )
    left_new, right_new, new_block = owner_update(
        grad_owned, weight_owned, left_stats, right_stats, left_roots, right_roots
    )
    returned = lax.all_to_all(
        new_block.astype(jnp.bfloat16), "fsdp", split_axis=0, concat_axis=1, tiled=True
    ).astype(new_block.dtype)
    vector_grads = jnp.concatenate([summed_attn, summed_mlp], axis=0)
    vector_stats_new = DECAY * vector_stats + (1.0 - DECAY) * vector_grads * vector_grads
    vectors_new = vectors - RATE_VECTOR * vector_grads * lax.rsqrt(vector_stats_new)
    head_stats_new = DECAY * head_stats + (1.0 - DECAY) * head_total * head_total
    head_new = head_scale - RATE_VECTOR * head_total * lax.rsqrt(head_stats_new)
    new_columns = jnp.take(returned, inverse, axis=1).reshape(shard_rows, -1)
    first_cut = w_qkv.shape[1]
    second_cut = first_cut + w_out.shape[1]
    third_cut = second_cut + w_up.shape[1]
    new_qkv = new_columns[:, :first_cut]
    new_out = new_columns[:, first_cut:second_cut]
    new_up = new_columns[:, second_cut:third_cut]
    new_down = new_columns[:, third_cut:]
    return (
        output,
        input_grad,
        summed_qkv,
        summed_out,
        summed_up,
        summed_down,
        vector_grads,
        head_total,
        left_new,
        right_new,
        new_qkv,
        new_out,
        new_up,
        new_down,
        vector_stats_new,
        vectors_new,
        head_stats_new,
        head_new,
    )


def solution(mesh):
    placed = (
        P(("dp", "fsdp"), None),
        P(("dp", "fsdp"), None),
        P(("dp", "fsdp")),
        P(("dp", "fsdp")),
        P(),
        P(("dp", "fsdp"), None),
        P(("dp", "fsdp"), None),
        P(("dp", "fsdp"), None),
        P(("dp", "fsdp"), None),
        P(None, ("dp", "fsdp")),
        P(),
        P("dp", "fsdp", None, None),
        P("dp", "fsdp", None, None),
        P("dp", "fsdp", None, None),
        P("dp", "fsdp", None, None),
        P(None, ("dp", "fsdp")),
        P(),
    )
    return jax.shard_map(
        shards,
        mesh=mesh,
        in_specs=placed,
        out_specs=(
            P(("dp", "fsdp"), None),
            P(("dp", "fsdp"), None),
            P(("dp", "fsdp"), None),
            P(("dp", "fsdp"), None),
            P(("dp", "fsdp"), None),
            P(("dp", "fsdp"), None),
            P(None, ("dp", "fsdp")),
            P(),
            P("dp", "fsdp", None, None),
            P("dp", "fsdp", None, None),
            P(("dp", "fsdp"), None),
            P(("dp", "fsdp"), None),
            P(("dp", "fsdp"), None),
            P(("dp", "fsdp"), None),
            P(None, ("dp", "fsdp")),
            P(None, ("dp", "fsdp")),
            P(),
            P(),
        ),
        check_vma=False,
    )
```

profile of v0, /device:TPU:0, one launch (start us, length us, event | category | flops | bytes accessed | tf_op | source)
XLA Modules:
  0.0 2808.5 jit_solution(11167141396845002070)
XLA Ops:
  14.3 59.6 %all_gather.19 = bf16[22,1024]{0,1:T(8,128)(2,1)S(1)} all-gather(bf16[22,8]{0,1:T(8,128)(2,1)S(1)} %convert_element_type.126), channel_id=1, replica_groups=mesh['dp'=8,'fsdp'=16] {'dp','fsdp'}, dimensions={1}, use_global_device_ids=true | all-gather | bytes 45408 | tf_op jit(solution)/shard_map/all_gather | solution.py:90
  83.1 6.9 add_convert_fusion.2
  98.2 9.9 fusion.1
  108.1 9.2 fusion.8
  117.3 12.3 convert_reduce_fusion
  136.0 12.9 all-gather.7.cloned.1.call-done
  156.8 63.4 %all-gather.9.cloned.1.call-done = bf16[1024,4096]{1,0:T(8,128)(2,1)} async-done(((bf16[8,4096]{1,0:T(8,128)(2,1)}), bf16[1024,4096]{1,0:T(8,128)(2,1)}) %all-gather.9.cloned.1.call-update) | async-done | bytes 8388624 | tf_op jit(solution)/shard_map/all_gather | solution.py:136
  220.2 28.3 %fusion.70 = (f32[512]{0:T(512)S(1)}, f32[512,4096]{1,0:T(8,128)}, f32[512,4096]{1,0:T(8,128)}, f32[512,4096]{1,0:T(8,128)}) fusion(f32[4096]{0:T(1024)} %bitcast.180, bf16[1024,4096]{1,0:T(8,128)(2,1)} %all-gather.9.cloned.1.call-done, f32[512,1024]{1,0:T(8,128)} %copy-done.5, f32[1024]{0:T(1024)} %get-tuple-element.54, f32[1024]{0:T(1024)} %get-tuple-element.52, ...), kind=kOutput, calls=%fused_computation.179 | convolution fusion | flops 4436000256 | bytes 35682304 | tf_op jit(solution)/shard_map/dot_general | solution.py:141
  249.1 42.4 %all-gather.11.cloned.1.call-done = bf16[1024,4096]{1,0:T(8,128)(2,1)} async-done(((bf16[8,4096]{1,0:T(8,128)(2,1)}), bf16[1024,4096]{1,0:T(8,128)(2,1)}) %all-gather.11.cloned.1.call-update) | async-done | bytes 8388624 | tf_op jit(solution)/shard_map/all_gather | solution.py:137
  291.5 12.3 multiply_reduce_fusion.2
  308.0 13.8 convert_reduce_fusion.1
  321.8 10.9 multiply_reduce_fusion.4
  344.1 13.3 multiply_reduce_fusion
  357.5 18.8 fusion.66
  376.4 8.8 multiply_convert_fusion
  385.2 9.4 multiply_convert_fusion.1
  396.1 8.5 fusion.63
  415.4 4.2 concatenate.21
  421.1 4.9 fusion.78
  426.1 9.5 fusion.56
  437.3 10.7 fusion.61
  451.1 14.4 fusion.34
  477.9 4.2 add_add_fusion.4
  482.3 11.4 add_convert_fusion.4
  493.8 63.3 %all-reduce.5.cloned.1.call-done = (f32[15,1024]{1,0:T(8,128)}, f32[7,1024]{1,0:T(8,128)}, f32[16]{0:T(128)}) async-done(((f32[15,1024]{1,0:T(8,128)}, f32[7,1024]{1,0:T(8,128)}, f32[16]{0:T(128)}), (f32[15,1024]{1,0:T(8,128)}, f32[7,1024]{1,0:T(8,128)}, f32[16]{0:T(128)})) %all-reduce.5.cloned.1.call-update) | async-done | bytes 90192
  559.4 642.0 %reduce-scatter.9.cloned.1.call-done = f32[8,1024]{1,0:T(8,128)} async-done(((f32[1024,1024]{1,0:T(8,128)}), f32[8,1024]{1,0:T(8,128)}) %reduce-scatter.9.cloned.1.call-update) | async-done | bytes 32784 | tf_op jit(solution)/shard_map/reduce_scatter | solution.py:241
  1201.4 221.8 %reduce-scatter.7.cloned.1.call-done = f32[8,3072]{1,0:T(8,128)} async-done(((f32[1024,3072]{1,0:T(8,128)}), f32[8,3072]{1,0:T(8,128)}) %reduce-scatter.7.cloned.1.call-update) | async-done | bytes 98320 | tf_op jit(solution)/shard_map/reduce_scatter | solution.py:240
  1423.2 668.4 %reduce-scatter.11.cloned.1.call-done = f32[8,4096]{1,0:T(8,128)} async-done(((f32[1024,4096]{1,0:T(8,128)}), f32[8,4096]{1,0:T(8,128)}) %reduce-scatter.11.cloned.1.call-update) | async-done | bytes 131088 | tf_op jit(solution)/shard_map/reduce_scatter | solution.py:173
  2091.6 665.9 %reduce-scatter.13.cloned.1.call-done = f32[8,4096]{1,0:T(8,128)} async-done(((f32[1024,4096]{1,0:T(8,128)}), f32[8,4096]{1,0:T(8,128)}) %reduce-scatter.13.cloned.1.call-update) | async-done | bytes 131088 | tf_op jit(solution)/shard_map/reduce_scatter | solution.py:174
  2764.9 7.2 all-to-all-done
  2777.1 6.8 all-to-all-done.1
  2790.5 7.6 all-to-all-done.2
  (292 shorter events, 110.0 us)
Async XLA Ops:
  7.2 2769.5 %copy-start = (f32[1,6,128,128]{3,2,1,0:T(8,128)S(1)}, f32[1,6,128,128]{3,2,1,0:T(8,128)}, u32[]{:S(2)}) copy-start(f32[1,6,128,128]{3,2,1,0:T(8,128)} %param.33) | copy-start | bytes 1179652
  7.2 71.0 %copy-start.4 = (bf16[512,1024]{1,0:T(8,128)(2,1)S(1)}, bf16[512,1024]{1,0:T(8,128)(2,1)}, u32[]{:S(2)}) copy-start(bf16[512,1024]{1,0:T(8,128)(2,1)} %param.19) | copy-start | bytes 3145732
  7.2 75.9 %all-gather.5.cloned.1.call-start = ((), (), s32[]{:S(2)}) async-start(), calls=%async_computation.7 | async-start | bytes 6340608 | tf_op jit(solution)/shard_map/all_gather | solution.py:88
  8.9 140.0 %all-gather.7.cloned.1.call-start = ((), (), s32[]{:S(2)}) async-start(), calls=%async_computation.8 | async-start | bytes 2113536 | tf_op jit(solution)/shard_map/all_gather | solution.py:89
  10.3 209.9 %all-gather.9.cloned.1.call-start = ((), (), s32[]{:S(2)}) async-start(), calls=%async_computation.9 | async-start | bytes 8454144 | tf_op jit(solution)/shard_map/all_gather | solution.py:136
  12.0 279.5 %all-gather.11.cloned.1.call-start = ((), (), s32[]{:S(2)}) async-start(), calls=%async_computation.10 | async-start | bytes 8454144 | tf_op jit(solution)/shard_map/all_gather | solution.py:137
  13.6 543.4 %all-reduce.5.cloned.1.call-start = ((), (), s32[]{:S(2)}) async-start(), calls=%async_computation.15 | async-start | bytes 197632
  79.7 37.6 %copy-start.11 = (pred[512,512]{0,1:T(8,128)(4,1)}, pred[512,512]{0,1:T(8,128)(4,1)S(1)}, u32[]{:S(2)}) copy-start(pred[512,512]{0,1:T(8,128)(4,1)S(1)} %fusion.33) | copy-start | bytes 786436
  93.2 36.4 %copy-start.9 = (bf16[512,1024]{0,1:T(8,128)(2,1)}, bf16[512,1024]{0,1:T(8,128)(2,1)S(1)}, u32[]{:S(2)}) copy-start(bf16[512,1024]{0,1:T(8,128)(2,1)S(1)} %copy.70) | copy-start | bytes 3145732
  117.3 15.5 copy-start.46
  344.1 52.1 %copy-start.15 = (bf16[16,64,512]{2,1,0:T(8,128)(2,1)}, bf16[16,64,512]{2,1,0:T(8,128)(2,1)S(1)}, u32[]{:S(2)}) copy-start(bf16[16,64,512]{2,1,0:T(8,128)(2,1)S(1)} %convolution_convert_fusion) | copy-start | bytes 3145732
  357.4 18.9 copy-start.35
  357.5 18.9 copy-start.13
  357.5 18.9 copy-start.17
  421.1 780.3 %reduce-scatter.9.cloned.1.call-start = ((), (), s32[]{:S(2)}) async-start(), calls=%async_computation.12 | async-start | bytes 4227072 | tf_op jit(solution)/shard_map/reduce_scatter | solution.py:241
  426.0 997.2 %reduce-scatter.7.cloned.1.call-start = ((), (), s32[]{:S(2)}) async-start(), calls=%async_computation.11 | async-start | bytes 12681216 | tf_op jit(solution)/shard_map/reduce_scatter | solution.py:240
  435.7 1655.9 %reduce-scatter.11.cloned.1.call-start = ((), (), s32[]{:S(2)}) async-start(), calls=%async_computation.13 | async-start | bytes 16908288 | tf_op jit(solution)/shard_map/reduce_scatter | solution.py:173
  447.9 2309.5 %reduce-scatter.13.cloned.1.call-start = ((), (), s32[]{:S(2)}) async-start(), calls=%async_computation.14 | async-start | bytes 16908288 | tf_op jit(solution)/shard_map/reduce_scatter | solution.py:174
  482.2 76.5 %copy-start.65 = (f32[22,8]{0,1:T(8,128)S(1)}, f32[22,8]{0,1:T(8,128)}, u32[]{:S(2)}) copy-start(f32[22,8]{0,1:T(8,128)} %param.28) | copy-start | bytes 2116
  482.2 76.5 %copy-start.77 = (f32[22,8]{0,1:T(8,128)S(1)}, f32[22,8]{0,1:T(8,128)}, u32[]{:S(2)}) copy-start(f32[22,8]{0,1:T(8,128)} %param.34) | copy-start | bytes 2116
  482.2 2277.1 %copy-start.26 = (bf16[96,8,128]{2,1,0:T(8,128)(2,1)S(1)}, bf16[96,8,128]{2,1,0:T(8,128)(2,1)}, u32[]{:S(2)}) copy-start(bf16[96,8,128]{2,1,0:T(8,128)(2,1)} %gather_fusion.1) | copy-start | bytes 589828
  482.2 2277.1 %copy-start.83 = (pred[96]{0:T(512)(128)(4,1)S(1)}, pred[96]{0:T(512)(128)(4,1)}, u32[]{:S(2)}) copy-start(pred[96]{0:T(512)(128)(4,1)} %compare_and_fusion.1) | copy-start | bytes 292
  482.3 2281.5 %copy-start.48 = (f32[16]{0:T(128)S(1)}, f32[16]{0:T(128)}, u32[]{:S(2)}) copy-start(f32[16]{0:T(128)} %param.29) | copy-start | bytes 196
  482.3 2281.5 %copy-start.79 = (f32[16]{0:T(128)S(1)}, f32[16]{0:T(128)}, u32[]{:S(2)}) copy-start(f32[16]{0:T(128)} %param.35) | copy-start | bytes 196
  482.3 2293.3 %copy-start.30 = (f32[1,6,128,128]{3,2,1,0:T(8,128)S(1)}, f32[1,6,128,128]{3,2,1,0:T(8,128)}, u32[]{:S(2)}) copy-start(f32[1,6,128,128]{3,2,1,0:T(8,128)} %param.30) | copy-start | bytes 1179652
  482.3 2301.8 %copy-start.31 = (f32[1,6,128,128]{3,2,1,0:T(8,128)S(1)}, f32[1,6,128,128]{3,2,1,0:T(8,128)}, u32[]{:S(2)}) copy-start(f32[1,6,128,128]{3,2,1,0:T(8,128)} %param.32) | copy-start | bytes 1179652
  493.7 2295.8 %copy-start.32 = (f32[1,6,128,128]{3,2,1,0:T(8,128)S(1)}, f32[1,6,128,128]{3,2,1,0:T(8,128)}, u32[]{:S(2)}) copy-start(f32[1,6,128,128]{3,2,1,0:T(8,128)} %param.31) | copy-start | bytes 1179652
  493.7 2305.3 %copy-start.82 = (pred[96]{0:T(512)(128)(4,1)S(1)}, pred[96]{0:T(512)(128)(4,1)}, u32[]{:S(2)}) copy-start(pred[96]{0:T(512)(128)(4,1)} %compare_and_fusion) | copy-start | bytes 292
  2758.5 42.7 %copy-start.80 = (f32[16]{0:T(128)S(1)}, f32[16]{0:T(128)}, u32[]{:S(2)}) copy-start(f32[16]{0:T(128)} %get-tuple-element.123) | copy-start | bytes 196
  2760.3 11.8 all-to-all-start
  2772.1 11.8 all-to-all-start.1
  2786.0 12.2 all-to-all-start.2
  (66 other events, 408.9 us)
Sparse Core Ops, SparseCore 0:
  11.7 71.3 all-gather.4
  86.6 62.2 all-gather.6
  152.6 67.5 all-gather.8
  223.8 67.6 all-gather.10
  421.1 135.8 all-reduce.4
  559.9 641.4 reduce-scatter.8
  1207.0 216.1 reduce-scatter.6
  1426.2 665.4 reduce-scatter.10
  2094.6 662.8 reduce-scatter.12
where the time goes:
time: 2810 us
  waiting for transfers between devices  2400 us (85%)
  matrix products  173 us (6%)
  other arithmetic  97.4 us (3%)
  blocking collectives  59.6 us (2%)
  local copies, waits for them, and re-layouts  48.9 us (2%)
    reduce_scatter x1, waiting for transfers between devices, shards(): lax.psum_scatter(grad_up_local, ('dp', 'fsdp'), scatter_dimension=0, tile...  668 us
    reduce_scatter x1, waiting for transfers between devices, shards(): lax.psum_scatter(grad_down_local, ('dp', 'fsdp'), scatter_dimension=0, ti...  666 us
    reduce_scatter x1, waiting for transfers between devices, shards(): lax.psum_scatter(grad_out_local, ('dp', 'fsdp'), scatter_dimension=0, til...  642 us
    reduce_scatter x1, waiting for transfers between devices, shards(): lax.psum_scatter(grad_qkv_local, ('dp', 'fsdp'), scatter_dimension=0, til...  222 us
    unnamed x10, waiting for transfers between devices  63.4 us
    all_gather x1, waiting for transfers between devices, shards(): lax.all_gather(w_up.astype(jnp.bfloat16), ('dp', 'fsdp'), axis=0, tiled=T...  63.4 us
    all_gather x1, blocking collectives, shards(): lax.all_gather(vectors.astype(jnp.bfloat16), ('dp', 'fsdp'), axis=1, tile...  59.6 us
  transfers between devices with their start and end apart: 12, of which 12 were waited for; matrix products, arithmetic and copies ran while one was open for 6% of the time, Pallas kernels for 0%

commit v1 on v0

--- a/solution.py
+++ b/solution.py
@@ -38,7 +38,39 @@
     )
 
 
-def owner_update(grad_owned, weight_owned, left_stats, right_stats, left_roots, right_roots):
+def reduce_rows(left, right):
+    tokens_here, rows = left.shape
+    columns = right.shape[1]
+    x_size, core_size = lax.axis_size("x"), lax.axis_size("core")
+    plane = lax.axis_size("fsdp")
+    me = lax.axis_index("core")
+    by_core = left.reshape(tokens_here, x_size, core_size, -1)
+
+    def rows_of(core):
+        return lax.dynamic_index_in_dim(by_core, core, axis=2, keepdims=False).reshape(
+            tokens_here, rows // core_size
+        )
+
+    sent = contract_first(rows_of(1 - me), right).astype(jnp.bfloat16)
+    swapped = lax.ppermute(sent, "core", [(0, 1), (1, 0)])
+    kept = (contract_first(rows_of(me), right) + swapped.astype(jnp.float32)).astype(jnp.bfloat16)
+    half = columns // 2
+    shard = rows // (x_size * core_size * plane)
+    first = lax.psum_scatter(kept[:, :half], "x", scatter_dimension=0, tiled=True)
+    first = lax.all_to_all(
+        first.reshape(plane, shard, half), "fsdp", split_axis=0, concat_axis=0, tiled=True
+    )
+    first = jnp.sum(first.astype(jnp.float32), axis=0)
+    second = kept[:, half:].reshape(x_size, plane, shard, columns - half).transpose(1, 0, 2, 3)
+    second = lax.all_to_all(second, "fsdp", split_axis=0, concat_axis=0, tiled=True)
+    second = jnp.sum(second.astype(jnp.float32), axis=0)
+    second = lax.psum_scatter(
+        second.reshape(x_size * shard, columns - half), "x", scatter_dimension=0, tiled=True
+    )
+    return jnp.concatenate([first, second], axis=1)
+
+
+def owner_update(grad_owned, left_stats, right_stats, left_roots, right_roots):
     group_rows = grad_owned.shape[0]
     own_slots = grad_owned.shape[1]
 
@@ -46,7 +78,6 @@
         return block_rows.reshape(group_rows // TILE, TILE, own_slots, TILE).transpose(0, 2, 1, 3)
 
     grad_tiles = as_tiles(grad_owned)
-    weight_tiles = as_tiles(weight_owned)
     left_new = DECAY * left_stats + (1.0 - DECAY) * jnp.einsum(
         "rsij,rskj->rsik", grad_tiles, grad_tiles, precision=HIGHEST
     )
@@ -55,9 +86,8 @@
     )
     right_side = jnp.einsum("rsij,rsjk->rsik", grad_tiles, right_roots, precision=HIGHEST)
     direction = jnp.einsum("rsij,rsjk->rsik", left_roots, right_side, precision=HIGHEST)
-    new_tiles = weight_tiles - RATE_MATRIX * direction
-    new_block = new_tiles.transpose(0, 2, 1, 3).reshape(group_rows, own_slots, TILE)
-    return (left_new, right_new, new_block)
+    direction = direction.transpose(0, 2, 1, 3).reshape(group_rows, own_slots, TILE)
+    return (left_new, right_new, direction)
 
 
 def shards(
@@ -84,11 +114,26 @@
     head_dim = model_width // head_count
     hidden_ratio = w_up.shape[1] // model_width
     root_dim = math.sqrt(head_dim)
-    gathered_qkv, gathered_out, gathered_vectors = (
-        lax.all_gather(w_qkv.astype(jnp.bfloat16), ("dp", "fsdp"), axis=0, tiled=True),
-        lax.all_gather(w_out.astype(jnp.bfloat16), ("dp", "fsdp"), axis=0, tiled=True),
-        lax.all_gather(vectors.astype(jnp.bfloat16), ("dp", "fsdp"), axis=1, tiled=True),
-    )
+    low_first = jnp.concatenate(
+        [
+            w_qkv.astype(jnp.bfloat16),
+            w_out.astype(jnp.bfloat16),
+            jnp.pad(vectors.astype(jnp.bfloat16).T, ((0, 0), (0, TILE - vectors.shape[0]))),
+        ],
+        axis=1,
+    )
+    qkv_cols = w_qkv.shape[1]
+    out_cols = qkv_cols + w_out.shape[1]
+    gathered_first = lax.all_gather(low_first, ("x", "core", "fsdp"), axis=0, tiled=True)
+    gathered_qkv = gathered_first[:, :qkv_cols]
+    gathered_out = gathered_first[:, qkv_cols:out_cols]
+    gathered_vectors = gathered_first[:, out_cols : out_cols + vectors.shape[0]].T
+    low_second = jnp.concatenate(
+        [w_up.astype(jnp.bfloat16), w_down.astype(jnp.bfloat16)], axis=1
+    )
+    gathered_second = lax.all_gather(low_second, ("x", "core", "fsdp"), axis=0, tiled=True)
+    gathered_up = gathered_second[:, : w_up.shape[1]]
+    gathered_down = gathered_second[:, w_up.shape[1] :]
     vector_rows = gathered_vectors.astype(jnp.float32)
     up_bias = vector_rows[9 : 9 + hidden_ratio].reshape(-1)
     ffn_gain = vector_rows[9 + hidden_ratio : 9 + 2 * hidden_ratio].reshape(-1)
@@ -132,10 +177,6 @@
     branch = jnp.dot(scaled_low, gathered_out, preferred_element_type=jnp.float32) + vector_rows[6]
     post_norm, post_back = jax.vjp(norm_rows, branch, vector_rows[4], vector_rows[5])
     attended = inputs + post_norm
-    gathered_up, gathered_down = (
-        lax.all_gather(w_up.astype(jnp.bfloat16), ("dp", "fsdp"), axis=0, tiled=True),
-        lax.all_gather(w_down.astype(jnp.bfloat16), ("dp", "fsdp"), axis=0, tiled=True),
-    )
     normed_mid, middle_back = jax.vjp(norm_rows, attended, vector_rows[7], vector_rows[8])
     normed_mid_low = normed_mid.astype(jnp.bfloat16)
     hidden = jnp.dot(normed_mid_low, gathered_up, preferred_element_type=jnp.float32) + up_bias
@@ -146,16 +187,12 @@
     )
     upstream = cotangent.astype(jnp.float32) * valid.astype(jnp.float32)[:, None]
     upstream_low = upstream.astype(jnp.bfloat16)
-    back_up, back_down = (
-        lax.all_gather(w_up.astype(jnp.bfloat16), ("dp", "fsdp"), axis=0, tiled=True),
-        lax.all_gather(w_down.astype(jnp.bfloat16), ("dp", "fsdp"), axis=0, tiled=True),
-    )
-    grad_down_local = contract_first(upstream_low, normed_top_low)
-    grad_top = jnp.dot(upstream_low, back_down, preferred_element_type=jnp.float32)
+    summed_down = reduce_rows(upstream_low, normed_top_low)
+    grad_top = jnp.dot(upstream_low, gathered_down, preferred_element_type=jnp.float32)
     grad_hidden, grad_ffn_gain, grad_ffn_shift = upper_back(grad_top)
     grad_hidden_low = grad_hidden.astype(jnp.bfloat16)
-    grad_up_local = contract_first(normed_mid_low, grad_hidden_low)
-    grad_mid = contract_last(grad_hidden_low, back_up)
+    summed_up = reduce_rows(normed_mid_low, grad_hidden_low)
+    grad_mid = contract_last(grad_hidden_low, gathered_up)
     grad_from_mid, grad_mid_gain, grad_mid_shift = middle_back(grad_mid)
     grad_attended = upstream + grad_from_mid
     mlp_vector_grads = jnp.concatenate(
@@ -169,19 +206,10 @@
         ],
         axis=0,
     )
-    summed_up, summed_down, summed_mlp = (
-        lax.psum_scatter(grad_up_local, ("dp", "fsdp"), scatter_dimension=0, tiled=True),
-        lax.psum_scatter(grad_down_local, ("dp", "fsdp"), scatter_dimension=0, tiled=True),
-        lax.psum_scatter(mlp_vector_grads, ("dp", "fsdp"), scatter_dimension=1, tiled=True),
-    )
-    back_qkv, back_out = (
-        lax.all_gather(w_qkv.astype(jnp.bfloat16), ("dp", "fsdp"), axis=0, tiled=True),
-        lax.all_gather(w_out.astype(jnp.bfloat16), ("dp", "fsdp"), axis=0, tiled=True),
-    )
     grad_branch, grad_post_gain, grad_post_shift = post_back(grad_attended)
     grad_branch_low = grad_branch.astype(jnp.bfloat16)
-    grad_out_local = contract_first(scaled_low, grad_branch_low)
-    grad_scaled = contract_last(grad_branch_low, back_out).reshape(row_count, head_count, head_dim)
+    summed_out = reduce_rows(scaled_low, grad_branch_low)
+    grad_scaled = contract_last(grad_branch_low, gathered_out).reshape(row_count, head_count, head_dim)
     grad_head = jnp.sum(grad_scaled * mixed_heads, axis=(0, 2))
     grad_mixed_low = (grad_scaled * head_scale[None, :, None]).astype(jnp.bfloat16)
     grad_attention = jnp.einsum(
@@ -207,8 +235,8 @@
         ],
         axis=1,
     ).astype(jnp.bfloat16)
-    grad_qkv_local = contract_first(normed_low, grad_projected_low)
-    grad_normed = contract_last(grad_projected_low, back_qkv)
+    summed_qkv = reduce_rows(normed_low, grad_projected_low)
+    grad_normed = contract_last(grad_projected_low, gathered_qkv)
     grad_from_first, grad_first_gain, grad_first_shift = first_back(grad_normed)
     input_grad = grad_attended + grad_from_first
     projected_sums = jnp.sum(grad_projected_low.astype(jnp.float32), axis=0)
@@ -224,45 +252,49 @@
         ],
         axis=0,
     )
-    head_total = lax.psum(grad_head, ("dp", "fsdp"))
+    vector_partials = jnp.concatenate([attn_vector_grads, mlp_vector_grads], axis=0)
+    devices = model_width // vectors.shape[1]
+    small = jnp.concatenate(
+        [
+            vector_partials.reshape(-1, devices, vectors.shape[1])
+            .transpose(1, 0, 2)
+            .reshape(devices, -1),
+            jnp.broadcast_to(grad_head[None], (devices, head_count)),
+        ],
+        axis=1,
+    )
+    small = jnp.sum(
+        lax.all_to_all(small, ("x", "core", "fsdp"), split_axis=0, concat_axis=0, tiled=True), axis=0
+    )
+    vector_grads = small[: vectors.size].reshape(vectors.shape)
+    head_total = small[vectors.size :]
     column_weights = jnp.concatenate([w_qkv, w_out, w_up, w_down], axis=1)
     shard_rows = column_weights.shape[0]
     tile_count = column_weights.shape[1] // TILE
-    weight_slots = jnp.take(
-        column_weights.reshape(shard_rows, tile_count, TILE), owner_perm, axis=1
-    )
     inverse = (
         jnp.zeros((tile_count,), jnp.int32)
         .at[owner_perm]
         .set(jnp.arange(tile_count, dtype=jnp.int32))
     )
-    summed_qkv, summed_out, summed_attn = (
-        lax.psum_scatter(grad_qkv_local, ("dp", "fsdp"), scatter_dimension=0, tiled=True),
-        lax.psum_scatter(grad_out_local, ("dp", "fsdp"), scatter_dimension=0, tiled=True),
-        lax.psum_scatter(attn_vector_grads, ("dp", "fsdp"), scatter_dimension=1, tiled=True),
-    )
     column_grads = jnp.concatenate([summed_qkv, summed_out, summed_up, summed_down], axis=1)
-    grad_slots = jnp.take(column_grads.reshape(shard_rows, tile_count, TILE), owner_perm, axis=1)
-    grad_owned, weight_owned = (
-        lax.all_to_all(
-            grad_slots.astype(jnp.bfloat16), "fsdp", split_axis=1, concat_axis=0, tiled=True
-        ).astype(grad_slots.dtype),
-        lax.all_to_all(
-            weight_slots.astype(jnp.bfloat16), "fsdp", split_axis=1, concat_axis=0, tiled=True
-        ).astype(weight_slots.dtype),
-    )
-    left_new, right_new, new_block = owner_update(
-        grad_owned, weight_owned, left_stats, right_stats, left_roots, right_roots
+    grad_slots = jnp.take(
+        column_grads.astype(jnp.bfloat16).reshape(shard_rows, tile_count, TILE), owner_perm, axis=1
+    )
+    grad_owned = lax.all_to_all(
+        grad_slots, "fsdp", split_axis=1, concat_axis=0, tiled=True
+    ).astype(jnp.float32)
+    left_new, right_new, direction = owner_update(
+        grad_owned, left_stats, right_stats, left_roots, right_roots
     )
     returned = lax.all_to_all(
-        new_block.astype(jnp.bfloat16), "fsdp", split_axis=0, concat_axis=1, tiled=True
-    ).astype(new_block.dtype)
-    vector_grads = jnp.concatenate([summed_attn, summed_mlp], axis=0)
+        direction.astype(jnp.bfloat16), "fsdp", split_axis=0, concat_axis=1, tiled=True
+    )
     vector_stats_new = DECAY * vector_stats + (1.0 - DECAY) * vector_grads * vector_grads
     vectors_new = vectors - RATE_VECTOR * vector_grads * lax.rsqrt(vector_stats_new)
     head_stats_new = DECAY * head_stats + (1.0 - DECAY) * head_total * head_total
     head_new = head_scale - RATE_VECTOR * head_total * lax.rsqrt(head_stats_new)
-    new_columns = jnp.take(returned, inverse, axis=1).reshape(shard_rows, -1)
+    steps = jnp.take(returned, inverse, axis=1).reshape(shard_rows, -1).astype(jnp.float32)
+    new_columns = column_weights - RATE_MATRIX * steps
     first_cut = w_qkv.shape[1]
     second_cut = first_cut + w_out.shape[1]
     third_cut = second_cut + w_up.shape[1]
@@ -294,45 +326,47 @@
 
 def solution(mesh):
     placed = (
-        P(("dp", "fsdp"), None),
-        P(("dp", "fsdp"), None),
-        P(("dp", "fsdp")),
-        P(("dp", "fsdp")),
+        P(("x", "core", "fsdp"), None),
+        P(("x", "core", "fsdp"), None),
+        P(("x", "core", "fsdp")),
+        P(("x", "core", "fsdp")),
         P(),
-        P(("dp", "fsdp"), None),
-        P(("dp", "fsdp"), None),
-        P(("dp", "fsdp"), None),
-        P(("dp", "fsdp"), None),
-        P(None, ("dp", "fsdp")),
+        P(("x", "core", "fsdp"), None),
+        P(("x", "core", "fsdp"), None),
+        P(("x", "core", "fsdp"), None),
+        P(("x", "core", "fsdp"), None),
+        P(None, ("x", "core", "fsdp")),
         P(),
-        P("dp", "fsdp", None, None),
-        P("dp", "fsdp", None, None),
-        P("dp", "fsdp", None, None),
-        P("dp", "fsdp", None, None),
-        P(None, ("dp", "fsdp")),
+        P(("x", "core"), "fsdp", None, None),
+        P(("x", "core"), "fsdp", None, None),
+        P(("x", "core"), "fsdp", None, None),
+        P(("x", "core"), "fsdp", None, None),
+        P(None, ("x", "core", "fsdp")),
         P(),
     )
+    dp, fsdp = mesh.devices.shape
+    mesh = jax.sharding.Mesh(mesh.devices.reshape(dp // 2, 2, fsdp), ("x", "core", "fsdp"))
     return jax.shard_map(
         shards,
         mesh=mesh,
         in_specs=placed,
         out_specs=(
-            P(("dp", "fsdp"), None),
-            P(("dp", "fsdp"), None),
-            P(("dp", "fsdp"), None),
-            P(("dp", "fsdp"), None),
-            P(("dp", "fsdp"), None),
-            P(("dp", "fsdp"), None),
-            P(None, ("dp", "fsdp")),
+            P(("x", "core", "fsdp"), None),
+            P(("x", "core", "fsdp"), None),
+            P(("x", "core", "fsdp"), None),
+            P(("x", "core", "fsdp"), None),
+            P(("x", "core", "fsdp"), None),
+            P(("x", "core", "fsdp"), None),
+            P(None, ("x", "core", "fsdp")),
             P(),
-            P("dp", "fsdp", None, None),
-            P("dp", "fsdp", None, None),
-            P(("dp", "fsdp"), None),
-            P(("dp", "fsdp"), None),
-            P(("dp", "fsdp"), None),
-            P(("dp", "fsdp"), None),
-            P(None, ("dp", "fsdp")),
-            P(None, ("dp", "fsdp")),
+            P(("x", "core"), "fsdp", None, None),
+            P(("x", "core"), "fsdp", None, None),
+            P(("x", "core", "fsdp"), None),
+            P(("x", "core", "fsdp"), None),
+            P(("x", "core", "fsdp"), None),
+            P(("x", "core", "fsdp"), None),
+            P(None, ("x", "core", "fsdp")),
+            P(None, ("x", "core", "fsdp")),
             P(),
             P(),
         ),

time: 2810 us -> 651 us (0.23)
  waiting for transfers between devices: 2400 us -> 140 us
  local copies, waits for them, and re-layouts: 48.9 us -> 142 us
  blocking collectives: 59.6 us -> 0 us
  starting transfers between devices: 10.9 us -> 51.3 us
    reduce_scatter x4 -> x8, waiting for transfers between devices: 2200 us -> 0.1 us  [the longest x4 0.08 us: reduce_rows(): lax.psum_scatter(second.reshape(x_size * shard, columns - half), 'x', sca...]
    unnamed x10, waiting for transfers between devices: 63.4 us -> 0.16 us
    all_gather x1 -> x0, blocking collectives: 59.6 us -> none  [shards(): lax.all_gather(vectors.astype(jnp.bfloat16), ('dp', 'fsdp'), axis=1, tile...]
    all_gather x4 -> x2, waiting for transfers between devices: 120 us -> 65.7 us  [the longest x1 64.1 us: shards(): lax.all_gather(low_first, ('x', 'core', 'fsdp'), axis=0, tiled=True)]
    all_to_all x3 -> x11, waiting for transfers between devices: 21.6 us -> 74 us  [the longest x4 36.5 us: reduce_rows(): lax.all_to_all(second, 'fsdp', split_axis=0, concat_axis=0, tiled=True)]
    all_to_all x3 -> x11, starting transfers between devices: 10.6 us -> 49.8 us  [the longest x4 21 us: reduce_rows(): lax.all_to_all(second, 'fsdp', split_axis=0, concat_axis=0, tiled=True)]
    concatenate x1 -> x24, local copies, waits for them, and re-layouts: 4.2 us -> 33.6 us  [the longest x23 33.6 us: shards(): jnp.concatenate([attn_vector_grads, mlp_vector_grads], axis=0)]
  transfers between devices with their start and end apart: 12 -> 25, of which waited for: 12 -> 13; matrix products, arithmetic and copies ran while one was open for 6% -> 45% of each run, Pallas kernels for 0% -> 0%
where the time goes in v1:
time: 651 us; the launch traced here: 639 us
  matrix products  172 us (26%)
  local copies, waits for them, and re-layouts  142 us (22%)
  waiting for transfers between devices  140 us (22%)
  other arithmetic  118 us (18%)
  starting transfers between devices  51.3 us (8%)
  between operations  16.5 us (3%)
    all_gather x1, waiting for transfers between devices, shards(): lax.all_gather(low_first, ('x', 'core', 'fsdp'), axis=0, tiled=True)  64.1 us
    dot_general x8, matrix products, contract_first(): lax.dot_general(left, right, (((0,), (0,)), ((), ())), preferred_element_...  45.2 us
    unnamed x194, local copies, waits for them, and re-layouts  37.7 us
    all_to_all x4, waiting for transfers between devices, reduce_rows(): lax.all_to_all(second, 'fsdp', split_axis=0, concat_axis=0, tiled=True)  36.5 us
    concatenate x23, local copies, waits for them, and re-layouts, shards(): jnp.concatenate([attn_vector_grads, mlp_vector_grads], axis=0)  33.6 us
    dot_general x4, matrix products, contract_last(): lax.dot_general(left, right, (((1,), (1,)), ((), ())), preferred_element_...  32.2 us
    dot_general x1, matrix products, shards(): jnp.dot(normed_mid_low, gathered_up, preferred_element_type=jnp.float32)  26.4 us
    all_to_all x4, waiting for transfers between devices, reduce_rows(): lax.all_to_all(first.reshape(plane, shard, half), 'fsdp', split_axis=0, c...  23 us
  transfers between devices with their start and end apart: 25, of which 13 were waited for; matrix products, arithmetic and copies ran while one was open for 45% of the time, Pallas kernels for 0%

profile of v1, /device:TPU:0, one launch (start us, length us, event | category | flops | bytes accessed | tf_op | source)
XLA Modules:
  0.0 639.3 jit_solution(14151275481025426414)
XLA Ops:
  20.2 64.1 %all-gather.3.cloned.1.call-done = bf16[1024,4224]{1,0:T(8,128)(2,1)} async-done(((bf16[8,4224]{1,0:T(8,128)(2,1)}), bf16[1024,4224]{1,0:T(8,128)(2,1)}) %all-gather.3.cloned.1.call-update) | async-done | bytes 8650768 | tf_op jit(solution)/shard_map/all_gather | solution.py:127
  90.3 6.4 %add_convert_fusion.5 = bf16[512,3072]{1,0:T(8,128)(2,1)S(1)} fusion(bf16[512,1024]{1,0:T(8,128)(2,1)S(1)} %fusion.31, bf16[1024,4224]{1,0:T(8,128)(2,1)} %all-gather.3.cloned.1.call-done, f32[3072]{0:T(1024)S(1)} %pad_maximum_fusion.6), kind=kOutput, calls=%fused_computation.47 | convolution fusion | flops 3224371200 | bytes 10498048 | tf_op jit(solution)/shard_map/dot_general | solution.py:149
  112.1 5.1 constant_dynamic-slice_fusion.7
  120.9 10.0 %fusion.1 = (f32[16,512]{1,0:T(8,128)S(1)}, f32[16,512,512]{1,2,0:T(8,128)}) fusion(pred[512,512]{0,1:T(8,128)(4,1)S(1)} %fusion.50, bf16[512,16,64]{0,2,1:T(8,128)(2,1)} %bitcast.178, bf16[512,16,64]{0,2,1:T(8,128)(2,1)} %bitcast.180), kind=kOutput, calls=%fused_computation.11 | convolution fusion | flops 549445632 | bytes 19169280 | tf_op jit(solution)/shard_map/qhd,khd->hqk/dot_general | solution.py:164
  130.9 9.2 %fusion.20 = f32[16,512]{1,0:T(8,128)S(1)} fusion(f32[16,512]{1,0:T(8,128)S(1)} %get-tuple-element.134, f32[16,512,512]{1,2,0:T(8,128)} %get-tuple-element.135, pred[512,512]{0,1:T(8,128)(4,1)S(1)} %fusion.50), kind=kLoop, calls=%fused_computation.55 | loop fusion | flops 16769024 | bytes 17104896 | tf_op jit(solution)/shard_map/jvp()/reduce_sum | solution.py:161
  140.1 12.8 %convert_reduce_fusion = (f32[16,512]{1,0:T(8,128)}, pred[16,512,512]{1,2,0:T(32,128)(4,1)}, bf16[16,512,512]{1,2,0:T(8,128)(2,1)S(1)}) fusion(f32[16,512]{1,0:T(8,128)S(1)} %get-tuple-element.134, f32[16,512,512]{1,2,0:T(8,128)} %get-tuple-element.135, pred[512,512]{0,1:T(8,128)(4,1)S(1)} %fusion.50, f32[16,512]{1,0:T(8,128)S(1)} %fusion.20), kind=kLoop, calls=%fused_computation.4 | loop fusion | flops 33546240 | bytes 29720576 | tf_op jit(solution)/shard_map/jvp()/reduce_sum | solution.py:159
  165.8 26.4 %fusion.79 = (f32[512]{0:T(512)S(1)}, f32[512,4096]{1,0:T(8,128)S(1)}, f32[512,4096]{1,0:T(8,128)}, f32[512,4096]{1,0:T(8,128)}) fusion(f32[4096]{0:T(1024)} %bitcast.214, bf16[512,1024]{1,0:T(8,128)(2,1)S(1)} %add_convert_fusion.9, bf16[1024,8192]{1,0:T(8,128)(2,1)} %all-gather.5.cloned.1.call-done), kind=kOutput, calls=%fused_computation.237 | convolution fusion | flops 4433378816 | bytes 34621440 | tf_op jit(solution)/shard_map/dot_general | solution.py:182
  192.3 8.7 %multiply_reduce_fusion.2 = (f32[512]{0:T(512)S(1)}, f32[512]{0:T(512)S(1)}, f32[4096]{0:T(1024)}, f32[512,4096]{1,0:T(8,128)S(1)}) fusion(f32[512,4096]{1,0:T(8,128)S(1)} %get-tuple-element.97, f32[4096]{0:T(1024)S(1)} %copy-done.44, f32[512]{0:T(512)S(1)} %broadcast_multiply_fusion, bf16[512,1024]{1,0:T(8,128)(2,1)S(1)} %copy-done.22, ...), kind=kOutput, calls=%fused_computation.20 | convolution fusion | flops 4309642240 | bytes 26253312 | tf_op jit(solution)/shard_map/dot_general | solution.py:191
  205.1 12.4 %convert_reduce_fusion.1 = (f32[4096]{0:T(1024)}, bf16[512,4096]{1,0:T(8,128)(2,1)S(1)}, bf16[512,4096]{1,0:T(8,128)(2,1)}) fusion(f32[512,4096]{1,0:T(8,128)} %get-tuple-element.98, f32[512]{0:T(512)S(1)} %negate_multiply_fusion.4, f32[512]{0:T(512)S(1)} %get-tuple-element.132, f32[512,4096]{1,0:T(8,128)S(1)} %get-tuple-element.97, ...), kind=kLoop, calls=%fused_computation.16 | loop fusion | flops 58716160 | bytes 42016768 | tf_op jit(solution)/shard_map/reduce_sum | solution.py:202
  217.6 9.6 %multiply_reduce_fusion.4 = (f32[1024]{0:T(1024)}, f32[512]{0:T(512)S(1)}, f32[1024]{0:T(1024)}, f32[512,1024]{1,0:T(8,128)S(1)}) fusion(f32[512,1024]{1,0:T(8,128)S(1)} %copy-done.5, f32[512]{0:T(512)S(1)} %copy-done.70, f32[512]{0:T(512)S(1)} %copy-done.62, f32[1024]{0:T(1024)S(1)} %get-tuple-element.72, bf16[512,4096]{1,0:T(8,128)(2,1)S(1)} %get-tuple-element.84, ...), kind=kOutput, calls=%fused_computation.84 | convolution fusion | flops 4299159040 | bytes 16795648 | tf_op jit(solution)/shard_map/dot_general | solution.py:30
  239.7 13.1 %multiply_reduce_fusion = (f32[16,512]{1,0:T(8,128)S(1)}, f32[16,512,512]{1,2,0:T(8,128)}) fusion(f32[16,512]{1,0:T(8,128)S(1)} %copy-done.48, f32[16,512]{1,0:T(8,128)S(1)} %copy-done.32, f32[16,512,512]{1,2,0:T(8,128)} %get-tuple-element.135, pred[512,512]{0,1:T(8,128)(4,1)S(1)} %copy-done.13, bf16[512,16,64]{0,2,1:T(8,128)(2,1)S(1)} %bitcast.166, ...), kind=kOutput, calls=%fused_computation.6 | convolution fusion | flops 563077120 | bytes 37060672 | tf_op jit(solution)/shard_map/qhd,khd->hqk/dot_general | solution.py:215
  252.8 18.8 %fusion.75 = (f32[16,512]{1,0:T(8,128)S(1)}, f32[16,512,512]{1,2,0:T(8,128)}) fusion(f32[16,512]{1,0:T(8,128)S(1)} %copy-done.32, f32[16,512,512]{1,2,0:T(8,128)} %get-tuple-element.135, pred[512,512]{0,1:T(8,128)(4,1)S(1)} %copy-done.13, f32[16,512]{1,0:T(8,128)S(1)} %neg.33, f32[16,512,512]{1,2,0:T(8,128)} %get-tuple-element.144, f32[16,512]{1,0:T(8,128)S(1)} %copy-done.39), kind=kLoop, calls=%fused_computation.234 | loop fusion | flops 29351936 | bytes 50724864 | tf_op jit(solution)/shard_map/transpose(jvp())/reduce_sum | solution.py:160
  271.6 7.8 %multiply_convert_fusion = bf16[16,64,512]{2,1,0:T(8,128)(2,1)S(1)} fusion(bf16[512,16,64]{0,2,1:T(8,128)(2,1)S(1)} %bitcast.179, f32[16,512,512]{1,2,0:T(8,128)} %get-tuple-element.88, pred[16,512,512]{1,2,0:T(32,128)(4,1)S(1)} %copy-done.25, f32[16,512]{1,0:T(8,128)S(1)} %negate_divide_fusion, pred[512,512]{0,1:T(8,128)(4,1)S(1)} %copy-done.13), kind=kOutput, calls=%fused_computation.89 | convolution fusion | flops 554696704 | bytes 23363584 | tf_op jit(solution)/shard_map/hqk,qhd->khd/dot_general | solution.py:227
  279.5 9.7 %multiply_convert_fusion.1 = bf16[16,64,512]{2,1,0:T(8,128)(2,1)S(1)} fusion(bf16[512,16,64]{0,2,1:T(8,128)(2,1)S(1)} %bitcast.181, f32[16,512,512]{1,2,0:T(8,128)} %get-tuple-element.88, pred[16,512,512]{1,2,0:T(32,128)(4,1)S(1)} %copy-done.25, f32[16,512]{1,0:T(8,128)S(1)} %negate_divide_fusion, pred[512,512]{0,1:T(8,128)(4,1)S(1)} %copy-done.13), kind=kOutput, calls=%fused_computation.90 | convolution fusion | flops 554696704 | bytes 23363584 | tf_op jit(solution)/shard_map/hqk,khd->qhd/dot_general | solution.py:223
  289.2 7.5 %convolution_convert_fusion.2 = bf16[512,3072]{1,0:T(8,128)(2,1)} fusion(bf16[512,512]{0,1:T(8,128)(2,1)S(1)} %bitcast.200, bf16[512,1024]{0,1:T(8,128)(2,1)S(1)} %bitcast.174, bf16[512,1024]{0,1:T(8,128)(2,1)S(1)} %bitcast.189, bf16[512,1024]{0,1:T(8,128)(2,1)S(1)} %bitcast.193), kind=kOutput, calls=%fused_computation.54 | convolution fusion | flops 1621622784 | bytes 6815744 | tf_op jit(solution)/shard_map/dot_general | solution.py:36
  307.6 6.9 %constant_dynamic-slice_fusion = (bf16[512,4,1,128]{3,2,1,0:T(2,128)(2,1)}, bf16[512,4,1,128]{3,2,1,0:T(2,128)(2,1)}, bf16[512,4,1,128]{3,2,1,0:T(2,128)(2,1)}, bf16[512,4,1,128]{3,2,1,0:T(2,128)(2,1)}) fusion(bf16[512,4,2,128]{3,2,1,0:T(2,128)(2,1)S(1)} %reshape.438, s32[]{:T(128)S(6)} %select_n.34, s32[]{:T(128)S(6)} %select_n.33, ...), kind=kLoop, calls=%fused_computation.193 | loop fusion | bytes 4194312 | tf_op jit(solution)/shard_map/jit(dynamic_index_in_dim)/dynamic_slice | solution.py:50
  318.1 6.8 %convolution_convert_fusion.1 = bf16[512,4096]{1,0:T(8,128)(2,1)} fusion(bf16[512,512]{0,1:T(8,128)(2,1)} %bitcast.204, bf16[512,4096]{1,0:T(8,128)(2,1)} %copy-done.16), kind=kOutput, calls=%fused_computation.49 | convolution fusion | flops 2149580800 | bytes 8912896 | tf_op jit(solution)/shard_map/dot_general | solution.py:36
  346.0 6.6 %all-to-all-start.3 = ((bf16[16,4,8,512]{3,2,1,0:T(8,128)(2,1)}), bf16[16,4,8,512]{3,2,1,0:T(8,128)(2,1)}, u32[]{:S(2)}, u32[]{:S(2)}) async-start(bf16[16,4,8,512]{3,2,1,0:T(8,128)(2,1)} %bitcast.158), calls=%async_computation.6 | async-start | bytes 1048576 | tf_op jit(solution)/shard_map/all_to_all | solution.py:65
  352.6 6.8 %convolution_convert_fusion = bf16[512,4096]{1,0:T(8,128)(2,1)} fusion(bf16[512,512]{0,1:T(8,128)(2,1)} %bitcast.203, bf16[512,4096]{1,0:T(8,128)(2,1)} %get-tuple-element.102), kind=kOutput, calls=%fused_computation.48 | convolution fusion | flops 2149580800 | bytes 8912896 | tf_op jit(solution)/shard_map/dot_general | solution.py:36
  369.0 9.5 %fusion.73 = (f32[1024]{0:T(1024)}, f32[512]{0:T(512)}, f32[512,1024]{1,0:T(8,128)}) fusion(f32[1024]{0:T(1024)S(1)} %copy-done.50, f32[512]{0:T(512)S(1)} %copy-done.56, bf16[512,1024]{1,0:T(8,128)(2,1)S(1)} %copy-done.3, bf16[1024,4224]{1,0:T(8,128)(2,1)} %all-gather.3.cloned.1.call-done, bf16[512,1024]{0,1:T(8,128)(2,1)} %bitcast.175, ...), kind=kOutput, calls=%fused_computation.233 | convolution fusion | flops 3233806848 | bytes 12595200 | tf_op jit(solution)/shard_map/dot_general | solution.py:30
  380.4 7.9 %add_convert_fusion.1 = bf16[512,4096]{1,0:T(8,128)(2,1)} fusion(bf16[512,4096]{1,0:T(8,128)(2,1)} %collective-permute-done.2, bf16[512,512]{0,1:T(8,128)(2,1)} %bitcast.201, bf16[512,4096]{1,0:T(8,128)(2,1)} %copy-done.16), kind=kOutput, calls=%fused_computation.18 | convolution fusion | flops 2153775104 | bytes 13107200 | tf_op jit(solution)/shard_map/dot_general | solution.py:36
  458.3 5.7 all-to-all-start.8
  464.1 7.9 %add_convert_fusion = bf16[512,4096]{1,0:T(8,128)(2,1)} fusion(bf16[512,4096]{1,0:T(8,128)(2,1)} %collective-permute-done.3, bf16[512,512]{0,1:T(8,128)(2,1)} %bitcast.199, bf16[512,4096]{1,0:T(8,128)(2,1)} %get-tuple-element.102), kind=kOutput, calls=%fused_computation.17 | convolution fusion | flops 2153775104 | bytes 13107200 | tf_op jit(solution)/shard_map/dot_general | solution.py:36
  473.6 5.3 all-to-all-start.2
  487.0 5.6 all-to-all-start.5
  508.2 15.4 %all-to-all-done.5 = bf16[16,4,8,2048]{3,2,1,0:T(8,128)(2,1)} async-done(((bf16[16,4,8,2048]{3,2,1,0:T(8,128)(2,1)}), bf16[16,4,8,2048]{3,2,1,0:T(8,128)(2,1)}, u32[]{:S(2)}, u32[]{:S(2)}) %all-to-all-start.5) | async-done | bytes 2097184 | tf_op jit(solution)/shard_map/all_to_all | solution.py:65
  528.1 10.2 %add_convert_fusion.8 = bf16[512,1024]{1,0:T(8,128)(2,1)} fusion(f32[512,1024]{1,0:T(8,128)S(1)} %copy-done.6, bf16[512,4096]{1,0:T(8,128)(2,1)} %get-tuple-element.102, bf16[1024,8192]{1,0:T(8,128)(2,1)} %all-gather.5.cloned.1.call-done, f32[1024]{0:T(1024)S(1)} %copy-done.79), kind=kOutput, calls=%fused_computation.99 | convolution fusion | flops 4296540160 | bytes 15732736 | tf_op jit(solution)/shard_map/dot_general | solution.py:30
  544.9 12.6 %all-to-all-done.7 = bf16[16,4,8,2048]{3,2,1,0:T(8,128)(2,1)} async-done(((bf16[16,4,8,2048]{3,2,1,0:T(8,128)(2,1)}), bf16[16,4,8,2048]{3,2,1,0:T(8,128)(2,1)}, u32[]{:S(2)}, u32[]{:S(2)}) %all-to-all-start.7) | async-done | bytes 2097184 | tf_op jit(solution)/shard_map/all_to_all | solution.py:65
  577.4 8.0 %all-to-all-done.4 = bf16[16,8,2048]{2,1,0:T(8,128)(2,1)S(1)} async-done(((bf16[16,8,2048]{2,1,0:T(8,128)(2,1)}), bf16[16,8,2048]{2,1,0:T(8,128)(2,1)S(1)}, u32[]{:S(2)}, u32[]{:S(2)}) %all-to-all-start.4) | async-done | bytes 524320 | tf_op jit(solution)/shard_map/all_to_all | solution.py:60
  589.9 9.1 %all-to-all-done.6 = bf16[16,8,2048]{2,1,0:T(8,128)(2,1)S(1)} async-done(((bf16[16,8,2048]{2,1,0:T(8,128)(2,1)}), bf16[16,8,2048]{2,1,0:T(8,128)(2,1)S(1)}, u32[]{:S(2)}, u32[]{:S(2)}) %all-to-all-start.6) | async-done | bytes 524320 | tf_op jit(solution)/shard_map/all_to_all | solution.py:60
  608.2 5.3 all-to-all-done.9
  621.4 7.6 %all-to-all-done.10 = bf16[128,6,128]{2,1,0:T(8,128)(2,1)S(1)} async-done(((bf16[128,6,128]{2,1,0:T(8,128)(2,1)}), bf16[128,6,128]{2,1,0:T(8,128)(2,1)S(1)}, u32[]{:S(2)}, u32[]{:S(2)}) %all-to-all-start.10) | async-done | bytes 196640 | tf_op jit(solution)/shard_map/all_to_all | solution.py:289
  (397 shorter events, 263.9 us)
Async XLA Ops:
  7.2 607.3 %copy-start = (f32[1,6,128,128]{3,2,1,0:T(8,128)S(1)}, f32[1,6,128,128]{3,2,1,0:T(8,128)}, u32[]{:S(2)}) copy-start(f32[1,6,128,128]{3,2,1,0:T(8,128)} %param.33) | copy-start | bytes 1179652
  7.2 81.1 %copy-start.2 = (bf16[512,1024]{1,0:T(8,128)(2,1)S(1)}, bf16[512,1024]{1,0:T(8,128)(2,1)}, u32[]{:S(2)}) copy-start(bf16[512,1024]{1,0:T(8,128)(2,1)} %param.19) | copy-start | bytes 3145732
  7.2 77.1 %all-gather.3.cloned.1.call-start = ((), (), s32[]{:S(2)}) async-start(), calls=%async_computation.19 | async-start | bytes 8718336 | tf_op jit(solution)/shard_map/all_gather | solution.py:127
  10.4 155.5 %all-gather.5.cloned.1.call-start = ((), (), s32[]{:S(2)}) async-start(), calls=%async_computation.20 | async-start | bytes 16908288 | tf_op jit(solution)/shard_map/all_gather | solution.py:134
  12.9 460.6 %reduce-scatter.13.cloned.1.call-start = ((), (), s32[]{:S(2)}) async-start(), calls=%async_computation.23 | async-start | bytes 655360 | tf_op jit(solution)/shard_map/reduce_scatter | solution.py:59
  15.8 74.5 %copy-start.55 = (f32[512]{0:T(512)}, f32[512]{0:T(512)S(1)}, u32[]{:S(2)}) copy-start(f32[512]{0:T(512)S(1)} %broadcast_multiply_fusion.3) | copy-start | bytes 6148
  17.4 72.9 %copy-start.71 = (f32[512]{0:T(512)}, f32[512]{0:T(512)S(1)}, u32[]{:S(2)}) copy-start(f32[512]{0:T(512)S(1)} %fusion.33) | copy-start | bytes 6148
  17.4 72.9 %copy-start.63 = (f32[512]{0:T(512)}, f32[512]{0:T(512)S(1)}, u32[]{:S(2)}) copy-start(f32[512]{0:T(512)S(1)} %fusion.63) | copy-start | bytes 6148
  17.6 122.5 %copy-start.12 = (pred[512,512]{0,1:T(8,128)(4,1)}, pred[512,512]{0,1:T(8,128)(4,1)S(1)}, u32[]{:S(2)}) copy-start(pred[512,512]{0,1:T(8,128)(4,1)S(1)} %fusion.50) | copy-start | bytes 786436
  296.7 31.5 %collective-permute-start = (bf16[512,3072]{1,0:T(8,128)(2,1)}, bf16[512,3072]{1,0:T(8,128)(2,1)}, u32[]{:S(2)}, u32[]{:S(2)}) collective-permute-start(bf16[512,3072]{1,0:T(8,128)(2,1)} %convolution_convert_fusion.2), channel_id=1, source_target_pairs={{0,16},{16,0},{1,17},{17,1},{2,18},{18,2},{3,19},{19,3},{4,20},{20... | collective-permute-start | bytes 9437192 | tf_op jit(solution)/shard_map/ppermute | solution.py:55
  299.5 25.6 %collective-permute-start.1 = (bf16[512,1024]{1,0:T(8,128)(2,1)}, bf16[512,1024]{1,0:T(8,128)(2,1)}, u32[]{:S(2)}, u32[]{:S(2)}) collective-permute-start(bf16[512,1024]{1,0:T(8,128)(2,1)} %convolution_convert_fusion.4), channel_id=1, source_target_pairs={{0,16},{16,0},{1,17},{17,1},{2,18},{18,2},{3,19},{19,3},{4,20},{20... | collective-permute-start | bytes 3145736 | tf_op jit(solution)/shard_map/ppermute | solution.py:55
  324.9 55.5 %collective-permute-start.2 = (bf16[512,4096]{1,0:T(8,128)(2,1)}, bf16[512,4096]{1,0:T(8,128)(2,1)}, u32[]{:S(2)}, u32[]{:S(2)}) collective-permute-start(bf16[512,4096]{1,0:T(8,128)(2,1)} %convolution_convert_fusion.1), channel_id=1, source_target_pairs={{0,16},{16,0},{1,17},{17,1},{2,18},{18,2},{3,19},{19,3},{4,20},{20... | collective-permute-start | bytes 12582920 | tf_op jit(solution)/shard_map/ppermute | solution.py:55
  328.2 229.3 %reduce-scatter.9.cloned.1.call-start = ((), (), s32[]{:S(2)}) async-start(), calls=%async_computation.21 | async-start | bytes 1966080 | tf_op jit(solution)/shard_map/reduce_scatter | solution.py:59
  346.0 18.6 %all-to-all-start.3 = ((bf16[16,4,8,512]{3,2,1,0:T(8,128)(2,1)}), bf16[16,4,8,512]{3,2,1,0:T(8,128)(2,1)}, u32[]{:S(2)}, u32[]{:S(2)}) async-start(bf16[16,4,8,512]{3,2,1,0:T(8,128)(2,1)} %bitcast.158), calls=%async_computation.6 | async-start | bytes 1048576 | tf_op jit(solution)/shard_map/all_to_all | solution.py:65
  359.4 104.6 %collective-permute-start.3 = (bf16[512,4096]{1,0:T(8,128)(2,1)}, bf16[512,4096]{1,0:T(8,128)(2,1)}, u32[]{:S(2)}, u32[]{:S(2)}) collective-permute-start(bf16[512,4096]{1,0:T(8,128)(2,1)} %convolution_convert_fusion), channel_id=1, source_target_pairs={{0,16},{16,0},{1,17},{17,1},{2,18},{18,2},{3,19},{19,3},{4,20},{20... | collective-permute-start | bytes 12582920 | tf_op jit(solution)/shard_map/ppermute | solution.py:55
  364.6 28.4 %all-to-all-start.1 = ((bf16[16,4,8,1536]{3,2,1,0:T(8,128)(2,1)}), bf16[16,4,8,1536]{3,2,1,0:T(8,128)(2,1)}, u32[]{:S(2)}, u32[]{:S(2)}) async-start(bf16[16,4,8,1536]{3,2,1,0:T(8,128)(2,1)} %bitcast.172), calls=%async_computation.2 | async-start | bytes 3145728 | tf_op jit(solution)/shard_map/all_to_all | solution.py:65
  369.0 193.3 %reduce-scatter.15.cloned.1.call-start = ((), (), s32[]{:S(2)}) async-start(), calls=%async_computation.24 | async-start | bytes 81920 | tf_op jit(solution)/shard_map/reduce_scatter | solution.py:67
  380.3 190.4 %reduce-scatter.11.cloned.1.call-start = ((), (), s32[]{:S(2)}) async-start(), calls=%async_computation.22 | async-start | bytes 245760 | tf_op jit(solution)/shard_map/reduce_scatter | solution.py:67
  395.3 176.3 %reduce-scatter.17.cloned.1.call-start = ((), (), s32[]{:S(2)}) async-start(), calls=%async_computation.25 | async-start | bytes 2621440 | tf_op jit(solution)/shard_map/reduce_scatter | solution.py:59
  458.3 15.2 %all-to-all-start.8 = ((f32[128,1,192]{2,1,0:T(1,128)}), f32[128,1,192]{2,1,0:T(1,128)}, u32[]{:S(2)}, u32[]{:S(2)}) async-start(f32[128,1,192]{2,1,0:T(1,128)} %copy.108), calls=%async_computation.16 | async-start | bytes 262144 | tf_op jit(solution)/shard_map/all_to_all | solution.py:267
  473.6 13.4 %all-to-all-start.2 = ((bf16[16,8,512]{2,1,0:T(8,128)(2,1)}), bf16[16,8,512]{2,1,0:T(8,128)(2,1)}, u32[]{:S(2)}, u32[]{:S(2)}) async-start(bf16[16,8,512]{2,1,0:T(8,128)(2,1)} %bitcast.212), calls=%async_computation.5 | async-start | bytes 262144 | tf_op jit(solution)/shard_map/all_to_all | solution.py:60
  478.9 98.4 %reduce-scatter.21.cloned.1.call-start = ((), (), s32[]{:S(2)}) async-start(), calls=%async_computation.27 | async-start | bytes 2621440 | tf_op jit(solution)/shard_map/reduce_scatter | solution.py:59
  487.0 36.6 %all-to-all-start.5 = ((bf16[16,4,8,2048]{3,2,1,0:T(8,128)(2,1)}), bf16[16,4,8,2048]{3,2,1,0:T(8,128)(2,1)}, u32[]{:S(2)}, u32[]{:S(2)}) async-start(bf16[16,4,8,2048]{3,2,1,0:T(8,128)(2,1)} %bitcast.156), calls=%async_computation.10 | async-start | bytes 4194304 | tf_op jit(solution)/shard_map/all_to_all | solution.py:65
  523.6 33.9 %all-to-all-start.7 = ((bf16[16,4,8,2048]{3,2,1,0:T(8,128)(2,1)}), bf16[16,4,8,2048]{3,2,1,0:T(8,128)(2,1)}, u32[]{:S(2)}, u32[]{:S(2)}) async-start(bf16[16,4,8,2048]{3,2,1,0:T(8,128)(2,1)} %bitcast.169), calls=%async_computation.14 | async-start | bytes 4194304 | tf_op jit(solution)/shard_map/all_to_all | solution.py:65
  528.0 61.0 %reduce-scatter.19.cloned.1.call-start = ((), (), s32[]{:S(2)}) async-start(), calls=%async_computation.26 | async-start | bytes 327680 | tf_op jit(solution)/shard_map/reduce_scatter | solution.py:67
  539.5 74.0 %copy-start.41 = (f32[1,6,128,128]{3,2,1,0:T(8,128)S(1)}, f32[1,6,128,128]{3,2,1,0:T(8,128)}, u32[]{:S(2)}) copy-start(f32[1,6,128,128]{3,2,1,0:T(8,128)} %param.30) | copy-start | bytes 1179652
  557.5 13.2 %all-to-all-start = ((bf16[16,8,1536]{2,1,0:T(8,128)(2,1)}), bf16[16,8,1536]{2,1,0:T(8,128)(2,1)S(1)}, u32[]{:S(2)}, u32[]{:S(2)}) async-start(bf16[16,8,1536]{2,1,0:T(8,128)(2,1)} %bitcast.209), calls=%async_computation.1 | async-start | bytes 786432 | tf_op jit(solution)/shard_map/all_to_all | solution.py:60
  561.0 38.1 %reduce-scatter.23.cloned.1.call-start = ((), (), s32[]{:S(2)}) async-start(), calls=%async_computation.28 | async-start | bytes 327680 | tf_op jit(solution)/shard_map/reduce_scatter | solution.py:67
  571.6 13.8 %all-to-all-start.4 = ((bf16[16,8,2048]{2,1,0:T(8,128)(2,1)}), bf16[16,8,2048]{2,1,0:T(8,128)(2,1)S(1)}, u32[]{:S(2)}, u32[]{:S(2)}) async-start(bf16[16,8,2048]{2,1,0:T(8,128)(2,1)} %bitcast.205), calls=%async_computation.9 | async-start | bytes 1048576 | tf_op jit(solution)/shard_map/all_to_all | solution.py:60
  585.4 13.7 %all-to-all-start.6 = ((bf16[16,8,2048]{2,1,0:T(8,128)(2,1)}), bf16[16,8,2048]{2,1,0:T(8,128)(2,1)S(1)}, u32[]{:S(2)}, u32[]{:S(2)}) async-start(bf16[16,8,2048]{2,1,0:T(8,128)(2,1)} %bitcast.206), calls=%async_computation.13 | async-start | bytes 1048576 | tf_op jit(solution)/shard_map/all_to_all | solution.py:60
  601.7 11.8 %all-to-all-start.9 = ((bf16[8,96,128]{2,0,1:T(8,128)(2,1)}), bf16[8,96,128]{2,0,1:T(8,128)(2,1)S(1)}, u32[]{:S(2)}, u32[]{:S(2)}) async-start(bf16[8,96,128]{2,0,1:T(8,128)(2,1)} %select_bitcast_fusion), calls=%async_computation.17 | async-start | bytes 393216 | tf_op jit(solution)/shard_map/all_to_all | solution.py:283
  616.8 12.2 %all-to-all-start.10 = ((bf16[128,6,128]{2,1,0:T(8,128)(2,1)}), bf16[128,6,128]{2,1,0:T(8,128)(2,1)S(1)}, u32[]{:S(2)}, u32[]{:S(2)}) async-start(bf16[128,6,128]{2,1,0:T(8,128)(2,1)} %copy.112), calls=%async_computation.18 | async-start | bytes 524288 | tf_op jit(solution)/shard_map/all_to_all | solution.py:289
  (78 other events, 1281.8 us)
Sparse Core Ops, SparseCore 0:
  11.6 72.6 all-gather.2
  88.0 77.7 all-gather.4
  328.3 20.8 reduce-scatter.12
  351.4 25.4 reduce-scatter.8
  380.4 20.2 reduce-scatter.14
  403.1 20.2 reduce-scatter.10
  425.8 29.3 reduce-scatter.16
  483.9 31.0 reduce-scatter.20
  542.4 22.0 reduce-scatter.18
  567.4 21.2 reduce-scatter.22

commit v2 on v0

v2 whole, which is shorter than its diff:
```python
import functools
import math

import jax
import jax.numpy as jnp
from jax import lax
from jax.experimental import pallas as pl
from jax.experimental.pallas import tpu as pltpu
from jax.sharding import PartitionSpec as P

TILE = 128
EPS = 1e-05
DECAY = 0.5
RATE_MATRIX = 0.1
RATE_VECTOR = 0.3
HIGHEST = lax.Precision.HIGHEST
HEAD_AT = 24
VMEM_BYTES = 56 * 1024 * 1024
F32 = jnp.float32
BF16 = jnp.bfloat16


def dot_nn(left, right):
    return lax.dot_general(left, right, (((1,), (0,)), ((), ())), preferred_element_type=F32)


def dot_nt(left, right):
    return lax.dot_general(left, right, (((1,), (1,)), ((), ())), preferred_element_type=F32)


def dot_tn(left, right):
    return lax.dot_general(left, right, (((0,), (0,)), ((), ())), preferred_element_type=F32)


def row_stats(values):
    mean = jnp.mean(values, axis=-1, keepdims=True)
    centered = values - mean
    spread = lax.rsqrt(jnp.mean(centered * centered, axis=-1, keepdims=True) + EPS)
    return centered, spread


def norm_back(scaled_grad, unit, spread):
    mean_grad = jnp.mean(scaled_grad, axis=-1, keepdims=True)
    mean_both = jnp.mean(scaled_grad * unit, axis=-1, keepdims=True)
    return spread * (scaled_grad - mean_grad - unit * mean_both)


def lane_sum(values):
    total = values[:, :TILE]
    for at in range(TILE, values.shape[1], TILE):
        total = total + values[:, at : at + TILE]
    return total


def call(body, grid, in_specs, out_specs, out_shape, scratch=(), flops=0, bytes_accessed=0, scalars=0):
    return pl.pallas_call(
        body,
        out_shape=out_shape,
        grid_spec=pltpu.PrefetchScalarGridSpec(
            num_scalar_prefetch=scalars,
            grid=grid,
            in_specs=in_specs,
            out_specs=out_specs,
            scratch_shapes=list(scratch),
        ),
        compiler_params=pltpu.CompilerParams(vmem_limit_bytes=VMEM_BYTES),
        cost_estimate=pl.CostEstimate(
            flops=flops, bytes_accessed=bytes_accessed, transcendentals=0
        ),
    )


def whole(shape):
    return pl.BlockSpec(shape, lambda *_: (0,) * len(shape))


def after(*arrays):
    return [pl.BlockSpec(memory_space=pl.ANY) for _ in arrays]


def split_parity(values):
    blocks = [values[:, at : at + TILE] for at in range(0, values.shape[1], TILE)]
    return jnp.concatenate(blocks[0::2], axis=1), jnp.concatenate(blocks[1::2], axis=1)


def join_parity(even, odd):
    blocks = []
    for at in range(0, even.shape[1], TILE):
        blocks += [even[:, at : at + TILE], odd[:, at : at + TILE]]
    return jnp.concatenate(blocks, axis=1)


def project_body(
    core, tokens, vectors, own_qk, other_qk, own_vo, other_vo, normed, projected, parts
):
    part = pl.program_id(0)

    @pl.when(part == 0)
    def _():
        centered, spread = row_stats(tokens[...].astype(F32))
        low = (centered * spread * vectors[0:1, :] + vectors[1:2, :]).astype(BF16)
        normed[...] = low
        parts[0], parts[1] = split_parity(low)

    gate_q = jnp.where(part == 0, 1.0, 0.0).astype(F32)
    gate_v = jnp.where(part == 2, 1.0, 0.0).astype(F32)
    bias = gate_q * vectors[2:3, :] + gate_v * vectors[3:4, :]
    me = core[0]

    @pl.when(part < 2)
    def _():
        projected[...] = (
            dot_nn(parts[me], own_qk[...]) + dot_nn(parts[1 - me], other_qk[...]) + bias
        ).astype(BF16)

    @pl.when(part == 2)
    def _():
        projected[...] = (
            dot_nn(parts[me], own_vo[...]) + dot_nn(parts[1 - me], other_vo[...]) + bias
        ).astype(BF16)


def project(core, tokens, vectors, weights):
    rows, width = tokens.shape
    parts = 3
    third = pl.BlockSpec((width // 2, width), lambda part, *_: (0, jnp.minimum(part, 1)))
    last = pl.BlockSpec((width // 2, width), lambda part, *_: (0, 0))
    return call(
        project_body,
        (parts,),
        [whole((rows, width)), whole(vectors.shape), third, third, last, last],
        [whole((rows, width)), pl.BlockSpec((rows, width), lambda part, *_: (0, part))],
        [
            jax.ShapeDtypeStruct((rows, width), BF16),
            jax.ShapeDtypeStruct((rows, parts * width), BF16),
        ],
        scratch=[pltpu.VMEM((2, rows, width // 2), BF16)],
        flops=2 * rows * width * width * parts,
        bytes_accessed=2 * width * width * parts,
        scalars=1,
    )(core, tokens, vectors, *weights)


def attend_body(length, scales, queries, keys, values, mixed, scaled, weights):
    rows = queries.shape[0]
    head_dim = TILE // 2
    pair = pl.program_id(0)
    block = rows // 2
    lane = lax.broadcasted_iota(jnp.int32, (rows, TILE), 1)
    spot = lax.broadcasted_iota(jnp.int32, (rows, TILE), 0)
    hidden_key = jnp.where(spot < length[0], 0.0, -1e30).astype(BF16)
    one = jnp.ones((rows, TILE), BF16)
    zero = jnp.zeros((rows, TILE), BF16)
    query = queries[...] * jnp.asarray(1.0 / math.sqrt(head_dim), BF16)
    key = keys[...]
    value = values[...]
    causal = lax.broadcasted_iota(jnp.int32, (block, block), 1) <= lax.broadcasted_iota(
        jnp.int32, (block, block), 0
    )
    total = [jnp.zeros((block, TILE), F32) for _ in range(2)]
    for head in range(2):
        mine = (lane < head_dim) if head == 0 else (lane >= head_dim)
        spare = lane == (head_dim if head == 0 else 0)
        query_one = jnp.where(mine, query, jnp.where(spare, one, zero))
        key_one = jnp.where(mine, key, jnp.where(spare, hidden_key, zero))
        value_one = jnp.where(mine, value, zero)
        for part in range(2):
            seen = (part + 1) * block
            score = dot_nt(query_one[part * block : seen], key_one[:seen])
            last = jnp.where(causal, score[:, part * block :], -1e30)
            score = last if part == 0 else jnp.concatenate([score[:, :block], last], axis=1)
            top = jnp.max(score, axis=1, keepdims=True)
            grown = jnp.exp(score - top)
            share = (grown * (1.0 / jnp.sum(grown, axis=1, keepdims=True))).astype(BF16)
            if part == 0:
                weights[head, :, :block] = share
            else:
                weights[head, :, block:] = share
            total[part] = total[part] + dot_nn(share, value_one[:seen])
    scale_row = jnp.where(
        lax.broadcasted_iota(jnp.int32, (1, TILE), 1) < head_dim,
        scales[2 * pair],
        scales[2 * pair + 1],
    )
    for part in range(2):
        mixed[part * block : (part + 1) * block, :] = total[part]
        scaled[part * block : (part + 1) * block, :] = (total[part] * scale_row).astype(BF16)


def attend(length, scales, projected):
    rows, width3 = projected.shape
    width = width3 // 3
    pairs = width // TILE
    block = rows // 2
    return call(
        attend_body,
        (pairs,),
        [
            pl.BlockSpec((rows, TILE), lambda pair, *_: (0, pair)),
            pl.BlockSpec((rows, TILE), lambda pair, *_: (0, pairs + pair)),
            pl.BlockSpec((rows, TILE), lambda pair, *_: (0, 2 * pairs + pair)),
        ],
        [
            pl.BlockSpec((rows, TILE), lambda pair, *_: (0, pair)),
            pl.BlockSpec((rows, TILE), lambda pair, *_: (0, pair)),
            pl.BlockSpec((2, block, 3 * block), lambda pair, *_: (pair, 0, 0)),
        ],
        [
            jax.ShapeDtypeStruct((rows, width), F32),
            jax.ShapeDtypeStruct((rows, width), BF16),
            jax.ShapeDtypeStruct((2 * pairs, block, 3 * block), BF16),
        ],
        flops=4 * rows * rows * width,
        bytes_accessed=20 * rows * width,
        scalars=2,
    )(length, scales, projected, projected, projected)


def attend_back_body(queries, keys, values, mixed, grads, weights, _, out):
    rows = queries.shape[0]
    head_dim = TILE // 2
    block = rows // 2
    lane = lax.broadcasted_iota(jnp.int32, (rows, TILE), 1)
    zero = jnp.zeros((rows, TILE), BF16)
    query, key, value, grad = queries[...], keys[...], values[...], grads[...]
    both = grad.astype(F32) * mixed[...]
    q_total = [jnp.zeros((block, TILE), F32) for _ in range(2)]
    k_total = [jnp.zeros((block, TILE), F32) for _ in range(2)]
    v_total = [jnp.zeros((block, TILE), F32) for _ in range(2)]
    for head in range(2):
        mine = (lane < head_dim) if head == 0 else (lane >= head_dim)
        query_one = jnp.where(mine, query, zero)
        key_one = jnp.where(mine, key, zero)
        grad_one = jnp.where(mine, grad, zero)
        delta = jnp.sum(jnp.where(mine, both, 0.0), axis=1, keepdims=True)
        for part in range(2):
            at = part * block
            seen = at + block
            share = weights[head, :, :block] if part == 0 else weights[head, :, block:]
            into = dot_nt(grad_one[at:seen], value[:seen])
            slope = (share.astype(F32) * (into - delta[at:seen])).astype(BF16)
            q_total[part] = q_total[part] + dot_nn(slope, key_one[:seen])
            k_new = dot_tn(slope, query_one[at:seen])
            v_new = dot_tn(share, grad_one[at:seen])
            for into_part in range(part + 1):
                cut = slice(into_part * block, (into_part + 1) * block)
                k_total[into_part] = k_total[into_part] + k_new[cut]
                v_total[into_part] = v_total[into_part] + v_new[cut]
    root = 1.0 / math.sqrt(head_dim)
    for part in range(2):
        cut = slice(part * block, (part + 1) * block)
        out[0, cut, :] = (q_total[part] * root).astype(BF16)
        out[1, cut, :] = (k_total[part] * root).astype(BF16)
        out[2, cut, :] = v_total[part].astype(BF16)


def attend_back(projected, mixed, grads, weights, wait):
    rows, width3 = projected.shape
    width = width3 // 3
    pairs = width // TILE
    block = rows // 2
    by_pair = pl.BlockSpec((rows, TILE), lambda pair, *_: (0, pair))
    return call(
        attend_back_body,
        (pairs,),
        [
            by_pair,
            pl.BlockSpec((rows, TILE), lambda pair, *_: (0, pairs + pair)),
            pl.BlockSpec((rows, TILE), lambda pair, *_: (0, 2 * pairs + pair)),
            by_pair,
            by_pair,
            pl.BlockSpec((2, block, 3 * block), lambda pair, *_: (pair, 0, 0)),
            *after(wait),
        ],
        pl.BlockSpec((3, rows, TILE), lambda pair, *_: (0, 0, pair)),
        jax.ShapeDtypeStruct((3, rows, width), BF16),
        flops=10 * rows * rows * width,
        bytes_accessed=24 * rows * width,
    )(projected, projected, projected, mixed, grads, weights, wait)


def branch_body(core, scaled, own, other, tokens, vectors, branch, attended, normed, parts):
    parts[0], parts[1] = split_parity(scaled[...])
    me = core[0]
    value = dot_nn(parts[me], own[...]) + dot_nn(parts[1 - me], other[...]) + vectors[6:7, :]
    branch[...] = value
    centered, spread = row_stats(value)
    total = tokens[...].astype(F32) + centered * spread * vectors[4:5, :] + vectors[5:6, :]
    attended[...] = total
    centered, spread = row_stats(total)
    normed[...] = (centered * spread * vectors[7:8, :] + vectors[8:9, :]).astype(BF16)


def branch_out(core, scaled, weights, tokens, vectors):
    rows, width = scaled.shape
    block = rows // 4
    by_row = pl.BlockSpec((block, width), lambda at, *_: (at, 0))
    fourth = pl.BlockSpec((width // 2, width), lambda at, *_: (0, 1))
    return call(
        branch_body,
        (rows // block,),
        [by_row, fourth, fourth, by_row, whole(vectors.shape)],
        [by_row, by_row, by_row],
        [
            jax.ShapeDtypeStruct((rows, width), F32),
            jax.ShapeDtypeStruct((rows, width), F32),
            jax.ShapeDtypeStruct((rows, width), BF16),
        ],
        scratch=[pltpu.VMEM((2, block, width // 2), BF16)],
        flops=2 * rows * width * width,
        bytes_accessed=2 * width * width + 14 * rows * width,
        scalars=1,
    )(core, scaled, *weights[2:], tokens, vectors)


def branch_back_body(
    core, grad_attended, branch, own, other, mixed, scales, vectors, _, grad_branch, grad_mixed, sums, parts
):
    @pl.when(pl.program_id(0) == 0)
    def _():
        sums[...] = jnp.zeros_like(sums)

    grad = grad_attended[...]
    centered, spread = row_stats(branch[...])
    unit = centered * spread
    low = norm_back(grad * vectors[4:5, :], unit, spread).astype(BF16)
    grad_branch[...] = low
    me = core[0]
    parts[me] = dot_nt(low, own[...])
    parts[1 - me] = dot_nt(low, other[...])
    grad_scaled = join_parity(parts[0], parts[1])
    grad_mixed[...] = (grad_scaled * scales[0:1, :]).astype(BF16)
    sums[0:1, :] += jnp.sum(grad * unit, axis=0, keepdims=True)
    sums[1:2, :] += jnp.sum(grad, axis=0, keepdims=True)
    sums[2:3, :] += jnp.sum(low.astype(F32), axis=0, keepdims=True)
    sums[3:4, :] += jnp.sum(grad_scaled * mixed[...], axis=0, keepdims=True)


def branch_back(core, grad_attended, branch, weights, mixed, scales, vectors, wait):
    rows, width = branch.shape
    block = rows // 4
    by_row = pl.BlockSpec((block, width), lambda at, *_: (at, 0))
    fourth = pl.BlockSpec((width // 2, width), lambda at, *_: (0, 1))
    return call(
        branch_back_body,
        (rows // block,),
        [
            by_row,
            by_row,
            fourth,
            fourth,
            by_row,
            whole(scales.shape),
            whole(vectors.shape),
            *after(wait),
        ],
        [by_row, by_row, whole((8, width))],
        [
            jax.ShapeDtypeStruct((rows, width), BF16),
            jax.ShapeDtypeStruct((rows, width), BF16),
            jax.ShapeDtypeStruct((8, width), F32),
        ],
        scratch=[pltpu.VMEM((2, block, width // 2), F32)],
        flops=2 * rows * width * width,
        bytes_accessed=2 * width * width + 16 * rows * width,
        scalars=1,
    )(core, grad_attended, branch, *weights[2:], mixed, scales, vectors, wait)


def forward_ffn_body(
    steps, normed, attended, vectors, rows_of, up, down, output, top, kept, slope, stats, held, total, sums
):
    at = pl.program_id(0)
    width = held.shape[2]

    @pl.when(at == 0)
    def _():
        sums[...] = jnp.zeros_like(sums)

    @pl.when(at < steps)
    def _():
        hidden = dot_nn(normed[...], up[...]) + rows_of[0:1, :]
        cdf = 0.5 + 0.5 * lax.erf(hidden * math.sqrt(0.5))
        value = hidden * cdf
        slope[...] = (
            cdf + hidden * (jnp.exp(-0.5 * hidden * hidden) * (1.0 / math.sqrt(2.0 * math.pi)))
        ).astype(BF16)
        held[at] = value
        kept[...] = value.astype(BF16)
        sums[...] += lane_sum(value)

    @pl.when(at == steps)
    def _():
        count = steps * width
        mean = jnp.sum(sums[...], axis=1, keepdims=True) * (1.0 / count)
        square = jnp.zeros(sums.shape, F32)
        for block in range(steps):
            centered = held[block] - mean
            square = square + lane_sum(centered * centered)
        spread = lax.rsqrt(jnp.sum(square, axis=1, keepdims=True) * (1.0 / count) + EPS)
        stats[:, :TILE] = jnp.broadcast_to(mean, sums.shape)
        stats[:, TILE:] = jnp.broadcast_to(spread, sums.shape)
        total[...] = attended[...] + vectors[21:22, :]

    @pl.when(at >= steps)
    def _():
        mean = stats[:, 0:1]
        spread = stats[:, TILE : TILE + 1]
        value = held[at - steps]
        low = ((value - mean) * spread * rows_of[1:2, :] + rows_of[2:3, :]).astype(BF16)
        top[...] = low
        total[...] += dot_nt(low, down[...])

    @pl.when(at == 2 * steps - 1)
    def _():
        output[...] = total[...].astype(BF16)


def forward_ffn(normed, attended, vectors, wide_rows, both):
    rows, width = attended.shape
    hidden = both.shape[1] // 2
    block = 1024
    steps = hidden // block
    early = lambda at: (0, jnp.minimum(at, steps - 1))
    late = lambda at: (0, jnp.maximum(at - steps, 0))
    return call(
        functools.partial(forward_ffn_body, steps),
        (2 * steps,),
        [
            whole((rows, width)),
            whole((rows, width)),
            whole(vectors.shape),
            pl.BlockSpec((8, block), lambda at: (0, lax.rem(at, steps))),
            pl.BlockSpec((width, block), early),
            pl.BlockSpec((width, block), lambda at: (0, steps + jnp.maximum(at - steps, 0))),
        ],
        [
            whole((rows, width)),
            pl.BlockSpec((rows, block), late),
            pl.BlockSpec((rows, block), early),
            pl.BlockSpec((rows, block), early),
            whole((rows, 2 * TILE)),
        ],
        [
            jax.ShapeDtypeStruct((rows, width), BF16),
            jax.ShapeDtypeStruct((rows, hidden), BF16),
            jax.ShapeDtypeStruct((rows, hidden), BF16),
            jax.ShapeDtypeStruct((rows, hidden), BF16),
            jax.ShapeDtypeStruct((rows, 2 * TILE), F32),
        ],
        scratch=[
            pltpu.VMEM((steps, rows, block), F32),
            pltpu.VMEM((rows, width), F32),
            pltpu.VMEM((rows, TILE), F32),
        ],
        flops=4 * rows * width * hidden,
        bytes_accessed=4 * width * hidden + 6 * rows * hidden,
    )(normed, attended, vectors, wide_rows, both, both)


def backward_ffn_body(
    steps,
    upstream,
    attended,
    vectors,
    rows_of,
    stats,
    kept,
    slope,
    down,
    up,
    _,
    grad_attended,
    grad_hidden,
    wide_sums,
    sums,
    held,
    total,
    first,
    second,
):
    at = pl.program_id(0)
    count = steps * held.shape[2]
    mean = stats[:, 0:1]
    spread = stats[:, TILE : TILE + 1]

    @pl.when(at == 0)
    def _():
        first[...] = jnp.zeros_like(first)
        second[...] = jnp.zeros_like(second)
        total[...] = jnp.zeros_like(total)
        wide_sums[...] = jnp.zeros_like(wide_sums)

    @pl.when(at < steps)
    def _():
        grad = dot_nn(upstream[...], down[...])
        unit = (kept[...].astype(F32) - mean) * spread
        both = grad * unit
        wide_sums[at, 0:1, :] = jnp.sum(both, axis=0, keepdims=True)
        wide_sums[at, 1:2, :] = jnp.sum(grad, axis=0, keepdims=True)
        gain = rows_of[1:2, :]
        held[at] = grad * gain
        first[...] += lane_sum(grad * gain)
        second[...] += lane_sum(both * gain)

    @pl.when(at == steps)
    def _():
        scale = 1.0 / count
        first[...] = jnp.broadcast_to(
            jnp.sum(first[...], axis=1, keepdims=True) * scale, first.shape
        )
        second[...] = jnp.broadcast_to(
            jnp.sum(second[...], axis=1, keepdims=True) * scale, second.shape
        )

    @pl.when(at >= steps)
    def _():
        unit = (kept[...].astype(F32) - mean) * spread
        grad = spread * (held[at - steps] - first[:, 0:1] - unit * second[:, 0:1])
        low = (grad * slope[...].astype(F32)).astype(BF16)
        grad_hidden[...] = low
        wide_sums[at - steps, 2:3, :] = jnp.sum(low.astype(F32), axis=0, keepdims=True)
        total[...] += dot_nt(low, up[...])

    @pl.when(at == 2 * steps - 1)
    def _():
        grad = total[...]
        centered, mid_spread = row_stats(attended[...])
        unit = centered * mid_spread
        top = upstream[...].astype(F32)
        grad_attended[...] = top + norm_back(grad * vectors[7:8, :], unit, mid_spread)
        sums[0:1, :] = jnp.sum(grad * unit, axis=0, keepdims=True)
        sums[1:2, :] = jnp.sum(grad, axis=0, keepdims=True)
        sums[2:3, :] = jnp.sum(top, axis=0, keepdims=True)
        sums[3:8, :] = jnp.zeros((5, sums.shape[1]), F32)


def backward_ffn(upstream, attended, vectors, wide_rows, stats, kept, slope, both, wait):
    rows, width = attended.shape
    hidden = both.shape[1] // 2
    block = 1024
    steps = hidden // block
    late = lambda at: (0, jnp.maximum(at - steps, 0))
    turn = lambda at: (0, lax.rem(at, steps))
    return call(
        functools.partial(backward_ffn_body, steps),
        (2 * steps,),
        [
            whole((rows, width)),
            whole((rows, width)),
            whole(vectors.shape),
            pl.BlockSpec((8, block), turn),
            whole((rows, 2 * TILE)),
            pl.BlockSpec((rows, block), turn),
            pl.BlockSpec((rows, block), late),
            pl.BlockSpec((width, block), lambda at: (0, steps + jnp.minimum(at, steps - 1))),
            pl.BlockSpec((width, block), late),
            *after(wait),
        ],
        [
            whole((rows, width)),
            pl.BlockSpec((rows, block), late),
            whole((steps, 8, block)),
            whole((8, width)),
        ],
        [
            jax.ShapeDtypeStruct((rows, width), F32),
            jax.ShapeDtypeStruct((rows, hidden), BF16),
            jax.ShapeDtypeStruct((steps, 8, block), F32),
            jax.ShapeDtypeStruct((8, width), F32),
        ],
        scratch=[
            pltpu.VMEM((steps, rows, block), F32),
            pltpu.VMEM((rows, width), F32),
            pltpu.VMEM((rows, TILE), F32),
            pltpu.VMEM((rows, TILE), F32),
        ],
        flops=4 * rows * width * hidden,
        bytes_accessed=4 * width * hidden + 8 * rows * hidden,
    )(upstream, attended, vectors, wide_rows, stats, kept, slope, both, both, wait)


def input_back_body(
    core,
    grads,
    own_qk,
    other_qk,
    own_vo,
    other_vo,
    tokens,
    grad_attended,
    vectors,
    branch_sums,
    mid_sums,
    wide_sums,
    _,
    input_grad,
    turned,
    parts,
    sums,
):
    part = pl.program_id(0)
    me = core[0]
    grad_part = grads[...]

    @pl.when(part == 0)
    def _():
        parts[me] = dot_nt(grad_part, own_qk[...])
        parts[1 - me] = dot_nt(grad_part, other_qk[...])
        sums[...] = jnp.zeros_like(sums)
        sums[2:3, :] = jnp.sum(grad_part.astype(F32), axis=0, keepdims=True)

    @pl.when(part == 1)
    def _():
        parts[me] += dot_nt(grad_part, own_qk[...])
        parts[1 - me] += dot_nt(grad_part, other_qk[...])

    @pl.when(part == 2)
    def _():
        parts[me] += dot_nt(grad_part, own_vo[...])
        parts[1 - me] += dot_nt(grad_part, other_vo[...])
        grad = join_parity(parts[0], parts[1])
        centered, spread = row_stats(tokens[...].astype(F32))
        unit = centered * spread
        input_grad[...] = grad_attended[...] + norm_back(grad * vectors[0:1, :], unit, spread)
        sums[0:1, :] = jnp.sum(grad * unit, axis=0, keepdims=True)
        sums[1:2, :] = jnp.sum(grad, axis=0, keepdims=True)
        sums[3:4, :] = jnp.sum(grad_part.astype(F32), axis=0, keepdims=True)
        sums[4:7, :] = branch_sums[0:3, :]
        sums[7:9, :] = mid_sums[0:2, :]
        for row in range(wide_sums.shape[0]):
            sums[9 + row : 10 + row, :] = wide_sums[row, 2:3, :]
            sums[13 + row : 14 + row, :] = wide_sums[row, 0:1, :]
            sums[17 + row : 18 + row, :] = wide_sums[row, 1:2, :]
        sums[21:22, :] = mid_sums[2:3, :]
        width = sums.shape[1]
        head_dim = TILE // 2
        picks = (
            lax.broadcasted_iota(jnp.int32, (width, TILE), 0) // head_dim + HEAD_AT
            == lax.broadcasted_iota(jnp.int32, (width, TILE), 1)
        ).astype(F32)
        heads = lax.dot_general(
            branch_sums[...],
            picks,
            (((1,), (0,)), ((), ())),
            precision=HIGHEST,
            preferred_element_type=F32,
        )[3:4, :]
        for block in range(turned.shape[0]):
            turned[block] = (
                jnp.transpose(sums[:, block * TILE : (block + 1) * TILE]) + heads
            )


def input_back(core, grads, weights, tokens, grad_attended, vectors, sums, wait):
    rows, width = tokens.shape
    full = whole((rows, width))
    third = pl.BlockSpec((width // 2, width), lambda part, *_: (0, jnp.minimum(part, 1)))
    last = pl.BlockSpec((width // 2, width), lambda part, *_: (0, 0))
    return call(
        input_back_body,
        (3,),
        [
            pl.BlockSpec((None, rows, width), lambda part, *_: (part, 0, 0)),
            third,
            third,
            last,
            last,
            full,
            full,
            whole(vectors.shape),
            *[whole(item.shape) for item in sums],
            *after(wait),
        ],
        [full, whole((width // TILE, TILE, TILE))],
        [
            jax.ShapeDtypeStruct((rows, width), F32),
            jax.ShapeDtypeStruct((width // TILE, TILE, TILE), F32),
        ],
        scratch=[pltpu.VMEM((2, rows, width // 2), F32), pltpu.VMEM((TILE, width), F32)],
        flops=1,
        bytes_accessed=1,
        scalars=1,
    )(core, grads, *weights, tokens, grad_attended, vectors, *sums, wait)


def outer_body(two_lefts, adds, _, *refs):
    lefts = refs[: 4 * (1 + two_lefts)]
    refs = refs[4 * (1 + two_lefts) :]
    early, late, upper, lower = refs[:4]
    refs = refs[4:]
    if adds:
        add_first, add_second = refs[:2]
        refs = refs[2:]
    first, second = refs[:2]
    turned = refs[2:]
    at = pl.program_id(0)

    @pl.when(at == 0)
    def _():
        for which in range(1 + two_lefts):
            for block in range(4):
                turned[which][block * TILE : (block + 1) * TILE, :] = jnp.transpose(
                    lefts[4 * which + block][...]
                )

    def write_first(left, right):
        value = dot_nn(left[...], right[...])
        if adds:
            value = value + add_first[...].astype(F32)
        first[...] = value.astype(BF16)

    pl.when(at == 0)(lambda: write_first(turned[two_lefts], early))
    pl.when(at == 1)(lambda: write_first(turned[0], late))

    @pl.when(at >= 2)
    def _():
        above = dot_nn(turned[0][...], upper[...])
        below = dot_nn(turned[0][...], lower[...])
        plane, chips = second.shape[:2]
        for chip in range(chips):
            cut = slice(chip * 8 * plane, (chip + 1) * 8 * plane)
            value = jnp.concatenate(
                [
                    above[cut].reshape(plane, 8, above.shape[1]),
                    below[cut].reshape(plane, 8, below.shape[1]),
                ],
                axis=1,
            )
            if adds:
                value = value + add_second[:, chip].astype(F32)
            second[:, chip] = value.astype(BF16)


def outer(core, chips, left, rights, other_left=None, add=None, wait=()):
    rows, width = left.shape
    lefts = [left] if other_left is None else [left, other_left]
    half = width // 2
    plane = half // (8 * chips)

    def left_spec(block):
        return pl.BlockSpec((rows, TILE), lambda at, core, block=block: (0, 2 * block + core[0]))

    def right_spec(index, start, columns, low, high):
        def where(at, *_):
            column = start // columns + jnp.clip(at - low, 0, high)
            return (index, 0, column)

        return pl.BlockSpec((None, rows, columns), where)

    specs, operands = [], []
    for one in lefts:
        for block in range(4):
            specs.append(left_spec(block))
            operands.append(one)
    for (array, index, start), columns, low, high in zip(
        rights, (1024, 1024, 512, 512), (0, 0, 2, 2), (0, 0, 1, 1)
    ):
        specs.append(right_spec(index, start, columns, low, high))
        operands.append(array)
    part_specs = [
        pl.BlockSpec((half, 1024), lambda at, *_: (0, jnp.clip(at, 0, 1))),
        pl.BlockSpec((plane, chips, 16, 512), lambda at, *_: (0, 0, 0, jnp.clip(at - 2, 0, 1))),
    ]
    if add is not None:
        specs += part_specs
        operands += list(add)

    def body(core, *refs):
        used = len(operands)
        outer_body(len(lefts) - 1, add is not None, core, *refs[:used], *refs[used + len(wait) :])

    return call(
        body,
        (4,),
        specs + after(*wait),
        part_specs,
        [
            jax.ShapeDtypeStruct((half, 2048), BF16),
            jax.ShapeDtypeStruct((plane, chips, 16, 1024), BF16),
        ],
        scratch=[pltpu.VMEM((half, rows), BF16) for _ in lefts],
        flops=4 * rows * half * 2048,
        bytes_accessed=4 * half * 4096,
        scalars=1,
    )(core, *operands, *wait)


def to_slots_body(perm, down, up, attn, own, *refs):
    more, (grad_qkv, grad_out, grad_up, grad_down, slots, tiles) = refs[:3], refs[3:]
    rest = own[...]
    for one in more:
        rest = rest + one[...].astype(F32)
    width = grad_out.shape[1]
    half = down.shape[1]
    grad_out[...] = attn[:, :width]
    grad_qkv[:, :width] = attn[:, width : 2 * width]
    grad_qkv[:, width : 2 * width] = rest[32:40]
    grad_qkv[:, 2 * width :] = rest[40:48]
    for result, first, at in ((grad_down, down, 0), (grad_up, up, 16)):
        result[:, :half] = first[...]
        result[:, half : half + width] = rest[at : at + 8]
        result[:, half + width :] = rest[at + 8 : at + 16]
    column = 0
    for result in (grad_qkv, grad_out, grad_up, grad_down):
        for at in range(0, result.shape[1], TILE):
            tiles[column] = result[:, at : at + TILE]
            column += 1
    planes, pairs = slots.shape[:2]
    for slot in range(planes * pairs):
        pair = [tiles[perm[2 * slot + which]] for which in range(2)]
        slots[slot // pairs, slot % pairs] = jnp.concatenate(pair, axis=0).astype(BF16)


def to_slots(perm, down, up, attn, rest, plane, widths):
    arrays = [down, up, attn, *rest]
    pairs = perm.shape[0] // (2 * plane)
    shapes = [jax.ShapeDtypeStruct((8, columns), F32) for columns in widths]
    shapes.append(jax.ShapeDtypeStruct((plane, pairs, 16, TILE), BF16))
    return call(
        to_slots_body,
        (1,),
        [whole(item.shape) for item in arrays],
        [whole(item.shape) for item in shapes],
        shapes,
        scratch=[pltpu.VMEM((perm.shape[0], 8, TILE), F32)],
        bytes_accessed=8 * 8 * sum(widths),
        scalars=1,
    )(perm, *arrays)


def update_body(grads, left_stats, right_stats, left_roots, right_roots, left_new, right_new, back):
    planes, pairs = grads.shape[:2]
    for pair in range(pairs):
        block = grads[:, pair].astype(F32)
        moved = []
        for which in range(2):
            slot = 2 * pair + which
            grad = block[:, which * 8 : which * 8 + 8, :].reshape(TILE, TILE)
            low = grad.astype(BF16)
            left_new[slot] = DECAY * left_stats[slot] + (1.0 - DECAY) * dot_nt(low, low)
            right_new[slot] = DECAY * right_stats[slot] + (1.0 - DECAY) * dot_tn(low, low)
            step = jnp.dot(grad, right_roots[slot], precision=HIGHEST, preferred_element_type=F32)
            step = jnp.dot(left_roots[slot], step, precision=HIGHEST, preferred_element_type=F32)
            moved.append(step.reshape(planes, 8, TILE))
        back[:, pair] = jnp.concatenate(moved, axis=1).astype(BF16)


def update(grads, left_stats, right_stats, left_roots, right_roots):
    arrays = [item[0] for item in (left_stats, right_stats, left_roots, right_roots)]
    stats = jax.ShapeDtypeStruct(arrays[0].shape, F32)
    left_new, right_new, back = call(
        update_body,
        (1,),
        [whole(grads.shape)] + [whole(item.shape) for item in arrays],
        [whole(stats.shape), whole(stats.shape), whole(grads.shape)],
        [stats, stats, jax.ShapeDtypeStruct(grads.shape, BF16)],
        bytes_accessed=24 * arrays[0].size,
    )(grads, *arrays)
    return left_new[None], right_new[None], back


def apply_body(perm, moved, *refs):
    olds, news, tiles = refs[:4], refs[4:8], refs[8]
    pairs = moved.shape[1]
    for slot in range(moved.shape[0] * pairs):
        value = moved[slot // pairs, slot % pairs].astype(F32)
        tiles[perm[2 * slot]] = value[:8]
        tiles[perm[2 * slot + 1]] = value[8:]
    column = 0
    for old, new in zip(olds, news):
        for at in range(0, old.shape[1], TILE):
            cut = slice(at, at + TILE)
            new[:, cut] = old[:, cut] - RATE_MATRIX * tiles[column]
            column += 1


def apply_steps(perm, moved, weights):
    shapes = [jax.ShapeDtypeStruct(item.shape, F32) for item in weights]
    return call(
        apply_body,
        (1,),
        [whole(moved.shape)] + [whole(item.shape) for item in weights],
        [whole(item.shape) for item in shapes],
        shapes,
        scratch=[pltpu.VMEM((perm.shape[0], 8, TILE), F32)],
        bytes_accessed=10 * 8 * TILE * perm.shape[0],
        scalars=1,
    )(perm, moved, *weights)


def swap_cores(values):
    return lax.ppermute(values, "core", [(0, 1), (1, 0)])


def turn_chips(values, step):
    count = lax.axis_size("x")
    return lax.ppermute(values, "x", [(at, (at + step) % count) for at in range(count)])


def sum_parts(parts):
    return jnp.sum(parts.astype(F32), axis=0)


def shards(
    tokens,
    cotangent,
    lengths,
    valid,
    owner_perm,
    w_qkv,
    w_out,
    w_up,
    w_down,
    vectors,
    head_scale,
    left_stats,
    right_stats,
    left_roots,
    right_roots,
    vector_stats,
    head_stats,
):
    rows, width = tokens.shape
    heads = head_scale.shape[0]
    hidden = w_up.shape[1]
    ratio = hidden // width
    shard = w_up.shape[0]
    plane = lax.axis_size("fsdp")
    chips = lax.axis_size("x")
    core = lax.axis_index("core")
    core_arg = core.astype(jnp.int32).reshape(1)

    both = lax.all_gather(
        jnp.concatenate([w_up.astype(BF16), w_down.astype(BF16)], axis=1),
        ("x", "core", "fsdp"),
        axis=0,
        tiled=True,
    )
    low_qk = jnp.concatenate(
        [
            w_qkv[:, : 2 * width].astype(BF16),
            jnp.pad(vectors.astype(BF16).T, ((0, 0), (0, TILE - vectors.shape[0]))),
        ],
        axis=1,
    )
    low_vo = jnp.concatenate([w_qkv[:, 2 * width :].astype(BF16), w_out.astype(BF16)], axis=1)

    def to_plane(part, concat):
        spread = jnp.broadcast_to(part[None], (plane,) + part.shape)
        return lax.all_to_all(spread, "fsdp", split_axis=0, concat_axis=concat, tiled=True)

    place = lax.axis_index("x")

    def roll_chips(parts, start):
        twice = jnp.concatenate([parts, parts], axis=0)
        begin = [start] + [0] * (parts.ndim - 1)
        return lax.dynamic_slice(twice, begin, parts.shape, allow_negative_indices=False)

    def in_order(parts):
        return roll_chips(jnp.stack(parts[::-1]), chips - 1 - place)

    def to_chips(part):
        return in_order([part] + [turn_chips(part, step) for step in range(1, chips)])

    def across_chips(parts):
        ahead = roll_chips(parts, place)
        return [ahead[0]] + [turn_chips(ahead[step], step) for step in range(1, chips)]

    own_vo = to_plane(to_chips(low_vo), 2).reshape(width // 2, -1)
    own_qk = to_chips(to_plane(low_qk, 0).reshape(plane * shard, -1)).reshape(width // 2, -1)
    other_qk, other_vo = swap_cores(own_qk), swap_cores(own_vo)
    weights = (own_qk, other_qk, own_vo, other_vo)
    vector_at = 2 * width
    vector_pair = jnp.stack([own_qk[:, vector_at:], other_qk[:, vector_at:]])
    vector_pair = jnp.where(core == 0, vector_pair, vector_pair[::-1])
    vector_rows = (
        vector_pair.reshape(2, -1, TILE, TILE)
        .transpose(1, 0, 2, 3)
        .reshape(width, TILE)
        .T[:24]
        .astype(F32)
    )
    wide_rows = jnp.concatenate(
        [
            vector_rows[9 : 9 + 3 * ratio].reshape(3, hidden),
            jnp.zeros((5, hidden), F32),
        ],
        axis=0,
    )
    upstream = jnp.where(valid[:, None] != 0, cotangent, jnp.zeros_like(cotangent))
    scales = jnp.broadcast_to(jnp.repeat(head_scale, width // heads)[None], (8, width))

    normed, projected = project(core_arg, tokens, vector_rows, weights)
    mixed, scaled, attention = attend(lengths, head_scale, projected)
    branch, attended, normed_mid = branch_out(core_arg, scaled, weights, tokens, vector_rows)
    output, normed_top, kept, slope, stats = forward_ffn(
        normed_mid, attended, vector_rows, wide_rows, both
    )

    def over_x(part):
        return lax.psum_scatter(part, "x", scatter_dimension=0, tiled=True)

    def over_plane(part):
        return sum_parts(
            lax.all_to_all(
                part.reshape(plane, shard, -1), "fsdp", split_axis=0, concat_axis=0, tiled=True
            )
        )

    def plane_first(part):
        total = lax.all_to_all(part, "fsdp", split_axis=0, concat_axis=0, tiled=True)
        return sum_parts(total)

    def four(array):
        return [(array[None], 0, start) for start in (0, 1024, 2048, 3072)]

    sent_down = outer(1 - core_arg, chips, upstream, four(normed_top))
    down_first, down_second = outer(
        core_arg, chips, upstream, four(normed_top), add=[swap_cores(part) for part in sent_down]
    )
    down_rest = plane_first(down_second)
    down_part = over_plane(over_x(down_first))
    grad_attended, grad_hidden, wide_sums, mid_sums = backward_ffn(
        upstream, attended, vector_rows, wide_rows, stats, kept, slope, both, down_second
    )
    sent_up = outer(1 - core_arg, chips, normed_mid, four(grad_hidden))
    grad_branch, grad_mixed, branch_sums = branch_back(
        core_arg, grad_attended, branch, weights, mixed, scales, vector_rows, sent_up[1]
    )
    up_first, up_second = outer(
        core_arg,
        chips,
        normed_mid,
        four(grad_hidden),
        add=[swap_cores(part) for part in sent_up],
        wait=(grad_branch, down_rest, down_part),
    )
    up_rest = plane_first(up_second)
    up_part = over_plane(over_x(up_first))
    grads = attend_back(projected, mixed, grad_mixed, attention, up_second)
    rights = [(grad_branch[None], 0, 0), (grads, 0, 0), (grads, 1, 0), (grads, 2, 0)]
    sent_attn = outer(1 - core_arg, chips, normed, rights, other_left=scaled)
    attn_first, attn_second = outer(
        core_arg,
        chips,
        normed,
        rights,
        other_left=scaled,
        add=[swap_cores(part) for part in sent_attn],
        wait=(up_rest, up_part),
    )
    input_grad, turned = input_back(
        core_arg,
        grads,
        weights,
        tokens,
        grad_attended,
        vector_rows,
        (branch_sums, mid_sums, wide_sums),
        attn_second,
    )
    attn_rest = plane_first(attn_second)

    turned = turned.reshape(chips, 2, TILE, TILE)
    kept_sums = lax.dynamic_slice_in_dim(turned, core, 1, 1, allow_negative_indices=False)[:, 0]
    sent_sums = lax.dynamic_slice_in_dim(
        turned, 1 - core, 1, 1, allow_negative_indices=False
    )[:, 0]
    small = jnp.sum(in_order(across_chips(kept_sums + swap_cores(sent_sums))), axis=0)

    rest = jnp.concatenate([down_rest, up_rest, attn_rest], axis=1).astype(BF16)
    rest = across_chips(rest)
    rest[0] = rest[0].astype(F32)
    attn_part = over_plane(jnp.concatenate([over_x(attn_first), small.astype(BF16)], axis=1))
    vector_grads = attn_part[:, 2 * width :].T[: vectors.shape[0]]
    head_total = attn_part[0, 2 * width + HEAD_AT : 2 * width + HEAD_AT + heads]

    masters = (w_qkv, w_out, w_up, w_down)
    grad_qkv, grad_out, grad_up, grad_down, slots = to_slots(
        owner_perm,
        down_part,
        up_part,
        attn_part,
        rest,
        plane,
        [item.shape[1] for item in masters],
    )
    slots = lax.all_to_all(slots, "fsdp", split_axis=0, concat_axis=0, tiled=True)
    left_new, right_new, back = update(slots, left_stats, right_stats, left_roots, right_roots)
    back = lax.all_to_all(back, "fsdp", split_axis=0, concat_axis=0, tiled=True)
    new_qkv, new_out, new_up, new_down = apply_steps(owner_perm, back, masters)
    vector_stats_new = DECAY * vector_stats + (1.0 - DECAY) * vector_grads * vector_grads
    vectors_new = vectors - RATE_VECTOR * vector_grads * lax.rsqrt(vector_stats_new)
    head_stats_new = DECAY * head_stats + (1.0 - DECAY) * head_total * head_total
    head_new = head_scale - RATE_VECTOR * head_total * lax.rsqrt(head_stats_new)
    return (
        output,
        input_grad,
        grad_qkv,
        grad_out,
        grad_up,
        grad_down,
        vector_grads,
        head_total,
        left_new,
        right_new,
        new_qkv,
        new_out,
        new_up,
        new_down,
        vector_stats_new,
        vectors_new,
        head_stats_new,
        head_new,
    )


def solution(mesh):
    everywhere = ("x", "core", "fsdp")
    by_rows = P(everywhere, None)
    by_columns = P(None, everywhere)
    by_block = P(("x", "core"), "fsdp", None, None)
    dp, fsdp = mesh.devices.shape
    mesh = jax.sharding.Mesh(mesh.devices.reshape(dp // 2, 2, fsdp), everywhere)
    return jax.shard_map(
        shards,
        mesh=mesh,
        in_specs=(
            (by_rows, by_rows, P(everywhere), P(everywhere), P())
            + (by_rows,) * 4
            + (by_columns, P())
            + (by_block,) * 4
            + (by_columns, P())
        ),
        out_specs=(
            (by_rows,) * 6
            + (by_columns, P())
            + (by_block,) * 2
            + (by_rows,) * 4
            + (by_columns, by_columns, P(), P())
        ),
        check_vma=False,
    )
```

time: 2810 us -> 407 us (0.14)
  waiting for transfers between devices: 2400 us -> 119 us
  matrix products: 173 us -> 0 us
  Pallas kernels: 0 us -> 164 us
  other arithmetic: 97.4 us -> 16.3 us
  starting transfers between devices: 10.9 us -> 70.6 us
  blocking collectives: 59.6 us -> 0 us
  local copies, waits for them, and re-layouts: 48.9 us -> 15.7 us
    reduce_scatter x4 -> x3, waiting for transfers between devices: 2200 us -> 0.1 us  [over_x(): return lax.psum_scatter(part, 'x', scatter_dimension=0, tiled=True)]
    dot_general x22 -> x0, matrix products: 173 us -> none  [the longest x4 39.4 us: contract_first(): lax.dot_general(left, right, (((0,), (0,)), ((), ())), preferred_element_...]
    pallas_call x0 -> x17, Pallas kernels: none -> 164 us  [the longest x6 45.9 us: outer(): call(body, (4,), specs + after(*wait), part_specs, [jax.ShapeDtypeStruct(...]
    all_gather x4 -> x1, waiting for transfers between devices: 120 us -> 0.01 us  [shards(): lax.all_gather(jnp.concatenate([w_up.astype(BF16), w_down.astype(BF16)],...]
    reduce_sum x17 -> x7, other arithmetic: 71.9 us -> 4.09 us  [the longest x6 4.06 us: sum_parts(): return jnp.sum(parts.astype(F32), axis=0)]
    unnamed x10 -> x4, waiting for transfers between devices: 63.4 us -> 0.07 us
    all_gather x1 -> x0, blocking collectives: 59.6 us -> none  [shards(): lax.all_gather(vectors.astype(jnp.bfloat16), ('dp', 'fsdp'), axis=1, tile...]
    all_to_all x3 -> x10, waiting for transfers between devices: 21.6 us -> 75.2 us  [the longest x3 32.5 us: plane_first(): lax.all_to_all(part, 'fsdp', split_axis=0, concat_axis=0, tiled=True)]
  transfers between devices with their start and end apart: 12 -> 35, of which waited for: 12 -> 18; matrix products, arithmetic and copies ran while one was open for 6% -> 6% of each run, Pallas kernels for 0% -> 25%
where the time goes in v2:
time: 407 us; the launch traced here: 401 us
  Pallas kernels  164 us (40%)
  waiting for transfers between devices  119 us (29%)
  starting transfers between devices  70.6 us (17%)
  other arithmetic  16.3 us (4%)
  local copies, waits for them, and re-layouts  15.7 us (4%)
  between operations  15.3 us (4%)
    pallas_call x6, Pallas kernels, outer(): call(body, (4,), specs + after(*wait), part_specs, [jax.ShapeDtypeStruct(...  45.9 us
    ppermute x12, waiting for transfers between devices, turn_chips(): lax.ppermute(values, 'x', [(at, (at + step) % count) for at in range(coun...  35.5 us
    all_to_all x3, waiting for transfers between devices, plane_first(): lax.all_to_all(part, 'fsdp', split_axis=0, concat_axis=0, tiled=True)  32.5 us
    pallas_call x1, Pallas kernels, backward_ffn(): call(functools.partial(backward_ffn_body, steps), (2 * steps,), [whole((r...  24.5 us
    pallas_call x1, Pallas kernels, forward_ffn(): call(functools.partial(forward_ffn_body, steps), (2 * steps,), [whole((ro...  22.1 us
    all_to_all x3, starting transfers between devices, plane_first(): lax.all_to_all(part, 'fsdp', split_axis=0, concat_axis=0, tiled=True)  16.7 us
    ppermute x12, starting transfers between devices, turn_chips(): lax.ppermute(values, 'x', [(at, (at + step) % count) for at in range(coun...  16.2 us
    all_to_all x3, waiting for transfers between devices, over_plane(): lax.all_to_all(part.reshape(plane, shard, -1), 'fsdp', split_axis=0, conc...  16.1 us
  transfers between devices with their start and end apart: 35, of which 18 were waited for; matrix products, arithmetic and copies ran while one was open for 6% of the time, Pallas kernels for 25%

profile of v2, /device:TPU:0, one launch (start us, length us, event | category | flops | bytes accessed | tf_op | source)
XLA Modules:
  0.0 400.8 jit_solution(14733242194978822992)
XLA Ops:
  17.6 8.0 %all-to-all-start = ((bf16[16,8,2176]{2,1,0:T(8,128)(2,1)}), bf16[16,8,2176]{2,1,0:T(8,128)(2,1)S(1)}, u32[]{:S(2)}, u32[]{:S(2)}) async-start(bf16[16,8,2176]{2,1,0:T(8,128)(2,1)} %broadcast_in_dim.30), calls=%async_computation | async-start | bytes 1114112 | tf_op jit(solution)/shard_map/all_to_all | solution.py:951
  25.7 11.9 %all-to-all-done = bf16[16,8,2176]{2,1,0:T(8,128)(2,1)S(1)} async-done(((bf16[16,8,2176]{2,1,0:T(8,128)(2,1)}), bf16[16,8,2176]{2,1,0:T(8,128)(2,1)S(1)}, u32[]{:S(2)}, u32[]{:S(2)}) %all-to-all-start) | async-done | bytes 557088 | tf_op jit(solution)/shard_map/all_to_all | solution.py:951
  41.6 3.7 all-to-all-start.1
  47.0 15.8 %collective-permute-done = bf16[128,2176]{1,0:T(8,128)(2,1)S(1)} collective-permute-done((bf16[128,2176]{1,0:T(8,128)(2,1)S(1)}, bf16[128,2176]{1,0:T(8,128)(2,1)S(1)}, u32[]{:S(2)}, u32[]{:S(2)}) %collective-permute-start) | collective-permute-done | bytes 557088 | tf_op jit(solution)/shard_map/ppermute | solution.py:898
  65.9 11.0 %collective-permute-done.2 = bf16[128,2176]{1,0:T(8,128)(2,1)S(1)} collective-permute-done((bf16[128,2176]{1,0:T(8,128)(2,1)S(1)}, bf16[128,2176]{1,0:T(8,128)(2,1)S(1)}, u32[]{:S(2)}, u32[]{:S(2)}) %collective-permute-start.2) | collective-permute-done | bytes 557088 | tf_op jit(solution)/shard_map/ppermute | solution.py:898
  87.6 8.6 %shard_map.304 = (bf16[512,1024]{1,0:T(8,128)(2,1)}, bf16[512,3072]{1,0:T(8,128)(2,1)}) custom-call(s32[1]{0:T(128)} %bitcast.core, bf16[512,1024]{1,0:T(8,128)(2,1)} %tokens.5, f32[24,1024]{1,0:T(8,128)} %copy-done.2, bf16[512,2176]{1,0:T(8,128)(2,1)} %bitcast.7.own_qk, bf16[512,2176]{1,0:T(8,128)(2,1)} %collective-permute-done.3.other_qk, ...), custom_call_target="tpu_custom_call" | custom-call | flops 3221225472 | bytes 6291456 | tf_op jit(solution)/shard_map/pallas_call | solution.py:128
  96.2 13.5 %shard_map.305 = (f32[512,1024]{1,0:T(8,128)}, bf16[512,1024]{1,0:T(8,128)(2,1)}, bf16[16,256,768]{2,1,0:T(8,128)(2,1)}) custom-call(s32[1]{0:T(128)S(6)} %copy.59.length, f32[16]{0:T(128)} %scales.1, bf16[512,3072]{1,0:T(8,128)(2,1)} %get-tuple-element.64.queries.keys.values, bf16[512,3072]{1,0:T(8,128)(2,1)} %get-tuple-element.64.queries.keys.values, ...), custom_call_target="tpu_custom_call" | custom-call | flops 1073741824 | bytes 10485760 | tf_op jit(solution)/shard_map/pallas_call | solution.py:195
  109.7 6.3 %shard_map.306 = (f32[512,1024]{1,0:T(8,128)}, f32[512,1024]{1,0:T(8,128)}, bf16[512,1024]{1,0:T(8,128)(2,1)}) custom-call(s32[1]{0:T(128)} %bitcast.core, bf16[512,1024]{1,0:T(8,128)(2,1)} %get-tuple-element.65.scaled.refs_4_.refs_5_.refs_6_.refs_7_, bf16[512,2048]{1,0:T(8,128)(2,1)} %bitcast.109, bf16[512,2048]{1,0:T(8,128)(2,1)} %collective-permute-done.7.other_vo.other, ...), custom_call_target="tpu_custom_call" | custom-call | flops 1073741824 | bytes 9437184 | tf_op jit(solution)/shard_map/pallas_call | solution.py:299
  116.0 22.1 %shard_map.307 = (bf16[512,1024]{1,0:T(8,128)(2,1)}, bf16[512,4096]{1,0:T(8,128)(2,1)}, bf16[512,4096]{1,0:T(8,128)(2,1)}, bf16[512,4096]{1,0:T(8,128)(2,1)}, f32[512,256]{1,0:T(8,128)}) custom-call(bf16[512,1024]{1,0:T(8,128)(2,1)} %get-tuple-element.66.normed.refs_0_.refs_1_.refs_2_.refs_3_, f32[512,1024]{1,0:T(8,128)} %get-tuple-element.67.attended, ...), custom_call_target="tpu_custom_call" | custom-call | flops 8589934592 | bytes 29360128 | tf_op jit(solution)/shard_map/pallas_call | solution.py:426
  138.2 7.1 %shard_map.308 = (bf16[512,2048]{1,0:T(8,128)(2,1)}, bf16[16,4,16,1024]{3,2,1,0:T(8,128)(2,1)}) custom-call(s32[1]{0:T(128)S(6)} %sub.20.core, bf16[512,1024]{1,0:T(8,128)(2,1)} %broadcast_select_fusion.refs_0_.refs_1_.refs_2_.refs_3_.upstream, bf16[512,1024]{1,0:T(8,128)(2,1)} %broadcast_select_fusion.refs_0_.refs_1_.refs_2_.refs_3_.upstream, ...), custom_call_target="tpu_custom_call" | custom-call | flops 2147483648 | bytes 8388608 | tf_op jit(solution)/shard_map/pallas_call | solution.py:773
  154.1 8.1 %shard_map.309 = (bf16[512,2048]{1,0:T(8,128)(2,1)}, bf16[16,4,16,1024]{3,2,1,0:T(8,128)(2,1)}) custom-call(s32[1]{0:T(128)} %bitcast.core, bf16[512,1024]{1,0:T(8,128)(2,1)} %broadcast_select_fusion.refs_0_.refs_1_.refs_2_.refs_3_.upstream, bf16[512,1024]{1,0:T(8,128)(2,1)} %broadcast_select_fusion.refs_0_.refs_1_.refs_2_.refs_3_.upstream, ...), custom_call_target="tpu_custom_call" | custom-call | flops 2147483648 | bytes 8388608 | tf_op jit(solution)/shard_map/pallas_call | solution.py:773
  162.2 7.1 %all-to-all-start.2 = ((bf16[16,4,16,1024]{3,2,1,0:T(8,128)(2,1)}), bf16[16,4,16,1024]{3,2,1,0:T(8,128)(2,1)S(1)}, u32[]{:S(2)}, u32[]{:S(2)}) async-start(bf16[16,4,16,1024]{3,2,1,0:T(8,128)(2,1)} %get-tuple-element.76._), calls=%async_computation.2 | async-start | bytes 4194304 | tf_op jit(solution)/shard_map/all_to_all | solution.py:1012
  169.2 24.5 %shard_map.310 = (f32[512,1024]{1,0:T(8,128)}, bf16[512,4096]{1,0:T(8,128)(2,1)}, f32[4,8,1024]{2,1,0:T(8,128)}, f32[8,1024]{1,0:T(8,128)}) custom-call(bf16[512,1024]{1,0:T(8,128)(2,1)} %broadcast_select_fusion.refs_0_.refs_1_.refs_2_.refs_3_.upstream, f32[512,1024]{1,0:T(8,128)} %get-tuple-element.67.attended, f32[24,1024]{1,0:T(8,128)} %copy-done.2, ...), custom_call_target="tpu_custom_call" | custom-call | flops 8589934592 | bytes 33554432 | tf_op jit(solution)/shard_map/pallas_call | solution.py:545
  193.7 7.1 %shard_map.311 = (bf16[512,2048]{1,0:T(8,128)(2,1)}, bf16[16,4,16,1024]{3,2,1,0:T(8,128)(2,1)}) custom-call(s32[1]{0:T(128)S(6)} %sub.20.core, bf16[512,1024]{1,0:T(8,128)(2,1)} %get-tuple-element.66.normed.refs_0_.refs_1_.refs_2_.refs_3_, bf16[512,1024]{1,0:T(8,128)(2,1)} %get-tuple-element.66.normed.refs_0_.refs_1_.refs_2_.refs_3_, ...), custom_call_target="tpu_custom_call" | custom-call | flops 2147483648 | bytes 8388608 | tf_op jit(solution)/shard_map/pallas_call | solution.py:773
  202.3 6.3 %all-to-all-start.3 = ((bf16[16,8,2048]{2,1,0:T(8,128)(2,1)}), bf16[16,8,2048]{2,1,0:T(8,128)(2,1)S(1)}, u32[]{:S(2)}, u32[]{:S(2)}) async-start(bf16[16,8,2048]{2,1,0:T(8,128)(2,1)} %bitcast.120), calls=%async_computation.4 | async-start | bytes 1048576 | tf_op jit(solution)/shard_map/all_to_all | solution.py:1006
  209.8 8.2 %shard_map.312 = (bf16[512,1024]{1,0:T(8,128)(2,1)}, bf16[512,1024]{1,0:T(8,128)(2,1)}, f32[8,1024]{1,0:T(8,128)}) custom-call(s32[1]{0:T(128)} %bitcast.core, f32[512,1024]{1,0:T(8,128)} %get-tuple-element.77.grad_attended, f32[512,1024]{1,0:T(8,128)} %get-tuple-element.78.branch, bf16[512,2048]{1,0:T(8,128)(2,1)} %bitcast.110, ...), custom_call_target="tpu_custom_call" | custom-call | flops 1073741824 | bytes 10485760 | tf_op jit(solution)/shard_map/pallas_call | solution.py:344
  221.1 8.1 %shard_map.313 = (bf16[512,2048]{1,0:T(8,128)(2,1)}, bf16[16,4,16,1024]{3,2,1,0:T(8,128)(2,1)}) custom-call(s32[1]{0:T(128)} %bitcast.core, bf16[512,1024]{1,0:T(8,128)(2,1)} %get-tuple-element.66.normed.refs_0_.refs_1_.refs_2_.refs_3_, bf16[512,1024]{1,0:T(8,128)(2,1)} %get-tuple-element.66.normed.refs_0_.refs_1_.refs_2_.refs_3_, ...), custom_call_target="tpu_custom_call" | custom-call | flops 2147483648 | bytes 8388608 | tf_op jit(solution)/shard_map/pallas_call | solution.py:773
  229.2 6.0 %all-to-all-start.4 = ((bf16[16,4,16,1024]{3,2,1,0:T(8,128)(2,1)}), bf16[16,4,16,1024]{3,2,1,0:T(8,128)(2,1)S(1)}, u32[]{:S(2)}, u32[]{:S(2)}) async-start(bf16[16,4,16,1024]{3,2,1,0:T(8,128)(2,1)} %get-tuple-element.86._), calls=%async_computation.5 | async-start | bytes 4194304 | tf_op jit(solution)/shard_map/all_to_all | solution.py:1012
  235.1 13.8 %shard_map.314.refs_9_.refs_10_.refs_11_.grads = bf16[3,512,1024]{2,1,0:T(8,128)(2,1)} custom-call(bf16[512,3072]{1,0:T(8,128)(2,1)} %get-tuple-element.64.queries.keys.values, bf16[512,3072]{1,0:T(8,128)(2,1)} %get-tuple-element.64.queries.keys.values, bf16[512,3072]{1,0:T(8,128)(2,1)} %get-tuple-element.64.queries.keys.values, ...), custom_call_target="tpu_custom_call" | custom-call | flops 2684354560 | bytes 12582912 | tf_op jit(solution)/shard_map/pallas_call | solution.py:263
  248.9 7.3 %shard_map.315 = (bf16[512,2048]{1,0:T(8,128)(2,1)}, bf16[16,4,16,1024]{3,2,1,0:T(8,128)(2,1)}) custom-call(s32[1]{0:T(128)S(6)} %sub.20.core, bf16[512,1024]{1,0:T(8,128)(2,1)} %get-tuple-element.90.refs_0_.refs_1_.refs_2_.refs_3_, bf16[512,1024]{1,0:T(8,128)(2,1)} %get-tuple-element.90.refs_0_.refs_1_.refs_2_.refs_3_, ...), custom_call_target="tpu_custom_call" | custom-call | flops 2147483648 | bytes 8388608 | tf_op jit(solution)/shard_map/pallas_call | solution.py:773
  256.7 9.2 %all-to-all-done.4 = bf16[16,4,16,1024]{3,2,1,0:T(8,128)(2,1)S(1)} async-done(((bf16[16,4,16,1024]{3,2,1,0:T(8,128)(2,1)}), bf16[16,4,16,1024]{3,2,1,0:T(8,128)(2,1)S(1)}, u32[]{:S(2)}, u32[]{:S(2)}) %all-to-all-start.4) | async-done | bytes 2097184 | tf_op jit(solution)/shard_map/all_to_all | solution.py:1012
  270.8 10.0 %all-to-all-done.5 = bf16[16,8,2048]{2,1,0:T(8,128)(2,1)S(1)} async-done(((bf16[16,8,2048]{2,1,0:T(8,128)(2,1)}), bf16[16,8,2048]{2,1,0:T(8,128)(2,1)S(1)}, u32[]{:S(2)}, u32[]{:S(2)}) %all-to-all-start.5) | async-done | bytes 524320 | tf_op jit(solution)/shard_map/all_to_all | solution.py:1006
  281.5 8.3 %shard_map.316 = (bf16[512,2048]{1,0:T(8,128)(2,1)}, bf16[16,4,16,1024]{3,2,1,0:T(8,128)(2,1)}) custom-call(s32[1]{0:T(128)} %bitcast.core, bf16[512,1024]{1,0:T(8,128)(2,1)} %get-tuple-element.90.refs_0_.refs_1_.refs_2_.refs_3_, bf16[512,1024]{1,0:T(8,128)(2,1)} %get-tuple-element.90.refs_0_.refs_1_.refs_2_.refs_3_, ...), custom_call_target="tpu_custom_call" | custom-call | flops 2147483648 | bytes 8388608 | tf_op jit(solution)/shard_map/pallas_call | solution.py:773
  289.8 11.2 %shard_map.317 = (f32[512,1024]{1,0:T(8,128)}, f32[8,128,128]{2,1,0:T(8,128)}) custom-call(s32[1]{0:T(128)} %bitcast.core, bf16[3,512,1024]{2,1,0:T(8,128)(2,1)} %shard_map.314.refs_9_.refs_10_.refs_11_.grads, bf16[512,2176]{1,0:T(8,128)(2,1)} %bitcast.7.own_qk, bf16[512,2176]{1,0:T(8,128)(2,1)} %collective-permute-done.3.other_qk, ...), custom_call_target="tpu_custom_call" | custom-call | flops 1 | bytes 1 | tf_op jit(solution)/shard_map/pallas_call | solution.py:660
  305.1 3.7 all-to-all-start.7
  311.4 4.9 %collective-permute-done.16 = f32[128,128]{1,0:T(8,128)S(1)} collective-permute-done((f32[128,128]{1,0:T(8,128)S(1)}, f32[128,128]{1,0:T(8,128)S(1)}, u32[]{:S(2)}, u32[]{:S(2)}) %collective-permute-start.16) | collective-permute-done | bytes 65568 | tf_op jit(solution)/shard_map/ppermute | solution.py:898
  319.3 22.3 %all-to-all-done.7 = bf16[16,4,16,1024]{3,2,1,0:T(8,128)(2,1)S(1)} async-done(((bf16[16,4,16,1024]{3,2,1,0:T(8,128)(2,1)}), bf16[16,4,16,1024]{3,2,1,0:T(8,128)(2,1)S(1)}, u32[]{:S(2)}, u32[]{:S(2)}) %all-to-all-start.7) | async-done | bytes 2097184 | tf_op jit(solution)/shard_map/all_to_all | solution.py:1012
  351.6 4.9 %all-to-all-done.6 = bf16[16,8,2176]{2,1,0:T(8,128)(2,1)S(1)} async-done(((bf16[16,8,2176]{2,1,0:T(8,128)(2,1)}), bf16[16,8,2176]{2,1,0:T(8,128)(2,1)S(1)}, u32[]{:S(2)}, u32[]{:S(2)}) %all-to-all-start.6) | async-done | bytes 557088 | tf_op jit(solution)/shard_map/all_to_all | solution.py:1006
  360.0 5.5 %all-to-all-start.8 = ((bf16[16,3,16,128]{3,2,1,0:T(8,128)(2,1)}), bf16[16,3,16,128]{3,2,1,0:T(8,128)(2,1)S(1)}, u32[]{:S(2)}, u32[]{:S(2)}) async-start(bf16[16,3,16,128]{3,2,1,0:T(8,128)(2,1)} %get-tuple-element.102), calls=%async_computation.11 | async-start | bytes 393216 | tf_op jit(solution)/shard_map/all_to_all | solution.py:1089
  366.2 7.7 %all-to-all-done.8.grads = bf16[16,3,16,128]{3,2,1,0:T(8,128)(2,1)S(1)} async-done(((bf16[16,3,16,128]{3,2,1,0:T(8,128)(2,1)}), bf16[16,3,16,128]{3,2,1,0:T(8,128)(2,1)S(1)}, u32[]{:S(2)}, u32[]{:S(2)}) %all-to-all-start.8) | async-done | bytes 196640 | tf_op jit(solution)/shard_map/all_to_all | solution.py:1089
  374.6 4.3 %shard_map.319 = (f32[6,128,128]{2,1,0:T(8,128)}, f32[6,128,128]{2,1,0:T(8,128)}, bf16[16,3,16,128]{3,2,1,0:T(8,128)(2,1)}) custom-call(bf16[16,3,16,128]{3,2,1,0:T(8,128)(2,1)} %copy-done.8, f32[6,128,128]{2,1,0:T(8,128)} %bitcast.124, f32[6,128,128]{2,1,0:T(8,128)} %bitcast.125, f32[6,128,128]{2,1,0:T(8,128)} %bitcast.126, f32[6,128,128]{2,1,0:T(8,128)} %bitcast.127), custom_call_target="tpu_custom_call" | custom-call | bytes 2359296 | tf_op jit(solution)/shard_map/pallas_call | solution.py:852
  383.7 7.0 %all-to-all-done.9.moved = bf16[16,3,16,128]{3,2,1,0:T(8,128)(2,1)S(1)} async-done(((bf16[16,3,16,128]{3,2,1,0:T(8,128)(2,1)}), bf16[16,3,16,128]{3,2,1,0:T(8,128)(2,1)S(1)}, u32[]{:S(2)}, u32[]{:S(2)}) %all-to-all-start.9) | async-done | bytes 196640 | tf_op jit(solution)/shard_map/all_to_all | solution.py:1091
  (170 shorter events, 81.9 us)
Async XLA Ops:
  7.2 108.8 %all-gather.2.cloned.1.call-start = ((), (), s32[]{:S(2)}) async-start(), calls=%async_computation.13 | async-start | bytes 16908288 | tf_op jit(solution)/shard_map/all_gather | solution.py:934
  11.4 14.2 %collective-permute-start.4 = (bf16[8,2048]{1,0:T(8,128)(2,1)S(1)}, bf16[8,2048]{1,0:T(8,128)(2,1)S(1)}, u32[]{:S(2)}, u32[]{:S(2)}) collective-permute-start(bf16[8,2048]{1,0:T(8,128)(2,1)S(1)} %pad_maximum_fusion.2), channel_id=1, source_target_pairs={{0,96},{32,0},{64,32},{96,64},{1,97},{33,1},{65,33},{97,65},{2,98}... | collective-permute-start | bytes 98312 | tf_op jit(solution)/shard_map/ppermute | solution.py:898
  14.3 11.3 %collective-permute-start.5 = (bf16[8,2048]{1,0:T(8,128)(2,1)S(1)}, bf16[8,2048]{1,0:T(8,128)(2,1)S(1)}, u32[]{:S(2)}, u32[]{:S(2)}) collective-permute-start(bf16[8,2048]{1,0:T(8,128)(2,1)S(1)} %pad_maximum_fusion.2), channel_id=1, source_target_pairs={{0,64},{32,96},{64,0},{96,32},{1,65},{33,97},{65,1},{97,33},{2,66}... | collective-permute-start | bytes 98312 | tf_op jit(solution)/shard_map/ppermute | solution.py:898
  15.1 10.5 %collective-permute-start.6 = (bf16[8,2048]{1,0:T(8,128)(2,1)S(1)}, bf16[8,2048]{1,0:T(8,128)(2,1)S(1)}, u32[]{:S(2)}, u32[]{:S(2)}) collective-permute-start(bf16[8,2048]{1,0:T(8,128)(2,1)S(1)} %pad_maximum_fusion.2), channel_id=1, source_target_pairs={{0,32},{32,64},{64,96},{96,0},{1,33},{33,65},{65,97},{97,1},{2,34}... | collective-permute-start | bytes 98312 | tf_op jit(solution)/shard_map/ppermute | solution.py:898
  17.6 20.1 %all-to-all-start = ((bf16[16,8,2176]{2,1,0:T(8,128)(2,1)}), bf16[16,8,2176]{2,1,0:T(8,128)(2,1)S(1)}, u32[]{:S(2)}, u32[]{:S(2)}) async-start(bf16[16,8,2176]{2,1,0:T(8,128)(2,1)} %broadcast_in_dim.30), calls=%async_computation | async-start | bytes 1114112 | tf_op jit(solution)/shard_map/all_to_all | solution.py:951
  37.6 25.2 %collective-permute-start = (bf16[128,2176]{1,0:T(8,128)(2,1)S(1)}, bf16[128,2176]{1,0:T(8,128)(2,1)S(1)}, u32[]{:S(2)}, u32[]{:S(2)}) collective-permute-start(bf16[128,2176]{1,0:T(8,128)(2,1)S(1)} %bitcast.115), channel_id=1, source_target_pairs={{0,96},{32,0},{64,32},{96,64},{1,97},{33,1},{65,33},{97,65},{2,98}... | collective-permute-start | bytes 1671176 | tf_op jit(solution)/shard_map/ppermute | solution.py:898
  41.6 37.2 %all-to-all-start.1 = ((bf16[16,4,8,2048]{3,2,1,0:T(8,128)(2,1)}), bf16[16,4,8,2048]{3,2,1,0:T(8,128)(2,1)S(1)}, u32[]{:S(2)}, u32[]{:S(2)}) async-start(bf16[16,4,8,2048]{3,2,1,0:T(8,128)(2,1)} %broadcast_in_dim.31), calls=%async_computation.1 | async-start | bytes 4194304 | tf_op jit(solution)/shard_map/all_to_all | solution.py:951
  45.3 156.9 %reduce-scatter.4.cloned.1.call-start = ((), (), s32[]{:S(2)}) async-start(), calls=%async_computation.14 | async-start | bytes 2621440 | tf_op jit(solution)/shard_map/reduce_scatter | solution.py:1002
  45.4 20.4 %collective-permute-start.1 = (bf16[128,2176]{1,0:T(8,128)(2,1)S(1)}, bf16[128,2176]{1,0:T(8,128)(2,1)S(1)}, u32[]{:S(2)}, u32[]{:S(2)}) collective-permute-start(bf16[128,2176]{1,0:T(8,128)(2,1)S(1)} %bitcast.116), channel_id=1, source_target_pairs={{0,64},{32,96},{64,0},{96,32},{1,65},{33,97},{65,1},{97,33},{2,66}... | collective-permute-start | bytes 1671176 | tf_op jit(solution)/shard_map/ppermute | solution.py:898
  47.0 29.9 %collective-permute-start.2 = (bf16[128,2176]{1,0:T(8,128)(2,1)S(1)}, bf16[128,2176]{1,0:T(8,128)(2,1)S(1)}, u32[]{:S(2)}, u32[]{:S(2)}) collective-permute-start(bf16[128,2176]{1,0:T(8,128)(2,1)S(1)} %bitcast.117), channel_id=1, source_target_pairs={{0,32},{32,64},{64,96},{96,0},{1,33},{33,65},{65,97},{97,1},{2,34}... | collective-permute-start | bytes 1671176 | tf_op jit(solution)/shard_map/ppermute | solution.py:898
  78.8 6.7 %collective-permute-start.3 = (bf16[512,2176]{1,0:T(8,128)(2,1)}, bf16[512,2176]{1,0:T(8,128)(2,1)}, u32[]{:S(2)}, u32[]{:S(2)}) collective-permute-start(bf16[512,2176]{1,0:T(8,128)(2,1)} %bitcast.7.own_qk), channel_id=1, source_target_pairs={{0,16},{16,0},{1,17},{17,1},{2,18},{18,2},{3,19},{19,3},{4,20},{20... | collective-permute-start | bytes 6684680 | tf_op jit(solution)/shard_map/ppermute | solution.py:893
  145.5 7.2 %collective-permute-start.9 = (bf16[16,4,16,1024]{3,2,1,0:T(8,128)(2,1)}, bf16[16,4,16,1024]{3,2,1,0:T(8,128)(2,1)S(1)}, u32[]{:S(2)}, u32[]{:S(2)}) collective-permute-start(bf16[16,4,16,1024]{3,2,1,0:T(8,128)(2,1)} %get-tuple-element.75), channel_id=1, source_target_pairs={{0,16},{16,0},{1,17},{17,1},{2,18},{18,2},{3,19},{19,3},{4,20},{20... | collective-permute-start | bytes 6291464 | tf_op jit(solution)/shard_map/ppermute | solution.py:893
  162.2 40.1 %all-to-all-start.2 = ((bf16[16,4,16,1024]{3,2,1,0:T(8,128)(2,1)}), bf16[16,4,16,1024]{3,2,1,0:T(8,128)(2,1)S(1)}, u32[]{:S(2)}, u32[]{:S(2)}) async-start(bf16[16,4,16,1024]{3,2,1,0:T(8,128)(2,1)} %get-tuple-element.76._), calls=%async_computation.2 | async-start | bytes 4194304 | tf_op jit(solution)/shard_map/all_to_all | solution.py:1012
  200.8 20.2 %collective-permute-start.10 = (bf16[512,2048]{1,0:T(8,128)(2,1)}, bf16[512,2048]{1,0:T(8,128)(2,1)}, u32[]{:S(2)}, u32[]{:S(2)}) collective-permute-start(bf16[512,2048]{1,0:T(8,128)(2,1)} %get-tuple-element.83), channel_id=1, source_target_pairs={{0,16},{16,0},{1,17},{17,1},{2,18},{18,2},{3,19},{19,3},{4,20},{20... | collective-permute-start | bytes 6291464 | tf_op jit(solution)/shard_map/ppermute | solution.py:893
  200.8 20.2 %collective-permute-start.11 = (bf16[16,4,16,1024]{3,2,1,0:T(8,128)(2,1)}, bf16[16,4,16,1024]{3,2,1,0:T(8,128)(2,1)}, u32[]{:S(2)}, u32[]{:S(2)}) collective-permute-start(bf16[16,4,16,1024]{3,2,1,0:T(8,128)(2,1)} %get-tuple-element.80._), channel_id=1, source_target_pairs={{0,16},{16,0},{1,17},{17,1},{2,18},{18,2},{3,19},{19,3},{4,20},{20... | collective-permute-start | bytes 6291464 | tf_op jit(solution)/shard_map/ppermute | solution.py:893
  202.3 18.1 %all-to-all-start.3 = ((bf16[16,8,2048]{2,1,0:T(8,128)(2,1)}), bf16[16,8,2048]{2,1,0:T(8,128)(2,1)S(1)}, u32[]{:S(2)}, u32[]{:S(2)}) async-start(bf16[16,8,2048]{2,1,0:T(8,128)(2,1)} %bitcast.120), calls=%async_computation.4 | async-start | bytes 1048576 | tf_op jit(solution)/shard_map/all_to_all | solution.py:1006
  208.6 57.3 %reduce-scatter.6.cloned.1.call-start = ((), (), s32[]{:S(2)}) async-start(), calls=%async_computation.15 | async-start | bytes 2621440 | tf_op jit(solution)/shard_map/reduce_scatter | solution.py:1002
  229.2 36.7 %all-to-all-start.4 = ((bf16[16,4,16,1024]{3,2,1,0:T(8,128)(2,1)}), bf16[16,4,16,1024]{3,2,1,0:T(8,128)(2,1)S(1)}, u32[]{:S(2)}, u32[]{:S(2)}) async-start(bf16[16,4,16,1024]{3,2,1,0:T(8,128)(2,1)} %get-tuple-element.86._), calls=%async_computation.5 | async-start | bytes 4194304 | tf_op jit(solution)/shard_map/all_to_all | solution.py:1012
  256.2 25.3 %collective-permute-start.12 = (bf16[512,2048]{1,0:T(8,128)(2,1)}, bf16[512,2048]{1,0:T(8,128)(2,1)}, u32[]{:S(2)}, u32[]{:S(2)}) collective-permute-start(bf16[512,2048]{1,0:T(8,128)(2,1)} %get-tuple-element.91), channel_id=1, source_target_pairs={{0,16},{16,0},{1,17},{17,1},{2,18},{18,2},{3,19},{19,3},{4,20},{20... | collective-permute-start | bytes 6291464 | tf_op jit(solution)/shard_map/ppermute | solution.py:893
  256.2 25.3 %collective-permute-start.13 = (bf16[16,4,16,1024]{3,2,1,0:T(8,128)(2,1)}, bf16[16,4,16,1024]{3,2,1,0:T(8,128)(2,1)}, u32[]{:S(2)}, u32[]{:S(2)}) collective-permute-start(bf16[16,4,16,1024]{3,2,1,0:T(8,128)(2,1)} %get-tuple-element.92), channel_id=1, source_target_pairs={{0,16},{16,0},{1,17},{17,1},{2,18},{18,2},{3,19},{19,3},{4,20},{20... | collective-permute-start | bytes 6291464 | tf_op jit(solution)/shard_map/ppermute | solution.py:893
  265.9 14.9 %all-to-all-start.5 = ((bf16[16,8,2048]{2,1,0:T(8,128)(2,1)}), bf16[16,8,2048]{2,1,0:T(8,128)(2,1)S(1)}, u32[]{:S(2)}, u32[]{:S(2)}) async-start(bf16[16,8,2048]{2,1,0:T(8,128)(2,1)} %bitcast.121), calls=%async_computation.7 | async-start | bytes 1048576 | tf_op jit(solution)/shard_map/all_to_all | solution.py:1006
  269.5 47.9 %reduce-scatter.8.cloned.1.call-start = ((), (), s32[]{:S(2)}) async-start(), calls=%async_computation.16 | async-start | bytes 2621440 | tf_op jit(solution)/shard_map/reduce_scatter | solution.py:1002
  304.7 6.8 %collective-permute-start.15 = (f32[128,128]{1,0:T(8,128)S(1)}, f32[128,128]{1,0:T(8,128)S(1)}, u32[]{:S(2)}, u32[]{:S(2)}) collective-permute-start(f32[128,128]{1,0:T(8,128)S(1)} %get-tuple-element.122), channel_id=1, source_target_pairs={{0,96},{32,0},{64,32},{96,64},{1,97},{33,1},{65,33},{97,65},{2,98}... | collective-permute-start | bytes 196616 | tf_op jit(solution)/shard_map/ppermute | solution.py:898
  305.1 36.5 %all-to-all-start.7 = ((bf16[16,4,16,1024]{3,2,1,0:T(8,128)(2,1)}), bf16[16,4,16,1024]{3,2,1,0:T(8,128)(2,1)S(1)}, u32[]{:S(2)}, u32[]{:S(2)}) async-start(bf16[16,4,16,1024]{3,2,1,0:T(8,128)(2,1)} %get-tuple-element.94._), calls=%async_computation.10 | async-start | bytes 4194304 | tf_op jit(solution)/shard_map/all_to_all | solution.py:1012
  308.8 7.5 %collective-permute-start.16 = (f32[128,128]{1,0:T(8,128)S(1)}, f32[128,128]{1,0:T(8,128)S(1)}, u32[]{:S(2)}, u32[]{:S(2)}) collective-permute-start(f32[128,128]{1,0:T(8,128)S(1)} %get-tuple-element.121), channel_id=1, source_target_pairs={{0,64},{32,96},{64,0},{96,32},{1,65},{33,97},{65,1},{97,33},{2,66}... | collective-permute-start | bytes 196616 | tf_op jit(solution)/shard_map/ppermute | solution.py:898
  310.6 6.6 %collective-permute-start.17 = (f32[128,128]{1,0:T(8,128)S(1)}, f32[128,128]{1,0:T(8,128)S(1)}, u32[]{:S(2)}, u32[]{:S(2)}) collective-permute-start(f32[128,128]{1,0:T(8,128)S(1)} %get-tuple-element.120), channel_id=1, source_target_pairs={{0,32},{32,64},{64,96},{96,0},{1,33},{33,65},{65,97},{97,1},{2,34}... | collective-permute-start | bytes 196616 | tf_op jit(solution)/shard_map/ppermute | solution.py:898
  341.6 14.9 %all-to-all-start.6 = ((bf16[16,8,2176]{2,1,0:T(8,128)(2,1)}), bf16[16,8,2176]{2,1,0:T(8,128)(2,1)S(1)}, u32[]{:S(2)}, u32[]{:S(2)}) async-start(bf16[16,8,2176]{2,1,0:T(8,128)(2,1)} %maximum_bitcast_fusion), calls=%async_computation.9 | async-start | bytes 1114112 | tf_op jit(solution)/shard_map/all_to_all | solution.py:1006
  346.9 9.6 %collective-permute-start.18 = (bf16[48,1024]{1,0:T(8,128)(2,1)S(1)}, bf16[48,1024]{1,0:T(8,128)(2,1)S(1)}, u32[]{:S(2)}, u32[]{:S(2)}) collective-permute-start(bf16[48,1024]{1,0:T(8,128)(2,1)S(1)} %get-tuple-element.118), channel_id=1, source_target_pairs={{0,32},{32,64},{64,96},{96,0},{1,33},{33,65},{65,97},{97,1},{2,34}... | collective-permute-start | bytes 294920 | tf_op jit(solution)/shard_map/ppermute | solution.py:898
  348.7 7.9 %collective-permute-start.19 = (bf16[48,1024]{1,0:T(8,128)(2,1)S(1)}, bf16[48,1024]{1,0:T(8,128)(2,1)S(1)}, u32[]{:S(2)}, u32[]{:S(2)}) collective-permute-start(bf16[48,1024]{1,0:T(8,128)(2,1)S(1)} %get-tuple-element.117), channel_id=1, source_target_pairs={{0,64},{32,96},{64,0},{96,32},{1,65},{33,97},{65,1},{97,33},{2,66}... | collective-permute-start | bytes 294920 | tf_op jit(solution)/shard_map/ppermute | solution.py:898
  350.1 6.5 %collective-permute-start.20 = (bf16[48,1024]{1,0:T(8,128)(2,1)S(1)}, bf16[48,1024]{1,0:T(8,128)(2,1)S(1)}, u32[]{:S(2)}, u32[]{:S(2)}) collective-permute-start(bf16[48,1024]{1,0:T(8,128)(2,1)S(1)} %get-tuple-element.116), channel_id=1, source_target_pairs={{0,96},{32,0},{64,32},{96,64},{1,97},{33,1},{65,33},{97,65},{2,98}... | collective-permute-start | bytes 294920 | tf_op jit(solution)/shard_map/ppermute | solution.py:898
  360.0 13.9 %all-to-all-start.8 = ((bf16[16,3,16,128]{3,2,1,0:T(8,128)(2,1)}), bf16[16,3,16,128]{3,2,1,0:T(8,128)(2,1)S(1)}, u32[]{:S(2)}, u32[]{:S(2)}) async-start(bf16[16,3,16,128]{3,2,1,0:T(8,128)(2,1)} %get-tuple-element.102), calls=%async_computation.11 | async-start | bytes 393216 | tf_op jit(solution)/shard_map/all_to_all | solution.py:1089
  378.9 11.8 %all-to-all-start.9 = ((bf16[16,3,16,128]{3,2,1,0:T(8,128)(2,1)}), bf16[16,3,16,128]{3,2,1,0:T(8,128)(2,1)S(1)}, u32[]{:S(2)}, u32[]{:S(2)}) async-start(bf16[16,3,16,128]{3,2,1,0:T(8,128)(2,1)} %get-tuple-element.105), calls=%async_computation.12 | async-start | bytes 393216 | tf_op jit(solution)/shard_map/all_to_all | solution.py:1091
  (22 other events, 200.2 us)
Sparse Core Ops, SparseCore 0:
  11.7 100.5 all-gather.1
  162.3 29.4 reduce-scatter.3
  229.3 28.3 reduce-scatter.5
  289.9 27.4 reduce-scatter.7

commit v3 on v2

--- a/solution.py
+++ b/solution.py
@@ -65,7 +65,7 @@
         ),
         compiler_params=pltpu.CompilerParams(vmem_limit_bytes=VMEM_BYTES),
         cost_estimate=pl.CostEstimate(
-            flops=flops, bytes_accessed=bytes_accessed, transcendentals=0
+            flops=7 * flops, bytes_accessed=bytes_accessed, transcendentals=0
         ),
     )
 
@@ -88,6 +88,19 @@
     for at in range(0, even.shape[1], TILE):
         blocks += [even[:, at : at + TILE], odd[:, at : at + TILE]]
     return jnp.concatenate(blocks, axis=1)
+
+
+def turn_rows(left, turned, parity):
+    for block in range(turned.shape[0] // TILE):
+        at = pl.multiple_of((2 * block + parity) * TILE, TILE)
+        turned[block * TILE : (block + 1) * TILE, :] = jnp.transpose(left[:, pl.ds(at, TILE)])
+
+
+def by_owner(values, plane):
+    rows, columns = values.shape
+    chips = rows // (8 * plane)
+    values = values.reshape(chips, plane, 8, columns)
+    return jnp.concatenate([values[chip] for chip in range(chips)], axis=1)
 
 
 def project_body(
@@ -216,7 +229,13 @@
     )(length, scales, projected, projected, projected)
 
 
-def attend_back_body(queries, keys, values, mixed, grads, weights, _, out):
+def attend_back_body(
+    core, queries, keys, values, mixed, grads, weights, normed, _, __, out, sent_qk, sent_v, turned
+):
+    @pl.when(pl.program_id(0) == 0)
+    def _():
+        turn_rows(normed, turned, 1 - core[0])
+
     rows = queries.shape[0]
     head_dim = TILE // 2
     block = rows // 2
@@ -247,16 +266,20 @@
                 k_total[into_part] = k_total[into_part] + k_new[cut]
                 v_total[into_part] = v_total[into_part] + v_new[cut]
     root = 1.0 / math.sqrt(head_dim)
-    for part in range(2):
-        cut = slice(part * block, (part + 1) * block)
-        out[0, cut, :] = (q_total[part] * root).astype(BF16)
-        out[1, cut, :] = (k_total[part] * root).astype(BF16)
-        out[2, cut, :] = v_total[part].astype(BF16)
-
-
-def attend_back(projected, mixed, grads, weights, wait):
+    low_q = (jnp.concatenate(q_total, axis=0) * root).astype(BF16)
+    low_k = (jnp.concatenate(k_total, axis=0) * root).astype(BF16)
+    low_v = jnp.concatenate(v_total, axis=0).astype(BF16)
+    out[0], out[1], out[2] = low_q, low_k, low_v
+    sent = dot_nn(turned[...], jnp.concatenate([low_q, low_k, low_v], axis=1))
+    sent_qk[0] = sent[:, :TILE].astype(BF16)
+    sent_qk[1] = sent[:, TILE : 2 * TILE].astype(BF16)
+    sent_v[...] = by_owner(sent[:, 2 * TILE :], sent_v.shape[0]).astype(BF16)
+
+
+def attend_back(core, plane, projected, mixed, grads, weights, normed, wait):
     rows, width3 = projected.shape
     width = width3 // 3
+    half = width // 2
     pairs = width // TILE
     block = rows // 2
     by_pair = pl.BlockSpec((rows, TILE), lambda pair, *_: (0, pair))
@@ -270,13 +293,24 @@
             by_pair,
             by_pair,
             pl.BlockSpec((2, block, 3 * block), lambda pair, *_: (pair, 0, 0)),
-            *after(wait),
-        ],
-        pl.BlockSpec((3, rows, TILE), lambda pair, *_: (0, 0, pair)),
-        jax.ShapeDtypeStruct((3, rows, width), BF16),
+            whole((rows, width)),
+            *after(*wait),
+        ],
+        [
+            pl.BlockSpec((3, rows, TILE), lambda pair, *_: (0, 0, pair)),
+            pl.BlockSpec((2, half, TILE), lambda pair, *_: (0, 0, pair)),
+            pl.BlockSpec((plane, half // plane, TILE), lambda pair, *_: (0, 0, pair)),
+        ],
+        [
+            jax.ShapeDtypeStruct((3, rows, width), BF16),
+            jax.ShapeDtypeStruct((2, half, width), BF16),
+            jax.ShapeDtypeStruct((plane, half // plane, width), BF16),
+        ],
+        scratch=[pltpu.VMEM((half, rows), BF16)],
         flops=10 * rows * rows * width,
         bytes_accessed=24 * rows * width,
-    )(projected, projected, projected, mixed, grads, weights, wait)
+        scalars=1,
+    )(core, projected, projected, projected, mixed, grads, weights, normed, *wait)
 
 
 def branch_body(core, scaled, own, other, tokens, vectors, branch, attended, normed, parts):
@@ -314,9 +348,29 @@
 
 
 def branch_back_body(
-    core, grad_attended, branch, own, other, mixed, scales, vectors, _, grad_branch, grad_mixed, sums, parts
+    core,
+    grad_attended,
+    branch,
+    own,
+    other,
+    mixed,
+    scales,
+    vectors,
+    scaled,
+    _,
+    __,
+    grad_branch,
+    grad_mixed,
+    sums,
+    sent,
+    staying,
+    parts,
+    lows,
+    turned,
 ):
-    @pl.when(pl.program_id(0) == 0)
+    at = pl.program_id(0)
+
+    @pl.when(at == 0)
     def _():
         sums[...] = jnp.zeros_like(sums)
 
@@ -325,6 +379,7 @@
     unit = centered * spread
     low = norm_back(grad * vectors[4:5, :], unit, spread).astype(BF16)
     grad_branch[...] = low
+    lows[at] = low
     me = core[0]
     parts[me] = dot_nt(low, own[...])
     parts[1 - me] = dot_nt(low, other[...])
@@ -335,8 +390,16 @@
     sums[2:3, :] += jnp.sum(low.astype(F32), axis=0, keepdims=True)
     sums[3:4, :] += jnp.sum(grad_scaled * mixed[...], axis=0, keepdims=True)
 
-
-def branch_back(core, grad_attended, branch, weights, mixed, scales, vectors, wait):
+    @pl.when(at == pl.num_programs(0) - 1)
+    def _():
+        right = lows[...].reshape(scaled.shape)
+        turn_rows(scaled, turned, 1 - me)
+        sent[...] = dot_nn(turned[...], right).astype(BF16)
+        turn_rows(scaled, turned, me)
+        staying[...] = dot_nn(turned[...], right)
+
+
+def branch_back(core, grad_attended, branch, weights, mixed, scales, vectors, scaled, *wait):
     rows, width = branch.shape
     block = rows // 4
     by_row = pl.BlockSpec((block, width), lambda at, *_: (at, 0))
@@ -352,29 +415,82 @@
             by_row,
             whole(scales.shape),
             whole(vectors.shape),
-            *after(wait),
-        ],
-        [by_row, by_row, whole((8, width))],
+            whole(scaled.shape),
+            *after(*wait),
+        ],
+        [by_row, by_row, whole((8, width)), whole((width // 2, width)), whole((width // 2, width))],
         [
             jax.ShapeDtypeStruct((rows, width), BF16),
             jax.ShapeDtypeStruct((rows, width), BF16),
             jax.ShapeDtypeStruct((8, width), F32),
-        ],
-        scratch=[pltpu.VMEM((2, block, width // 2), F32)],
-        flops=2 * rows * width * width,
+            jax.ShapeDtypeStruct((width // 2, width), BF16),
+            jax.ShapeDtypeStruct((width // 2, width), F32),
+        ],
+        scratch=[
+            pltpu.VMEM((2, block, width // 2), F32),
+            pltpu.VMEM((rows // block, block, width), BF16),
+            pltpu.VMEM((width // 2, rows), BF16),
+        ],
+        flops=4 * rows * width * width,
         bytes_accessed=2 * width * width + 16 * rows * width,
         scalars=1,
-    )(core, grad_attended, branch, *weights[2:], mixed, scales, vectors, wait)
+    )(core, grad_attended, branch, *weights[2:], mixed, scales, vectors, scaled, *wait)
+
+
+def send_part(values, step, first, second):
+    @pl.when(step < 2)
+    def _():
+        first[...] = values.astype(BF16)
+
+    @pl.when(step >= 2)
+    def _():
+        second[...] = by_owner(values, second.shape[0]).astype(BF16)
+
+
+def part_specs(half, plane, start):
+    return [
+        pl.BlockSpec((half, 1024), lambda at, *_: (0, jnp.clip(at - start, 0, 1))),
+        pl.BlockSpec(
+            (plane, half // plane, 1024), lambda at, *_: (0, 0, jnp.clip(at - start - 2, 0, 1))
+        ),
+    ]
+
+
+def part_shapes(half, plane):
+    return [
+        jax.ShapeDtypeStruct((half, 2048), BF16),
+        jax.ShapeDtypeStruct((plane, half // plane, 2048), BF16),
+    ]
 
 
 def forward_ffn_body(
-    steps, normed, attended, vectors, rows_of, up, down, output, top, kept, slope, stats, held, total, sums
+    steps,
+    core,
+    normed,
+    attended,
+    vectors,
+    rows_of,
+    up,
+    down,
+    upstream,
+    output,
+    top,
+    kept,
+    slope,
+    stats,
+    sent_first,
+    sent_second,
+    held,
+    total,
+    sums,
+    turned,
 ):
     at = pl.program_id(0)
     width = held.shape[2]
 
     @pl.when(at == 0)
     def _():
+        turn_rows(upstream, turned, 1 - core[0])
         sums[...] = jnp.zeros_like(sums)
 
     @pl.when(at < steps)
@@ -410,19 +526,20 @@
         low = ((value - mean) * spread * rows_of[1:2, :] + rows_of[2:3, :]).astype(BF16)
         top[...] = low
         total[...] += dot_nt(low, down[...])
+        send_part(dot_nn(turned[...], low), at - steps, sent_first, sent_second)
 
     @pl.when(at == 2 * steps - 1)
     def _():
         output[...] = total[...].astype(BF16)
 
 
-def forward_ffn(normed, attended, vectors, wide_rows, both):
+def forward_ffn(core, plane, normed, attended, vectors, wide_rows, both, upstream):
     rows, width = attended.shape
     hidden = both.shape[1] // 2
     block = 1024
     steps = hidden // block
-    early = lambda at: (0, jnp.minimum(at, steps - 1))
-    late = lambda at: (0, jnp.maximum(at - steps, 0))
+    early = lambda at, *_: (0, jnp.minimum(at, steps - 1))
+    late = lambda at, *_: (0, jnp.maximum(at - steps, 0))
     return call(
         functools.partial(forward_ffn_body, steps),
         (2 * steps,),
@@ -430,9 +547,10 @@
             whole((rows, width)),
             whole((rows, width)),
             whole(vectors.shape),
-            pl.BlockSpec((8, block), lambda at: (0, lax.rem(at, steps))),
+            pl.BlockSpec((8, block), lambda at, *_: (0, lax.rem(at, steps))),
             pl.BlockSpec((width, block), early),
-            pl.BlockSpec((width, block), lambda at: (0, steps + jnp.maximum(at - steps, 0))),
+            pl.BlockSpec((width, block), lambda at, *_: (0, steps + jnp.maximum(at - steps, 0))),
+            whole((rows, width)),
         ],
         [
             whole((rows, width)),
@@ -440,6 +558,7 @@
             pl.BlockSpec((rows, block), early),
             pl.BlockSpec((rows, block), early),
             whole((rows, 2 * TILE)),
+            *part_specs(width // 2, plane, steps),
         ],
         [
             jax.ShapeDtypeStruct((rows, width), BF16),
@@ -447,19 +566,23 @@
             jax.ShapeDtypeStruct((rows, hidden), BF16),
             jax.ShapeDtypeStruct((rows, hidden), BF16),
             jax.ShapeDtypeStruct((rows, 2 * TILE), F32),
+            *part_shapes(width // 2, plane),
         ],
         scratch=[
             pltpu.VMEM((steps, rows, block), F32),
             pltpu.VMEM((rows, width), F32),
             pltpu.VMEM((rows, TILE), F32),
-        ],
-        flops=4 * rows * width * hidden,
+            pltpu.VMEM((width // 2, rows), BF16),
+        ],
+        flops=5 * rows * width * hidden,
         bytes_accessed=4 * width * hidden + 6 * rows * hidden,
-    )(normed, attended, vectors, wide_rows, both, both)
+        scalars=1,
+    )(core, normed, attended, vectors, wide_rows, both, both, upstream)
 
 
 def backward_ffn_body(
     steps,
+    core,
     upstream,
     attended,
     vectors,
@@ -469,15 +592,19 @@
     slope,
     down,
     up,
+    normed,
     _,
     grad_attended,
     grad_hidden,
     wide_sums,
     sums,
+    sent_first,
+    sent_second,
     held,
     total,
     first,
     second,
+    turned,
 ):
     at = pl.program_id(0)
     count = steps * held.shape[2]
@@ -486,6 +613,7 @@
 
     @pl.when(at == 0)
     def _():
+        turn_rows(normed, turned, 1 - core[0])
         first[...] = jnp.zeros_like(first)
         second[...] = jnp.zeros_like(second)
         total[...] = jnp.zeros_like(total)
@@ -521,6 +649,7 @@
         grad_hidden[...] = low
         wide_sums[at - steps, 2:3, :] = jnp.sum(low.astype(F32), axis=0, keepdims=True)
         total[...] += dot_nt(low, up[...])
+        send_part(dot_nn(turned[...], low), at - steps, sent_first, sent_second)
 
     @pl.when(at == 2 * steps - 1)
     def _():
@@ -535,13 +664,15 @@
         sums[3:8, :] = jnp.zeros((5, sums.shape[1]), F32)
 
 
-def backward_ffn(upstream, attended, vectors, wide_rows, stats, kept, slope, both, wait):
+def backward_ffn(
+    core, plane, upstream, attended, vectors, wide_rows, stats, kept, slope, both, normed, wait
+):
     rows, width = attended.shape
     hidden = both.shape[1] // 2
     block = 1024
     steps = hidden // block
-    late = lambda at: (0, jnp.maximum(at - steps, 0))
-    turn = lambda at: (0, lax.rem(at, steps))
+    late = lambda at, *_: (0, jnp.maximum(at - steps, 0))
+    turn = lambda at, *_: (0, lax.rem(at, steps))
     return call(
         functools.partial(backward_ffn_body, steps),
         (2 * steps,),
@@ -553,8 +684,9 @@
             whole((rows, 2 * TILE)),
             pl.BlockSpec((rows, block), turn),
             pl.BlockSpec((rows, block), late),
-            pl.BlockSpec((width, block), lambda at: (0, steps + jnp.minimum(at, steps - 1))),
+            pl.BlockSpec((width, block), lambda at, *_: (0, steps + jnp.minimum(at, steps - 1))),
             pl.BlockSpec((width, block), late),
+            whole((rows, width)),
             *after(wait),
         ],
         [
@@ -562,22 +694,26 @@
             pl.BlockSpec((rows, block), late),
             whole((steps, 8, block)),
             whole((8, width)),
+            *part_specs(width // 2, plane, steps),
         ],
         [
             jax.ShapeDtypeStruct((rows, width), F32),
             jax.ShapeDtypeStruct((rows, hidden), BF16),
             jax.ShapeDtypeStruct((steps, 8, block), F32),
             jax.ShapeDtypeStruct((8, width), F32),
+            *part_shapes(width // 2, plane),
         ],
         scratch=[
             pltpu.VMEM((steps, rows, block), F32),
             pltpu.VMEM((rows, width), F32),
             pltpu.VMEM((rows, TILE), F32),
             pltpu.VMEM((rows, TILE), F32),
-        ],
-        flops=4 * rows * width * hidden,
+            pltpu.VMEM((width // 2, rows), BF16),
+        ],
+        flops=5 * rows * width * hidden,
         bytes_accessed=4 * width * hidden + 8 * rows * hidden,
-    )(upstream, attended, vectors, wide_rows, stats, kept, slope, both, both, wait)
+        scalars=1,
+    )(core, upstream, attended, vectors, wide_rows, stats, kept, slope, both, both, normed, wait)
 
 
 def input_back_body(
@@ -593,7 +729,6 @@
     branch_sums,
     mid_sums,
     wide_sums,
-    _,
     input_grad,
     turned,
     parts,
@@ -652,7 +787,7 @@
             )
 
 
-def input_back(core, grads, weights, tokens, grad_attended, vectors, sums, wait):
+def input_back(core, grads, weights, tokens, grad_attended, vectors, sums):
     rows, width = tokens.shape
     full = whole((rows, width))
     third = pl.BlockSpec((width // 2, width), lambda part, *_: (0, jnp.minimum(part, 1)))
@@ -670,7 +805,6 @@
             full,
             whole(vectors.shape),
             *[whole(item.shape) for item in sums],
-            *after(wait),
         ],
         [full, whole((width // TILE, TILE, TILE))],
         [
@@ -678,129 +812,77 @@
             jax.ShapeDtypeStruct((width // TILE, TILE, TILE), F32),
         ],
         scratch=[pltpu.VMEM((2, rows, width // 2), F32), pltpu.VMEM((TILE, width), F32)],
-        flops=1,
-        bytes_accessed=1,
+        flops=6 * rows * width * width,
+        bytes_accessed=6 * width * width + 16 * rows * width,
         scalars=1,
-    )(core, grads, *weights, tokens, grad_attended, vectors, *sums, wait)
-
-
-def outer_body(two_lefts, adds, _, *refs):
-    lefts = refs[: 4 * (1 + two_lefts)]
-    refs = refs[4 * (1 + two_lefts) :]
-    early, late, upper, lower = refs[:4]
-    refs = refs[4:]
-    if adds:
-        add_first, add_second = refs[:2]
-        refs = refs[2:]
-    first, second = refs[:2]
-    turned = refs[2:]
+    )(core, grads, *weights, tokens, grad_attended, vectors, *sums)
+
+
+def outer_body(firsts, core, left, right, add_first, add_second, *refs):
+    first, second, turned = refs[-3:]
     at = pl.program_id(0)
 
     @pl.when(at == 0)
     def _():
-        for which in range(1 + two_lefts):
-            for block in range(4):
-                turned[which][block * TILE : (block + 1) * TILE, :] = jnp.transpose(
-                    lefts[4 * which + block][...]
-                )
-
-    def write_first(left, right):
-        value = dot_nn(left[...], right[...])
-        if adds:
-            value = value + add_first[...].astype(F32)
-        first[...] = value.astype(BF16)
-
-    pl.when(at == 0)(lambda: write_first(turned[two_lefts], early))
-    pl.when(at == 1)(lambda: write_first(turned[0], late))
-
-    @pl.when(at >= 2)
-    def _():
-        above = dot_nn(turned[0][...], upper[...])
-        below = dot_nn(turned[0][...], lower[...])
-        plane, chips = second.shape[:2]
-        for chip in range(chips):
-            cut = slice(chip * 8 * plane, (chip + 1) * 8 * plane)
-            value = jnp.concatenate(
-                [
-                    above[cut].reshape(plane, 8, above.shape[1]),
-                    below[cut].reshape(plane, 8, below.shape[1]),
-                ],
-                axis=1,
-            )
-            if adds:
-                value = value + add_second[:, chip].astype(F32)
-            second[:, chip] = value.astype(BF16)
-
-
-def outer(core, chips, left, rights, other_left=None, add=None, wait=()):
+        turn_rows(left, turned, core[0])
+
+    value = dot_nn(turned[...], right[...])
+
+    @pl.when(at < firsts)
+    def _():
+        first[...] = (value + add_first[...].astype(F32)).astype(BF16)
+
+    @pl.when(at >= firsts)
+    def _():
+        second[...] = (
+            by_owner(value, second.shape[0]) + add_second[...].astype(F32)
+        ).astype(BF16)
+
+
+def outer(core, left, right, add, wait=()):
     rows, width = left.shape
-    lefts = [left] if other_left is None else [left, other_left]
     half = width // 2
-    plane = half // (8 * chips)
-
-    def left_spec(block):
-        return pl.BlockSpec((rows, TILE), lambda at, core, block=block: (0, 2 * block + core[0]))
-
-    def right_spec(index, start, columns, low, high):
-        def where(at, *_):
-            column = start // columns + jnp.clip(at - low, 0, high)
-            return (index, 0, column)
-
-        return pl.BlockSpec((None, rows, columns), where)
-
-    specs, operands = [], []
-    for one in lefts:
-        for block in range(4):
-            specs.append(left_spec(block))
-            operands.append(one)
-    for (array, index, start), columns, low, high in zip(
-        rights, (1024, 1024, 512, 512), (0, 0, 2, 2), (0, 0, 1, 1)
-    ):
-        specs.append(right_spec(index, start, columns, low, high))
-        operands.append(array)
-    part_specs = [
-        pl.BlockSpec((half, 1024), lambda at, *_: (0, jnp.clip(at, 0, 1))),
-        pl.BlockSpec((plane, chips, 16, 512), lambda at, *_: (0, 0, 0, jnp.clip(at - 2, 0, 1))),
-    ]
-    if add is not None:
-        specs += part_specs
-        operands += list(add)
-
-    def body(core, *refs):
-        used = len(operands)
-        outer_body(len(lefts) - 1, add is not None, core, *refs[:used], *refs[used + len(wait) :])
-
+    block = 1024
+    add_first, add_second = add
+    plane, owned = add_second.shape[:2]
+    firsts = 2
+    seconds = add_second.shape[2] // block
+    if right.ndim == 2:
+        right_spec = pl.BlockSpec((rows, block), lambda at, *_: (0, at))
+        add_spec = pl.BlockSpec((half, block), lambda at, *_: (0, jnp.clip(at, 0, 1)))
+    else:
+        right_spec = pl.BlockSpec((None, rows, block), lambda at, *_: (at, 0, 0))
+        add_spec = pl.BlockSpec((None, half, block), lambda at, *_: (jnp.clip(at, 0, 1), 0, 0))
+    second_spec = pl.BlockSpec(
+        (plane, owned, block), lambda at, *_: (0, 0, jnp.clip(at - firsts, 0, seconds - 1))
+    )
     return call(
-        body,
-        (4,),
-        specs + after(*wait),
-        part_specs,
-        [
-            jax.ShapeDtypeStruct((half, 2048), BF16),
-            jax.ShapeDtypeStruct((plane, chips, 16, 1024), BF16),
-        ],
-        scratch=[pltpu.VMEM((half, rows), BF16) for _ in lefts],
-        flops=4 * rows * half * 2048,
-        bytes_accessed=4 * half * 4096,
+        functools.partial(outer_body, firsts),
+        (firsts + seconds,),
+        [whole((rows, width)), right_spec, add_spec, second_spec, *after(*wait)],
+        [pl.BlockSpec((half, block), lambda at, *_: (0, jnp.clip(at, 0, 1))), second_spec],
+        [
+            jax.ShapeDtypeStruct((half, firsts * block), BF16),
+            jax.ShapeDtypeStruct(add_second.shape, BF16),
+        ],
+        scratch=[pltpu.VMEM((half, rows), BF16)],
+        flops=2 * rows * half * block * (firsts + seconds),
+        bytes_accessed=6 * half * block * (firsts + seconds),
         scalars=1,
-    )(core, *operands, *wait)
-
-
-def to_slots_body(perm, down, up, attn, own, *refs):
-    more, (grad_qkv, grad_out, grad_up, grad_down, slots, tiles) = refs[:3], refs[3:]
-    rest = own[...]
-    for one in more:
-        rest = rest + one[...].astype(F32)
+    )(core, left, right, add_first, add_second, *wait)
+
+
+def to_slots_body(perm, down, parts, rest, *refs):
+    grad_qkv, grad_out, grad_up, grad_down, slots, tiles = refs
     width = grad_out.shape[1]
     half = down.shape[1]
-    grad_out[...] = attn[:, :width]
-    grad_qkv[:, :width] = attn[:, width : 2 * width]
-    grad_qkv[:, width : 2 * width] = rest[32:40]
-    grad_qkv[:, 2 * width :] = rest[40:48]
-    for result, first, at in ((grad_down, down, 0), (grad_up, up, 16)):
-        result[:, :half] = first[...]
-        result[:, half : half + width] = rest[at : at + 8]
-        result[:, half + width :] = rest[at + 8 : at + 16]
+    grad_out[...] = parts[:, half : half + width]
+    grad_qkv[:, : 2 * width] = parts[:, half + width : half + 3 * width]
+    grad_qkv[:, 2 * width :] = rest[:, 2 * half :]
+    grad_down[:, :half] = down[...]
+    grad_down[:, half:] = rest[:, :half]
+    grad_up[:, :half] = parts[:, :half]
+    grad_up[:, half:] = rest[:, half : 2 * half]
     column = 0
     for result in (grad_qkv, grad_out, grad_up, grad_down):
         for at in range(0, result.shape[1], TILE):
@@ -812,8 +894,8 @@
         slots[slot // pairs, slot % pairs] = jnp.concatenate(pair, axis=0).astype(BF16)
 
 
-def to_slots(perm, down, up, attn, rest, plane, widths):
-    arrays = [down, up, attn, *rest]
+def to_slots(perm, down, parts, rest, plane, widths):
+    arrays = [down, parts, rest]
     pairs = perm.shape[0] // (2 * plane)
     shapes = [jax.ShapeDtypeStruct((8, columns), F32) for columns in widths]
     shapes.append(jax.ShapeDtypeStruct((plane, pairs, 16, TILE), BF16))
@@ -994,8 +1076,8 @@
     normed, projected = project(core_arg, tokens, vector_rows, weights)
     mixed, scaled, attention = attend(lengths, head_scale, projected)
     branch, attended, normed_mid = branch_out(core_arg, scaled, weights, tokens, vector_rows)
-    output, normed_top, kept, slope, stats = forward_ffn(
-        normed_mid, attended, vector_rows, wide_rows, both
+    output, normed_top, kept, slope, stats, *sent_down = forward_ffn(
+        core_arg, plane, normed_mid, attended, vector_rows, wide_rows, both, upstream
     )
 
     def over_x(part):
@@ -1012,43 +1094,57 @@
         total = lax.all_to_all(part, "fsdp", split_axis=0, concat_axis=0, tiled=True)
         return sum_parts(total)
 
-    def four(array):
-        return [(array[None], 0, start) for start in (0, 1024, 2048, 3072)]
-
-    sent_down = outer(1 - core_arg, chips, upstream, four(normed_top))
     down_first, down_second = outer(
-        core_arg, chips, upstream, four(normed_top), add=[swap_cores(part) for part in sent_down]
+        core_arg, upstream, normed_top, [swap_cores(part) for part in sent_down]
     )
     down_rest = plane_first(down_second)
-    down_part = over_plane(over_x(down_first))
-    grad_attended, grad_hidden, wide_sums, mid_sums = backward_ffn(
-        upstream, attended, vector_rows, wide_rows, stats, kept, slope, both, down_second
-    )
-    sent_up = outer(1 - core_arg, chips, normed_mid, four(grad_hidden))
-    grad_branch, grad_mixed, branch_sums = branch_back(
-        core_arg, grad_attended, branch, weights, mixed, scales, vector_rows, sent_up[1]
+    down_chips = over_x(down_first)
+    down_part = over_plane(down_chips)
+    grad_attended, grad_hidden, wide_sums, mid_sums, *sent_up = backward_ffn(
+        core_arg,
+        plane,
+        upstream,
+        attended,
+        vector_rows,
+        wide_rows,
+        stats,
+        kept,
+        slope,
+        both,
+        normed_mid,
+        down_second,
+    )
+    grad_branch, grad_mixed, branch_sums, out_sent, out_stays = branch_back(
+        core_arg,
+        grad_attended,
+        branch,
+        weights,
+        mixed,
+        scales,
+        vector_rows,
+        scaled,
+        down_rest,
+        down_chips,
     )
     up_first, up_second = outer(
         core_arg,
-        chips,
         normed_mid,
-        four(grad_hidden),
-        add=[swap_cores(part) for part in sent_up],
-        wait=(grad_branch, down_rest, down_part),
-    )
+        grad_hidden,
+        [swap_cores(part) for part in sent_up],
+        wait=(grad_branch,),
+    )
+    up_second, _ = lax.optimization_barrier((up_second, down_part))
     up_rest = plane_first(up_second)
-    up_part = over_plane(over_x(up_first))
-    grads = attend_back(projected, mixed, grad_mixed, attention, up_second)
-    rights = [(grad_branch[None], 0, 0), (grads, 0, 0), (grads, 1, 0), (grads, 2, 0)]
-    sent_attn = outer(1 - core_arg, chips, normed, rights, other_left=scaled)
-    attn_first, attn_second = outer(
+    out_first = (out_stays + swap_cores(out_sent).astype(F32)).astype(BF16)
+    grads, *sent_attn = attend_back(
         core_arg,
-        chips,
+        plane,
+        projected,
+        mixed,
+        grad_mixed,
+        attention,
         normed,
-        rights,
-        other_left=scaled,
-        add=[swap_cores(part) for part in sent_attn],
-        wait=(up_rest, up_part),
+        (up_second, out_first),
     )
     input_grad, turned = input_back(
         core_arg,
@@ -1058,30 +1154,42 @@
         grad_attended,
         vector_rows,
         (branch_sums, mid_sums, wide_sums),
-        attn_second,
-    )
-    attn_rest = plane_first(attn_second)
-
+    )
     turned = turned.reshape(chips, 2, TILE, TILE)
     kept_sums = lax.dynamic_slice_in_dim(turned, core, 1, 1, allow_negative_indices=False)[:, 0]
     sent_sums = lax.dynamic_slice_in_dim(
         turned, 1 - core, 1, 1, allow_negative_indices=False
     )[:, 0]
-    small = jnp.sum(in_order(across_chips(kept_sums + swap_cores(sent_sums))), axis=0)
-
-    rest = jnp.concatenate([down_rest, up_rest, attn_rest], axis=1).astype(BF16)
-    rest = across_chips(rest)
-    rest[0] = rest[0].astype(F32)
-    attn_part = over_plane(jnp.concatenate([over_x(attn_first), small.astype(BF16)], axis=1))
-    vector_grads = attn_part[:, 2 * width :].T[: vectors.shape[0]]
-    head_total = attn_part[0, 2 * width + HEAD_AT : 2 * width + HEAD_AT + heads]
+    half_sums = kept_sums + swap_cores(sent_sums)
+    attn_first, attn_second = outer(
+        core_arg,
+        normed,
+        grads,
+        [swap_cores(part) for part in sent_attn],
+        wait=(half_sums, up_rest),
+    )
+    attn_rest = plane_first(attn_second)
+
+    half_sums, _ = lax.optimization_barrier((half_sums, attn_second))
+    small = jnp.sum(in_order(across_chips(half_sums)), axis=0)
+
+    rest = jnp.concatenate([down_rest, up_rest, attn_rest], axis=1)
+    rest = across_chips(rest.astype(BF16).reshape(chips, shard, -1))
+    rest = sum(part.astype(F32) for part in rest)
+    parts = over_plane(
+        jnp.concatenate(
+            [over_x(up_first), over_x(out_first), over_x(attn_first), small.astype(BF16)], axis=1
+        )
+    )
+    small = parts[:, hidden // 2 + 3 * width :]
+    vector_grads = small.T[: vectors.shape[0]]
+    head_total = small[0, HEAD_AT : HEAD_AT + heads]
 
     masters = (w_qkv, w_out, w_up, w_down)
     grad_qkv, grad_out, grad_up, grad_down, slots = to_slots(
         owner_perm,
         down_part,
-        up_part,
-        attn_part,
+        parts,
         rest,
         plane,
         [item.shape[1] for item in masters],

time: 407 us -> 393 us (0.966)
  Pallas kernels: 164 us -> 155 us
  waiting for transfers between devices: 119 us -> 112 us
  other arithmetic: 16.3 us -> 22.6 us
    pallas_call x6 -> x3, Pallas kernels: 45.9 us -> 24.6 us  [outer(): call(functools.partial(outer_body, firsts), (firsts + seconds,), [whole((...]
    all_to_all x3, waiting for transfers between devices: 32.5 us -> 12.1 us  [plane_first(): lax.all_to_all(part, 'fsdp', split_axis=0, concat_axis=0, tiled=True)]
    ppermute x12, waiting for transfers between devices: 35.5 us -> 42.3 us  [turn_chips(): lax.ppermute(values, 'x', [(at, (at + step) % count) for at in range(coun...]
    ppermute x9 -> x10, waiting for transfers between devices: 8.2 us -> 11.2 us  [swap_cores(): return lax.ppermute(values, 'core', [(0, 1), (1, 0)])]
    all_to_all x3 -> x2, starting transfers between devices: 13.5 us -> 12.9 us  [over_plane(): lax.all_to_all(part.reshape(plane, shard, -1), 'fsdp', split_axis=0, conc...]
    all_to_all x3 -> x2, waiting for transfers between devices: 16.1 us -> 15.8 us  [over_plane(): lax.all_to_all(part.reshape(plane, shard, -1), 'fsdp', split_axis=0, conc...]
  transfers between devices with their start and end apart: 35 -> 36, of which waited for: 18 -> 20; matrix products, arithmetic and copies ran while one was open for 6% -> 7% of each run, Pallas kernels for 25% -> 29%
where the time goes in v3:
time: 393 us; the launch traced here: 387 us
  Pallas kernels  155 us (39%)
  waiting for transfers between devices  112 us (28%)
  starting transfers between devices  67 us (17%)
  other arithmetic  22.6 us (6%)
  between operations  15.2 us (4%)
  local copies, waits for them, and re-layouts  14.7 us (4%)
    ppermute x12, waiting for transfers between devices, turn_chips(): lax.ppermute(values, 'x', [(at, (at + step) % count) for at in range(coun...  42.3 us
    pallas_call x1, Pallas kernels, backward_ffn(): call(functools.partial(backward_ffn_body, steps), (2 * steps,), [whole((r...  27.6 us
    pallas_call x1, Pallas kernels, forward_ffn(): call(functools.partial(forward_ffn_body, steps), (2 * steps,), [whole((ro...  25.7 us
    pallas_call x3, Pallas kernels, outer(): call(functools.partial(outer_body, firsts), (firsts + seconds,), [whole((...  24.6 us
    all_to_all x3, starting transfers between devices, plane_first(): lax.all_to_all(part, 'fsdp', split_axis=0, concat_axis=0, tiled=True)  18.3 us
    pallas_call x1, Pallas kernels, attend_back(): call(attend_back_body, (pairs,), [by_pair, pl.BlockSpec((rows, TILE), lam...  16.8 us
    all_to_all x2, waiting for transfers between devices, over_plane(): lax.all_to_all(part.reshape(plane, shard, -1), 'fsdp', split_axis=0, conc...  15.8 us
    ppermute x12, starting transfers between devices, turn_chips(): lax.ppermute(values, 'x', [(at, (at + step) % count) for at in range(coun...  13.7 us
  transfers between devices with their start and end apart: 36, of which 20 were waited for; matrix products, arithmetic and copies ran while one was open for 7% of the time, Pallas kernels for 29%

profile of v3, /device:TPU:0, one launch (start us, length us, event | category | flops | bytes accessed | tf_op | source)
XLA Modules:
  0.0 386.6 jit_solution(1743376268247062604)
XLA Ops:
  17.6 8.0 %all-to-all-start = ((bf16[16,8,2176]{2,1,0:T(8,128)(2,1)}), bf16[16,8,2176]{2,1,0:T(8,128)(2,1)S(1)}, u32[]{:S(2)}, u32[]{:S(2)}) async-start(bf16[16,8,2176]{2,1,0:T(8,128)(2,1)} %broadcast_in_dim.41), calls=%async_computation | async-start | bytes 1114112 | tf_op jit(solution)/shard_map/all_to_all | solution.py:1033
  25.7 11.9 %all-to-all-done = bf16[16,8,2176]{2,1,0:T(8,128)(2,1)S(1)} async-done(((bf16[16,8,2176]{2,1,0:T(8,128)(2,1)}), bf16[16,8,2176]{2,1,0:T(8,128)(2,1)S(1)}, u32[]{:S(2)}, u32[]{:S(2)}) %all-to-all-start) | async-done | bytes 557088 | tf_op jit(solution)/shard_map/all_to_all | solution.py:1033
  41.6 3.7 all-to-all-start.1
  46.9 15.8 %collective-permute-done = bf16[128,2176]{1,0:T(8,128)(2,1)S(1)} collective-permute-done((bf16[128,2176]{1,0:T(8,128)(2,1)S(1)}, bf16[128,2176]{1,0:T(8,128)(2,1)S(1)}, u32[]{:S(2)}, u32[]{:S(2)}) %collective-permute-start) | collective-permute-done | bytes 557088 | tf_op jit(solution)/shard_map/ppermute | solution.py:980
  65.8 11.0 %collective-permute-done.2 = bf16[128,2176]{1,0:T(8,128)(2,1)S(1)} collective-permute-done((bf16[128,2176]{1,0:T(8,128)(2,1)S(1)}, bf16[128,2176]{1,0:T(8,128)(2,1)S(1)}, u32[]{:S(2)}, u32[]{:S(2)}) %collective-permute-start.2) | collective-permute-done | bytes 557088 | tf_op jit(solution)/shard_map/ppermute | solution.py:980
  87.0 8.6 %shard_map.304 = (bf16[512,1024]{1,0:T(8,128)(2,1)}, bf16[512,3072]{1,0:T(8,128)(2,1)}) custom-call(s32[1]{0:T(128)} %bitcast.core, bf16[512,1024]{1,0:T(8,128)(2,1)} %tokens.5, f32[24,1024]{1,0:T(8,128)} %copy-done.6, bf16[512,2176]{1,0:T(8,128)(2,1)} %bitcast.7.own_qk, bf16[512,2176]{1,0:T(8,128)(2,1)} %collective-permute-done.3.other_qk, ...), custom_call_target="tpu_custom_call" | custom-call | flops 22548578304 | bytes 6291456 | tf_op jit(solution)/shard_map/pallas_call | solution.py:141
  95.6 13.5 %shard_map.305 = (f32[512,1024]{1,0:T(8,128)}, bf16[512,1024]{1,0:T(8,128)(2,1)}, bf16[16,256,768]{2,1,0:T(8,128)(2,1)}) custom-call(s32[1]{0:T(128)S(6)} %copy.65.length, f32[16]{0:T(128)} %scales.1, bf16[512,3072]{1,0:T(8,128)(2,1)} %get-tuple-element.69.queries.keys.values, bf16[512,3072]{1,0:T(8,128)(2,1)} %get-tuple-element.69.queries.keys.values, ...), custom_call_target="tpu_custom_call" | custom-call | flops 7516192768 | bytes 10485760 | tf_op jit(solution)/shard_map/pallas_call | solution.py:208
  109.1 6.5 %shard_map.306 = (f32[512,1024]{1,0:T(8,128)}, f32[512,1024]{1,0:T(8,128)}, bf16[512,1024]{1,0:T(8,128)(2,1)}) custom-call(s32[1]{0:T(128)} %bitcast.core, bf16[512,1024]{1,0:T(8,128)(2,1)} %get-tuple-element.70.scaled, bf16[512,2048]{1,0:T(8,128)(2,1)} %bitcast.19.own_vo.own, bf16[512,2048]{1,0:T(8,128)(2,1)} %collective-permute-done.7.other_vo.other, ...), custom_call_target="tpu_custom_call" | custom-call | flops 7516192768 | bytes 9437184 | tf_op jit(solution)/shard_map/pallas_call | solution.py:333
  115.6 25.7 %shard_map.307 = (bf16[512,1024]{1,0:T(8,128)(2,1)}, bf16[512,4096]{1,0:T(8,128)(2,1)}, bf16[512,4096]{1,0:T(8,128)(2,1)}, bf16[512,4096]{1,0:T(8,128)(2,1)}, f3...) custom-call(s32[1]{0:T(128)} %bitcast.core, ...), custom_call_target="tpu_custom_call" | custom-call | flops 75161927680 | bytes 29360128 | tf_op jit(solution)/shard_map/pallas_call | solution.py:543
  141.9 3.8 collective-permute-done.8.add_first
  148.8 8.4 %shard_map.308 = (bf16[512,2048]{1,0:T(8,128)(2,1)}, bf16[16,32,2048]{2,1,0:T(8,128)(2,1)}) custom-call(s32[1]{0:T(128)} %bitcast.core, bf16[512,1024]{1,0:T(8,128)(2,1)} %broadcast_select_fusion.upstream.left, bf16[512,4096]{1,0:T(8,128)(2,1)} %get-tuple-element.78.right, bf16[512,2048]{1,0:T(8,128)(2,1)} %collective-permute-done.8.add_first, ...), custom_call_target="tpu_custom_call" | custom-call | flops 15032385536 | bytes 12582912 | tf_op jit(solution)/shard_map/pallas_call | solution.py:859
  157.2 6.8 %all-to-all-start.2 = ((bf16[16,32,2048]{2,1,0:T(8,128)(2,1)}), bf16[16,32,2048]{2,1,0:T(8,128)(2,1)S(1)}, u32[]{:S(2)}, u32[]{:S(2)}) async-start(bf16[16,32,2048]{2,1,0:T(8,128)(2,1)} %get-tuple-element.81._), calls=%async_computation.2 | async-start | bytes 4194304 | tf_op jit(solution)/shard_map/all_to_all | solution.py:1094
  165.1 27.6 %shard_map.309 = (f32[512,1024]{1,0:T(8,128)}, bf16[512,4096]{1,0:T(8,128)(2,1)}, f32[4,8,1024]{2,1,0:T(8,128)}, f32[8,1024]{1,0:T(8,128)}, bf16[512,2048]{1,0:T(8,128)(2,1)}, /*index=5*/bf16[16,32,2048]{2,1,0:T(8,128)(2,1)}) custom-call(s32[1]{0:T(128)} %bitcast.core, bf16[512,1024]{1,0:T(8,128)(2,1)} %broadcast_select_fusion.upstream.left, ...), custom_call_target="tpu_custom_call" | custom-call | flops 75161927680 | bytes 33554432 | tf_op jit(solution)/shard_map/pallas_call | solution.py:676
  193.2 3.7 all-to-all-done.2
  198.6 11.2 %shard_map.310 = (bf16[512,1024]{1,0:T(8,128)(2,1)}, bf16[512,1024]{1,0:T(8,128)(2,1)}, f32[8,1024]{1,0:T(8,128)}, bf16[512,1024]{1,0:T(8,128)(2,1)}, f32[512,1024]{1,0:T(8,128)}) custom-call(s32[1]{0:T(128)} %bitcast.core, f32[512,1024]{1,0:T(8,128)} %get-tuple-element.82.grad_attended, f32[512,1024]{1,0:T(8,128)} %get-tuple-element.83.branch, ...), custom_call_target="tpu_custom_call" | custom-call | flops 15032385536 | bytes 10485760 | tf_op jit(solution)/shard_map/pallas_call | solution.py:407
  215.8 5.9 %all-to-all-start.3 = ((bf16[16,8,2048]{2,1,0:T(8,128)(2,1)}), bf16[16,8,2048]{2,1,0:T(8,128)(2,1)S(1)}, u32[]{:S(2)}, u32[]{:S(2)}) async-start(bf16[16,8,2048]{2,1,0:T(8,128)(2,1)} %bitcast.20), calls=%async_computation.4 | async-start | bytes 1048576 | tf_op jit(solution)/shard_map/all_to_all | solution.py:1088
  221.8 8.7 %shard_map.311 = (bf16[512,2048]{1,0:T(8,128)(2,1)}, bf16[16,32,2048]{2,1,0:T(8,128)(2,1)}) custom-call(s32[1]{0:T(128)} %bitcast.core, bf16[512,1024]{1,0:T(8,128)(2,1)} %get-tuple-element.71.normed.left, bf16[512,4096]{1,0:T(8,128)(2,1)} %get-tuple-element.88.right, bf16[512,2048]{1,0:T(8,128)(2,1)} %collective-permute-done.10.add_first, ...), custom_call_target="tpu_custom_call" | custom-call | flops 15032385536 | bytes 12582912 | tf_op jit(solution)/shard_map/pallas_call | solution.py:859
  234.2 4.2 %all-to-all-start.4 = ((bf16[16,32,2048]{2,1,0:T(8,128)(2,1)}), bf16[16,32,2048]{2,1,0:T(8,128)(2,1)S(1)}, u32[]{:S(2)}, u32[]{:S(2)}) async-start(bf16[16,32,2048]{2,1,0:T(8,128)(2,1)} %get-tuple-element.93._), calls=%async_computation.7 | async-start | bytes 4194304 | tf_op jit(solution)/shard_map/all_to_all | solution.py:1094
  238.9 16.8 %shard_map.312 = (bf16[3,512,1024]{2,1,0:T(8,128)(2,1)}, bf16[2,512,1024]{2,1,0:T(8,128)(2,1)}, bf16[16,32,1024]{2,1,0:T(8,128)(2,1)}) custom-call(s32[1]{0:T(128)} %bitcast.core, bf16[512,3072]{1,0:T(8,128)(2,1)} %get-tuple-element.69.queries.keys.values, bf16[512,3072]{1,0:T(8,128)(2,1)} %get-tuple-element.69.queries.keys.values, ...), custom_call_target="tpu_custom_call" | custom-call | flops 18790481920 | bytes 12582912 | tf_op jit(solution)/shard_map/pallas_call | solution.py:286
  256.2 11.2 %shard_map.313 = (f32[512,1024]{1,0:T(8,128)}, f32[8,128,128]{2,1,0:T(8,128)}) custom-call(s32[1]{0:T(128)} %bitcast.core, bf16[3,512,1024]{2,1,0:T(8,128)(2,1)} %get-tuple-element.96.grads.right, bf16[512,2176]{1,0:T(8,128)(2,1)} %bitcast.7.own_qk, bf16[512,2176]{1,0:T(8,128)(2,1)} %collective-permute-done.3.other_qk, ...), custom_call_target="tpu_custom_call" | custom-call | flops 22548578304 | bytes 14680064 | tf_op jit(solution)/shard_map/pallas_call | solution.py:795
  273.8 7.4 %shard_map.314 = (bf16[512,2048]{1,0:T(8,128)(2,1)}, bf16[16,32,1024]{2,1,0:T(8,128)(2,1)}) custom-call(s32[1]{0:T(128)} %bitcast.core, bf16[512,1024]{1,0:T(8,128)(2,1)} %get-tuple-element.87.normed.left, bf16[3,512,1024]{2,1,0:T(8,128)(2,1)} %get-tuple-element.96.grads.right, bf16[2,512,1024]{2,1,0:T(8,128)(2,1)} %collective-permute-done.13.add_first, ...), custom_call_target="tpu_custom_call" | custom-call | flops 11274289152 | bytes 9437184 | tf_op jit(solution)/shard_map/pallas_call | solution.py:859
  283.0 7.3 %all-to-all-start.6 = ((bf16[16,32,1024]{2,1,0:T(8,128)(2,1)}), bf16[16,32,1024]{2,1,0:T(8,128)(2,1)S(1)}, u32[]{:S(2)}, u32[]{:S(2)}) async-start(bf16[16,32,1024]{2,1,0:T(8,128)(2,1)} %get-tuple-element.106), calls=%async_computation.10 | async-start | bytes 2097152 | tf_op jit(solution)/shard_map/all_to_all | solution.py:1094
  292.6 5.7 %collective-permute-done.17 = f32[128,128]{1,0:T(8,128)S(1)} collective-permute-done((f32[128,128]{1,0:T(8,128)S(1)}, f32[128,128]{1,0:T(8,128)S(1)}, u32[]{:S(2)}, u32[]{:S(2)}) %collective-permute-start.17) | collective-permute-done | bytes 65568 | tf_op jit(solution)/shard_map/ppermute | solution.py:980
  299.6 8.4 %all-to-all-done.6 = bf16[16,32,1024]{2,1,0:T(8,128)(2,1)S(1)} async-done(((bf16[16,32,1024]{2,1,0:T(8,128)(2,1)}), bf16[16,32,1024]{2,1,0:T(8,128)(2,1)S(1)}, u32[]{:S(2)}, u32[]{:S(2)}) %all-to-all-start.6) | async-done | bytes 1048608 | tf_op jit(solution)/shard_map/all_to_all | solution.py:1094
  310.5 3.1 reduce-scatter.11.cloned.1.call-done
  316.1 7.0 %all-to-all-start.5 = ((bf16[16,8,5248]{2,1,0:T(8,128)(2,1)}), bf16[16,8,5248]{2,1,0:T(8,128)(2,1)S(1)}, u32[]{:S(2)}, u32[]{:S(2)}) async-start(bf16[16,8,5248]{2,1,0:T(8,128)(2,1)} %maximum_bitcast_fusion), calls=%async_computation.9 | async-start | bytes 2686976 | tf_op jit(solution)/shard_map/all_to_all | solution.py:1088
  331.8 12.7 %all-to-all-done.5 = bf16[16,8,5248]{2,1,0:T(8,128)(2,1)S(1)} async-done(((bf16[16,8,5248]{2,1,0:T(8,128)(2,1)}), bf16[16,8,5248]{2,1,0:T(8,128)(2,1)S(1)}, u32[]{:S(2)}, u32[]{:S(2)}) %all-to-all-start.5) | async-done | bytes 1343520 | tf_op jit(solution)/shard_map/all_to_all | solution.py:1088
  347.9 3.5 all-to-all-start.7
  352.1 7.7 %all-to-all-done.7.grads = bf16[16,3,16,128]{3,2,1,0:T(8,128)(2,1)S(1)} async-done(((bf16[16,3,16,128]{3,2,1,0:T(8,128)(2,1)}), bf16[16,3,16,128]{3,2,1,0:T(8,128)(2,1)S(1)}, u32[]{:S(2)}, u32[]{:S(2)}) %all-to-all-start.7) | async-done | bytes 196640 | tf_op jit(solution)/shard_map/all_to_all | solution.py:1197
  360.4 4.3 %shard_map.316 = (f32[6,128,128]{2,1,0:T(8,128)}, f32[6,128,128]{2,1,0:T(8,128)}, bf16[16,3,16,128]{3,2,1,0:T(8,128)(2,1)}) custom-call(bf16[16,3,16,128]{3,2,1,0:T(8,128)(2,1)} %copy-done.3, f32[6,128,128]{2,1,0:T(8,128)} %bitcast.104, f32[6,128,128]{2,1,0:T(8,128)} %bitcast.105, f32[6,128,128]{2,1,0:T(8,128)} %bitcast.106, f32[6,128,128]{2,1,0:T(8,128)} %bitcast.107), custom_call_target="tpu_custom_call" | custom-call | bytes 2359296 | tf_op jit(solution)/shard_map/pallas_call | solution.py:934
  364.8 3.5 all-to-all-start.8
  369.6 7.0 %all-to-all-done.8.moved = bf16[16,3,16,128]{3,2,1,0:T(8,128)(2,1)S(1)} async-done(((bf16[16,3,16,128]{3,2,1,0:T(8,128)(2,1)}), bf16[16,3,16,128]{3,2,1,0:T(8,128)(2,1)S(1)}, u32[]{:S(2)}, u32[]{:S(2)}) %all-to-all-start.8) | async-done | bytes 196640 | tf_op jit(solution)/shard_map/all_to_all | solution.py:1199
  (161 shorter events, 80.4 us)
Async XLA Ops:
  7.2 108.4 %all-gather.2.cloned.1.call-start = ((), (), s32[]{:S(2)}) async-start(), calls=%async_computation.13 | async-start | bytes 16908288 | tf_op jit(solution)/shard_map/all_gather | solution.py:1016
  11.4 14.2 %collective-permute-start.4 = (bf16[8,2048]{1,0:T(8,128)(2,1)S(1)}, bf16[8,2048]{1,0:T(8,128)(2,1)S(1)}, u32[]{:S(2)}, u32[]{:S(2)}) collective-permute-start(bf16[8,2048]{1,0:T(8,128)(2,1)S(1)} %pad_maximum_fusion.2), channel_id=1, source_target_pairs={{0,96},{32,0},{64,32},{96,64},{1,97},{33,1},{65,33},{97,65},{2,98}... | collective-permute-start | bytes 98312 | tf_op jit(solution)/shard_map/ppermute | solution.py:980
  14.3 11.3 %collective-permute-start.5 = (bf16[8,2048]{1,0:T(8,128)(2,1)S(1)}, bf16[8,2048]{1,0:T(8,128)(2,1)S(1)}, u32[]{:S(2)}, u32[]{:S(2)}) collective-permute-start(bf16[8,2048]{1,0:T(8,128)(2,1)S(1)} %pad_maximum_fusion.2), channel_id=1, source_target_pairs={{0,64},{32,96},{64,0},{96,32},{1,65},{33,97},{65,1},{97,33},{2,66}... | collective-permute-start | bytes 98312 | tf_op jit(solution)/shard_map/ppermute | solution.py:980
  15.1 10.5 %collective-permute-start.6 = (bf16[8,2048]{1,0:T(8,128)(2,1)S(1)}, bf16[8,2048]{1,0:T(8,128)(2,1)S(1)}, u32[]{:S(2)}, u32[]{:S(2)}) collective-permute-start(bf16[8,2048]{1,0:T(8,128)(2,1)S(1)} %pad_maximum_fusion.2), channel_id=1, source_target_pairs={{0,32},{32,64},{64,96},{96,0},{1,33},{33,65},{65,97},{97,1},{2,34}... | collective-permute-start | bytes 98312 | tf_op jit(solution)/shard_map/ppermute | solution.py:980
  17.6 20.1 %all-to-all-start = ((bf16[16,8,2176]{2,1,0:T(8,128)(2,1)}), bf16[16,8,2176]{2,1,0:T(8,128)(2,1)S(1)}, u32[]{:S(2)}, u32[]{:S(2)}) async-start(bf16[16,8,2176]{2,1,0:T(8,128)(2,1)} %broadcast_in_dim.41), calls=%async_computation | async-start | bytes 1114112 | tf_op jit(solution)/shard_map/all_to_all | solution.py:1033
  37.6 25.2 %collective-permute-start = (bf16[128,2176]{1,0:T(8,128)(2,1)S(1)}, bf16[128,2176]{1,0:T(8,128)(2,1)S(1)}, u32[]{:S(2)}, u32[]{:S(2)}) collective-permute-start(bf16[128,2176]{1,0:T(8,128)(2,1)S(1)} %bitcast.97), channel_id=1, source_target_pairs={{0,96},{32,0},{64,32},{96,64},{1,97},{33,1},{65,33},{97,65},{2,98}... | collective-permute-start | bytes 1671176 | tf_op jit(solution)/shard_map/ppermute | solution.py:980
  41.6 37.1 %all-to-all-start.1 = ((bf16[16,4,8,2048]{3,2,1,0:T(8,128)(2,1)}), bf16[16,4,8,2048]{3,2,1,0:T(8,128)(2,1)S(1)}, u32[]{:S(2)}, u32[]{:S(2)}) async-start(bf16[16,4,8,2048]{3,2,1,0:T(8,128)(2,1)} %broadcast_in_dim.42), calls=%async_computation.1 | async-start | bytes 4194304 | tf_op jit(solution)/shard_map/all_to_all | solution.py:1033
  45.3 20.4 %collective-permute-start.1 = (bf16[128,2176]{1,0:T(8,128)(2,1)S(1)}, bf16[128,2176]{1,0:T(8,128)(2,1)S(1)}, u32[]{:S(2)}, u32[]{:S(2)}) collective-permute-start(bf16[128,2176]{1,0:T(8,128)(2,1)S(1)} %bitcast.98), channel_id=1, source_target_pairs={{0,64},{32,96},{64,0},{96,32},{1,65},{33,97},{65,1},{97,33},{2,66}... | collective-permute-start | bytes 1671176 | tf_op jit(solution)/shard_map/ppermute | solution.py:980
  46.9 29.9 %collective-permute-start.2 = (bf16[128,2176]{1,0:T(8,128)(2,1)S(1)}, bf16[128,2176]{1,0:T(8,128)(2,1)S(1)}, u32[]{:S(2)}, u32[]{:S(2)}) collective-permute-start(bf16[128,2176]{1,0:T(8,128)(2,1)S(1)} %bitcast.99), channel_id=1, source_target_pairs={{0,32},{32,64},{64,96},{96,0},{1,33},{33,65},{65,97},{97,1},{2,34}... | collective-permute-start | bytes 1671176 | tf_op jit(solution)/shard_map/ppermute | solution.py:980
  78.7 6.2 %collective-permute-start.3 = (bf16[512,2176]{1,0:T(8,128)(2,1)}, bf16[512,2176]{1,0:T(8,128)(2,1)}, u32[]{:S(2)}, u32[]{:S(2)}) collective-permute-start(bf16[512,2176]{1,0:T(8,128)(2,1)} %bitcast.7.own_qk), channel_id=1, source_target_pairs={{0,16},{16,0},{1,17},{17,1},{2,18},{18,2},{3,19},{19,3},{4,20},{20... | collective-permute-start | bytes 6684680 | tf_op jit(solution)/shard_map/ppermute | solution.py:975
  80.2 6.8 %collective-permute-start.7 = (bf16[512,2048]{1,0:T(8,128)(2,1)}, bf16[512,2048]{1,0:T(8,128)(2,1)}, u32[]{:S(2)}, u32[]{:S(2)}) collective-permute-start(bf16[512,2048]{1,0:T(8,128)(2,1)} %bitcast.19.own_vo.own), channel_id=1, source_target_pairs={{0,16},{16,0},{1,17},{17,1},{2,18},{18,2},{3,19},{19,3},{4,20},{20... | collective-permute-start | bytes 6291464 | tf_op jit(solution)/shard_map/ppermute | solution.py:975
  141.3 7.5 %collective-permute-start.9 = (bf16[16,32,2048]{2,1,0:T(8,128)(2,1)}, bf16[16,32,2048]{2,1,0:T(8,128)(2,1)}, u32[]{:S(2)}, u32[]{:S(2)}) collective-permute-start(bf16[16,32,2048]{2,1,0:T(8,128)(2,1)} %get-tuple-element.80), channel_id=1, source_target_pairs={{0,16},{16,0},{1,17},{17,1},{2,18},{18,2},{3,19},{19,3},{4,20},{20... | collective-permute-start | bytes 6291464 | tf_op jit(solution)/shard_map/ppermute | solution.py:975
  157.2 39.7 %all-to-all-start.2 = ((bf16[16,32,2048]{2,1,0:T(8,128)(2,1)}), bf16[16,32,2048]{2,1,0:T(8,128)(2,1)S(1)}, u32[]{:S(2)}, u32[]{:S(2)}) async-start(bf16[16,32,2048]{2,1,0:T(8,128)(2,1)} %get-tuple-element.81._), calls=%async_computation.2 | async-start | bytes 4194304 | tf_op jit(solution)/shard_map/all_to_all | solution.py:1094
  164.1 34.0 %reduce-scatter.5.cloned.1.call-start = ((), (), s32[]{:S(2)}) async-start(), calls=%async_computation.14 | async-start | bytes 2621440 | tf_op jit(solution)/shard_map/reduce_scatter | solution.py:1084
  164.8 145.6 %reduce-scatter.9.cloned.1.call-start = ((), (), s32[]{:S(2)}) async-start(), calls=%async_computation.16 | async-start | bytes 1310720 | tf_op jit(solution)/shard_map/reduce_scatter | solution.py:1084
  192.7 29.1 %collective-permute-start.10 = (bf16[512,2048]{1,0:T(8,128)(2,1)}, bf16[512,2048]{1,0:T(8,128)(2,1)}, u32[]{:S(2)}, u32[]{:S(2)}) collective-permute-start(bf16[512,2048]{1,0:T(8,128)(2,1)} %get-tuple-element.89), channel_id=1, source_target_pairs={{0,16},{16,0},{1,17},{17,1},{2,18},{18,2},{3,19},{19,3},{4,20},{20... | collective-permute-start | bytes 6291464 | tf_op jit(solution)/shard_map/ppermute | solution.py:975
  192.7 29.1 %collective-permute-start.11 = (bf16[16,32,2048]{2,1,0:T(8,128)(2,1)}, bf16[16,32,2048]{2,1,0:T(8,128)(2,1)}, u32[]{:S(2)}, u32[]{:S(2)}) collective-permute-start(bf16[16,32,2048]{2,1,0:T(8,128)(2,1)} %get-tuple-element.90), channel_id=1, source_target_pairs={{0,16},{16,0},{1,17},{17,1},{2,18},{18,2},{3,19},{19,3},{4,20},{20... | collective-permute-start | bytes 6291464 | tf_op jit(solution)/shard_map/ppermute | solution.py:975
  215.8 17.7 %all-to-all-start.3 = ((bf16[16,8,2048]{2,1,0:T(8,128)(2,1)}), bf16[16,8,2048]{2,1,0:T(8,128)(2,1)S(1)}, u32[]{:S(2)}, u32[]{:S(2)}) async-start(bf16[16,8,2048]{2,1,0:T(8,128)(2,1)} %bitcast.20), calls=%async_computation.4 | async-start | bytes 1048576 | tf_op jit(solution)/shard_map/all_to_all | solution.py:1088
  221.7 88.8 %reduce-scatter.7.cloned.1.call-start = ((), (), s32[]{:S(2)}) async-start(), calls=%async_computation.15 | async-start | bytes 2621440 | tf_op jit(solution)/shard_map/reduce_scatter | solution.py:1084
  234.2 37.5 %all-to-all-start.4 = ((bf16[16,32,2048]{2,1,0:T(8,128)(2,1)}), bf16[16,32,2048]{2,1,0:T(8,128)(2,1)S(1)}, u32[]{:S(2)}, u32[]{:S(2)}) async-start(bf16[16,32,2048]{2,1,0:T(8,128)(2,1)} %get-tuple-element.93._), calls=%async_computation.7 | async-start | bytes 4194304 | tf_op jit(solution)/shard_map/all_to_all | solution.py:1094
  238.4 75.2 %reduce-scatter.11.cloned.1.call-start = ((), (), s32[]{:S(2)}) async-start(), calls=%async_computation.17 | async-start | bytes 2621440 | tf_op jit(solution)/shard_map/reduce_scatter | solution.py:1084
  255.7 17.1 %collective-permute-start.13 = (bf16[2,512,1024]{2,1,0:T(8,128)(2,1)}, bf16[2,512,1024]{2,1,0:T(8,128)(2,1)}, u32[]{:S(2)}, u32[]{:S(2)}) collective-permute-start(bf16[2,512,1024]{2,1,0:T(8,128)(2,1)} %get-tuple-element.102), channel_id=1, source_target_pairs={{0,16},{16,0},{1,17},{17,1},{2,18},{18,2},{3,19},{19,3},{4,20},{20... | collective-permute-start | bytes 6291464 | tf_op jit(solution)/shard_map/ppermute | solution.py:975
  255.7 17.1 %collective-permute-start.14 = (bf16[16,32,1024]{2,1,0:T(8,128)(2,1)}, bf16[16,32,1024]{2,1,0:T(8,128)(2,1)S(1)}, u32[]{:S(2)}, u32[]{:S(2)}) collective-permute-start(bf16[16,32,1024]{2,1,0:T(8,128)(2,1)} %get-tuple-element.103), channel_id=1, source_target_pairs={{0,16},{16,0},{1,17},{17,1},{2,18},{18,2},{3,19},{19,3},{4,20},{20... | collective-permute-start | bytes 3145736 | tf_op jit(solution)/shard_map/ppermute | solution.py:975
  282.4 10.2 %collective-permute-start.16 = (f32[128,128]{1,0:T(8,128)S(1)}, f32[128,128]{1,0:T(8,128)S(1)}, u32[]{:S(2)}, u32[]{:S(2)}) collective-permute-start(f32[128,128]{1,0:T(8,128)S(1)} %get-tuple-element.131), channel_id=1, source_target_pairs={{0,96},{32,0},{64,32},{96,64},{1,97},{33,1},{65,33},{97,65},{2,98}... | collective-permute-start | bytes 196616 | tf_op jit(solution)/shard_map/ppermute | solution.py:980
  283.0 25.0 %all-to-all-start.6 = ((bf16[16,32,1024]{2,1,0:T(8,128)(2,1)}), bf16[16,32,1024]{2,1,0:T(8,128)(2,1)S(1)}, u32[]{:S(2)}, u32[]{:S(2)}) async-start(bf16[16,32,1024]{2,1,0:T(8,128)(2,1)} %get-tuple-element.106), calls=%async_computation.10 | async-start | bytes 2097152 | tf_op jit(solution)/shard_map/all_to_all | solution.py:1094
  290.3 7.9 %collective-permute-start.17 = (f32[128,128]{1,0:T(8,128)S(1)}, f32[128,128]{1,0:T(8,128)S(1)}, u32[]{:S(2)}, u32[]{:S(2)}) collective-permute-start(f32[128,128]{1,0:T(8,128)S(1)} %get-tuple-element.130), channel_id=1, source_target_pairs={{0,64},{32,96},{64,0},{96,32},{1,65},{33,97},{65,1},{97,33},{2,66}... | collective-permute-start | bytes 196616 | tf_op jit(solution)/shard_map/ppermute | solution.py:980
  291.8 7.7 %collective-permute-start.18 = (f32[128,128]{1,0:T(8,128)S(1)}, f32[128,128]{1,0:T(8,128)S(1)}, u32[]{:S(2)}, u32[]{:S(2)}) collective-permute-start(f32[128,128]{1,0:T(8,128)S(1)} %get-tuple-element.129), channel_id=1, source_target_pairs={{0,32},{32,64},{64,96},{96,0},{1,33},{33,65},{65,97},{97,1},{2,34}... | collective-permute-start | bytes 196616 | tf_op jit(solution)/shard_map/ppermute | solution.py:980
  316.1 28.4 %all-to-all-start.5 = ((bf16[16,8,5248]{2,1,0:T(8,128)(2,1)}), bf16[16,8,5248]{2,1,0:T(8,128)(2,1)S(1)}, u32[]{:S(2)}, u32[]{:S(2)}) async-start(bf16[16,8,5248]{2,1,0:T(8,128)(2,1)} %maximum_bitcast_fusion), calls=%async_computation.9 | async-start | bytes 2686976 | tf_op jit(solution)/shard_map/all_to_all | solution.py:1088
  324.1 6.7 %collective-permute-start.20 = (bf16[8,5120]{1,0:T(8,128)(2,1)S(1)}, bf16[8,5120]{1,0:T(8,128)(2,1)S(1)}, u32[]{:S(2)}, u32[]{:S(2)}) collective-permute-start(bf16[8,5120]{1,0:T(8,128)(2,1)S(1)} %get-tuple-element.127), channel_id=1, source_target_pairs={{0,64},{32,96},{64,0},{96,32},{1,65},{33,97},{65,1},{97,33},{2,66}... | collective-permute-start | bytes 245768 | tf_op jit(solution)/shard_map/ppermute | solution.py:980
  324.6 6.4 %collective-permute-start.19 = (bf16[8,5120]{1,0:T(8,128)(2,1)S(1)}, bf16[8,5120]{1,0:T(8,128)(2,1)S(1)}, u32[]{:S(2)}, u32[]{:S(2)}) collective-permute-start(bf16[8,5120]{1,0:T(8,128)(2,1)S(1)} %get-tuple-element.126), channel_id=1, source_target_pairs={{0,32},{32,64},{64,96},{96,0},{1,33},{33,65},{65,97},{97,1},{2,34}... | collective-permute-start | bytes 245768 | tf_op jit(solution)/shard_map/ppermute | solution.py:980
  347.9 11.8 %all-to-all-start.7 = ((bf16[16,3,16,128]{3,2,1,0:T(8,128)(2,1)}), bf16[16,3,16,128]{3,2,1,0:T(8,128)(2,1)S(1)}, u32[]{:S(2)}, u32[]{:S(2)}) async-start(bf16[16,3,16,128]{3,2,1,0:T(8,128)(2,1)} %get-tuple-element.112), calls=%async_computation.11 | async-start | bytes 393216 | tf_op jit(solution)/shard_map/all_to_all | solution.py:1197
  364.8 11.8 %all-to-all-start.8 = ((bf16[16,3,16,128]{3,2,1,0:T(8,128)(2,1)}), bf16[16,3,16,128]{3,2,1,0:T(8,128)(2,1)S(1)}, u32[]{:S(2)}, u32[]{:S(2)}) async-start(bf16[16,3,16,128]{3,2,1,0:T(8,128)(2,1)} %get-tuple-element.115), calls=%async_computation.12 | async-start | bytes 393216 | tf_op jit(solution)/shard_map/all_to_all | solution.py:1199
  (18 other events, 180.3 us)
Sparse Core Ops, SparseCore 0:
  11.7 100.5 all-gather.1
  167.3 29.5 reduce-scatter.4
  215.9 22.1 reduce-scatter.8
  240.4 29.3 reduce-scatter.6
  281.4 32.1 reduce-scatter.10

commit v4 on v3

--- a/solution.py
+++ b/solution.py
@@ -65,7 +65,7 @@
         ),
         compiler_params=pltpu.CompilerParams(vmem_limit_bytes=VMEM_BYTES),
         cost_estimate=pl.CostEstimate(
-            flops=7 * flops, bytes_accessed=bytes_accessed, transcendentals=0
+            flops=flops, bytes_accessed=bytes_accessed, transcendentals=0
         ),
     )
 
@@ -230,7 +230,7 @@
 
 
 def attend_back_body(
-    core, queries, keys, values, mixed, grads, weights, normed, _, __, out, sent_qk, sent_v, turned
+    core, queries, keys, values, mixed, grads, weights, normed, _, out, sent_q, sent_k, sent_v, turned
 ):
     @pl.when(pl.program_id(0) == 0)
     def _():
@@ -270,13 +270,12 @@
     low_k = (jnp.concatenate(k_total, axis=0) * root).astype(BF16)
     low_v = jnp.concatenate(v_total, axis=0).astype(BF16)
     out[0], out[1], out[2] = low_q, low_k, low_v
-    sent = dot_nn(turned[...], jnp.concatenate([low_q, low_k, low_v], axis=1))
-    sent_qk[0] = sent[:, :TILE].astype(BF16)
-    sent_qk[1] = sent[:, TILE : 2 * TILE].astype(BF16)
-    sent_v[...] = by_owner(sent[:, 2 * TILE :], sent_v.shape[0]).astype(BF16)
-
-
-def attend_back(core, plane, projected, mixed, grads, weights, normed, wait):
+    values = dot_nn(turned[...], jnp.concatenate([low_q, low_k, low_v], axis=1)).astype(BF16)
+    for which, sent in enumerate((sent_q, sent_k, sent_v)):
+        sent[...] = values[:, which * TILE : (which + 1) * TILE]
+
+
+def attend_back(core, projected, mixed, grads, weights, normed, wait):
     rows, width3 = projected.shape
     width = width3 // 3
     half = width // 2
@@ -298,13 +297,11 @@
         ],
         [
             pl.BlockSpec((3, rows, TILE), lambda pair, *_: (0, 0, pair)),
-            pl.BlockSpec((2, half, TILE), lambda pair, *_: (0, 0, pair)),
-            pl.BlockSpec((plane, half // plane, TILE), lambda pair, *_: (0, 0, pair)),
+            *[pl.BlockSpec((half, TILE), lambda pair, *_: (0, pair)) for _ in range(3)],
         ],
         [
             jax.ShapeDtypeStruct((3, rows, width), BF16),
-            jax.ShapeDtypeStruct((2, half, width), BF16),
-            jax.ShapeDtypeStruct((plane, half // plane, width), BF16),
+            *[jax.ShapeDtypeStruct((half, width), BF16) for _ in range(3)],
         ],
         scratch=[pltpu.VMEM((half, rows), BF16)],
         flops=10 * rows * rows * width,
@@ -729,6 +726,7 @@
     branch_sums,
     mid_sums,
     wide_sums,
+    _,
     input_grad,
     turned,
     parts,
@@ -787,7 +785,7 @@
             )
 
 
-def input_back(core, grads, weights, tokens, grad_attended, vectors, sums):
+def input_back(core, grads, weights, tokens, grad_attended, vectors, sums, wait):
     rows, width = tokens.shape
     full = whole((rows, width))
     third = pl.BlockSpec((width // 2, width), lambda part, *_: (0, jnp.minimum(part, 1)))
@@ -805,6 +803,7 @@
             full,
             whole(vectors.shape),
             *[whole(item.shape) for item in sums],
+            *after(wait),
         ],
         [full, whole((width // TILE, TILE, TILE))],
         [
@@ -815,10 +814,10 @@
         flops=6 * rows * width * width,
         bytes_accessed=6 * width * width + 16 * rows * width,
         scalars=1,
-    )(core, grads, *weights, tokens, grad_attended, vectors, *sums)
-
-
-def outer_body(firsts, core, left, right, add_first, add_second, *refs):
+    )(core, grads, *weights, tokens, grad_attended, vectors, *sums, wait)
+
+
+def outer_body(firsts, more, core, left, right, add_first, add_second, *refs):
     first, second, turned = refs[-3:]
     at = pl.program_id(0)
 
@@ -831,6 +830,12 @@
     @pl.when(at < firsts)
     def _():
         first[...] = (value + add_first[...].astype(F32)).astype(BF16)
+
+    if more:
+
+        @pl.when(at == firsts)
+        def _():
+            first[...] = (refs[0][...] + refs[1][...].astype(F32)).astype(BF16)
 
     @pl.when(at >= firsts)
     def _():
@@ -839,7 +844,7 @@
         ).astype(BF16)
 
 
-def outer(core, left, right, add, wait=()):
+def outer(core, left, right, add, wait=(), more=()):
     rows, width = left.shape
     half = width // 2
     block = 1024
@@ -847,41 +852,86 @@
     plane, owned = add_second.shape[:2]
     firsts = 2
     seconds = add_second.shape[2] // block
-    if right.ndim == 2:
-        right_spec = pl.BlockSpec((rows, block), lambda at, *_: (0, at))
-        add_spec = pl.BlockSpec((half, block), lambda at, *_: (0, jnp.clip(at, 0, 1)))
-    else:
-        right_spec = pl.BlockSpec((None, rows, block), lambda at, *_: (at, 0, 0))
-        add_spec = pl.BlockSpec((None, half, block), lambda at, *_: (jnp.clip(at, 0, 1), 0, 0))
+    right_spec = pl.BlockSpec((rows, block), lambda at, *_: (0, at))
+    add_spec = pl.BlockSpec((half, block), lambda at, *_: (0, jnp.clip(at, 0, 1)))
     second_spec = pl.BlockSpec(
         (plane, owned, block), lambda at, *_: (0, 0, jnp.clip(at - firsts, 0, seconds - 1))
     )
+    kinds = firsts + len(more) // 2
+    out_specs = [
+        pl.BlockSpec((half, block), lambda at, *_: (0, jnp.clip(at, 0, kinds - 1))),
+        second_spec,
+    ]
+    out_shape = [
+        jax.ShapeDtypeStruct((half, kinds * block), BF16),
+        jax.ShapeDtypeStruct(add_second.shape, BF16),
+    ]
     return call(
-        functools.partial(outer_body, firsts),
+        functools.partial(outer_body, firsts, len(more) > 0),
         (firsts + seconds,),
-        [whole((rows, width)), right_spec, add_spec, second_spec, *after(*wait)],
-        [pl.BlockSpec((half, block), lambda at, *_: (0, jnp.clip(at, 0, 1))), second_spec],
-        [
-            jax.ShapeDtypeStruct((half, firsts * block), BF16),
-            jax.ShapeDtypeStruct(add_second.shape, BF16),
-        ],
+        [
+            whole((rows, width)),
+            right_spec,
+            add_spec,
+            second_spec,
+            *[whole(item.shape) for item in more],
+            *after(*wait),
+        ],
+        out_specs,
+        out_shape,
         scratch=[pltpu.VMEM((half, rows), BF16)],
         flops=2 * rows * half * block * (firsts + seconds),
         bytes_accessed=6 * half * block * (firsts + seconds),
         scalars=1,
-    )(core, left, right, add_first, add_second, *wait)
-
-
-def to_slots_body(perm, down, parts, rest, *refs):
+    )(core, left, right, add_first, add_second, *more, *wait)
+
+
+def outer_stack_body(core, left, right, *refs):
+    adds, (out, turned) = refs[:3], refs[-2:]
+    at = pl.program_id(0)
+
+    @pl.when(at == 0)
+    def _():
+        turn_rows(left, turned, core[0])
+
+    value = dot_nn(turned[...], right[...])
+    for which, add in enumerate(adds):
+
+        @pl.when(at == which)
+        def _(add=add):
+            out[...] = (value + add[...].astype(F32)).astype(BF16)
+
+
+def outer_stack(core, left, rights, adds, *wait):
+    count, rows, width = rights.shape
+    half = width // 2
+    return call(
+        outer_stack_body,
+        (count,),
+        [
+            whole((rows, width)),
+            pl.BlockSpec((None, rows, width), lambda at, *_: (at, 0, 0)),
+            *[whole((half, width)) for _ in adds],
+            *after(*wait),
+        ],
+        pl.BlockSpec((half, width), lambda at, *_: (0, at)),
+        jax.ShapeDtypeStruct((half, count * width), BF16),
+        scratch=[pltpu.VMEM((half, rows), BF16)],
+        flops=2 * rows * half * width * count,
+        bytes_accessed=6 * half * width * count,
+        scalars=1,
+    )(core, left, rights, *adds, *wait)
+
+
+def to_slots_body(perm, early, late, rest, *refs):
     grad_qkv, grad_out, grad_up, grad_down, slots, tiles = refs
     width = grad_out.shape[1]
-    half = down.shape[1]
-    grad_out[...] = parts[:, half : half + width]
-    grad_qkv[:, : 2 * width] = parts[:, half + width : half + 3 * width]
-    grad_qkv[:, 2 * width :] = rest[:, 2 * half :]
-    grad_down[:, :half] = down[...]
+    half = 2 * width
+    grad_out[...] = early[:, half : half + width]
+    grad_qkv[...] = late[:, : 3 * width]
+    grad_down[:, :half] = early[:, half + width :]
     grad_down[:, half:] = rest[:, :half]
-    grad_up[:, :half] = parts[:, :half]
+    grad_up[:, :half] = early[:, :half]
     grad_up[:, half:] = rest[:, half : 2 * half]
     column = 0
     for result in (grad_qkv, grad_out, grad_up, grad_down):
@@ -894,8 +944,8 @@
         slots[slot // pairs, slot % pairs] = jnp.concatenate(pair, axis=0).astype(BF16)
 
 
-def to_slots(perm, down, parts, rest, plane, widths):
-    arrays = [down, parts, rest]
+def to_slots(perm, early, late, rest, plane, widths):
+    arrays = [early, late, rest]
     pairs = perm.shape[0] // (2 * plane)
     shapes = [jax.ShapeDtypeStruct((8, columns), F32) for columns in widths]
     shapes.append(jax.ShapeDtypeStruct((plane, pairs, 16, TILE), BF16))
@@ -1099,7 +1149,6 @@
     )
     down_rest = plane_first(down_second)
     down_chips = over_x(down_first)
-    down_part = over_plane(down_chips)
     grad_attended, grad_hidden, wide_sums, mid_sums, *sent_up = backward_ffn(
         core_arg,
         plane,
@@ -1132,19 +1181,18 @@
         grad_hidden,
         [swap_cores(part) for part in sent_up],
         wait=(grad_branch,),
-    )
-    up_second, _ = lax.optimization_barrier((up_second, down_part))
+        more=(out_stays, swap_cores(out_sent)),
+    )
     up_rest = plane_first(up_second)
-    out_first = (out_stays + swap_cores(out_sent).astype(F32)).astype(BF16)
+    up_chips = over_x(up_first)
     grads, *sent_attn = attend_back(
         core_arg,
-        plane,
         projected,
         mixed,
         grad_mixed,
         attention,
         normed,
-        (up_second, out_first),
+        (up_second,),
     )
     input_grad, turned = input_back(
         core_arg,
@@ -1154,42 +1202,35 @@
         grad_attended,
         vector_rows,
         (branch_sums, mid_sums, wide_sums),
-    )
+        up_second,
+    )
+
     turned = turned.reshape(chips, 2, TILE, TILE)
     kept_sums = lax.dynamic_slice_in_dim(turned, core, 1, 1, allow_negative_indices=False)[:, 0]
     sent_sums = lax.dynamic_slice_in_dim(
         turned, 1 - core, 1, 1, allow_negative_indices=False
     )[:, 0]
     half_sums = kept_sums + swap_cores(sent_sums)
-    attn_first, attn_second = outer(
-        core_arg,
-        normed,
-        grads,
-        [swap_cores(part) for part in sent_attn],
-        wait=(half_sums, up_rest),
-    )
-    attn_rest = plane_first(attn_second)
-
-    half_sums, _ = lax.optimization_barrier((half_sums, attn_second))
+    attn_first = outer_stack(
+        core_arg, normed, grads, [swap_cores(part) for part in sent_attn], half_sums, up_rest
+    )
+    half_sums, _ = lax.optimization_barrier((half_sums, attn_first))
     small = jnp.sum(in_order(across_chips(half_sums)), axis=0)
 
-    rest = jnp.concatenate([down_rest, up_rest, attn_rest], axis=1)
+    early_parts = over_plane(jnp.concatenate([up_chips, down_chips], axis=1))
+    rest = jnp.concatenate([down_rest, up_rest], axis=1)
     rest = across_chips(rest.astype(BF16).reshape(chips, shard, -1))
     rest = sum(part.astype(F32) for part in rest)
-    parts = over_plane(
-        jnp.concatenate(
-            [over_x(up_first), over_x(out_first), over_x(attn_first), small.astype(BF16)], axis=1
-        )
-    )
-    small = parts[:, hidden // 2 + 3 * width :]
+    late_parts = over_plane(jnp.concatenate([over_x(attn_first), small.astype(BF16)], axis=1))
+    small = late_parts[:, 3 * width :]
     vector_grads = small.T[: vectors.shape[0]]
     head_total = small[0, HEAD_AT : HEAD_AT + heads]
 
     masters = (w_qkv, w_out, w_up, w_down)
     grad_qkv, grad_out, grad_up, grad_down, slots = to_slots(
         owner_perm,
-        down_part,
-        parts,
+        early_parts,
+        late_parts,
         rest,
         plane,
         [item.shape[1] for item in masters],

time: 393 us -> 385 us (0.980)
  waiting for transfers between devices: 112 us -> 105 us
    reduce_scatter x4 -> x3, waiting for transfers between devices: 3.16 us -> 20.5 us  [over_x(): return lax.psum_scatter(part, 'x', scatter_dimension=0, tiled=True)]
    ppermute x12, waiting for transfers between devices: 42.3 us -> 29.8 us  [turn_chips(): lax.ppermute(values, 'x', [(at, (at + step) % count) for at in range(coun...]
    all_to_all x3 -> x2, waiting for transfers between devices: 12.1 us -> 3.94 us  [plane_first(): lax.all_to_all(part, 'fsdp', split_axis=0, concat_axis=0, tiled=True)]
    all_to_all x3 -> x2, starting transfers between devices: 18.3 us -> 10.8 us  [plane_first(): lax.all_to_all(part, 'fsdp', split_axis=0, concat_axis=0, tiled=True)]
    unnamed x48 -> x60, local copies, waits for them, and re-layouts: 4.49 us -> 8.07 us
    ppermute x10 -> x11, waiting for transfers between devices: 11.2 us -> 10.9 us  [swap_cores(): return lax.ppermute(values, 'core', [(0, 1), (1, 0)])]
  transfers between devices with their start and end apart: 36 -> 35, of which waited for: 20 -> 13; matrix products, arithmetic and copies ran while one was open for 7% -> 7% of each run, Pallas kernels for 29% -> 27%
where the time goes in v4:
time: 385 us; the launch traced here: 379 us
  Pallas kernels  157 us (41%)
  waiting for transfers between devices  105 us (27%)
  starting transfers between devices  64.3 us (17%)
  other arithmetic  18.9 us (5%)
  local copies, waits for them, and re-layouts  18.6 us (5%)
  between operations  15.2 us (4%)
    ppermute x12, waiting for transfers between devices, turn_chips(): lax.ppermute(values, 'x', [(at, (at + step) % count) for at in range(coun...  29.8 us
    pallas_call x1, Pallas kernels, backward_ffn(): call(functools.partial(backward_ffn_body, steps), (2 * steps,), [whole((r...  28 us
    pallas_call x1, Pallas kernels, forward_ffn(): call(functools.partial(forward_ffn_body, steps), (2 * steps,), [whole((ro...  25.7 us
    reduce_scatter x3, waiting for transfers between devices, over_x(): return lax.psum_scatter(part, 'x', scatter_dimension=0, tiled=True)  20.5 us
    pallas_call x2, Pallas kernels, outer(): call(functools.partial(outer_body, firsts, len(more) > 0), (firsts + seco...  18.2 us
    pallas_call x1, Pallas kernels, attend_back(): call(attend_back_body, (pairs,), [by_pair, pl.BlockSpec((rows, TILE), lam...  17.3 us
    ppermute x12, starting transfers between devices, turn_chips(): lax.ppermute(values, 'x', [(at, (at + step) % count) for at in range(coun...  16.5 us
    all_to_all x2, starting transfers between devices, over_plane(): lax.all_to_all(part.reshape(plane, shard, -1), 'fsdp', split_axis=0, conc...  14.4 us
  transfers between devices with their start and end apart: 35, of which 13 were waited for; matrix products, arithmetic and copies ran while one was open for 7% of the time, Pallas kernels for 27%

profile of v4, /device:TPU:0, one launch (start us, length us, event | category | flops | bytes accessed | tf_op | source)
XLA Modules:
  0.0 378.9 jit_solution(813664460530039994)
XLA Ops:
  11.4 2.9 collective-permute-start.4
  17.6 8.0 %all-to-all-start = ((bf16[16,8,2176]{2,1,0:T(8,128)(2,1)}), bf16[16,8,2176]{2,1,0:T(8,128)(2,1)S(1)}, u32[]{:S(2)}, u32[]{:S(2)}) async-start(bf16[16,8,2176]{2,1,0:T(8,128)(2,1)} %broadcast_in_dim.41), calls=%async_computation | async-start | bytes 1114112 | tf_op jit(solution)/shard_map/all_to_all | solution.py:1083
  25.7 11.9 %all-to-all-done = bf16[16,8,2176]{2,1,0:T(8,128)(2,1)S(1)} async-done(((bf16[16,8,2176]{2,1,0:T(8,128)(2,1)}), bf16[16,8,2176]{2,1,0:T(8,128)(2,1)S(1)}, u32[]{:S(2)}, u32[]{:S(2)}) %all-to-all-start) | async-done | bytes 557088 | tf_op jit(solution)/shard_map/all_to_all | solution.py:1083
  41.6 3.7 all-to-all-start.1
  47.0 15.8 %collective-permute-done = bf16[128,2176]{1,0:T(8,128)(2,1)S(1)} collective-permute-done((bf16[128,2176]{1,0:T(8,128)(2,1)S(1)}, bf16[128,2176]{1,0:T(8,128)(2,1)S(1)}, u32[]{:S(2)}, u32[]{:S(2)}) %collective-permute-start) | collective-permute-done | bytes 557088 | tf_op jit(solution)/shard_map/ppermute | solution.py:1030
  62.8 3.0 collective-permute-done.1
  65.9 11.0 %collective-permute-done.2 = bf16[128,2176]{1,0:T(8,128)(2,1)S(1)} collective-permute-done((bf16[128,2176]{1,0:T(8,128)(2,1)S(1)}, bf16[128,2176]{1,0:T(8,128)(2,1)S(1)}, u32[]{:S(2)}, u32[]{:S(2)}) %collective-permute-start.2) | collective-permute-done | bytes 557088 | tf_op jit(solution)/shard_map/ppermute | solution.py:1030
  87.5 8.6 %shard_map.304 = (bf16[512,1024]{1,0:T(8,128)(2,1)}, bf16[512,3072]{1,0:T(8,128)(2,1)}) custom-call(s32[1]{0:T(128)} %bitcast.core, bf16[512,1024]{1,0:T(8,128)(2,1)} %tokens.5, f32[24,1024]{1,0:T(8,128)} %copy-done.2, bf16[512,2176]{1,0:T(8,128)(2,1)} %bitcast.7.own_qk, bf16[512,2176]{1,0:T(8,128)(2,1)} %collective-permute-done.3.other_qk, ...), custom_call_target="tpu_custom_call" | custom-call | flops 3221225472 | bytes 6291456 | tf_op jit(solution)/shard_map/pallas_call | solution.py:141
  96.1 13.5 %shard_map.305 = (f32[512,1024]{1,0:T(8,128)}, bf16[512,1024]{1,0:T(8,128)(2,1)}, bf16[16,256,768]{2,1,0:T(8,128)(2,1)}) custom-call(s32[1]{0:T(128)S(6)} %copy.65.length, f32[16]{0:T(128)} %scales.1, bf16[512,3072]{1,0:T(8,128)(2,1)} %get-tuple-element.67.queries.keys.values, bf16[512,3072]{1,0:T(8,128)(2,1)} %get-tuple-element.67.queries.keys.values, ...), custom_call_target="tpu_custom_call" | custom-call | flops 1073741824 | bytes 10485760 | tf_op jit(solution)/shard_map/pallas_call | solution.py:208
  109.6 6.3 %shard_map.306 = (f32[512,1024]{1,0:T(8,128)}, f32[512,1024]{1,0:T(8,128)}, bf16[512,1024]{1,0:T(8,128)(2,1)}) custom-call(s32[1]{0:T(128)} %bitcast.core, bf16[512,1024]{1,0:T(8,128)(2,1)} %get-tuple-element.68.scaled, bf16[512,2048]{1,0:T(8,128)(2,1)} %bitcast.98, bf16[512,2048]{1,0:T(8,128)(2,1)} %collective-permute-done.7.other_vo.other, ...), custom_call_target="tpu_custom_call" | custom-call | flops 1073741824 | bytes 9437184 | tf_op jit(solution)/shard_map/pallas_call | solution.py:330
  115.9 25.7 %shard_map.307 = (bf16[512,1024]{1,0:T(8,128)(2,1)}, bf16[512,4096]{1,0:T(8,128)(2,1)}, bf16[512,4096]{1,0:T(8,128)(2,1)}, bf16[512,4096]{1,0:T(8,128)(2,1)}, f3...) custom-call(s32[1]{0:T(128)} %bitcast.core, ...), custom_call_target="tpu_custom_call" | custom-call | flops 10737418240 | bytes 29360128 | tf_op jit(solution)/shard_map/pallas_call | solution.py:540
  142.1 3.9 %collective-permute-done.8.add_first = bf16[512,2048]{1,0:T(8,128)(2,1)S(1)} collective-permute-done((bf16[512,2048]{1,0:T(8,128)(2,1)}, bf16[512,2048]{1,0:T(8,128)(2,1)S(1)}, u32[]{:S(2)}, u32[]{:S(2)}) %collective-permute-start.8) | collective-permute-done | bytes 2097184 | tf_op jit(solution)/shard_map/ppermute | solution.py:1025
  146.0 3.0 collective-permute-done.9.add_second
  150.3 8.5 %shard_map.308 = (bf16[512,2048]{1,0:T(8,128)(2,1)}, bf16[16,32,2048]{2,1,0:T(8,128)(2,1)}) custom-call(s32[1]{0:T(128)} %bitcast.core, bf16[512,1024]{1,0:T(8,128)(2,1)} %broadcast_select_fusion.upstream.left, bf16[512,4096]{1,0:T(8,128)(2,1)} %get-tuple-element.76.right, bf16[512,2048]{1,0:T(8,128)(2,1)} %copy-done.6, bf16[16,32,2048]{2,1,0:T(8,128)(2,1)} %copy-done.7), custom_call_target="tpu_custom_call" | custom-call | flops 2147483648 | bytes 12582912 | tf_op jit(solution)/shard_map/pallas_call | solution.py:869
  158.8 7.1 %all-to-all-start.2 = ((bf16[16,32,2048]{2,1,0:T(8,128)(2,1)}), bf16[16,32,2048]{2,1,0:T(8,128)(2,1)S(1)}, u32[]{:S(2)}, u32[]{:S(2)}) async-start(bf16[16,32,2048]{2,1,0:T(8,128)(2,1)} %get-tuple-element.79._), calls=%async_computation.2 | async-start | bytes 4194304 | tf_op jit(solution)/shard_map/all_to_all | solution.py:1144
  166.2 28.0 %shard_map.309 = (f32[512,1024]{1,0:T(8,128)}, bf16[512,4096]{1,0:T(8,128)(2,1)}, f32[4,8,1024]{2,1,0:T(8,128)}, f32[8,1024]{1,0:T(8,128)}, bf16[512,2048]{1,0:T(8,128)(2,1)}, /*index=5*/bf16[16,32,2048]{2,1,0:T(8,128)(2,1)}) custom-call(s32[1]{0:T(128)} %bitcast.core, bf16[512,1024]{1,0:T(8,128)(2,1)} %broadcast_select_fusion.upstream.left, ...), custom_call_target="tpu_custom_call" | custom-call | flops 10737418240 | bytes 33554432 | tf_op jit(solution)/shard_map/pallas_call | solution.py:673
  194.9 3.9 %all-to-all-done.2 = bf16[16,32,2048]{2,1,0:T(8,128)(2,1)S(1)} async-done(((bf16[16,32,2048]{2,1,0:T(8,128)(2,1)}), bf16[16,32,2048]{2,1,0:T(8,128)(2,1)S(1)}, u32[]{:S(2)}, u32[]{:S(2)}) %all-to-all-start.2) | async-done | bytes 2097184 | tf_op jit(solution)/shard_map/all_to_all | solution.py:1144
  200.5 11.3 %shard_map.310 = (bf16[512,1024]{1,0:T(8,128)(2,1)}, bf16[512,1024]{1,0:T(8,128)(2,1)}, f32[8,1024]{1,0:T(8,128)}, bf16[512,1024]{1,0:T(8,128)(2,1)}, f32[512,1024]{1,0:T(8,128)}) custom-call(s32[1]{0:T(128)} %bitcast.core, f32[512,1024]{1,0:T(8,128)} %get-tuple-element.80.grad_attended, f32[512,1024]{1,0:T(8,128)} %get-tuple-element.81.branch, ...), custom_call_target="tpu_custom_call" | custom-call | flops 2147483648 | bytes 10485760 | tf_op jit(solution)/shard_map/pallas_call | solution.py:404
  215.7 9.7 %shard_map.311 = (bf16[512,3072]{1,0:T(8,128)(2,1)}, bf16[16,32,2048]{2,1,0:T(8,128)(2,1)}) custom-call(s32[1]{0:T(128)} %bitcast.core, bf16[512,1024]{1,0:T(8,128)(2,1)} %get-tuple-element.69.normed.left, bf16[512,4096]{1,0:T(8,128)(2,1)} %get-tuple-element.86.right, bf16[512,2048]{1,0:T(8,128)(2,1)} %collective-permute-done.10.add_first, ...), custom_call_target="tpu_custom_call" | custom-call | flops 2147483648 | bytes 12582912 | tf_op jit(solution)/shard_map/pallas_call | solution.py:869
  225.5 3.7 all-to-all-start.4
  229.7 17.3 %shard_map.312 = (bf16[3,512,1024]{2,1,0:T(8,128)(2,1)}, bf16[512,1024]{1,0:T(8,128)(2,1)}, bf16[512,1024]{1,0:T(8,128)(2,1)}, bf16[512,1024]{1,0:T(8,128)(2,1)}) custom-call(s32[1]{0:T(128)} %bitcast.core, bf16[512,3072]{1,0:T(8,128)(2,1)} %get-tuple-element.67.queries.keys.values, bf16[512,3072]{1,0:T(8,128)(2,1)} %get-tuple-element.67.queries.keys.values, ...), custom_call_target="tpu_custom_call" | custom-call | flops 2684354560 | bytes 12582912 | tf_op jit(solution)/shard_map/pallas_call | solution.py:285
  247.7 11.2 %shard_map.313 = (f32[512,1024]{1,0:T(8,128)}, f32[8,128,128]{2,1,0:T(8,128)}) custom-call(s32[1]{0:T(128)} %bitcast.core, bf16[3,512,1024]{2,1,0:T(8,128)(2,1)} %get-tuple-element.93.grads.right, bf16[512,2176]{1,0:T(8,128)(2,1)} %bitcast.7.own_qk, bf16[512,2176]{1,0:T(8,128)(2,1)} %collective-permute-done.3.other_qk, bf16[512,2048]{1,0:T(8,128)(2,1)} %bitcast.100, ...), custom_call_target="tpu_custom_call" | custom-call | flops 3221225472 | bytes 14680064 | tf_op jit(solution)/shard_map/pallas_call | solution.py:793
  265.3 7.1 %shard_map.314 = bf16[512,3072]{1,0:T(8,128)(2,1)} custom-call(s32[1]{0:T(128)} %bitcast.core, bf16[512,1024]{1,0:T(8,128)(2,1)} %get-tuple-element.85.normed.left, bf16[3,512,1024]{2,1,0:T(8,128)(2,1)} %get-tuple-element.93.grads.right, bf16[512,1024]{1,0:T(8,128)(2,1)} %copy-done.10, bf16[512,1024]{1,0:T(8,128)(2,1)} %collective-permute-done.14.refs_1_, ...), custom_call_target="tpu_custom_call" | custom-call | flops 1610612736 | bytes 9437184 | tf_op jit(solution)/shard_map/pallas_call | solution.py:908
  284.8 7.1 %all-to-all-start.3 = ((bf16[16,8,5120]{2,1,0:T(8,128)(2,1)}), bf16[16,8,5120]{2,1,0:T(8,128)(2,1)S(1)}, u32[]{:S(2)}, u32[]{:S(2)}) async-start(bf16[16,8,5120]{2,1,0:T(8,128)(2,1)} %maximum_bitcast_fusion), calls=%async_computation.5 | async-start | bytes 2621440 | tf_op jit(solution)/shard_map/all_to_all | solution.py:1138
  292.0 20.4 %reduce-scatter.8.cloned.1.call-done = bf16[128,3072]{1,0:T(8,128)(2,1)} async-done(((bf16[512,3072]{1,0:T(8,128)(2,1)}), bf16[128,3072]{1,0:T(8,128)(2,1)}) %reduce-scatter.8.cloned.1.call-update) | async-done | bytes 786448 | tf_op jit(solution)/shard_map/reduce_scatter | solution.py:1134
  314.6 7.3 %all-to-all-start.5 = ((bf16[16,8,3200]{2,1,0:T(8,128)(2,1)}), bf16[16,8,3200]{2,1,0:T(8,128)(2,1)S(1)}, u32[]{:S(2)}, u32[]{:S(2)}) async-start(bf16[16,8,3200]{2,1,0:T(8,128)(2,1)} %maximum_bitcast_fusion.1), calls=%async_computation.8 | async-start | bytes 1638400 | tf_op jit(solution)/shard_map/all_to_all | solution.py:1138
  323.4 13.5 %all-to-all-done.5 = bf16[16,8,3200]{2,1,0:T(8,128)(2,1)S(1)} async-done(((bf16[16,8,3200]{2,1,0:T(8,128)(2,1)}), bf16[16,8,3200]{2,1,0:T(8,128)(2,1)S(1)}, u32[]{:S(2)}, u32[]{:S(2)}) %all-to-all-start.5) | async-done | bytes 819232 | tf_op jit(solution)/shard_map/all_to_all | solution.py:1138
  340.2 3.5 all-to-all-start.6
  344.4 7.7 %all-to-all-done.6.grads = bf16[16,3,16,128]{3,2,1,0:T(8,128)(2,1)S(1)} async-done(((bf16[16,3,16,128]{3,2,1,0:T(8,128)(2,1)}), bf16[16,3,16,128]{3,2,1,0:T(8,128)(2,1)S(1)}, u32[]{:S(2)}, u32[]{:S(2)}) %all-to-all-start.6) | async-done | bytes 196640 | tf_op jit(solution)/shard_map/all_to_all | solution.py:1238
  352.7 4.3 %shard_map.316 = (f32[6,128,128]{2,1,0:T(8,128)}, f32[6,128,128]{2,1,0:T(8,128)}, bf16[16,3,16,128]{3,2,1,0:T(8,128)(2,1)}) custom-call(bf16[16,3,16,128]{3,2,1,0:T(8,128)(2,1)} %copy-done.12, f32[6,128,128]{2,1,0:T(8,128)} %bitcast.109, f32[6,128,128]{2,1,0:T(8,128)} %bitcast.110, f32[6,128,128]{2,1,0:T(8,128)} %bitcast.111, f32[6,128,128]{2,1,0:T(8,128)} %bitcast.112), custom_call_target="tpu_custom_call" | custom-call | bytes 2359296 | tf_op jit(solution)/shard_map/pallas_call | solution.py:984
  357.1 3.5 all-to-all-start.7
  361.9 7.0 %all-to-all-done.7.moved = bf16[16,3,16,128]{3,2,1,0:T(8,128)(2,1)S(1)} async-done(((bf16[16,3,16,128]{3,2,1,0:T(8,128)(2,1)}), bf16[16,3,16,128]{3,2,1,0:T(8,128)(2,1)S(1)}, u32[]{:S(2)}, u32[]{:S(2)}) %all-to-all-start.7) | async-done | bytes 196640 | tf_op jit(solution)/shard_map/all_to_all | solution.py:1240
  (169 shorter events, 64.2 us)
Async XLA Ops:
  7.2 108.7 %all-gather.2.cloned.1.call-start = ((), (), s32[]{:S(2)}) async-start(), calls=%async_computation.11 | async-start | bytes 16908288 | tf_op jit(solution)/shard_map/all_gather | solution.py:1066
  11.4 14.2 %collective-permute-start.4 = (bf16[8,2048]{1,0:T(8,128)(2,1)S(1)}, bf16[8,2048]{1,0:T(8,128)(2,1)S(1)}, u32[]{:S(2)}, u32[]{:S(2)}) collective-permute-start(bf16[8,2048]{1,0:T(8,128)(2,1)S(1)} %pad_maximum_fusion.2), channel_id=1, source_target_pairs={{0,96},{32,0},{64,32},{96,64},{1,97},{33,1},{65,33},{97,65},{2,98}... | collective-permute-start | bytes 98312 | tf_op jit(solution)/shard_map/ppermute | solution.py:1030
  14.3 11.3 %collective-permute-start.5 = (bf16[8,2048]{1,0:T(8,128)(2,1)S(1)}, bf16[8,2048]{1,0:T(8,128)(2,1)S(1)}, u32[]{:S(2)}, u32[]{:S(2)}) collective-permute-start(bf16[8,2048]{1,0:T(8,128)(2,1)S(1)} %pad_maximum_fusion.2), channel_id=1, source_target_pairs={{0,64},{32,96},{64,0},{96,32},{1,65},{33,97},{65,1},{97,33},{2,66}... | collective-permute-start | bytes 98312 | tf_op jit(solution)/shard_map/ppermute | solution.py:1030
  15.1 10.5 %collective-permute-start.6 = (bf16[8,2048]{1,0:T(8,128)(2,1)S(1)}, bf16[8,2048]{1,0:T(8,128)(2,1)S(1)}, u32[]{:S(2)}, u32[]{:S(2)}) collective-permute-start(bf16[8,2048]{1,0:T(8,128)(2,1)S(1)} %pad_maximum_fusion.2), channel_id=1, source_target_pairs={{0,32},{32,64},{64,96},{96,0},{1,33},{33,65},{65,97},{97,1},{2,34}... | collective-permute-start | bytes 98312 | tf_op jit(solution)/shard_map/ppermute | solution.py:1030
  17.6 20.1 %all-to-all-start = ((bf16[16,8,2176]{2,1,0:T(8,128)(2,1)}), bf16[16,8,2176]{2,1,0:T(8,128)(2,1)S(1)}, u32[]{:S(2)}, u32[]{:S(2)}) async-start(bf16[16,8,2176]{2,1,0:T(8,128)(2,1)} %broadcast_in_dim.41), calls=%async_computation | async-start | bytes 1114112 | tf_op jit(solution)/shard_map/all_to_all | solution.py:1083
  37.6 25.2 %collective-permute-start = (bf16[128,2176]{1,0:T(8,128)(2,1)S(1)}, bf16[128,2176]{1,0:T(8,128)(2,1)S(1)}, u32[]{:S(2)}, u32[]{:S(2)}) collective-permute-start(bf16[128,2176]{1,0:T(8,128)(2,1)S(1)} %bitcast.102), channel_id=1, source_target_pairs={{0,96},{32,0},{64,32},{96,64},{1,97},{33,1},{65,33},{97,65},{2,98}... | collective-permute-start | bytes 1671176 | tf_op jit(solution)/shard_map/ppermute | solution.py:1030
  41.6 37.2 %all-to-all-start.1 = ((bf16[16,4,8,2048]{3,2,1,0:T(8,128)(2,1)}), bf16[16,4,8,2048]{3,2,1,0:T(8,128)(2,1)S(1)}, u32[]{:S(2)}, u32[]{:S(2)}) async-start(bf16[16,4,8,2048]{3,2,1,0:T(8,128)(2,1)} %broadcast_in_dim.42), calls=%async_computation.1 | async-start | bytes 4194304 | tf_op jit(solution)/shard_map/all_to_all | solution.py:1083
  45.3 154.5 %reduce-scatter.4.cloned.1.call-start = ((), (), s32[]{:S(2)}) async-start(), calls=%async_computation.12 | async-start | bytes 2621440 | tf_op jit(solution)/shard_map/reduce_scatter | solution.py:1134
  45.4 20.4 %collective-permute-start.1 = (bf16[128,2176]{1,0:T(8,128)(2,1)S(1)}, bf16[128,2176]{1,0:T(8,128)(2,1)S(1)}, u32[]{:S(2)}, u32[]{:S(2)}) collective-permute-start(bf16[128,2176]{1,0:T(8,128)(2,1)S(1)} %bitcast.103), channel_id=1, source_target_pairs={{0,64},{32,96},{64,0},{96,32},{1,65},{33,97},{65,1},{97,33},{2,66}... | collective-permute-start | bytes 1671176 | tf_op jit(solution)/shard_map/ppermute | solution.py:1030
  47.0 29.9 %collective-permute-start.2 = (bf16[128,2176]{1,0:T(8,128)(2,1)S(1)}, bf16[128,2176]{1,0:T(8,128)(2,1)S(1)}, u32[]{:S(2)}, u32[]{:S(2)}) collective-permute-start(bf16[128,2176]{1,0:T(8,128)(2,1)S(1)} %bitcast.104), channel_id=1, source_target_pairs={{0,32},{32,64},{64,96},{96,0},{1,33},{33,65},{65,97},{97,1},{2,34}... | collective-permute-start | bytes 1671176 | tf_op jit(solution)/shard_map/ppermute | solution.py:1030
  78.8 6.6 %collective-permute-start.3 = (bf16[512,2176]{1,0:T(8,128)(2,1)}, bf16[512,2176]{1,0:T(8,128)(2,1)}, u32[]{:S(2)}, u32[]{:S(2)}) collective-permute-start(bf16[512,2176]{1,0:T(8,128)(2,1)} %bitcast.7.own_qk), channel_id=1, source_target_pairs={{0,16},{16,0},{1,17},{17,1},{2,18},{18,2},{3,19},{19,3},{4,20},{20... | collective-permute-start | bytes 6684680 | tf_op jit(solution)/shard_map/ppermute | solution.py:1025
  81.8 5.7 %collective-permute-start.7 = (bf16[512,2048]{1,0:T(8,128)(2,1)S(1)}, bf16[512,2048]{1,0:T(8,128)(2,1)}, u32[]{:S(2)}, u32[]{:S(2)}) collective-permute-start(bf16[512,2048]{1,0:T(8,128)(2,1)S(1)} %bitcast.96), channel_id=1, source_target_pairs={{0,16},{16,0},{1,17},{17,1},{2,18},{18,2},{3,19},{19,3},{4,20},{20... | collective-permute-start | bytes 6291464 | tf_op jit(solution)/shard_map/ppermute | solution.py:1025
  141.7 7.2 %collective-permute-start.9 = (bf16[16,32,2048]{2,1,0:T(8,128)(2,1)}, bf16[16,32,2048]{2,1,0:T(8,128)(2,1)S(1)}, u32[]{:S(2)}, u32[]{:S(2)}) collective-permute-start(bf16[16,32,2048]{2,1,0:T(8,128)(2,1)} %get-tuple-element.78), channel_id=1, source_target_pairs={{0,16},{16,0},{1,17},{17,1},{2,18},{18,2},{3,19},{19,3},{4,20},{20... | collective-permute-start | bytes 6291464 | tf_op jit(solution)/shard_map/ppermute | solution.py:1025
  158.8 40.0 %all-to-all-start.2 = ((bf16[16,32,2048]{2,1,0:T(8,128)(2,1)}), bf16[16,32,2048]{2,1,0:T(8,128)(2,1)S(1)}, u32[]{:S(2)}, u32[]{:S(2)}) async-start(bf16[16,32,2048]{2,1,0:T(8,128)(2,1)} %get-tuple-element.79._), calls=%async_computation.2 | async-start | bytes 4194304 | tf_op jit(solution)/shard_map/all_to_all | solution.py:1144
  165.9 116.6 %reduce-scatter.6.cloned.1.call-start = ((), (), s32[]{:S(2)}) async-start(), calls=%async_computation.13 | async-start | bytes 3932160 | tf_op jit(solution)/shard_map/reduce_scatter | solution.py:1134
  194.2 17.6 %collective-permute-start.10 = (bf16[512,2048]{1,0:T(8,128)(2,1)}, bf16[512,2048]{1,0:T(8,128)(2,1)}, u32[]{:S(2)}, u32[]{:S(2)}) collective-permute-start(bf16[512,2048]{1,0:T(8,128)(2,1)} %get-tuple-element.87), channel_id=1, source_target_pairs={{0,16},{16,0},{1,17},{17,1},{2,18},{18,2},{3,19},{19,3},{4,20},{20... | collective-permute-start | bytes 6291464 | tf_op jit(solution)/shard_map/ppermute | solution.py:1025
  194.2 17.6 %collective-permute-start.11 = (bf16[16,32,2048]{2,1,0:T(8,128)(2,1)}, bf16[16,32,2048]{2,1,0:T(8,128)(2,1)}, u32[]{:S(2)}, u32[]{:S(2)}) collective-permute-start(bf16[16,32,2048]{2,1,0:T(8,128)(2,1)} %get-tuple-element.88), channel_id=1, source_target_pairs={{0,16},{16,0},{1,17},{17,1},{2,18},{18,2},{3,19},{19,3},{4,20},{20... | collective-permute-start | bytes 6291464 | tf_op jit(solution)/shard_map/ppermute | solution.py:1025
  225.5 37.7 %all-to-all-start.4 = ((bf16[16,32,2048]{2,1,0:T(8,128)(2,1)}), bf16[16,32,2048]{2,1,0:T(8,128)(2,1)S(1)}, u32[]{:S(2)}, u32[]{:S(2)}) async-start(bf16[16,32,2048]{2,1,0:T(8,128)(2,1)} %get-tuple-element.92._), calls=%async_computation.6 | async-start | bytes 4194304 | tf_op jit(solution)/shard_map/all_to_all | solution.py:1144
  229.2 83.3 %reduce-scatter.8.cloned.1.call-start = ((), (), s32[]{:S(2)}) async-start(), calls=%async_computation.14 | async-start | bytes 3932160 | tf_op jit(solution)/shard_map/reduce_scatter | solution.py:1134
  247.0 17.3 %collective-permute-start.13 = (bf16[512,1024]{1,0:T(8,128)(2,1)}, bf16[512,1024]{1,0:T(8,128)(2,1)S(1)}, u32[]{:S(2)}, u32[]{:S(2)}) collective-permute-start(bf16[512,1024]{1,0:T(8,128)(2,1)} %get-tuple-element.99), channel_id=1, source_target_pairs={{0,16},{16,0},{1,17},{17,1},{2,18},{18,2},{3,19},{19,3},{4,20},{20... | collective-permute-start | bytes 3145736 | tf_op jit(solution)/shard_map/ppermute | solution.py:1025
  247.2 17.1 %collective-permute-start.14 = (bf16[512,1024]{1,0:T(8,128)(2,1)}, bf16[512,1024]{1,0:T(8,128)(2,1)}, u32[]{:S(2)}, u32[]{:S(2)}) collective-permute-start(bf16[512,1024]{1,0:T(8,128)(2,1)} %get-tuple-element.100), channel_id=1, source_target_pairs={{0,16},{16,0},{1,17},{17,1},{2,18},{18,2},{3,19},{19,3},{4,20},{20... | collective-permute-start | bytes 3145736 | tf_op jit(solution)/shard_map/ppermute | solution.py:1025
  247.6 16.7 %collective-permute-start.15 = (bf16[512,1024]{1,0:T(8,128)(2,1)}, bf16[512,1024]{1,0:T(8,128)(2,1)}, u32[]{:S(2)}, u32[]{:S(2)}) collective-permute-start(bf16[512,1024]{1,0:T(8,128)(2,1)} %get-tuple-element.101), channel_id=1, source_target_pairs={{0,16},{16,0},{1,17},{17,1},{2,18},{18,2},{3,19},{19,3},{4,20},{20... | collective-permute-start | bytes 3145736 | tf_op jit(solution)/shard_map/ppermute | solution.py:1025
  273.5 7.6 %collective-permute-start.17 = (f32[128,128]{1,0:T(8,128)S(1)}, f32[128,128]{1,0:T(8,128)S(1)}, u32[]{:S(2)}, u32[]{:S(2)}) collective-permute-start(f32[128,128]{1,0:T(8,128)S(1)} %get-tuple-element.127), channel_id=1, source_target_pairs={{0,96},{32,0},{64,32},{96,64},{1,97},{33,1},{65,33},{97,65},{2,98}... | collective-permute-start | bytes 196616 | tf_op jit(solution)/shard_map/ppermute | solution.py:1030
  273.9 8.5 %collective-permute-start.18 = (f32[128,128]{1,0:T(8,128)S(1)}, f32[128,128]{1,0:T(8,128)S(1)}, u32[]{:S(2)}, u32[]{:S(2)}) collective-permute-start(f32[128,128]{1,0:T(8,128)S(1)} %get-tuple-element.126), channel_id=1, source_target_pairs={{0,64},{32,96},{64,0},{96,32},{1,65},{33,97},{65,1},{97,33},{2,66}... | collective-permute-start | bytes 196616 | tf_op jit(solution)/shard_map/ppermute | solution.py:1030
  275.8 6.6 %collective-permute-start.19 = (f32[128,128]{1,0:T(8,128)S(1)}, f32[128,128]{1,0:T(8,128)S(1)}, u32[]{:S(2)}, u32[]{:S(2)}) collective-permute-start(f32[128,128]{1,0:T(8,128)S(1)} %get-tuple-element.125), channel_id=1, source_target_pairs={{0,32},{32,64},{64,96},{96,0},{1,33},{33,65},{65,97},{97,1},{2,34}... | collective-permute-start | bytes 196616 | tf_op jit(solution)/shard_map/ppermute | solution.py:1030
  277.5 44.4 %collective-permute-start.22 = (bf16[8,4096]{1,0:T(8,128)(2,1)S(1)}, bf16[8,4096]{1,0:T(8,128)(2,1)S(1)}, u32[]{:S(2)}, u32[]{:S(2)}) collective-permute-start(bf16[8,4096]{1,0:T(8,128)(2,1)S(1)} %get-tuple-element.124), channel_id=1, source_target_pairs={{0,96},{32,0},{64,32},{96,64},{1,97},{33,1},{65,33},{97,65},{2,98}... | collective-permute-start | bytes 196616 | tf_op jit(solution)/shard_map/ppermute | solution.py:1030
  280.2 41.6 %collective-permute-start.21 = (bf16[8,4096]{1,0:T(8,128)(2,1)S(1)}, bf16[8,4096]{1,0:T(8,128)(2,1)S(1)}, u32[]{:S(2)}, u32[]{:S(2)}) collective-permute-start(bf16[8,4096]{1,0:T(8,128)(2,1)S(1)} %get-tuple-element.123), channel_id=1, source_target_pairs={{0,64},{32,96},{64,0},{96,32},{1,65},{33,97},{65,1},{97,33},{2,66}... | collective-permute-start | bytes 196616 | tf_op jit(solution)/shard_map/ppermute | solution.py:1030
  281.1 40.8 %collective-permute-start.20 = (bf16[8,4096]{1,0:T(8,128)(2,1)S(1)}, bf16[8,4096]{1,0:T(8,128)(2,1)S(1)}, u32[]{:S(2)}, u32[]{:S(2)}) collective-permute-start(bf16[8,4096]{1,0:T(8,128)(2,1)S(1)} %get-tuple-element.122), channel_id=1, source_target_pairs={{0,32},{32,64},{64,96},{96,0},{1,33},{33,65},{65,97},{97,1},{2,34}... | collective-permute-start | bytes 196616 | tf_op jit(solution)/shard_map/ppermute | solution.py:1030
  284.8 29.8 %all-to-all-start.3 = ((bf16[16,8,5120]{2,1,0:T(8,128)(2,1)}), bf16[16,8,5120]{2,1,0:T(8,128)(2,1)S(1)}, u32[]{:S(2)}, u32[]{:S(2)}) async-start(bf16[16,8,5120]{2,1,0:T(8,128)(2,1)} %maximum_bitcast_fusion), calls=%async_computation.5 | async-start | bytes 2621440 | tf_op jit(solution)/shard_map/all_to_all | solution.py:1138
  314.6 22.3 %all-to-all-start.5 = ((bf16[16,8,3200]{2,1,0:T(8,128)(2,1)}), bf16[16,8,3200]{2,1,0:T(8,128)(2,1)S(1)}, u32[]{:S(2)}, u32[]{:S(2)}) async-start(bf16[16,8,3200]{2,1,0:T(8,128)(2,1)} %maximum_bitcast_fusion.1), calls=%async_computation.8 | async-start | bytes 1638400 | tf_op jit(solution)/shard_map/all_to_all | solution.py:1138
  340.2 11.8 %all-to-all-start.6 = ((bf16[16,3,16,128]{3,2,1,0:T(8,128)(2,1)}), bf16[16,3,16,128]{3,2,1,0:T(8,128)(2,1)S(1)}, u32[]{:S(2)}, u32[]{:S(2)}) async-start(bf16[16,3,16,128]{3,2,1,0:T(8,128)(2,1)} %get-tuple-element.108), calls=%async_computation.9 | async-start | bytes 393216 | tf_op jit(solution)/shard_map/all_to_all | solution.py:1238
  357.1 11.8 %all-to-all-start.7 = ((bf16[16,3,16,128]{3,2,1,0:T(8,128)(2,1)}), bf16[16,3,16,128]{3,2,1,0:T(8,128)(2,1)S(1)}, u32[]{:S(2)}, u32[]{:S(2)}) async-start(bf16[16,3,16,128]{3,2,1,0:T(8,128)(2,1)} %get-tuple-element.111), calls=%async_computation.10 | async-start | bytes 393216 | tf_op jit(solution)/shard_map/all_to_all | solution.py:1240
  (23 other events, 175.1 us)
Sparse Core Ops, SparseCore 0:
  11.7 100.5 all-gather.1
  158.9 29.5 reduce-scatter.3
  225.6 34.6 reduce-scatter.5
  272.5 39.8 reduce-scatter.7

commit v5 on v4

--- a/solution.py
+++ b/solution.py
@@ -15,6 +15,8 @@
 RATE_VECTOR = 0.3
 HIGHEST = lax.Precision.HIGHEST
 HEAD_AT = 24
+DOWN_FIRSTS = 3
+UP_FIRSTS = 2
 VMEM_BYTES = 56 * 1024 * 1024
 F32 = jnp.float32
 BF16 = jnp.bfloat16
@@ -94,6 +96,11 @@
     for block in range(turned.shape[0] // TILE):
         at = pl.multiple_of((2 * block + parity) * TILE, TILE)
         turned[block * TILE : (block + 1) * TILE, :] = jnp.transpose(left[:, pl.ds(at, TILE)])
+
+
+def turn_all(left, turned):
+    for at in range(0, turned.shape[0], TILE):
+        turned[at : at + TILE, :] = jnp.transpose(left[:, at : at + TILE])
 
 
 def by_owner(values, plane):
@@ -230,7 +237,7 @@
 
 
 def attend_back_body(
-    core, queries, keys, values, mixed, grads, weights, normed, _, out, sent_q, sent_k, sent_v, turned
+    core, queries, keys, values, mixed, grads, weights, normed, _, __, out, sent_q, sent_k, sent_v, turned
 ):
     @pl.when(pl.program_id(0) == 0)
     def _():
@@ -354,8 +361,6 @@
     scales,
     vectors,
     scaled,
-    _,
-    __,
     grad_branch,
     grad_mixed,
     sums,
@@ -434,35 +439,35 @@
     )(core, grad_attended, branch, *weights[2:], mixed, scales, vectors, scaled, *wait)
 
 
-def send_part(values, step, first, second):
-    @pl.when(step < 2)
+def send_part(values, step, firsts, first, second):
+    @pl.when(step < firsts)
     def _():
         first[...] = values.astype(BF16)
 
-    @pl.when(step >= 2)
+    @pl.when(step >= firsts)
     def _():
         second[...] = by_owner(values, second.shape[0]).astype(BF16)
 
 
-def part_specs(half, plane, start):
+def part_specs(half, plane, start, firsts):
     return [
-        pl.BlockSpec((half, 1024), lambda at, *_: (0, jnp.clip(at - start, 0, 1))),
+        pl.BlockSpec((half, 1024), lambda at, *_: (0, jnp.clip(at - start, 0, firsts - 1))),
         pl.BlockSpec(
-            (plane, half // plane, 1024), lambda at, *_: (0, 0, jnp.clip(at - start - 2, 0, 1))
+            (plane, half // plane, 1024),
+            lambda at, *_: (0, 0, jnp.clip(at - start - firsts, 0, 3 - firsts)),
         ),
     ]
 
 
-def part_shapes(half, plane):
+def part_shapes(half, plane, firsts):
     return [
-        jax.ShapeDtypeStruct((half, 2048), BF16),
-        jax.ShapeDtypeStruct((plane, half // plane, 2048), BF16),
+        jax.ShapeDtypeStruct((half, firsts * 1024), BF16),
+        jax.ShapeDtypeStruct((plane, half // plane, (4 - firsts) * 1024), BF16),
     ]
 
 
 def forward_ffn_body(
     steps,
-    core,
     normed,
     attended,
     vectors,
@@ -487,7 +492,7 @@
 
     @pl.when(at == 0)
     def _():
-        turn_rows(upstream, turned, 1 - core[0])
+        turn_all(upstream, turned)
         sums[...] = jnp.zeros_like(sums)
 
     @pl.when(at < steps)
@@ -523,14 +528,14 @@
         low = ((value - mean) * spread * rows_of[1:2, :] + rows_of[2:3, :]).astype(BF16)
         top[...] = low
         total[...] += dot_nt(low, down[...])
-        send_part(dot_nn(turned[...], low), at - steps, sent_first, sent_second)
+        send_part(dot_nn(turned[...], low), at - steps, DOWN_FIRSTS, sent_first, sent_second)
 
     @pl.when(at == 2 * steps - 1)
     def _():
         output[...] = total[...].astype(BF16)
 
 
-def forward_ffn(core, plane, normed, attended, vectors, wide_rows, both, upstream):
+def forward_ffn(plane, normed, attended, vectors, wide_rows, both, upstream):
     rows, width = attended.shape
     hidden = both.shape[1] // 2
     block = 1024
@@ -555,7 +560,7 @@
             pl.BlockSpec((rows, block), early),
             pl.BlockSpec((rows, block), early),
             whole((rows, 2 * TILE)),
-            *part_specs(width // 2, plane, steps),
+            *part_specs(width, plane, steps, DOWN_FIRSTS),
         ],
         [
             jax.ShapeDtypeStruct((rows, width), BF16),
@@ -563,18 +568,17 @@
             jax.ShapeDtypeStruct((rows, hidden), BF16),
             jax.ShapeDtypeStruct((rows, hidden), BF16),
             jax.ShapeDtypeStruct((rows, 2 * TILE), F32),
-            *part_shapes(width // 2, plane),
+            *part_shapes(width, plane, DOWN_FIRSTS),
         ],
         scratch=[
             pltpu.VMEM((steps, rows, block), F32),
             pltpu.VMEM((rows, width), F32),
             pltpu.VMEM((rows, TILE), F32),
-            pltpu.VMEM((width // 2, rows), BF16),
-        ],
-        flops=5 * rows * width * hidden,
+            pltpu.VMEM((width, rows), BF16),
+        ],
+        flops=6 * rows * width * hidden,
         bytes_accessed=4 * width * hidden + 6 * rows * hidden,
-        scalars=1,
-    )(core, normed, attended, vectors, wide_rows, both, both, upstream)
+    )(normed, attended, vectors, wide_rows, both, both, upstream)
 
 
 def backward_ffn_body(
@@ -646,7 +650,7 @@
         grad_hidden[...] = low
         wide_sums[at - steps, 2:3, :] = jnp.sum(low.astype(F32), axis=0, keepdims=True)
         total[...] += dot_nt(low, up[...])
-        send_part(dot_nn(turned[...], low), at - steps, sent_first, sent_second)
+        send_part(dot_nn(turned[...], low), at - steps, UP_FIRSTS, sent_first, sent_second)
 
     @pl.when(at == 2 * steps - 1)
     def _():
@@ -691,14 +695,14 @@
             pl.BlockSpec((rows, block), late),
             whole((steps, 8, block)),
             whole((8, width)),
-            *part_specs(width // 2, plane, steps),
+            *part_specs(width // 2, plane, steps, UP_FIRSTS),
         ],
         [
             jax.ShapeDtypeStruct((rows, width), F32),
             jax.ShapeDtypeStruct((rows, hidden), BF16),
             jax.ShapeDtypeStruct((steps, 8, block), F32),
             jax.ShapeDtypeStruct((8, width), F32),
-            *part_shapes(width // 2, plane),
+            *part_shapes(width // 2, plane, UP_FIRSTS),
         ],
         scratch=[
             pltpu.VMEM((steps, rows, block), F32),
@@ -850,10 +854,10 @@
     block = 1024
     add_first, add_second = add
     plane, owned = add_second.shape[:2]
-    firsts = 2
+    firsts = UP_FIRSTS
     seconds = add_second.shape[2] // block
     right_spec = pl.BlockSpec((rows, block), lambda at, *_: (0, at))
-    add_spec = pl.BlockSpec((half, block), lambda at, *_: (0, jnp.clip(at, 0, 1)))
+    add_spec = pl.BlockSpec((half, block), lambda at, *_: (0, jnp.clip(at, 0, firsts - 1)))
     second_spec = pl.BlockSpec(
         (plane, owned, block), lambda at, *_: (0, 0, jnp.clip(at - firsts, 0, seconds - 1))
     )
@@ -887,7 +891,7 @@
 
 
 def outer_stack_body(core, left, right, *refs):
-    adds, (out, turned) = refs[:3], refs[-2:]
+    adds, (first, last, turned) = refs[:3], refs[-3:]
     at = pl.program_id(0)
 
     @pl.when(at == 0)
@@ -899,6 +903,7 @@
 
         @pl.when(at == which)
         def _(add=add):
+            out = first if which < 2 else last
             out[...] = (value + add[...].astype(F32)).astype(BF16)
 
 
@@ -914,8 +919,14 @@
             *[whole((half, width)) for _ in adds],
             *after(*wait),
         ],
-        pl.BlockSpec((half, width), lambda at, *_: (0, at)),
-        jax.ShapeDtypeStruct((half, count * width), BF16),
+        [
+            pl.BlockSpec((half, width), lambda at, *_: (0, jnp.minimum(at, count - 2))),
+            whole((half, width)),
+        ],
+        [
+            jax.ShapeDtypeStruct((half, (count - 1) * width), BF16),
+            jax.ShapeDtypeStruct((half, width), BF16),
+        ],
         scratch=[pltpu.VMEM((half, rows), BF16)],
         flops=2 * rows * half * width * count,
         bytes_accessed=6 * half * width * count,
@@ -923,16 +934,17 @@
     )(core, left, rights, *adds, *wait)
 
 
-def to_slots_body(perm, early, late, rest, *refs):
+def to_slots_body(perm, early, late, last, rest, *refs):
     grad_qkv, grad_out, grad_up, grad_down, slots, tiles = refs
     width = grad_out.shape[1]
     half = 2 * width
     grad_out[...] = early[:, half : half + width]
-    grad_qkv[...] = late[:, : 3 * width]
-    grad_down[:, :half] = early[:, half + width :]
-    grad_down[:, half:] = rest[:, :half]
+    grad_qkv[:, :half] = late[...]
+    grad_qkv[:, half:] = last[:, :width]
+    grad_down[:, : DOWN_FIRSTS * width] = early[:, half + width :]
+    grad_down[:, DOWN_FIRSTS * width :] = rest[:, :width]
     grad_up[:, :half] = early[:, :half]
-    grad_up[:, half:] = rest[:, half : 2 * half]
+    grad_up[:, half:] = rest[:, width : width + half]
     column = 0
     for result in (grad_qkv, grad_out, grad_up, grad_down):
         for at in range(0, result.shape[1], TILE):
@@ -944,8 +956,8 @@
         slots[slot // pairs, slot % pairs] = jnp.concatenate(pair, axis=0).astype(BF16)
 
 
-def to_slots(perm, early, late, rest, plane, widths):
-    arrays = [early, late, rest]
+def to_slots(perm, early, late, last, rest, plane, widths):
+    arrays = [early, late, last, rest]
     pairs = perm.shape[0] // (2 * plane)
     shapes = [jax.ShapeDtypeStruct((8, columns), F32) for columns in widths]
     shapes.append(jax.ShapeDtypeStruct((plane, pairs, 16, TILE), BF16))
@@ -1023,6 +1035,10 @@
 
 def swap_cores(values):
     return lax.ppermute(values, "core", [(0, 1), (1, 0)])
+
+
+def take_core(values, core):
+    return lax.dynamic_slice_in_dim(values, core, 1, 1, allow_negative_indices=False)[:, 0]
 
 
 def turn_chips(values, step):
@@ -1126,8 +1142,8 @@
     normed, projected = project(core_arg, tokens, vector_rows, weights)
     mixed, scaled, attention = attend(lengths, head_scale, projected)
     branch, attended, normed_mid = branch_out(core_arg, scaled, weights, tokens, vector_rows)
-    output, normed_top, kept, slope, stats, *sent_down = forward_ffn(
-        core_arg, plane, normed_mid, attended, vector_rows, wide_rows, both, upstream
+    output, normed_top, kept, slope, stats, down_first, down_second = forward_ffn(
+        plane, normed_mid, attended, vector_rows, wide_rows, both, upstream
     )
 
     def over_x(part):
@@ -1144,11 +1160,8 @@
         total = lax.all_to_all(part, "fsdp", split_axis=0, concat_axis=0, tiled=True)
         return sum_parts(total)
 
-    down_first, down_second = outer(
-        core_arg, upstream, normed_top, [swap_cores(part) for part in sent_down]
-    )
+    down_chips = lax.psum_scatter(down_first, ("x", "core"), scatter_dimension=0, tiled=True)
     down_rest = plane_first(down_second)
-    down_chips = over_x(down_first)
     grad_attended, grad_hidden, wide_sums, mid_sums, *sent_up = backward_ffn(
         core_arg,
         plane,
@@ -1172,15 +1185,13 @@
         scales,
         vector_rows,
         scaled,
-        down_rest,
-        down_chips,
     )
     up_first, up_second = outer(
         core_arg,
         normed_mid,
         grad_hidden,
         [swap_cores(part) for part in sent_up],
-        wait=(grad_branch,),
+        wait=(grad_branch, down_rest),
         more=(out_stays, swap_cores(out_sent)),
     )
     up_rest = plane_first(up_second)
@@ -1192,7 +1203,7 @@
         grad_mixed,
         attention,
         normed,
-        (up_second,),
+        (up_second, down_chips),
     )
     input_grad, turned = input_back(
         core_arg,
@@ -1206,23 +1217,26 @@
     )
 
     turned = turned.reshape(chips, 2, TILE, TILE)
-    kept_sums = lax.dynamic_slice_in_dim(turned, core, 1, 1, allow_negative_indices=False)[:, 0]
-    sent_sums = lax.dynamic_slice_in_dim(
-        turned, 1 - core, 1, 1, allow_negative_indices=False
-    )[:, 0]
-    half_sums = kept_sums + swap_cores(sent_sums)
-    attn_first = outer_stack(
+    half_sums = take_core(turned, core) + swap_cores(take_core(turned, 1 - core))
+    query_key, value_last = outer_stack(
         core_arg, normed, grads, [swap_cores(part) for part in sent_attn], half_sums, up_rest
     )
-    half_sums, _ = lax.optimization_barrier((half_sums, attn_first))
+
+    early_parts = over_plane(jnp.concatenate([up_chips, down_chips], axis=1))
+    half_sums, down_rest, up_rest, early_parts = lax.optimization_barrier(
+        (half_sums, down_rest, up_rest, early_parts)
+    )
     small = jnp.sum(in_order(across_chips(half_sums)), axis=0)
-
-    early_parts = over_plane(jnp.concatenate([up_chips, down_chips], axis=1))
-    rest = jnp.concatenate([down_rest, up_rest], axis=1)
-    rest = across_chips(rest.astype(BF16).reshape(chips, shard, -1))
+    down_rest = down_rest.reshape(chips, 2, shard, -1)
+    down_rest = take_core(down_rest, core) + swap_cores(
+        take_core(down_rest, 1 - core).astype(BF16)
+    ).astype(F32)
+    rest = jnp.concatenate([down_rest, up_rest.reshape(chips, shard, -1)], axis=2)
+    rest = across_chips(rest.astype(BF16))
     rest = sum(part.astype(F32) for part in rest)
-    late_parts = over_plane(jnp.concatenate([over_x(attn_first), small.astype(BF16)], axis=1))
-    small = late_parts[:, 3 * width :]
+    late_parts = over_plane(over_x(query_key))
+    last_parts = over_plane(jnp.concatenate([over_x(value_last), small.astype(BF16)], axis=1))
+    small = last_parts[:, width:]
     vector_grads = small.T[: vectors.shape[0]]
     head_total = small[0, HEAD_AT : HEAD_AT + heads]
 
@@ -1231,6 +1245,7 @@
         owner_perm,
         early_parts,
         late_parts,
+        last_parts,
         rest,
         plane,
         [item.shape[1] for item in masters],

time: 385 us -> 381 us (0.990)
  Pallas kernels: 157 us -> 152 us
    all_to_all x2 -> x3, waiting for transfers between devices: 13.5 us -> 40.9 us  [over_plane(): lax.all_to_all(part.reshape(plane, shard, -1), 'fsdp', split_axis=0, conc...]
    reduce_scatter x3, waiting for transfers between devices: 20.5 us -> 0.04 us  [over_x(): return lax.psum_scatter(part, 'x', scatter_dimension=0, tiled=True)]
    ppermute x11 -> x10, waiting for transfers between devices: 10.9 us -> 1.69 us  [swap_cores(): return lax.ppermute(values, 'core', [(0, 1), (1, 0)])]
    pallas_call x2 -> x1, Pallas kernels: 18.2 us -> 9.79 us  [outer(): call(functools.partial(outer_body, firsts, len(more) > 0), (firsts + seco...]
    ppermute x12, waiting for transfers between devices: 29.8 us -> 36.9 us  [turn_chips(): lax.ppermute(values, 'x', [(at, (at + step) % count) for at in range(coun...]
    unnamed x60 -> x56, local copies, waits for them, and re-layouts: 8.07 us -> 5.09 us
    all_to_all x2 -> x3, starting transfers between devices: 14.4 us -> 13 us  [over_plane(): lax.all_to_all(part.reshape(plane, shard, -1), 'fsdp', split_axis=0, conc...]
  transfers between devices with their start and end apart: 35 -> 36, of which waited for: 13 -> 14; matrix products, arithmetic and copies ran while one was open for 7% -> 7% of each run, Pallas kernels for 27% -> 30%
where the time goes in v5:
time: 381 us; the launch traced here: 375 us
  Pallas kernels  152 us (40%)
  waiting for transfers between devices  108 us (28%)
  starting transfers between devices  64.5 us (17%)
  other arithmetic  18.9 us (5%)
  local copies, waits for them, and re-layouts  15.6 us (4%)
  between operations  15.3 us (4%)
    all_to_all x3, waiting for transfers between devices, over_plane(): lax.all_to_all(part.reshape(plane, shard, -1), 'fsdp', split_axis=0, conc...  40.9 us
    ppermute x12, waiting for transfers between devices, turn_chips(): lax.ppermute(values, 'x', [(at, (at + step) % count) for at in range(coun...  36.9 us
    pallas_call x1, Pallas kernels, forward_ffn(): call(functools.partial(forward_ffn_body, steps), (2 * steps,), [whole((ro...  28.9 us
    pallas_call x1, Pallas kernels, backward_ffn(): call(functools.partial(backward_ffn_body, steps), (2 * steps,), [whole((r...  28.3 us
    pallas_call x1, Pallas kernels, attend_back(): call(attend_back_body, (pairs,), [by_pair, pl.BlockSpec((rows, TILE), lam...  17.3 us
    ppermute x12, starting transfers between devices, turn_chips(): lax.ppermute(values, 'x', [(at, (at + step) % count) for at in range(coun...  14.9 us
    all_to_all x2, starting transfers between devices, plane_first(): lax.all_to_all(part, 'fsdp', split_axis=0, concat_axis=0, tiled=True)  14.3 us
    pallas_call x1, Pallas kernels, attend(): call(attend_body, (pairs,), [pl.BlockSpec((rows, TILE), lambda pair, *_:...  13.5 us
  transfers between devices with their start and end apart: 36, of which 14 were waited for; matrix products, arithmetic and copies ran while one was open for 7% of the time, Pallas kernels for 30%

profile of v5, /device:TPU:0, one launch (start us, length us, event | category | flops | bytes accessed | tf_op | source)
XLA Modules:
  0.0 375.1 jit_solution(8227182084615365042)
XLA Ops:
  11.4 2.8 collective-permute-start.4
  17.5 8.0 %all-to-all-start = ((bf16[16,8,2176]{2,1,0:T(8,128)(2,1)}), bf16[16,8,2176]{2,1,0:T(8,128)(2,1)S(1)}, u32[]{:S(2)}, u32[]{:S(2)}) async-start(bf16[16,8,2176]{2,1,0:T(8,128)(2,1)} %broadcast_in_dim.41), calls=%async_computation | async-start | bytes 1114112 | tf_op jit(solution)/shard_map/all_to_all | solution.py:1099
  25.7 11.9 %all-to-all-done = bf16[16,8,2176]{2,1,0:T(8,128)(2,1)S(1)} async-done(((bf16[16,8,2176]{2,1,0:T(8,128)(2,1)}), bf16[16,8,2176]{2,1,0:T(8,128)(2,1)S(1)}, u32[]{:S(2)}, u32[]{:S(2)}) %all-to-all-start) | async-done | bytes 557088 | tf_op jit(solution)/shard_map/all_to_all | solution.py:1099
  41.6 3.7 all-to-all-start.1
  46.9 15.3 %collective-permute-done = bf16[128,2176]{1,0:T(8,128)(2,1)S(1)} collective-permute-done((bf16[128,2176]{1,0:T(8,128)(2,1)S(1)}, bf16[128,2176]{1,0:T(8,128)(2,1)S(1)}, u32[]{:S(2)}, u32[]{:S(2)}) %collective-permute-start) | collective-permute-done | bytes 557088 | tf_op jit(solution)/shard_map/ppermute | solution.py:1046
  62.3 3.4 collective-permute-done.1
  65.8 11.0 %collective-permute-done.2 = bf16[128,2176]{1,0:T(8,128)(2,1)S(1)} collective-permute-done((bf16[128,2176]{1,0:T(8,128)(2,1)S(1)}, bf16[128,2176]{1,0:T(8,128)(2,1)S(1)}, u32[]{:S(2)}, u32[]{:S(2)}) %collective-permute-start.2) | collective-permute-done | bytes 557088 | tf_op jit(solution)/shard_map/ppermute | solution.py:1046
  87.5 8.6 %shard_map.304 = (bf16[512,1024]{1,0:T(8,128)(2,1)}, bf16[512,3072]{1,0:T(8,128)(2,1)}) custom-call(s32[1]{0:T(128)} %bitcast.core, bf16[512,1024]{1,0:T(8,128)(2,1)} %tokens.5, f32[24,1024]{1,0:T(8,128)} %copy-done.2, bf16[512,2176]{1,0:T(8,128)(2,1)} %bitcast.7.own_qk, bf16[512,2176]{1,0:T(8,128)(2,1)} %collective-permute-done.3.other_qk, ...), custom_call_target="tpu_custom_call" | custom-call | flops 3221225472 | bytes 6291456 | tf_op jit(solution)/shard_map/pallas_call | solution.py:148
  96.1 13.5 %shard_map.305 = (f32[512,1024]{1,0:T(8,128)}, bf16[512,1024]{1,0:T(8,128)(2,1)}, bf16[16,256,768]{2,1,0:T(8,128)(2,1)}) custom-call(s32[1]{0:T(128)S(6)} %copy.71.length, f32[16]{0:T(128)} %scales.1, bf16[512,3072]{1,0:T(8,128)(2,1)} %get-tuple-element.69.queries.keys.values, bf16[512,3072]{1,0:T(8,128)(2,1)} %get-tuple-element.69.queries.keys.values, ...), custom_call_target="tpu_custom_call" | custom-call | flops 1073741824 | bytes 10485760 | tf_op jit(solution)/shard_map/pallas_call | solution.py:215
  109.6 6.3 %shard_map.306 = (f32[512,1024]{1,0:T(8,128)}, f32[512,1024]{1,0:T(8,128)}, bf16[512,1024]{1,0:T(8,128)(2,1)}) custom-call(s32[1]{0:T(128)} %bitcast.core, bf16[512,1024]{1,0:T(8,128)(2,1)} %get-tuple-element.70.scaled, bf16[512,2048]{1,0:T(8,128)(2,1)} %bitcast.108, bf16[512,2048]{1,0:T(8,128)(2,1)} %collective-permute-done.7.other_vo.other, ...), custom_call_target="tpu_custom_call" | custom-call | flops 1073741824 | bytes 9437184 | tf_op jit(solution)/shard_map/pallas_call | solution.py:337
  115.9 28.9 %shard_map.307 = (bf16[512,1024]{1,0:T(8,128)(2,1)}, bf16[512,4096]{1,0:T(8,128)(2,1)}, bf16[512,4096]{1,0:T(8,128)(2,1)}, bf16[512,4096]{1,0:T(8,128)(2,1)}, f3...) custom-call(bf16[512,1024]{1,0:T(8,128)(2,1)} %get-tuple-element.71.normed.left, ...), custom_call_target="tpu_custom_call" | custom-call | flops 12884901888 | bytes 29360128 | tf_op jit(solution)/shard_map/pallas_call | solution.py:545
  144.9 7.1 %all-to-all-start.2 = ((bf16[16,64,1024]{2,1,0:T(8,128)(2,1)}), bf16[16,64,1024]{2,1,0:T(8,128)(2,1)S(1)}, u32[]{:S(2)}, u32[]{:S(2)}) async-start(bf16[16,64,1024]{2,1,0:T(8,128)(2,1)} %get-tuple-element.78._), calls=%async_computation.2 | async-start | bytes 4194304 | tf_op jit(solution)/shard_map/all_to_all | solution.py:1160
  152.2 28.3 %shard_map.308 = (f32[512,1024]{1,0:T(8,128)}, bf16[512,4096]{1,0:T(8,128)(2,1)}, f32[4,8,1024]{2,1,0:T(8,128)}, f32[8,1024]{1,0:T(8,128)}, bf16[512,2048]{1,0:T(8,128)(2,1)}, /*index=5*/bf16[16,32,2048]{2,1,0:T(8,128)(2,1)}) custom-call(s32[1]{0:T(128)} %bitcast.core, bf16[512,1024]{1,0:T(8,128)(2,1)} %broadcast_select_fusion.upstream, ...), custom_call_target="tpu_custom_call" | custom-call | flops 10737418240 | bytes 33554432 | tf_op jit(solution)/shard_map/pallas_call | solution.py:677
  181.8 11.3 %shard_map.309 = (bf16[512,1024]{1,0:T(8,128)(2,1)}, bf16[512,1024]{1,0:T(8,128)(2,1)}, f32[8,1024]{1,0:T(8,128)}, bf16[512,1024]{1,0:T(8,128)(2,1)}, f32[512,1024]{1,0:T(8,128)}) custom-call(s32[1]{0:T(128)} %bitcast.core, f32[512,1024]{1,0:T(8,128)} %get-tuple-element.79.grad_attended, f32[512,1024]{1,0:T(8,128)} %get-tuple-element.80.branch, ...), custom_call_target="tpu_custom_call" | custom-call | flops 2147483648 | bytes 10485760 | tf_op jit(solution)/shard_map/pallas_call | solution.py:409
  197.1 9.8 %shard_map.310 = (bf16[512,3072]{1,0:T(8,128)(2,1)}, bf16[16,32,2048]{2,1,0:T(8,128)(2,1)}) custom-call(s32[1]{0:T(128)} %bitcast.core, bf16[512,1024]{1,0:T(8,128)(2,1)} %get-tuple-element.71.normed.left, bf16[512,4096]{1,0:T(8,128)(2,1)} %get-tuple-element.84.right, bf16[512,2048]{1,0:T(8,128)(2,1)} %collective-permute-done.8.add_first, ...), custom_call_target="tpu_custom_call" | custom-call | flops 2147483648 | bytes 12582912 | tf_op jit(solution)/shard_map/pallas_call | solution.py:873
  206.9 7.2 %all-to-all-start.3 = ((bf16[16,32,2048]{2,1,0:T(8,128)(2,1)}), bf16[16,32,2048]{2,1,0:T(8,128)(2,1)S(1)}, u32[]{:S(2)}, u32[]{:S(2)}) async-start(bf16[16,32,2048]{2,1,0:T(8,128)(2,1)} %get-tuple-element.90._), calls=%async_computation.4 | async-start | bytes 4194304 | tf_op jit(solution)/shard_map/all_to_all | solution.py:1160
  214.6 17.3 %shard_map.311 = (bf16[3,512,1024]{2,1,0:T(8,128)(2,1)}, bf16[512,1024]{1,0:T(8,128)(2,1)}, bf16[512,1024]{1,0:T(8,128)(2,1)}, bf16[512,1024]{1,0:T(8,128)(2,1)}) custom-call(s32[1]{0:T(128)} %bitcast.core, bf16[512,3072]{1,0:T(8,128)(2,1)} %get-tuple-element.69.queries.keys.values, bf16[512,3072]{1,0:T(8,128)(2,1)} %get-tuple-element.69.queries.keys.values, ...), custom_call_target="tpu_custom_call" | custom-call | flops 2684354560 | bytes 12582912 | tf_op jit(solution)/shard_map/pallas_call | solution.py:292
  232.6 11.2 %shard_map.312 = (f32[512,1024]{1,0:T(8,128)}, f32[8,128,128]{2,1,0:T(8,128)}) custom-call(s32[1]{0:T(128)} %bitcast.core, bf16[3,512,1024]{2,1,0:T(8,128)(2,1)} %get-tuple-element.92.grads.right, bf16[512,2176]{1,0:T(8,128)(2,1)} %bitcast.7.own_qk, bf16[512,2176]{1,0:T(8,128)(2,1)} %collective-permute-done.3.other_qk, bf16[512,2048]{1,0:T(8,128)(2,1)} %bitcast.110, ...), custom_call_target="tpu_custom_call" | custom-call | flops 3221225472 | bytes 14680064 | tf_op jit(solution)/shard_map/pallas_call | solution.py:797
  250.8 7.4 %shard_map.313 = (bf16[512,2048]{1,0:T(8,128)(2,1)}, bf16[512,1024]{1,0:T(8,128)(2,1)}) custom-call(s32[1]{0:T(128)} %bitcast.core, bf16[512,1024]{1,0:T(8,128)(2,1)} %get-tuple-element.83.normed.left, bf16[3,512,1024]{2,1,0:T(8,128)(2,1)} %get-tuple-element.92.grads.right, bf16[512,1024]{1,0:T(8,128)(2,1)} %copy-done.7, ...), custom_call_target="tpu_custom_call" | custom-call | flops 1610612736 | bytes 9437184 | tf_op jit(solution)/shard_map/pallas_call | solution.py:913
  260.7 5.8 %all-to-all-start.4 = ((bf16[16,8,6144]{2,1,0:T(8,128)(2,1)}), bf16[16,8,6144]{2,1,0:T(8,128)(2,1)S(1)}, u32[]{:S(2)}, u32[]{:S(2)}) async-start(bf16[16,8,6144]{2,1,0:T(8,128)(2,1)} %maximum_bitcast_fusion), calls=%async_computation.6 | async-start | bytes 3145728 | tf_op jit(solution)/shard_map/all_to_all | solution.py:1154
  267.1 25.1 %all-to-all-done.4 = bf16[16,8,6144]{2,1,0:T(8,128)(2,1)S(1)} async-done(((bf16[16,8,6144]{2,1,0:T(8,128)(2,1)}), bf16[16,8,6144]{2,1,0:T(8,128)(2,1)S(1)}, u32[]{:S(2)}, u32[]{:S(2)}) %all-to-all-start.4) | async-done | bytes 1572896 | tf_op jit(solution)/shard_map/all_to_all | solution.py:1154
  296.0 3.7 collective-permute-done.15
  305.5 3.7 all-to-all-start.6
  310.1 2.6 collective-permute-start.20
  313.0 5.5 %all-to-all-done.6 = bf16[16,8,1152]{2,1,0:T(8,128)(2,1)S(1)} async-done(((bf16[16,8,1152]{2,1,0:T(8,128)(2,1)}), bf16[16,8,1152]{2,1,0:T(8,128)(2,1)S(1)}, u32[]{:S(2)}, u32[]{:S(2)}) %all-to-all-start.6) | async-done | bytes 294944 | tf_op jit(solution)/shard_map/all_to_all | solution.py:1154
  318.5 3.6 all-to-all-start.5
  322.8 10.3 %all-to-all-done.5 = bf16[16,8,2048]{2,1,0:T(8,128)(2,1)S(1)} async-done(((bf16[16,8,2048]{2,1,0:T(8,128)(2,1)}), bf16[16,8,2048]{2,1,0:T(8,128)(2,1)S(1)}, u32[]{:S(2)}, u32[]{:S(2)}) %all-to-all-start.5) | async-done | bytes 524320 | tf_op jit(solution)/shard_map/all_to_all | solution.py:1154
  336.4 3.5 all-to-all-start.7
  340.5 7.7 %all-to-all-done.7.grads = bf16[16,3,16,128]{3,2,1,0:T(8,128)(2,1)S(1)} async-done(((bf16[16,3,16,128]{3,2,1,0:T(8,128)(2,1)}), bf16[16,3,16,128]{3,2,1,0:T(8,128)(2,1)S(1)}, u32[]{:S(2)}, u32[]{:S(2)}) %all-to-all-start.7) | async-done | bytes 196640 | tf_op jit(solution)/shard_map/all_to_all | solution.py:1253
  348.9 4.3 %shard_map.315 = (f32[6,128,128]{2,1,0:T(8,128)}, f32[6,128,128]{2,1,0:T(8,128)}, bf16[16,3,16,128]{3,2,1,0:T(8,128)(2,1)}) custom-call(bf16[16,3,16,128]{3,2,1,0:T(8,128)(2,1)} %copy-done.10, f32[6,128,128]{2,1,0:T(8,128)} %bitcast.122, f32[6,128,128]{2,1,0:T(8,128)} %bitcast.123, f32[6,128,128]{2,1,0:T(8,128)} %bitcast.124, f32[6,128,128]{2,1,0:T(8,128)} %bitcast.125), custom_call_target="tpu_custom_call" | custom-call | bytes 2359296 | tf_op jit(solution)/shard_map/pallas_call | solution.py:996
  353.2 3.5 all-to-all-start.8
  358.0 7.0 %all-to-all-done.8.moved = bf16[16,3,16,128]{3,2,1,0:T(8,128)(2,1)S(1)} async-done(((bf16[16,3,16,128]{3,2,1,0:T(8,128)(2,1)}), bf16[16,3,16,128]{3,2,1,0:T(8,128)(2,1)S(1)}, u32[]{:S(2)}, u32[]{:S(2)}) %all-to-all-start.8) | async-done | bytes 196640 | tf_op jit(solution)/shard_map/all_to_all | solution.py:1255
  (169 shorter events, 60.2 us)
Async XLA Ops:
  7.2 108.7 %all-gather.2.cloned.1.call-start = ((), (), s32[]{:S(2)}) async-start(), calls=%async_computation.13 | async-start | bytes 16908288 | tf_op jit(solution)/shard_map/all_gather | solution.py:1082
  11.4 14.1 %collective-permute-start.4 = (bf16[8,2048]{1,0:T(8,128)(2,1)S(1)}, bf16[8,2048]{1,0:T(8,128)(2,1)S(1)}, u32[]{:S(2)}, u32[]{:S(2)}) collective-permute-start(bf16[8,2048]{1,0:T(8,128)(2,1)S(1)} %pad_maximum_fusion.2), channel_id=1, source_target_pairs={{0,96},{32,0},{64,32},{96,64},{1,97},{33,1},{65,33},{97,65},{2,98}... | collective-permute-start | bytes 98312 | tf_op jit(solution)/shard_map/ppermute | solution.py:1046
  14.3 11.3 %collective-permute-start.5 = (bf16[8,2048]{1,0:T(8,128)(2,1)S(1)}, bf16[8,2048]{1,0:T(8,128)(2,1)S(1)}, u32[]{:S(2)}, u32[]{:S(2)}) collective-permute-start(bf16[8,2048]{1,0:T(8,128)(2,1)S(1)} %pad_maximum_fusion.2), channel_id=1, source_target_pairs={{0,64},{32,96},{64,0},{96,32},{1,65},{33,97},{65,1},{97,33},{2,66}... | collective-permute-start | bytes 98312 | tf_op jit(solution)/shard_map/ppermute | solution.py:1046
  15.1 10.5 %collective-permute-start.6 = (bf16[8,2048]{1,0:T(8,128)(2,1)S(1)}, bf16[8,2048]{1,0:T(8,128)(2,1)S(1)}, u32[]{:S(2)}, u32[]{:S(2)}) collective-permute-start(bf16[8,2048]{1,0:T(8,128)(2,1)S(1)} %pad_maximum_fusion.2), channel_id=1, source_target_pairs={{0,32},{32,64},{64,96},{96,0},{1,33},{33,65},{65,97},{97,1},{2,34}... | collective-permute-start | bytes 98312 | tf_op jit(solution)/shard_map/ppermute | solution.py:1046
  17.5 20.0 %all-to-all-start = ((bf16[16,8,2176]{2,1,0:T(8,128)(2,1)}), bf16[16,8,2176]{2,1,0:T(8,128)(2,1)S(1)}, u32[]{:S(2)}, u32[]{:S(2)}) async-start(bf16[16,8,2176]{2,1,0:T(8,128)(2,1)} %broadcast_in_dim.41), calls=%async_computation | async-start | bytes 1114112 | tf_op jit(solution)/shard_map/all_to_all | solution.py:1099
  37.5 24.7 %collective-permute-start = (bf16[128,2176]{1,0:T(8,128)(2,1)S(1)}, bf16[128,2176]{1,0:T(8,128)(2,1)S(1)}, u32[]{:S(2)}, u32[]{:S(2)}) collective-permute-start(bf16[128,2176]{1,0:T(8,128)(2,1)S(1)} %bitcast.112), channel_id=1, source_target_pairs={{0,96},{32,0},{64,32},{96,64},{1,97},{33,1},{65,33},{97,65},{2,98}... | collective-permute-start | bytes 1671176 | tf_op jit(solution)/shard_map/ppermute | solution.py:1046
  41.6 37.2 %all-to-all-start.1 = ((bf16[16,4,8,2048]{3,2,1,0:T(8,128)(2,1)}), bf16[16,4,8,2048]{3,2,1,0:T(8,128)(2,1)S(1)}, u32[]{:S(2)}, u32[]{:S(2)}) async-start(bf16[16,4,8,2048]{3,2,1,0:T(8,128)(2,1)} %broadcast_in_dim.42), calls=%async_computation.1 | async-start | bytes 4194304 | tf_op jit(solution)/shard_map/all_to_all | solution.py:1099
  45.3 169.3 %reduce-scatter.5.cloned.1.call-start = ((), (), s32[]{:S(2)}) async-start(), calls=%async_computation.14 | async-start | bytes 7077888 | tf_op jit(solution)/shard_map/reduce_scatter | solution.py:1163
  45.3 20.4 %collective-permute-start.1 = (bf16[128,2176]{1,0:T(8,128)(2,1)S(1)}, bf16[128,2176]{1,0:T(8,128)(2,1)S(1)}, u32[]{:S(2)}, u32[]{:S(2)}) collective-permute-start(bf16[128,2176]{1,0:T(8,128)(2,1)S(1)} %bitcast.113), channel_id=1, source_target_pairs={{0,64},{32,96},{64,0},{96,32},{1,65},{33,97},{65,1},{97,33},{2,66}... | collective-permute-start | bytes 1671176 | tf_op jit(solution)/shard_map/ppermute | solution.py:1046
  46.9 29.9 %collective-permute-start.2 = (bf16[128,2176]{1,0:T(8,128)(2,1)S(1)}, bf16[128,2176]{1,0:T(8,128)(2,1)S(1)}, u32[]{:S(2)}, u32[]{:S(2)}) collective-permute-start(bf16[128,2176]{1,0:T(8,128)(2,1)S(1)} %bitcast.114), channel_id=1, source_target_pairs={{0,32},{32,64},{64,96},{96,0},{1,33},{33,65},{65,97},{97,1},{2,34}... | collective-permute-start | bytes 1671176 | tf_op jit(solution)/shard_map/ppermute | solution.py:1046
  78.7 6.6 %collective-permute-start.3 = (bf16[512,2176]{1,0:T(8,128)(2,1)}, bf16[512,2176]{1,0:T(8,128)(2,1)}, u32[]{:S(2)}, u32[]{:S(2)}) collective-permute-start(bf16[512,2176]{1,0:T(8,128)(2,1)} %bitcast.7.own_qk), channel_id=1, source_target_pairs={{0,16},{16,0},{1,17},{17,1},{2,18},{18,2},{3,19},{19,3},{4,20},{20... | collective-permute-start | bytes 6684680 | tf_op jit(solution)/shard_map/ppermute | solution.py:1037
  144.9 48.5 %all-to-all-start.2 = ((bf16[16,64,1024]{2,1,0:T(8,128)(2,1)}), bf16[16,64,1024]{2,1,0:T(8,128)(2,1)S(1)}, u32[]{:S(2)}, u32[]{:S(2)}) async-start(bf16[16,64,1024]{2,1,0:T(8,128)(2,1)} %get-tuple-element.78._), calls=%async_computation.2 | async-start | bytes 4194304 | tf_op jit(solution)/shard_map/all_to_all | solution.py:1160
  151.9 106.4 %reduce-scatter.7.cloned.1.call-start = ((), (), s32[]{:S(2)}) async-start(), calls=%async_computation.15 | async-start | bytes 3932160 | tf_op jit(solution)/shard_map/reduce_scatter | solution.py:1150
  180.6 15.6 %collective-permute-start.8 = (bf16[512,2048]{1,0:T(8,128)(2,1)}, bf16[512,2048]{1,0:T(8,128)(2,1)}, u32[]{:S(2)}, u32[]{:S(2)}) collective-permute-start(bf16[512,2048]{1,0:T(8,128)(2,1)} %get-tuple-element.85), channel_id=1, source_target_pairs={{0,16},{16,0},{1,17},{17,1},{2,18},{18,2},{3,19},{19,3},{4,20},{20... | collective-permute-start | bytes 6291464 | tf_op jit(solution)/shard_map/ppermute | solution.py:1037
  180.6 15.6 %collective-permute-start.9 = (bf16[16,32,2048]{2,1,0:T(8,128)(2,1)}, bf16[16,32,2048]{2,1,0:T(8,128)(2,1)}, u32[]{:S(2)}, u32[]{:S(2)}) collective-permute-start(bf16[16,32,2048]{2,1,0:T(8,128)(2,1)} %get-tuple-element.86), channel_id=1, source_target_pairs={{0,16},{16,0},{1,17},{17,1},{2,18},{18,2},{3,19},{19,3},{4,20},{20... | collective-permute-start | bytes 6291464 | tf_op jit(solution)/shard_map/ppermute | solution.py:1037
  206.9 40.1 %all-to-all-start.3 = ((bf16[16,32,2048]{2,1,0:T(8,128)(2,1)}), bf16[16,32,2048]{2,1,0:T(8,128)(2,1)S(1)}, u32[]{:S(2)}, u32[]{:S(2)}) async-start(bf16[16,32,2048]{2,1,0:T(8,128)(2,1)} %get-tuple-element.90._), calls=%async_computation.4 | async-start | bytes 4194304 | tf_op jit(solution)/shard_map/all_to_all | solution.py:1160
  214.1 89.7 %reduce-scatter.11.cloned.1.call-start = ((), (), s32[]{:S(2)}) async-start(), calls=%async_computation.17 | async-start | bytes 1310720 | tf_op jit(solution)/shard_map/reduce_scatter | solution.py:1150
  231.9 17.9 %collective-permute-start.12 = (bf16[512,1024]{1,0:T(8,128)(2,1)}, bf16[512,1024]{1,0:T(8,128)(2,1)S(1)}, u32[]{:S(2)}, u32[]{:S(2)}) collective-permute-start(bf16[512,1024]{1,0:T(8,128)(2,1)} %get-tuple-element.100), channel_id=1, source_target_pairs={{0,16},{16,0},{1,17},{17,1},{2,18},{18,2},{3,19},{19,3},{4,20},{20... | collective-permute-start | bytes 3145736 | tf_op jit(solution)/shard_map/ppermute | solution.py:1037
  232.0 17.9 %collective-permute-start.13 = (bf16[512,1024]{1,0:T(8,128)(2,1)}, bf16[512,1024]{1,0:T(8,128)(2,1)}, u32[]{:S(2)}, u32[]{:S(2)}) collective-permute-start(bf16[512,1024]{1,0:T(8,128)(2,1)} %get-tuple-element.101), channel_id=1, source_target_pairs={{0,16},{16,0},{1,17},{17,1},{2,18},{18,2},{3,19},{19,3},{4,20},{20... | collective-permute-start | bytes 3145736 | tf_op jit(solution)/shard_map/ppermute | solution.py:1037
  232.5 17.4 %collective-permute-start.14 = (bf16[512,1024]{1,0:T(8,128)(2,1)}, bf16[512,1024]{1,0:T(8,128)(2,1)}, u32[]{:S(2)}, u32[]{:S(2)}) collective-permute-start(bf16[512,1024]{1,0:T(8,128)(2,1)} %get-tuple-element.102), channel_id=1, source_target_pairs={{0,16},{16,0},{1,17},{17,1},{2,18},{18,2},{3,19},{19,3},{4,20},{20... | collective-permute-start | bytes 3145736 | tf_op jit(solution)/shard_map/ppermute | solution.py:1037
  260.7 31.5 %all-to-all-start.4 = ((bf16[16,8,6144]{2,1,0:T(8,128)(2,1)}), bf16[16,8,6144]{2,1,0:T(8,128)(2,1)S(1)}, u32[]{:S(2)}, u32[]{:S(2)}) async-start(bf16[16,8,6144]{2,1,0:T(8,128)(2,1)} %maximum_bitcast_fusion), calls=%async_computation.6 | async-start | bytes 3145728 | tf_op jit(solution)/shard_map/all_to_all | solution.py:1154
  266.5 51.9 %reduce-scatter.9.cloned.1.call-start = ((), (), s32[]{:S(2)}) async-start(), calls=%async_computation.16 | async-start | bytes 2621440 | tf_op jit(solution)/shard_map/reduce_scatter | solution.py:1150
  293.2 10.1 %collective-permute-start.18 = (bf16[4,8,1024]{2,1,0:T(8,128)(2,1)S(1)}, bf16[4,8,1024]{2,1,0:T(8,128)(2,1)S(1)}, u32[]{:S(2)}, u32[]{:S(2)}) collective-permute-start(bf16[4,8,1024]{2,1,0:T(8,128)(2,1)S(1)} %fusion.8), channel_id=1, source_target_pairs={{0,16},{16,0},{1,17},{17,1},{2,18},{18,2},{3,19},{19,3},{4,20},{20... | collective-permute-start | bytes 196616 | tf_op jit(solution)/shard_map/ppermute | solution.py:1037
  293.5 7.9 %collective-permute-start.16 = (f32[128,128]{1,0:T(8,128)S(1)}, f32[128,128]{1,0:T(8,128)S(1)}, u32[]{:S(2)}, u32[]{:S(2)}) collective-permute-start(f32[128,128]{1,0:T(8,128)S(1)} %get-tuple-element.127), channel_id=1, source_target_pairs={{0,64},{32,96},{64,0},{96,32},{1,65},{33,97},{65,1},{97,33},{2,66}... | collective-permute-start | bytes 196616 | tf_op jit(solution)/shard_map/ppermute | solution.py:1046
  295.0 8.1 %collective-permute-start.17 = (f32[128,128]{1,0:T(8,128)S(1)}, f32[128,128]{1,0:T(8,128)S(1)}, u32[]{:S(2)}, u32[]{:S(2)}) collective-permute-start(f32[128,128]{1,0:T(8,128)S(1)} %get-tuple-element.126), channel_id=1, source_target_pairs={{0,32},{32,64},{64,96},{96,0},{1,33},{33,65},{65,97},{97,1},{2,34}... | collective-permute-start | bytes 196616 | tf_op jit(solution)/shard_map/ppermute | solution.py:1046
  305.5 12.9 %all-to-all-start.6 = ((bf16[16,8,1152]{2,1,0:T(8,128)(2,1)}), bf16[16,8,1152]{2,1,0:T(8,128)(2,1)S(1)}, u32[]{:S(2)}, u32[]{:S(2)}) async-start(bf16[16,8,1152]{2,1,0:T(8,128)(2,1)} %maximum_bitcast_fusion.1), calls=%async_computation.10 | async-start | bytes 589824 | tf_op jit(solution)/shard_map/all_to_all | solution.py:1154
  309.2 12.8 %collective-permute-start.19 = (bf16[8,3072]{1,0:T(8,128)(2,1)S(1)}, bf16[8,3072]{1,0:T(8,128)(2,1)S(1)}, u32[]{:S(2)}, u32[]{:S(2)}) collective-permute-start(bf16[8,3072]{1,0:T(8,128)(2,1)S(1)} %get-tuple-element.129), channel_id=1, source_target_pairs={{0,32},{32,64},{64,96},{96,0},{1,33},{33,65},{65,97},{97,1},{2,34}... | collective-permute-start | bytes 147464 | tf_op jit(solution)/shard_map/ppermute | solution.py:1046
  310.1 12.0 %collective-permute-start.20 = (bf16[8,3072]{1,0:T(8,128)(2,1)S(1)}, bf16[8,3072]{1,0:T(8,128)(2,1)S(1)}, u32[]{:S(2)}, u32[]{:S(2)}) collective-permute-start(bf16[8,3072]{1,0:T(8,128)(2,1)S(1)} %get-tuple-element.130), channel_id=1, source_target_pairs={{0,64},{32,96},{64,0},{96,32},{1,65},{33,97},{65,1},{97,33},{2,66}... | collective-permute-start | bytes 147464 | tf_op jit(solution)/shard_map/ppermute | solution.py:1046
  312.7 9.3 %collective-permute-start.21 = (bf16[8,3072]{1,0:T(8,128)(2,1)S(1)}, bf16[8,3072]{1,0:T(8,128)(2,1)S(1)}, u32[]{:S(2)}, u32[]{:S(2)}) collective-permute-start(bf16[8,3072]{1,0:T(8,128)(2,1)S(1)} %get-tuple-element.131), channel_id=1, source_target_pairs={{0,96},{32,0},{64,32},{96,64},{1,97},{33,1},{65,33},{97,65},{2,98}... | collective-permute-start | bytes 147464 | tf_op jit(solution)/shard_map/ppermute | solution.py:1046
  318.5 14.7 %all-to-all-start.5 = ((bf16[16,8,2048]{2,1,0:T(8,128)(2,1)}), bf16[16,8,2048]{2,1,0:T(8,128)(2,1)S(1)}, u32[]{:S(2)}, u32[]{:S(2)}) async-start(bf16[16,8,2048]{2,1,0:T(8,128)(2,1)} %bitcast.119), calls=%async_computation.8 | async-start | bytes 1048576 | tf_op jit(solution)/shard_map/all_to_all | solution.py:1154
  336.4 11.8 %all-to-all-start.7 = ((bf16[16,3,16,128]{3,2,1,0:T(8,128)(2,1)}), bf16[16,3,16,128]{3,2,1,0:T(8,128)(2,1)S(1)}, u32[]{:S(2)}, u32[]{:S(2)}) async-start(bf16[16,3,16,128]{3,2,1,0:T(8,128)(2,1)} %get-tuple-element.112), calls=%async_computation.11 | async-start | bytes 393216 | tf_op jit(solution)/shard_map/all_to_all | solution.py:1253
  353.2 11.8 %all-to-all-start.8 = ((bf16[16,3,16,128]{3,2,1,0:T(8,128)(2,1)}), bf16[16,3,16,128]{3,2,1,0:T(8,128)(2,1)S(1)}, u32[]{:S(2)}, u32[]{:S(2)}) async-start(bf16[16,3,16,128]{3,2,1,0:T(8,128)(2,1)} %get-tuple-element.115), calls=%async_computation.12 | async-start | bytes 393216 | tf_op jit(solution)/shard_map/all_to_all | solution.py:1255
  (22 other events, 307.0 us)
Sparse Core Ops, SparseCore 0:
  11.7 100.4 all-gather.1
  145.0 42.3 reduce-scatter.4
  207.0 38.1 reduce-scatter.6
  258.4 21.3 reduce-scatter.10
  282.2 32.4 reduce-scatter.8

commit v6 on v5

--- a/solution.py
+++ b/solution.py
@@ -476,7 +476,6 @@
     down,
     upstream,
     output,
-    top,
     kept,
     slope,
     stats,
@@ -526,7 +525,6 @@
         spread = stats[:, TILE : TILE + 1]
         value = held[at - steps]
         low = ((value - mean) * spread * rows_of[1:2, :] + rows_of[2:3, :]).astype(BF16)
-        top[...] = low
         total[...] += dot_nt(low, down[...])
         send_part(dot_nn(turned[...], low), at - steps, DOWN_FIRSTS, sent_first, sent_second)
 
@@ -541,7 +539,6 @@
     block = 1024
     steps = hidden // block
     early = lambda at, *_: (0, jnp.minimum(at, steps - 1))
-    late = lambda at, *_: (0, jnp.maximum(at - steps, 0))
     return call(
         functools.partial(forward_ffn_body, steps),
         (2 * steps,),
@@ -556,7 +553,6 @@
         ],
         [
             whole((rows, width)),
-            pl.BlockSpec((rows, block), late),
             pl.BlockSpec((rows, block), early),
             pl.BlockSpec((rows, block), early),
             whole((rows, 2 * TILE)),
@@ -564,7 +560,6 @@
         ],
         [
             jax.ShapeDtypeStruct((rows, width), BF16),
-            jax.ShapeDtypeStruct((rows, hidden), BF16),
             jax.ShapeDtypeStruct((rows, hidden), BF16),
             jax.ShapeDtypeStruct((rows, hidden), BF16),
             jax.ShapeDtypeStruct((rows, 2 * TILE), F32),
@@ -891,7 +886,7 @@
 
 
 def outer_stack_body(core, left, right, *refs):
-    adds, (first, last, turned) = refs[:3], refs[-3:]
+    adds, (out, turned) = refs[:3], refs[-2:]
     at = pl.program_id(0)
 
     @pl.when(at == 0)
@@ -903,7 +898,6 @@
 
         @pl.when(at == which)
         def _(add=add):
-            out = first if which < 2 else last
             out[...] = (value + add[...].astype(F32)).astype(BF16)
 
 
@@ -919,14 +913,8 @@
             *[whole((half, width)) for _ in adds],
             *after(*wait),
         ],
-        [
-            pl.BlockSpec((half, width), lambda at, *_: (0, jnp.minimum(at, count - 2))),
-            whole((half, width)),
-        ],
-        [
-            jax.ShapeDtypeStruct((half, (count - 1) * width), BF16),
-            jax.ShapeDtypeStruct((half, width), BF16),
-        ],
+        pl.BlockSpec((half, width), lambda at, *_: (0, at)),
+        jax.ShapeDtypeStruct((half, count * width), BF16),
         scratch=[pltpu.VMEM((half, rows), BF16)],
         flops=2 * rows * half * width * count,
         bytes_accessed=6 * half * width * count,
@@ -934,13 +922,12 @@
     )(core, left, rights, *adds, *wait)
 
 
-def to_slots_body(perm, early, late, last, rest, *refs):
+def to_slots_body(perm, early, late, rest, *refs):
     grad_qkv, grad_out, grad_up, grad_down, slots, tiles = refs
     width = grad_out.shape[1]
     half = 2 * width
     grad_out[...] = early[:, half : half + width]
-    grad_qkv[:, :half] = late[...]
-    grad_qkv[:, half:] = last[:, :width]
+    grad_qkv[...] = late[:, : 3 * width]
     grad_down[:, : DOWN_FIRSTS * width] = early[:, half + width :]
     grad_down[:, DOWN_FIRSTS * width :] = rest[:, :width]
     grad_up[:, :half] = early[:, :half]
@@ -956,8 +943,8 @@
         slots[slot // pairs, slot % pairs] = jnp.concatenate(pair, axis=0).astype(BF16)
 
 
-def to_slots(perm, early, late, last, rest, plane, widths):
-    arrays = [early, late, last, rest]
+def to_slots(perm, early, late, rest, plane, widths):
+    arrays = [early, late, rest]
     pairs = perm.shape[0] // (2 * plane)
     shapes = [jax.ShapeDtypeStruct((8, columns), F32) for columns in widths]
     shapes.append(jax.ShapeDtypeStruct((plane, pairs, 16, TILE), BF16))
@@ -1142,7 +1129,7 @@
     normed, projected = project(core_arg, tokens, vector_rows, weights)
     mixed, scaled, attention = attend(lengths, head_scale, projected)
     branch, attended, normed_mid = branch_out(core_arg, scaled, weights, tokens, vector_rows)
-    output, normed_top, kept, slope, stats, down_first, down_second = forward_ffn(
+    output, kept, slope, stats, down_first, down_second = forward_ffn(
         plane, normed_mid, attended, vector_rows, wide_rows, both, upstream
     )
 
@@ -1218,14 +1205,13 @@
 
     turned = turned.reshape(chips, 2, TILE, TILE)
     half_sums = take_core(turned, core) + swap_cores(take_core(turned, 1 - core))
-    query_key, value_last = outer_stack(
+    attn_first = outer_stack(
         core_arg, normed, grads, [swap_cores(part) for part in sent_attn], half_sums, up_rest
     )
 
     early_parts = over_plane(jnp.concatenate([up_chips, down_chips], axis=1))
-    half_sums, down_rest, up_rest, early_parts = lax.optimization_barrier(
-        (half_sums, down_rest, up_rest, early_parts)
-    )
+    half_sums, _ = lax.optimization_barrier((half_sums, attn_first))
+    down_rest, up_rest, early_parts = lax.optimization_barrier((down_rest, up_rest, early_parts))
     small = jnp.sum(in_order(across_chips(half_sums)), axis=0)
     down_rest = down_rest.reshape(chips, 2, shard, -1)
     down_rest = take_core(down_rest, core) + swap_cores(
@@ -1234,9 +1220,8 @@
     rest = jnp.concatenate([down_rest, up_rest.reshape(chips, shard, -1)], axis=2)
     rest = across_chips(rest.astype(BF16))
     rest = sum(part.astype(F32) for part in rest)
-    late_parts = over_plane(over_x(query_key))
-    last_parts = over_plane(jnp.concatenate([over_x(value_last), small.astype(BF16)], axis=1))
-    small = last_parts[:, width:]
+    late_parts = over_plane(jnp.concatenate([over_x(attn_first), small.astype(BF16)], axis=1))
+    small = late_parts[:, 3 * width :]
     vector_grads = small.T[: vectors.shape[0]]
     head_total = small[0, HEAD_AT : HEAD_AT + heads]
 
@@ -1245,7 +1230,6 @@
         owner_perm,
         early_parts,
         late_parts,
-        last_parts,
         rest,
         plane,
         [item.shape[1] for item in masters],

time: 381 us -> 369 us (0.969)
  waiting for transfers between devices: 108 us -> 96.1 us
    all_to_all x3 -> x2, waiting for transfers between devices: 40.9 us -> 23.8 us  [over_plane(): lax.all_to_all(part.reshape(plane, shard, -1), 'fsdp', split_axis=0, conc...]
    all_to_all x3 -> x2, starting transfers between devices: 13 us -> 12.4 us  [over_plane(): lax.all_to_all(part.reshape(plane, shard, -1), 'fsdp', split_axis=0, conc...]
  transfers between devices with their start and end apart: 36 -> 34, of which waited for: 14 -> 16; matrix products, arithmetic and copies ran while one was open for 7% -> 7% of each run, Pallas kernels for 30% -> 31%
where the time goes in v6:
time: 369 us; the launch traced here: 363 us
  Pallas kernels  152 us (41%)
  waiting for transfers between devices  96.1 us (26%)
  starting transfers between devices  64.2 us (17%)
  other arithmetic  18.7 us (5%)
  local copies, waits for them, and re-layouts  17.2 us (5%)
  between operations  15.2 us (4%)
    ppermute x12, waiting for transfers between devices, turn_chips(): lax.ppermute(values, 'x', [(at, (at + step) % count) for at in range(coun...  40 us
    pallas_call x1, Pallas kernels, forward_ffn(): call(functools.partial(forward_ffn_body, steps), (2 * steps,), [whole((ro...  28.7 us
    pallas_call x1, Pallas kernels, backward_ffn(): call(functools.partial(backward_ffn_body, steps), (2 * steps,), [whole((r...  28.3 us
    all_to_all x2, waiting for transfers between devices, over_plane(): lax.all_to_all(part.reshape(plane, shard, -1), 'fsdp', split_axis=0, conc...  23.8 us
    pallas_call x1, Pallas kernels, attend_back(): call(attend_back_body, (pairs,), [by_pair, pl.BlockSpec((rows, TILE), lam...  17.3 us
    ppermute x12, starting transfers between devices, turn_chips(): lax.ppermute(values, 'x', [(at, (at + step) % count) for at in range(coun...  15 us
    all_to_all x2, starting transfers between devices, plane_first(): lax.all_to_all(part, 'fsdp', split_axis=0, concat_axis=0, tiled=True)  14.3 us
    pallas_call x1, Pallas kernels, attend(): call(attend_body, (pairs,), [pl.BlockSpec((rows, TILE), lambda pair, *_:...  13.5 us
  transfers between devices with their start and end apart: 34, of which 16 were waited for; matrix products, arithmetic and copies ran while one was open for 7% of the time, Pallas kernels for 31%

profile of v6, /device:TPU:0, one launch (start us, length us, event | category | flops | bytes accessed | tf_op | source)
XLA Modules:
  0.0 363.1 jit_solution(1705873167110763557)
XLA Ops:
  11.4 2.8 collective-permute-start.4
  17.5 8.0 %all-to-all-start = ((bf16[16,8,2176]{2,1,0:T(8,128)(2,1)}), bf16[16,8,2176]{2,1,0:T(8,128)(2,1)S(1)}, u32[]{:S(2)}, u32[]{:S(2)}) async-start(bf16[16,8,2176]{2,1,0:T(8,128)(2,1)} %broadcast_in_dim.41), calls=%async_computation | async-start | bytes 1114112 | tf_op jit(solution)/shard_map/all_to_all | solution.py:1086
  25.7 11.9 %all-to-all-done = bf16[16,8,2176]{2,1,0:T(8,128)(2,1)S(1)} async-done(((bf16[16,8,2176]{2,1,0:T(8,128)(2,1)}), bf16[16,8,2176]{2,1,0:T(8,128)(2,1)S(1)}, u32[]{:S(2)}, u32[]{:S(2)}) %all-to-all-start) | async-done | bytes 557088 | tf_op jit(solution)/shard_map/all_to_all | solution.py:1086
  37.5 2.4 collective-permute-start
  41.6 3.7 %all-to-all-start.1 = ((bf16[16,4,8,2048]{3,2,1,0:T(8,128)(2,1)}), bf16[16,4,8,2048]{3,2,1,0:T(8,128)(2,1)S(1)}, u32[]{:S(2)}, u32[]{:S(2)}) async-start(bf16[16,4,8,2048]{3,2,1,0:T(8,128)(2,1)} %broadcast_in_dim.42), calls=%async_computation.1 | async-start | bytes 4194304 | tf_op jit(solution)/shard_map/all_to_all | solution.py:1086
  46.9 15.3 %collective-permute-done = bf16[128,2176]{1,0:T(8,128)(2,1)S(1)} collective-permute-done((bf16[128,2176]{1,0:T(8,128)(2,1)S(1)}, bf16[128,2176]{1,0:T(8,128)(2,1)S(1)}, u32[]{:S(2)}, u32[]{:S(2)}) %collective-permute-start) | collective-permute-done | bytes 557088 | tf_op jit(solution)/shard_map/ppermute | solution.py:1033
  62.3 3.4 collective-permute-done.1
  65.8 11.0 %collective-permute-done.2 = bf16[128,2176]{1,0:T(8,128)(2,1)S(1)} collective-permute-done((bf16[128,2176]{1,0:T(8,128)(2,1)S(1)}, bf16[128,2176]{1,0:T(8,128)(2,1)S(1)}, u32[]{:S(2)}, u32[]{:S(2)}) %collective-permute-start.2) | collective-permute-done | bytes 557088 | tf_op jit(solution)/shard_map/ppermute | solution.py:1033
  87.5 8.6 %shard_map.304 = (bf16[512,1024]{1,0:T(8,128)(2,1)}, bf16[512,3072]{1,0:T(8,128)(2,1)}) custom-call(s32[1]{0:T(128)} %bitcast.core, bf16[512,1024]{1,0:T(8,128)(2,1)} %tokens.5, f32[24,1024]{1,0:T(8,128)} %copy-done.2, bf16[512,2176]{1,0:T(8,128)(2,1)} %bitcast.7.own_qk, bf16[512,2176]{1,0:T(8,128)(2,1)} %collective-permute-done.3.other_qk, ...), custom_call_target="tpu_custom_call" | custom-call | flops 3221225472 | bytes 6291456 | tf_op jit(solution)/shard_map/pallas_call | solution.py:148
  96.1 13.5 %shard_map.305 = (f32[512,1024]{1,0:T(8,128)}, bf16[512,1024]{1,0:T(8,128)(2,1)}, bf16[16,256,768]{2,1,0:T(8,128)(2,1)}) custom-call(s32[1]{0:T(128)S(6)} %copy.71.length, f32[16]{0:T(128)} %scales.1, bf16[512,3072]{1,0:T(8,128)(2,1)} %get-tuple-element.67.queries.keys.values, bf16[512,3072]{1,0:T(8,128)(2,1)} %get-tuple-element.67.queries.keys.values, ...), custom_call_target="tpu_custom_call" | custom-call | flops 1073741824 | bytes 10485760 | tf_op jit(solution)/shard_map/pallas_call | solution.py:215
  109.6 6.3 %shard_map.306 = (f32[512,1024]{1,0:T(8,128)}, f32[512,1024]{1,0:T(8,128)}, bf16[512,1024]{1,0:T(8,128)(2,1)}) custom-call(s32[1]{0:T(128)} %bitcast.core, bf16[512,1024]{1,0:T(8,128)(2,1)} %get-tuple-element.68.scaled, bf16[512,2048]{1,0:T(8,128)(2,1)} %bitcast.107, bf16[512,2048]{1,0:T(8,128)(2,1)} %collective-permute-done.7.other_vo.other, ...), custom_call_target="tpu_custom_call" | custom-call | flops 1073741824 | bytes 9437184 | tf_op jit(solution)/shard_map/pallas_call | solution.py:337
  115.9 28.7 %shard_map.307 = (bf16[512,1024]{1,0:T(8,128)(2,1)}, bf16[512,4096]{1,0:T(8,128)(2,1)}, bf16[512,4096]{1,0:T(8,128)(2,1)}, f32[512,256]{1,0:T(8,128)}, bf16[1024...) custom-call(bf16[512,1024]{1,0:T(8,128)(2,1)} %get-tuple-element.69.normed.left, ...), custom_call_target="tpu_custom_call" | custom-call | flops 12884901888 | bytes 29360128 | tf_op jit(solution)/shard_map/pallas_call | solution.py:542
  144.6 7.1 %all-to-all-start.2 = ((bf16[16,64,1024]{2,1,0:T(8,128)(2,1)}), bf16[16,64,1024]{2,1,0:T(8,128)(2,1)S(1)}, u32[]{:S(2)}, u32[]{:S(2)}) async-start(bf16[16,64,1024]{2,1,0:T(8,128)(2,1)} %get-tuple-element.76._), calls=%async_computation.2 | async-start | bytes 4194304 | tf_op jit(solution)/shard_map/all_to_all | solution.py:1147
  152.0 28.3 %shard_map.308 = (f32[512,1024]{1,0:T(8,128)}, bf16[512,4096]{1,0:T(8,128)(2,1)}, f32[4,8,1024]{2,1,0:T(8,128)}, f32[8,1024]{1,0:T(8,128)}, bf16[512,2048]{1,0:T(8,128)(2,1)}, /*index=5*/bf16[16,32,2048]{2,1,0:T(8,128)(2,1)}) custom-call(s32[1]{0:T(128)} %bitcast.core, bf16[512,1024]{1,0:T(8,128)(2,1)} %broadcast_select_fusion.upstream, ...), custom_call_target="tpu_custom_call" | custom-call | flops 10737418240 | bytes 33554432 | tf_op jit(solution)/shard_map/pallas_call | solution.py:672
  181.6 11.3 %shard_map.309 = (bf16[512,1024]{1,0:T(8,128)(2,1)}, bf16[512,1024]{1,0:T(8,128)(2,1)}, f32[8,1024]{1,0:T(8,128)}, bf16[512,1024]{1,0:T(8,128)(2,1)}, f32[512,1024]{1,0:T(8,128)}) custom-call(s32[1]{0:T(128)} %bitcast.core, f32[512,1024]{1,0:T(8,128)} %get-tuple-element.77.grad_attended, f32[512,1024]{1,0:T(8,128)} %get-tuple-element.78.branch, ...), custom_call_target="tpu_custom_call" | custom-call | flops 2147483648 | bytes 10485760 | tf_op jit(solution)/shard_map/pallas_call | solution.py:409
  196.9 9.8 %shard_map.310 = (bf16[512,3072]{1,0:T(8,128)(2,1)}, bf16[16,32,2048]{2,1,0:T(8,128)(2,1)}) custom-call(s32[1]{0:T(128)} %bitcast.core, bf16[512,1024]{1,0:T(8,128)(2,1)} %get-tuple-element.69.normed.left, bf16[512,4096]{1,0:T(8,128)(2,1)} %get-tuple-element.82.right, bf16[512,2048]{1,0:T(8,128)(2,1)} %collective-permute-done.8.add_first, ...), custom_call_target="tpu_custom_call" | custom-call | flops 2147483648 | bytes 12582912 | tf_op jit(solution)/shard_map/pallas_call | solution.py:868
  206.7 7.2 %all-to-all-start.3 = ((bf16[16,32,2048]{2,1,0:T(8,128)(2,1)}), bf16[16,32,2048]{2,1,0:T(8,128)(2,1)S(1)}, u32[]{:S(2)}, u32[]{:S(2)}) async-start(bf16[16,32,2048]{2,1,0:T(8,128)(2,1)} %get-tuple-element.88._), calls=%async_computation.4 | async-start | bytes 4194304 | tf_op jit(solution)/shard_map/all_to_all | solution.py:1147
  214.4 17.3 %shard_map.311 = (bf16[3,512,1024]{2,1,0:T(8,128)(2,1)}, bf16[512,1024]{1,0:T(8,128)(2,1)}, bf16[512,1024]{1,0:T(8,128)(2,1)}, bf16[512,1024]{1,0:T(8,128)(2,1)}) custom-call(s32[1]{0:T(128)} %bitcast.core, bf16[512,3072]{1,0:T(8,128)(2,1)} %get-tuple-element.67.queries.keys.values, bf16[512,3072]{1,0:T(8,128)(2,1)} %get-tuple-element.67.queries.keys.values, ...), custom_call_target="tpu_custom_call" | custom-call | flops 2684354560 | bytes 12582912 | tf_op jit(solution)/shard_map/pallas_call | solution.py:292
  232.4 11.2 %shard_map.312 = (f32[512,1024]{1,0:T(8,128)}, f32[8,128,128]{2,1,0:T(8,128)}) custom-call(s32[1]{0:T(128)} %bitcast.core, bf16[3,512,1024]{2,1,0:T(8,128)(2,1)} %get-tuple-element.90.grads.right, bf16[512,2176]{1,0:T(8,128)(2,1)} %bitcast.7.own_qk, bf16[512,2176]{1,0:T(8,128)(2,1)} %collective-permute-done.3.other_qk, bf16[512,2048]{1,0:T(8,128)(2,1)} %bitcast.109, ...), custom_call_target="tpu_custom_call" | custom-call | flops 3221225472 | bytes 14680064 | tf_op jit(solution)/shard_map/pallas_call | solution.py:792
  250.7 7.1 %shard_map.313 = bf16[512,3072]{1,0:T(8,128)(2,1)} custom-call(s32[1]{0:T(128)} %bitcast.core, bf16[512,1024]{1,0:T(8,128)(2,1)} %get-tuple-element.81.normed.left, bf16[3,512,1024]{2,1,0:T(8,128)(2,1)} %get-tuple-element.90.grads.right, bf16[512,1024]{1,0:T(8,128)(2,1)} %copy-done.8, bf16[512,1024]{1,0:T(8,128)(2,1)} %collective-permute-done.12.refs_1_, ...), custom_call_target="tpu_custom_call" | custom-call | flops 1610612736 | bytes 9437184 | tf_op jit(solution)/shard_map/pallas_call | solution.py:907
  261.9 5.3 %all-to-all-start.4 = ((bf16[16,8,6144]{2,1,0:T(8,128)(2,1)}), bf16[16,8,6144]{2,1,0:T(8,128)(2,1)S(1)}, u32[]{:S(2)}, u32[]{:S(2)}) async-start(bf16[16,8,6144]{2,1,0:T(8,128)(2,1)} %maximum_bitcast_fusion), calls=%async_computation.6 | async-start | bytes 3145728 | tf_op jit(solution)/shard_map/all_to_all | solution.py:1141
  269.5 5.6 %collective-permute-done.16 = f32[128,128]{1,0:T(8,128)S(1)} collective-permute-done((f32[128,128]{1,0:T(8,128)S(1)}, f32[128,128]{1,0:T(8,128)S(1)}, u32[]{:S(2)}, u32[]{:S(2)}) %collective-permute-start.16) | collective-permute-done | bytes 65568 | tf_op jit(solution)/shard_map/ppermute | solution.py:1033
  276.6 16.2 %all-to-all-done.4 = bf16[16,8,6144]{2,1,0:T(8,128)(2,1)S(1)} async-done(((bf16[16,8,6144]{2,1,0:T(8,128)(2,1)}), bf16[16,8,6144]{2,1,0:T(8,128)(2,1)S(1)}, u32[]{:S(2)}, u32[]{:S(2)}) %all-to-all-start.4) | async-done | bytes 1572896 | tf_op jit(solution)/shard_map/all_to_all | solution.py:1141
  299.0 7.1 %all-to-all-start.5 = ((bf16[16,8,3200]{2,1,0:T(8,128)(2,1)}), bf16[16,8,3200]{2,1,0:T(8,128)(2,1)S(1)}, u32[]{:S(2)}, u32[]{:S(2)}) async-start(bf16[16,8,3200]{2,1,0:T(8,128)(2,1)} %maximum_bitcast_fusion.1), calls=%async_computation.8 | async-start | bytes 1638400 | tf_op jit(solution)/shard_map/all_to_all | solution.py:1141
  313.6 7.5 %all-to-all-done.5 = bf16[16,8,3200]{2,1,0:T(8,128)(2,1)S(1)} async-done(((bf16[16,8,3200]{2,1,0:T(8,128)(2,1)}), bf16[16,8,3200]{2,1,0:T(8,128)(2,1)S(1)}, u32[]{:S(2)}, u32[]{:S(2)}) %all-to-all-start.5) | async-done | bytes 819232 | tf_op jit(solution)/shard_map/all_to_all | solution.py:1141
  321.8 2.6 shard_map.314
  324.4 3.5 all-to-all-start.6
  328.5 7.7 %all-to-all-done.6.grads = bf16[16,3,16,128]{3,2,1,0:T(8,128)(2,1)S(1)} async-done(((bf16[16,3,16,128]{3,2,1,0:T(8,128)(2,1)}), bf16[16,3,16,128]{3,2,1,0:T(8,128)(2,1)S(1)}, u32[]{:S(2)}, u32[]{:S(2)}) %all-to-all-start.6) | async-done | bytes 196640 | tf_op jit(solution)/shard_map/all_to_all | solution.py:1237
  336.9 4.3 %shard_map.315 = (f32[6,128,128]{2,1,0:T(8,128)}, f32[6,128,128]{2,1,0:T(8,128)}, bf16[16,3,16,128]{3,2,1,0:T(8,128)(2,1)}) custom-call(bf16[16,3,16,128]{3,2,1,0:T(8,128)(2,1)} %copy-done.10, f32[6,128,128]{2,1,0:T(8,128)} %bitcast.120, f32[6,128,128]{2,1,0:T(8,128)} %bitcast.121, f32[6,128,128]{2,1,0:T(8,128)} %bitcast.122, f32[6,128,128]{2,1,0:T(8,128)} %bitcast.123), custom_call_target="tpu_custom_call" | custom-call | bytes 2359296 | tf_op jit(solution)/shard_map/pallas_call | solution.py:983
  341.2 3.5 all-to-all-start.7
  346.0 7.0 %all-to-all-done.7.moved = bf16[16,3,16,128]{3,2,1,0:T(8,128)(2,1)S(1)} async-done(((bf16[16,3,16,128]{3,2,1,0:T(8,128)(2,1)}), bf16[16,3,16,128]{3,2,1,0:T(8,128)(2,1)S(1)}, u32[]{:S(2)}, u32[]{:S(2)}) %all-to-all-start.7) | async-done | bytes 196640 | tf_op jit(solution)/shard_map/all_to_all | solution.py:1239
  353.7 2.6 shard_map.316
  (163 shorter events, 59.8 us)
Async XLA Ops:
  7.2 108.7 %all-gather.2.cloned.1.call-start = ((), (), s32[]{:S(2)}) async-start(), calls=%async_computation.11 | async-start | bytes 16908288 | tf_op jit(solution)/shard_map/all_gather | solution.py:1069
  11.4 14.1 %collective-permute-start.4 = (bf16[8,2048]{1,0:T(8,128)(2,1)S(1)}, bf16[8,2048]{1,0:T(8,128)(2,1)S(1)}, u32[]{:S(2)}, u32[]{:S(2)}) collective-permute-start(bf16[8,2048]{1,0:T(8,128)(2,1)S(1)} %pad_maximum_fusion.2), channel_id=1, source_target_pairs={{0,96},{32,0},{64,32},{96,64},{1,97},{33,1},{65,33},{97,65},{2,98}... | collective-permute-start | bytes 98312 | tf_op jit(solution)/shard_map/ppermute | solution.py:1033
  14.3 11.3 %collective-permute-start.5 = (bf16[8,2048]{1,0:T(8,128)(2,1)S(1)}, bf16[8,2048]{1,0:T(8,128)(2,1)S(1)}, u32[]{:S(2)}, u32[]{:S(2)}) collective-permute-start(bf16[8,2048]{1,0:T(8,128)(2,1)S(1)} %pad_maximum_fusion.2), channel_id=1, source_target_pairs={{0,64},{32,96},{64,0},{96,32},{1,65},{33,97},{65,1},{97,33},{2,66}... | collective-permute-start | bytes 98312 | tf_op jit(solution)/shard_map/ppermute | solution.py:1033
  15.1 10.5 %collective-permute-start.6 = (bf16[8,2048]{1,0:T(8,128)(2,1)S(1)}, bf16[8,2048]{1,0:T(8,128)(2,1)S(1)}, u32[]{:S(2)}, u32[]{:S(2)}) collective-permute-start(bf16[8,2048]{1,0:T(8,128)(2,1)S(1)} %pad_maximum_fusion.2), channel_id=1, source_target_pairs={{0,32},{32,64},{64,96},{96,0},{1,33},{33,65},{65,97},{97,1},{2,34}... | collective-permute-start | bytes 98312 | tf_op jit(solution)/shard_map/ppermute | solution.py:1033
  17.5 20.0 %all-to-all-start = ((bf16[16,8,2176]{2,1,0:T(8,128)(2,1)}), bf16[16,8,2176]{2,1,0:T(8,128)(2,1)S(1)}, u32[]{:S(2)}, u32[]{:S(2)}) async-start(bf16[16,8,2176]{2,1,0:T(8,128)(2,1)} %broadcast_in_dim.41), calls=%async_computation | async-start | bytes 1114112 | tf_op jit(solution)/shard_map/all_to_all | solution.py:1086
  37.5 24.7 %collective-permute-start = (bf16[128,2176]{1,0:T(8,128)(2,1)S(1)}, bf16[128,2176]{1,0:T(8,128)(2,1)S(1)}, u32[]{:S(2)}, u32[]{:S(2)}) collective-permute-start(bf16[128,2176]{1,0:T(8,128)(2,1)S(1)} %bitcast.111), channel_id=1, source_target_pairs={{0,96},{32,0},{64,32},{96,64},{1,97},{33,1},{65,33},{97,65},{2,98}... | collective-permute-start | bytes 1671176 | tf_op jit(solution)/shard_map/ppermute | solution.py:1033
  41.6 37.2 %all-to-all-start.1 = ((bf16[16,4,8,2048]{3,2,1,0:T(8,128)(2,1)}), bf16[16,4,8,2048]{3,2,1,0:T(8,128)(2,1)S(1)}, u32[]{:S(2)}, u32[]{:S(2)}) async-start(bf16[16,4,8,2048]{3,2,1,0:T(8,128)(2,1)} %broadcast_in_dim.42), calls=%async_computation.1 | async-start | bytes 4194304 | tf_op jit(solution)/shard_map/all_to_all | solution.py:1086
  45.3 169.1 %reduce-scatter.4.cloned.1.call-start = ((), (), s32[]{:S(2)}) async-start(), calls=%async_computation.12 | async-start | bytes 7077888 | tf_op jit(solution)/shard_map/reduce_scatter | solution.py:1150
  45.3 20.4 %collective-permute-start.1 = (bf16[128,2176]{1,0:T(8,128)(2,1)S(1)}, bf16[128,2176]{1,0:T(8,128)(2,1)S(1)}, u32[]{:S(2)}, u32[]{:S(2)}) collective-permute-start(bf16[128,2176]{1,0:T(8,128)(2,1)S(1)} %bitcast.112), channel_id=1, source_target_pairs={{0,64},{32,96},{64,0},{96,32},{1,65},{33,97},{65,1},{97,33},{2,66}... | collective-permute-start | bytes 1671176 | tf_op jit(solution)/shard_map/ppermute | solution.py:1033
  46.9 29.9 %collective-permute-start.2 = (bf16[128,2176]{1,0:T(8,128)(2,1)S(1)}, bf16[128,2176]{1,0:T(8,128)(2,1)S(1)}, u32[]{:S(2)}, u32[]{:S(2)}) collective-permute-start(bf16[128,2176]{1,0:T(8,128)(2,1)S(1)} %bitcast.113), channel_id=1, source_target_pairs={{0,32},{32,64},{64,96},{96,0},{1,33},{33,65},{65,97},{97,1},{2,34}... | collective-permute-start | bytes 1671176 | tf_op jit(solution)/shard_map/ppermute | solution.py:1033
  78.7 6.6 %collective-permute-start.3 = (bf16[512,2176]{1,0:T(8,128)(2,1)}, bf16[512,2176]{1,0:T(8,128)(2,1)}, u32[]{:S(2)}, u32[]{:S(2)}) collective-permute-start(bf16[512,2176]{1,0:T(8,128)(2,1)} %bitcast.7.own_qk), channel_id=1, source_target_pairs={{0,16},{16,0},{1,17},{17,1},{2,18},{18,2},{3,19},{19,3},{4,20},{20... | collective-permute-start | bytes 6684680 | tf_op jit(solution)/shard_map/ppermute | solution.py:1024
  81.8 5.7 %collective-permute-start.7 = (bf16[512,2048]{1,0:T(8,128)(2,1)S(1)}, bf16[512,2048]{1,0:T(8,128)(2,1)}, u32[]{:S(2)}, u32[]{:S(2)}) collective-permute-start(bf16[512,2048]{1,0:T(8,128)(2,1)S(1)} %bitcast.105), channel_id=1, source_target_pairs={{0,16},{16,0},{1,17},{17,1},{2,18},{18,2},{3,19},{19,3},{4,20},{20... | collective-permute-start | bytes 6291464 | tf_op jit(solution)/shard_map/ppermute | solution.py:1024
  144.6 48.5 %all-to-all-start.2 = ((bf16[16,64,1024]{2,1,0:T(8,128)(2,1)}), bf16[16,64,1024]{2,1,0:T(8,128)(2,1)S(1)}, u32[]{:S(2)}, u32[]{:S(2)}) async-start(bf16[16,64,1024]{2,1,0:T(8,128)(2,1)} %get-tuple-element.76._), calls=%async_computation.2 | async-start | bytes 4194304 | tf_op jit(solution)/shard_map/all_to_all | solution.py:1147
  151.7 107.7 %reduce-scatter.6.cloned.1.call-start = ((), (), s32[]{:S(2)}) async-start(), calls=%async_computation.13 | async-start | bytes 3932160 | tf_op jit(solution)/shard_map/reduce_scatter | solution.py:1137
  180.3 15.6 %collective-permute-start.8 = (bf16[512,2048]{1,0:T(8,128)(2,1)}, bf16[512,2048]{1,0:T(8,128)(2,1)}, u32[]{:S(2)}, u32[]{:S(2)}) collective-permute-start(bf16[512,2048]{1,0:T(8,128)(2,1)} %get-tuple-element.83), channel_id=1, source_target_pairs={{0,16},{16,0},{1,17},{17,1},{2,18},{18,2},{3,19},{19,3},{4,20},{20... | collective-permute-start | bytes 6291464 | tf_op jit(solution)/shard_map/ppermute | solution.py:1024
  180.3 15.6 %collective-permute-start.9 = (bf16[16,32,2048]{2,1,0:T(8,128)(2,1)}, bf16[16,32,2048]{2,1,0:T(8,128)(2,1)}, u32[]{:S(2)}, u32[]{:S(2)}) collective-permute-start(bf16[16,32,2048]{2,1,0:T(8,128)(2,1)} %get-tuple-element.84), channel_id=1, source_target_pairs={{0,16},{16,0},{1,17},{17,1},{2,18},{18,2},{3,19},{19,3},{4,20},{20... | collective-permute-start | bytes 6291464 | tf_op jit(solution)/shard_map/ppermute | solution.py:1024
  206.7 40.1 %all-to-all-start.3 = ((bf16[16,32,2048]{2,1,0:T(8,128)(2,1)}), bf16[16,32,2048]{2,1,0:T(8,128)(2,1)S(1)}, u32[]{:S(2)}, u32[]{:S(2)}) async-start(bf16[16,32,2048]{2,1,0:T(8,128)(2,1)} %get-tuple-element.88._), calls=%async_computation.4 | async-start | bytes 4194304 | tf_op jit(solution)/shard_map/all_to_all | solution.py:1147
  213.9 83.0 %reduce-scatter.8.cloned.1.call-start = ((), (), s32[]{:S(2)}) async-start(), calls=%async_computation.14 | async-start | bytes 3932160 | tf_op jit(solution)/shard_map/reduce_scatter | solution.py:1137
  231.7 17.9 %collective-permute-start.11 = (bf16[512,1024]{1,0:T(8,128)(2,1)}, bf16[512,1024]{1,0:T(8,128)(2,1)S(1)}, u32[]{:S(2)}, u32[]{:S(2)}) collective-permute-start(bf16[512,1024]{1,0:T(8,128)(2,1)} %get-tuple-element.97), channel_id=1, source_target_pairs={{0,16},{16,0},{1,17},{17,1},{2,18},{18,2},{3,19},{19,3},{4,20},{20... | collective-permute-start | bytes 3145736 | tf_op jit(solution)/shard_map/ppermute | solution.py:1024
  231.8 17.9 %collective-permute-start.12 = (bf16[512,1024]{1,0:T(8,128)(2,1)}, bf16[512,1024]{1,0:T(8,128)(2,1)}, u32[]{:S(2)}, u32[]{:S(2)}) collective-permute-start(bf16[512,1024]{1,0:T(8,128)(2,1)} %get-tuple-element.98), channel_id=1, source_target_pairs={{0,16},{16,0},{1,17},{17,1},{2,18},{18,2},{3,19},{19,3},{4,20},{20... | collective-permute-start | bytes 3145736 | tf_op jit(solution)/shard_map/ppermute | solution.py:1024
  232.3 17.4 %collective-permute-start.13 = (bf16[512,1024]{1,0:T(8,128)(2,1)}, bf16[512,1024]{1,0:T(8,128)(2,1)}, u32[]{:S(2)}, u32[]{:S(2)}) collective-permute-start(bf16[512,1024]{1,0:T(8,128)(2,1)} %get-tuple-element.99), channel_id=1, source_target_pairs={{0,16},{16,0},{1,17},{17,1},{2,18},{18,2},{3,19},{19,3},{4,20},{20... | collective-permute-start | bytes 3145736 | tf_op jit(solution)/shard_map/ppermute | solution.py:1024
  244.5 3.4 collective-permute-start.14
  258.8 10.7 %collective-permute-start.15 = (f32[128,128]{1,0:T(8,128)S(1)}, f32[128,128]{1,0:T(8,128)S(1)}, u32[]{:S(2)}, u32[]{:S(2)}) collective-permute-start(f32[128,128]{1,0:T(8,128)S(1)} %get-tuple-element.124), channel_id=1, source_target_pairs={{0,96},{32,0},{64,32},{96,64},{1,97},{33,1},{65,33},{97,65},{2,98}... | collective-permute-start | bytes 196616 | tf_op jit(solution)/shard_map/ppermute | solution.py:1033
  261.9 31.0 %all-to-all-start.4 = ((bf16[16,8,6144]{2,1,0:T(8,128)(2,1)}), bf16[16,8,6144]{2,1,0:T(8,128)(2,1)S(1)}, u32[]{:S(2)}, u32[]{:S(2)}) async-start(bf16[16,8,6144]{2,1,0:T(8,128)(2,1)} %maximum_bitcast_fusion), calls=%async_computation.6 | async-start | bytes 3145728 | tf_op jit(solution)/shard_map/all_to_all | solution.py:1141
  267.1 7.9 %collective-permute-start.16 = (f32[128,128]{1,0:T(8,128)S(1)}, f32[128,128]{1,0:T(8,128)S(1)}, u32[]{:S(2)}, u32[]{:S(2)}) collective-permute-start(f32[128,128]{1,0:T(8,128)S(1)} %get-tuple-element.123), channel_id=1, source_target_pairs={{0,64},{32,96},{64,0},{96,32},{1,65},{33,97},{65,1},{97,33},{2,66}... | collective-permute-start | bytes 196616 | tf_op jit(solution)/shard_map/ppermute | solution.py:1033
  268.7 7.9 %collective-permute-start.17 = (f32[128,128]{1,0:T(8,128)S(1)}, f32[128,128]{1,0:T(8,128)S(1)}, u32[]{:S(2)}, u32[]{:S(2)}) collective-permute-start(f32[128,128]{1,0:T(8,128)S(1)} %get-tuple-element.122), channel_id=1, source_target_pairs={{0,32},{32,64},{64,96},{96,0},{1,33},{33,65},{65,97},{97,1},{2,34}... | collective-permute-start | bytes 196616 | tf_op jit(solution)/shard_map/ppermute | solution.py:1033
  299.0 22.1 %all-to-all-start.5 = ((bf16[16,8,3200]{2,1,0:T(8,128)(2,1)}), bf16[16,8,3200]{2,1,0:T(8,128)(2,1)S(1)}, u32[]{:S(2)}, u32[]{:S(2)}) async-start(bf16[16,8,3200]{2,1,0:T(8,128)(2,1)} %maximum_bitcast_fusion.1), calls=%async_computation.8 | async-start | bytes 1638400 | tf_op jit(solution)/shard_map/all_to_all | solution.py:1141
  306.1 5.9 %collective-permute-start.19 = (bf16[8,3072]{1,0:T(8,128)(2,1)S(1)}, bf16[8,3072]{1,0:T(8,128)(2,1)S(1)}, u32[]{:S(2)}, u32[]{:S(2)}) collective-permute-start(bf16[8,3072]{1,0:T(8,128)(2,1)S(1)} %get-tuple-element.125), channel_id=1, source_target_pairs={{0,32},{32,64},{64,96},{96,0},{1,33},{33,65},{65,97},{97,1},{2,34}... | collective-permute-start | bytes 147464 | tf_op jit(solution)/shard_map/ppermute | solution.py:1033
  306.2 5.8 %collective-permute-start.20 = (bf16[8,3072]{1,0:T(8,128)(2,1)S(1)}, bf16[8,3072]{1,0:T(8,128)(2,1)S(1)}, u32[]{:S(2)}, u32[]{:S(2)}) collective-permute-start(bf16[8,3072]{1,0:T(8,128)(2,1)S(1)} %get-tuple-element.126), channel_id=1, source_target_pairs={{0,64},{32,96},{64,0},{96,32},{1,65},{33,97},{65,1},{97,33},{2,66}... | collective-permute-start | bytes 147464 | tf_op jit(solution)/shard_map/ppermute | solution.py:1033
  308.5 4.4 %collective-permute-start.21 = (bf16[8,3072]{1,0:T(8,128)(2,1)S(1)}, bf16[8,3072]{1,0:T(8,128)(2,1)S(1)}, u32[]{:S(2)}, u32[]{:S(2)}) collective-permute-start(bf16[8,3072]{1,0:T(8,128)(2,1)S(1)} %get-tuple-element.127), channel_id=1, source_target_pairs={{0,96},{32,0},{64,32},{96,64},{1,97},{33,1},{65,33},{97,65},{2,98}... | collective-permute-start | bytes 147464 | tf_op jit(solution)/shard_map/ppermute | solution.py:1033
  324.4 11.8 %all-to-all-start.6 = ((bf16[16,3,16,128]{3,2,1,0:T(8,128)(2,1)}), bf16[16,3,16,128]{3,2,1,0:T(8,128)(2,1)S(1)}, u32[]{:S(2)}, u32[]{:S(2)}) async-start(bf16[16,3,16,128]{3,2,1,0:T(8,128)(2,1)} %get-tuple-element.108), calls=%async_computation.9 | async-start | bytes 393216 | tf_op jit(solution)/shard_map/all_to_all | solution.py:1237
  341.2 11.8 %all-to-all-start.7 = ((bf16[16,3,16,128]{3,2,1,0:T(8,128)(2,1)}), bf16[16,3,16,128]{3,2,1,0:T(8,128)(2,1)S(1)}, u32[]{:S(2)}, u32[]{:S(2)}) async-start(bf16[16,3,16,128]{3,2,1,0:T(8,128)(2,1)} %get-tuple-element.111), calls=%async_computation.10 | async-start | bytes 393216 | tf_op jit(solution)/shard_map/all_to_all | solution.py:1239
  (20 other events, 234.2 us)
Sparse Core Ops, SparseCore 0:
  11.7 100.4 all-gather.1
  144.8 42.3 reduce-scatter.3
  206.8 38.2 reduce-scatter.5
  257.9 38.9 reduce-scatter.7

commit v7 on v6

--- a/solution.py
+++ b/solution.py
@@ -15,7 +15,6 @@
 RATE_VECTOR = 0.3
 HIGHEST = lax.Precision.HIGHEST
 HEAD_AT = 24
-DOWN_FIRSTS = 3
 UP_FIRSTS = 2
 VMEM_BYTES = 56 * 1024 * 1024
 F32 = jnp.float32
@@ -96,11 +95,6 @@
     for block in range(turned.shape[0] // TILE):
         at = pl.multiple_of((2 * block + parity) * TILE, TILE)
         turned[block * TILE : (block + 1) * TILE, :] = jnp.transpose(left[:, pl.ds(at, TILE)])
-
-
-def turn_all(left, turned):
-    for at in range(0, turned.shape[0], TILE):
-        turned[at : at + TILE, :] = jnp.transpose(left[:, at : at + TILE])
 
 
 def by_owner(values, plane):
@@ -472,15 +466,13 @@
     attended,
     vectors,
     rows_of,
-    up,
-    down,
+    weights,
     upstream,
     output,
     kept,
     slope,
     stats,
-    sent_first,
-    sent_second,
+    sent,
     held,
     total,
     sums,
@@ -491,12 +483,11 @@
 
     @pl.when(at == 0)
     def _():
-        turn_all(upstream, turned)
         sums[...] = jnp.zeros_like(sums)
 
     @pl.when(at < steps)
     def _():
-        hidden = dot_nn(normed[...], up[...]) + rows_of[0:1, :]
+        hidden = dot_nn(normed[...], weights[...]) + rows_of[0:1, :]
         cdf = 0.5 + 0.5 * lax.erf(hidden * math.sqrt(0.5))
         value = hidden * cdf
         slope[...] = (
@@ -505,6 +496,13 @@
         held[at] = value
         kept[...] = value.astype(BF16)
         sums[...] += lane_sum(value)
+        share = attended.shape[1]
+        start = pl.multiple_of(at * share, share)
+        total[:, pl.ds(start, share)] = attended[...] + vectors[21:22, pl.ds(start, share)]
+        for block in range(0, share, TILE):
+            turned[pl.ds(start + block, TILE), :] = jnp.transpose(
+                upstream[:, block : block + TILE]
+            )
 
     @pl.when(at == steps)
     def _():
@@ -517,7 +515,6 @@
         spread = lax.rsqrt(jnp.sum(square, axis=1, keepdims=True) * (1.0 / count) + EPS)
         stats[:, :TILE] = jnp.broadcast_to(mean, sums.shape)
         stats[:, TILE:] = jnp.broadcast_to(spread, sums.shape)
-        total[...] = attended[...] + vectors[21:22, :]
 
     @pl.when(at >= steps)
     def _():
@@ -525,15 +522,15 @@
         spread = stats[:, TILE : TILE + 1]
         value = held[at - steps]
         low = ((value - mean) * spread * rows_of[1:2, :] + rows_of[2:3, :]).astype(BF16)
-        total[...] += dot_nt(low, down[...])
-        send_part(dot_nn(turned[...], low), at - steps, DOWN_FIRSTS, sent_first, sent_second)
+        total[...] += dot_nt(low, weights[...])
+        sent[...] = dot_nn(turned[...], low).astype(BF16)
 
     @pl.when(at == 2 * steps - 1)
     def _():
         output[...] = total[...].astype(BF16)
 
 
-def forward_ffn(plane, normed, attended, vectors, wide_rows, both, upstream):
+def forward_ffn(normed, attended, vectors, wide_rows, both, upstream):
     rows, width = attended.shape
     hidden = both.shape[1] // 2
     block = 1024
@@ -544,26 +541,25 @@
         (2 * steps,),
         [
             whole((rows, width)),
-            whole((rows, width)),
+            pl.BlockSpec((rows, width // steps), early),
             whole(vectors.shape),
             pl.BlockSpec((8, block), lambda at, *_: (0, lax.rem(at, steps))),
-            pl.BlockSpec((width, block), early),
-            pl.BlockSpec((width, block), lambda at, *_: (0, steps + jnp.maximum(at - steps, 0))),
-            whole((rows, width)),
+            pl.BlockSpec((width, block), lambda at, *_: (0, at)),
+            pl.BlockSpec((rows, width // steps), early),
         ],
         [
             whole((rows, width)),
             pl.BlockSpec((rows, block), early),
             pl.BlockSpec((rows, block), early),
             whole((rows, 2 * TILE)),
-            *part_specs(width, plane, steps, DOWN_FIRSTS),
+            pl.BlockSpec((width, block), lambda at, *_: (0, jnp.maximum(at - steps, 0))),
         ],
         [
             jax.ShapeDtypeStruct((rows, width), BF16),
             jax.ShapeDtypeStruct((rows, hidden), BF16),
             jax.ShapeDtypeStruct((rows, hidden), BF16),
             jax.ShapeDtypeStruct((rows, 2 * TILE), F32),
-            *part_shapes(width, plane, DOWN_FIRSTS),
+            jax.ShapeDtypeStruct((width, hidden), BF16),
         ],
         scratch=[
             pltpu.VMEM((steps, rows, block), F32),
@@ -573,7 +569,7 @@
         ],
         flops=6 * rows * width * hidden,
         bytes_accessed=4 * width * hidden + 6 * rows * hidden,
-    )(normed, attended, vectors, wide_rows, both, both, upstream)
+    )(normed, attended, vectors, wide_rows, both, upstream)
 
 
 def backward_ffn_body(
@@ -586,8 +582,7 @@
     stats,
     kept,
     slope,
-    down,
-    up,
+    weights,
     normed,
     _,
     grad_attended,
@@ -601,6 +596,8 @@
     first,
     second,
     turned,
+    saved,
+    units,
 ):
     at = pl.program_id(0)
     count = steps * held.shape[2]
@@ -609,7 +606,6 @@
 
     @pl.when(at == 0)
     def _():
-        turn_rows(normed, turned, 1 - core[0])
         first[...] = jnp.zeros_like(first)
         second[...] = jnp.zeros_like(second)
         total[...] = jnp.zeros_like(total)
@@ -617,9 +613,16 @@
 
     @pl.when(at < steps)
     def _():
-        grad = dot_nn(upstream[...], down[...])
+        grad = dot_nn(upstream[...], weights[...])
         unit = (kept[...].astype(F32) - mean) * spread
+        units[at] = unit.astype(BF16)
         both = grad * unit
+        share = attended.shape[1]
+        saved[:, pl.ds(pl.multiple_of(at * share, share), share)] = attended[...]
+        lane = pl.multiple_of((1 - core[0]) * TILE, TILE)
+        turned[pl.ds(pl.multiple_of(at * TILE, TILE), TILE), :] = jnp.transpose(
+            normed[:, pl.ds(lane, TILE)]
+        )
         wide_sums[at, 0:1, :] = jnp.sum(both, axis=0, keepdims=True)
         wide_sums[at, 1:2, :] = jnp.sum(grad, axis=0, keepdims=True)
         gain = rows_of[1:2, :]
@@ -639,18 +642,18 @@
 
     @pl.when(at >= steps)
     def _():
-        unit = (kept[...].astype(F32) - mean) * spread
+        unit = units[at - steps].astype(F32)
         grad = spread * (held[at - steps] - first[:, 0:1] - unit * second[:, 0:1])
         low = (grad * slope[...].astype(F32)).astype(BF16)
         grad_hidden[...] = low
         wide_sums[at - steps, 2:3, :] = jnp.sum(low.astype(F32), axis=0, keepdims=True)
-        total[...] += dot_nt(low, up[...])
+        total[...] += dot_nt(low, weights[...])
         send_part(dot_nn(turned[...], low), at - steps, UP_FIRSTS, sent_first, sent_second)
 
     @pl.when(at == 2 * steps - 1)
     def _():
         grad = total[...]
-        centered, mid_spread = row_stats(attended[...])
+        centered, mid_spread = row_stats(saved[...])
         unit = centered * mid_spread
         top = upstream[...].astype(F32)
         grad_attended[...] = top + norm_back(grad * vectors[7:8, :], unit, mid_spread)
@@ -668,21 +671,21 @@
     block = 1024
     steps = hidden // block
     late = lambda at, *_: (0, jnp.maximum(at - steps, 0))
+    early = lambda at, *_: (0, jnp.minimum(at, steps - 1))
     turn = lambda at, *_: (0, lax.rem(at, steps))
     return call(
         functools.partial(backward_ffn_body, steps),
         (2 * steps,),
         [
             whole((rows, width)),
-            whole((rows, width)),
+            pl.BlockSpec((rows, width // steps), early),
             whole(vectors.shape),
             pl.BlockSpec((8, block), turn),
             whole((rows, 2 * TILE)),
-            pl.BlockSpec((rows, block), turn),
+            pl.BlockSpec((rows, block), early),
             pl.BlockSpec((rows, block), late),
-            pl.BlockSpec((width, block), lambda at, *_: (0, steps + jnp.minimum(at, steps - 1))),
-            pl.BlockSpec((width, block), late),
-            whole((rows, width)),
+            pl.BlockSpec((width, block), lambda at, *_: (0, lax.rem(at + steps, 2 * steps))),
+            pl.BlockSpec((rows, width // steps), early),
             *after(wait),
         ],
         [
@@ -705,11 +708,13 @@
             pltpu.VMEM((rows, TILE), F32),
             pltpu.VMEM((rows, TILE), F32),
             pltpu.VMEM((width // 2, rows), BF16),
+            pltpu.VMEM((rows, width), F32),
+            pltpu.VMEM((steps, rows, block), BF16),
         ],
         flops=5 * rows * width * hidden,
         bytes_accessed=4 * width * hidden + 8 * rows * hidden,
         scalars=1,
-    )(core, upstream, attended, vectors, wide_rows, stats, kept, slope, both, both, normed, wait)
+    )(core, upstream, attended, vectors, wide_rows, stats, kept, slope, both, normed, wait)
 
 
 def input_back_body(
@@ -928,10 +933,9 @@
     half = 2 * width
     grad_out[...] = early[:, half : half + width]
     grad_qkv[...] = late[:, : 3 * width]
-    grad_down[:, : DOWN_FIRSTS * width] = early[:, half + width :]
-    grad_down[:, DOWN_FIRSTS * width :] = rest[:, :width]
+    grad_down[...] = early[:, half + width :]
     grad_up[:, :half] = early[:, :half]
-    grad_up[:, half:] = rest[:, width : width + half]
+    grad_up[:, half:] = rest[...]
     column = 0
     for result in (grad_qkv, grad_out, grad_up, grad_down):
         for at in range(0, result.shape[1], TILE):
@@ -1129,8 +1133,8 @@
     normed, projected = project(core_arg, tokens, vector_rows, weights)
     mixed, scaled, attention = attend(lengths, head_scale, projected)
     branch, attended, normed_mid = branch_out(core_arg, scaled, weights, tokens, vector_rows)
-    output, kept, slope, stats, down_first, down_second = forward_ffn(
-        plane, normed_mid, attended, vector_rows, wide_rows, both, upstream
+    output, kept, slope, stats, down_local = forward_ffn(
+        normed_mid, attended, vector_rows, wide_rows, both, upstream
     )
 
     def over_x(part):
@@ -1147,8 +1151,7 @@
         total = lax.all_to_all(part, "fsdp", split_axis=0, concat_axis=0, tiled=True)
         return sum_parts(total)
 
-    down_chips = lax.psum_scatter(down_first, ("x", "core"), scatter_dimension=0, tiled=True)
-    down_rest = plane_first(down_second)
+    down_chips = lax.psum_scatter(down_local, ("x", "core"), scatter_dimension=0, tiled=True)
     grad_attended, grad_hidden, wide_sums, mid_sums, *sent_up = backward_ffn(
         core_arg,
         plane,
@@ -1161,7 +1164,7 @@
         slope,
         both,
         normed_mid,
-        down_second,
+        down_local,
     )
     grad_branch, grad_mixed, branch_sums, out_sent, out_stays = branch_back(
         core_arg,
@@ -1178,7 +1181,7 @@
         normed_mid,
         grad_hidden,
         [swap_cores(part) for part in sent_up],
-        wait=(grad_branch, down_rest),
+        wait=(grad_branch,),
         more=(out_stays, swap_cores(out_sent)),
     )
     up_rest = plane_first(up_second)
@@ -1211,13 +1214,9 @@
 
     early_parts = over_plane(jnp.concatenate([up_chips, down_chips], axis=1))
     half_sums, _ = lax.optimization_barrier((half_sums, attn_first))
-    down_rest, up_rest, early_parts = lax.optimization_barrier((down_rest, up_rest, early_parts))
+    up_rest, early_parts = lax.optimization_barrier((up_rest, early_parts))
     small = jnp.sum(in_order(across_chips(half_sums)), axis=0)
-    down_rest = down_rest.reshape(chips, 2, shard, -1)
-    down_rest = take_core(down_rest, core) + swap_cores(
-        take_core(down_rest, 1 - core).astype(BF16)
-    ).astype(F32)
-    rest = jnp.concatenate([down_rest, up_rest.reshape(chips, shard, -1)], axis=2)
+    rest = up_rest.reshape(chips, shard, -1)
     rest = across_chips(rest.astype(BF16))
     rest = sum(part.astype(F32) for part in rest)
     late_parts = over_plane(jnp.concatenate([over_x(attn_first), small.astype(BF16)], axis=1))

time: 369 us -> 357 us (0.967)
  starting transfers between devices: 64.2 us -> 52.6 us
  Pallas kernels: 152 us -> 146 us
  waiting for transfers between devices: 96.1 us -> 102 us
    all_to_all x2 -> x1, starting transfers between devices: 14.3 us -> 6.54 us  [plane_first(): lax.all_to_all(part, 'fsdp', split_axis=0, concat_axis=0, tiled=True)]
    all_to_all x2, waiting for transfers between devices: 23.8 us -> 27.7 us  [over_plane(): lax.all_to_all(part.reshape(plane, shard, -1), 'fsdp', split_axis=0, conc...]
  transfers between devices with their start and end apart: 34 -> 32, of which waited for: 16 -> 15; matrix products, arithmetic and copies ran while one was open for 7% -> 7% of each run, Pallas kernels for 31% -> 32%
where the time goes in v7:
time: 357 us; the launch traced here: 351 us
  Pallas kernels  146 us (41%)
  waiting for transfers between devices  102 us (29%)
  starting transfers between devices  52.6 us (15%)
  local copies, waits for them, and re-layouts  18 us (5%)
  other arithmetic  17.3 us (5%)
  between operations  15.5 us (4%)
    ppermute x12, waiting for transfers between devices, turn_chips(): lax.ppermute(values, 'x', [(at, (at + step) % count) for at in range(coun...  41.7 us
    all_to_all x2, waiting for transfers between devices, over_plane(): lax.all_to_all(part.reshape(plane, shard, -1), 'fsdp', split_axis=0, conc...  27.7 us
    pallas_call x1, Pallas kernels, backward_ffn(): call(functools.partial(backward_ffn_body, steps), (2 * steps,), [whole((r...  25.9 us
    pallas_call x1, Pallas kernels, forward_ffn(): call(functools.partial(forward_ffn_body, steps), (2 * steps,), [whole((ro...  25.3 us
    pallas_call x1, Pallas kernels, attend_back(): call(attend_back_body, (pairs,), [by_pair, pl.BlockSpec((rows, TILE), lam...  16.8 us
    pallas_call x1, Pallas kernels, attend(): call(attend_body, (pairs,), [pl.BlockSpec((rows, TILE), lambda pair, *_:...  13.5 us
    ppermute x12, starting transfers between devices, turn_chips(): lax.ppermute(values, 'x', [(at, (at + step) % count) for at in range(coun...  12.9 us
    all_to_all x2, waiting for transfers between devices, to_plane(): lax.all_to_all(spread, 'fsdp', split_axis=0, concat_axis=concat, tiled=True)  11.9 us
  transfers between devices with their start and end apart: 32, of which 15 were waited for; matrix products, arithmetic and copies ran while one was open for 7% of the time, Pallas kernels for 32%

profile of v7, /device:TPU:0, one launch (start us, length us, event | category | flops | bytes accessed | tf_op | source)
XLA Modules:
  0.0 351.1 jit_solution(14097029927050075720)
XLA Ops:
  11.4 2.9 collective-permute-start.4
  17.6 8.0 %all-to-all-start = ((bf16[16,8,2176]{2,1,0:T(8,128)(2,1)}), bf16[16,8,2176]{2,1,0:T(8,128)(2,1)S(1)}, u32[]{:S(2)}, u32[]{:S(2)}) async-start(bf16[16,8,2176]{2,1,0:T(8,128)(2,1)} %broadcast_in_dim.41), calls=%async_computation | async-start | bytes 1114112 | tf_op jit(solution)/shard_map/all_to_all | solution.py:1090
  25.7 11.9 %all-to-all-done = bf16[16,8,2176]{2,1,0:T(8,128)(2,1)S(1)} async-done(((bf16[16,8,2176]{2,1,0:T(8,128)(2,1)}), bf16[16,8,2176]{2,1,0:T(8,128)(2,1)S(1)}, u32[]{:S(2)}, u32[]{:S(2)}) %all-to-all-start) | async-done | bytes 557088 | tf_op jit(solution)/shard_map/all_to_all | solution.py:1090
  41.6 3.7 %all-to-all-start.1 = ((bf16[16,4,8,2048]{3,2,1,0:T(8,128)(2,1)}), bf16[16,4,8,2048]{3,2,1,0:T(8,128)(2,1)S(1)}, u32[]{:S(2)}, u32[]{:S(2)}) async-start(bf16[16,4,8,2048]{3,2,1,0:T(8,128)(2,1)} %broadcast_in_dim.42), calls=%async_computation.1 | async-start | bytes 4194304 | tf_op jit(solution)/shard_map/all_to_all | solution.py:1090
  47.0 15.8 %collective-permute-done = bf16[128,2176]{1,0:T(8,128)(2,1)S(1)} collective-permute-done((bf16[128,2176]{1,0:T(8,128)(2,1)S(1)}, bf16[128,2176]{1,0:T(8,128)(2,1)S(1)}, u32[]{:S(2)}, u32[]{:S(2)}) %collective-permute-start) | collective-permute-done | bytes 557088 | tf_op jit(solution)/shard_map/ppermute | solution.py:1037
  62.8 3.0 collective-permute-done.1
  65.9 11.0 %collective-permute-done.2 = bf16[128,2176]{1,0:T(8,128)(2,1)S(1)} collective-permute-done((bf16[128,2176]{1,0:T(8,128)(2,1)S(1)}, bf16[128,2176]{1,0:T(8,128)(2,1)S(1)}, u32[]{:S(2)}, u32[]{:S(2)}) %collective-permute-start.2) | collective-permute-done | bytes 557088 | tf_op jit(solution)/shard_map/ppermute | solution.py:1037
  87.6 8.9 %shard_map.304 = (bf16[512,1024]{1,0:T(8,128)(2,1)}, bf16[512,3072]{1,0:T(8,128)(2,1)}) custom-call(s32[1]{0:T(128)} %bitcast.core, bf16[512,1024]{1,0:T(8,128)(2,1)} %tokens.5, f32[24,1024]{1,0:T(8,128)} %copy-done.5, bf16[512,2176]{1,0:T(8,128)(2,1)} %bitcast.7.own_qk, bf16[512,2176]{1,0:T(8,128)(2,1)} %collective-permute-done.3.other_qk, ...), custom_call_target="tpu_custom_call" | custom-call | flops 3221225472 | bytes 6291456 | tf_op jit(solution)/shard_map/pallas_call | solution.py:142
  96.4 13.5 %shard_map.305 = (f32[512,1024]{1,0:T(8,128)}, bf16[512,1024]{1,0:T(8,128)(2,1)}, bf16[16,256,768]{2,1,0:T(8,128)(2,1)}) custom-call(s32[1]{0:T(128)S(6)} %copy.65.length, f32[16]{0:T(128)} %scales.1, bf16[512,3072]{1,0:T(8,128)(2,1)} %get-tuple-element.65.queries.keys.values, bf16[512,3072]{1,0:T(8,128)(2,1)} %get-tuple-element.65.queries.keys.values, ...), custom_call_target="tpu_custom_call" | custom-call | flops 1073741824 | bytes 10485760 | tf_op jit(solution)/shard_map/pallas_call | solution.py:209
  109.9 6.4 %shard_map.306 = (f32[512,1024]{1,0:T(8,128)}, f32[512,1024]{1,0:T(8,128)}, bf16[512,1024]{1,0:T(8,128)(2,1)}) custom-call(s32[1]{0:T(128)} %bitcast.core, bf16[512,1024]{1,0:T(8,128)(2,1)} %get-tuple-element.66.scaled, bf16[512,2048]{1,0:T(8,128)(2,1)} %bitcast.96, bf16[512,2048]{1,0:T(8,128)(2,1)} %collective-permute-done.7.other_vo.other, ...), custom_call_target="tpu_custom_call" | custom-call | flops 1073741824 | bytes 9437184 | tf_op jit(solution)/shard_map/pallas_call | solution.py:331
  116.3 25.3 %shard_map.307 = (bf16[512,1024]{1,0:T(8,128)(2,1)}, bf16[512,4096]{1,0:T(8,128)(2,1)}, bf16[512,4096]{1,0:T(8,128)(2,1)}, f32[512,256]{1,0:T(8,128)}, bf16[1024,4096]{1,0:T(8,128)(2,1)}) custom-call(bf16[512,1024]{1,0:T(8,128)(2,1)} %get-tuple-element.67.normed.left, f32[512,1024]{1,0:T(8,128)} %get-tuple-element.68.attended, f32[24,1024]{1,0:T(8,128)} %copy-done.5, ...), custom_call_target="tpu_custom_call" | custom-call | flops 12884901888 | bytes 29360128 | tf_op jit(solution)/shard_map/pallas_call | solution.py:539
  142.0 25.9 %shard_map.308 = (f32[512,1024]{1,0:T(8,128)}, bf16[512,4096]{1,0:T(8,128)(2,1)}, f32[4,8,1024]{2,1,0:T(8,128)}, f32[8,1024]{1,0:T(8,128)}, bf16[512,2048]{1,0:T(8,128)(2,1)}, /*index=5*/bf16[16,32,2048]{2,1,0:T(8,128)(2,1)}) custom-call(s32[1]{0:T(128)} %bitcast.core, bf16[512,1024]{1,0:T(8,128)(2,1)} %broadcast_select_fusion.upstream, ...), custom_call_target="tpu_custom_call" | custom-call | flops 10737418240 | bytes 33554432 | tf_op jit(solution)/shard_map/pallas_call | solution.py:676
  169.2 11.4 %shard_map.309 = (bf16[512,1024]{1,0:T(8,128)(2,1)}, bf16[512,1024]{1,0:T(8,128)(2,1)}, f32[8,1024]{1,0:T(8,128)}, bf16[512,1024]{1,0:T(8,128)(2,1)}, f32[512,1024]{1,0:T(8,128)}) custom-call(s32[1]{0:T(128)} %bitcast.core, f32[512,1024]{1,0:T(8,128)} %get-tuple-element.75.grad_attended, f32[512,1024]{1,0:T(8,128)} %get-tuple-element.76.branch, ...), custom_call_target="tpu_custom_call" | custom-call | flops 2147483648 | bytes 10485760 | tf_op jit(solution)/shard_map/pallas_call | solution.py:403
  180.9 2.7 collective-permute-done.10.refs_1_
  185.3 9.9 %shard_map.310 = (bf16[512,3072]{1,0:T(8,128)(2,1)}, bf16[16,32,2048]{2,1,0:T(8,128)(2,1)}) custom-call(s32[1]{0:T(128)} %bitcast.core, bf16[512,1024]{1,0:T(8,128)(2,1)} %get-tuple-element.67.normed.left, bf16[512,4096]{1,0:T(8,128)(2,1)} %get-tuple-element.80.right, bf16[512,2048]{1,0:T(8,128)(2,1)} %copy-done.6, ...), custom_call_target="tpu_custom_call" | custom-call | flops 2147483648 | bytes 12582912 | tf_op jit(solution)/shard_map/pallas_call | solution.py:873
  195.3 6.5 %all-to-all-start.2 = ((bf16[16,32,2048]{2,1,0:T(8,128)(2,1)}), bf16[16,32,2048]{2,1,0:T(8,128)(2,1)S(1)}, u32[]{:S(2)}, u32[]{:S(2)}) async-start(bf16[16,32,2048]{2,1,0:T(8,128)(2,1)} %get-tuple-element.86._), calls=%async_computation.3 | async-start | bytes 4194304 | tf_op jit(solution)/shard_map/all_to_all | solution.py:1151
  201.9 16.8 %shard_map.311 = (bf16[3,512,1024]{2,1,0:T(8,128)(2,1)}, bf16[512,1024]{1,0:T(8,128)(2,1)}, bf16[512,1024]{1,0:T(8,128)(2,1)}, bf16[512,1024]{1,0:T(8,128)(2,1)}) custom-call(s32[1]{0:T(128)} %bitcast.core, bf16[512,3072]{1,0:T(8,128)(2,1)} %get-tuple-element.65.queries.keys.values, bf16[512,3072]{1,0:T(8,128)(2,1)} %get-tuple-element.65.queries.keys.values, ...), custom_call_target="tpu_custom_call" | custom-call | flops 2684354560 | bytes 12582912 | tf_op jit(solution)/shard_map/pallas_call | solution.py:286
  219.6 11.4 %shard_map.312 = (f32[512,1024]{1,0:T(8,128)}, f32[8,128,128]{2,1,0:T(8,128)}) custom-call(s32[1]{0:T(128)} %bitcast.core, bf16[3,512,1024]{2,1,0:T(8,128)(2,1)} %get-tuple-element.87.grads.right, bf16[512,2176]{1,0:T(8,128)(2,1)} %bitcast.7.own_qk, bf16[512,2176]{1,0:T(8,128)(2,1)} %collective-permute-done.3.other_qk, bf16[512,2048]{1,0:T(8,128)(2,1)} %bitcast.98, ...), custom_call_target="tpu_custom_call" | custom-call | flops 3221225472 | bytes 14680064 | tf_op jit(solution)/shard_map/pallas_call | solution.py:797
  232.5 2.9 all-to-all-done.2
  239.2 7.1 %shard_map.313 = bf16[512,3072]{1,0:T(8,128)(2,1)} custom-call(s32[1]{0:T(128)} %bitcast.core, bf16[512,1024]{1,0:T(8,128)(2,1)} %get-tuple-element.79.normed.left, bf16[3,512,1024]{2,1,0:T(8,128)(2,1)} %get-tuple-element.87.grads.right, bf16[512,1024]{1,0:T(8,128)(2,1)} %copy-done.8, bf16[512,1024]{1,0:T(8,128)(2,1)} %collective-permute-done.12.refs_1_, ...), custom_call_target="tpu_custom_call" | custom-call | flops 1610612736 | bytes 9437184 | tf_op jit(solution)/shard_map/pallas_call | solution.py:912
  250.1 4.7 %all-to-all-start.3 = ((bf16[16,8,7168]{2,1,0:T(8,128)(2,1)}), bf16[16,8,7168]{2,1,0:T(8,128)(2,1)S(1)}, u32[]{:S(2)}, u32[]{:S(2)}) async-start(bf16[16,8,7168]{2,1,0:T(8,128)(2,1)} %maximum_bitcast_fusion), calls=%async_computation.5 | async-start | bytes 3670016 | tf_op jit(solution)/shard_map/all_to_all | solution.py:1145
  256.7 6.0 %collective-permute-done.16 = f32[128,128]{1,0:T(8,128)S(1)} collective-permute-done((f32[128,128]{1,0:T(8,128)S(1)}, f32[128,128]{1,0:T(8,128)S(1)}, u32[]{:S(2)}, u32[]{:S(2)}) %collective-permute-start.16) | collective-permute-done | bytes 65568 | tf_op jit(solution)/shard_map/ppermute | solution.py:1037
  264.2 20.3 %all-to-all-done.3 = bf16[16,8,7168]{2,1,0:T(8,128)(2,1)S(1)} async-done(((bf16[16,8,7168]{2,1,0:T(8,128)(2,1)}), bf16[16,8,7168]{2,1,0:T(8,128)(2,1)S(1)}, u32[]{:S(2)}, u32[]{:S(2)}) %all-to-all-start.3) | async-done | bytes 1835040 | tf_op jit(solution)/shard_map/all_to_all | solution.py:1145
  287.8 6.2 %all-to-all-start.4 = ((bf16[16,8,3200]{2,1,0:T(8,128)(2,1)}), bf16[16,8,3200]{2,1,0:T(8,128)(2,1)S(1)}, u32[]{:S(2)}, u32[]{:S(2)}) async-start(bf16[16,8,3200]{2,1,0:T(8,128)(2,1)} %maximum_bitcast_fusion.1), calls=%async_computation.7 | async-start | bytes 1638400 | tf_op jit(solution)/shard_map/all_to_all | solution.py:1145
  298.0 2.7 collective-permute-done.19
  301.5 7.4 %all-to-all-done.4 = bf16[16,8,3200]{2,1,0:T(8,128)(2,1)S(1)} async-done(((bf16[16,8,3200]{2,1,0:T(8,128)(2,1)}), bf16[16,8,3200]{2,1,0:T(8,128)(2,1)S(1)}, u32[]{:S(2)}, u32[]{:S(2)}) %all-to-all-start.4) | async-done | bytes 819232 | tf_op jit(solution)/shard_map/all_to_all | solution.py:1145
  312.2 3.5 %all-to-all-start.5 = ((bf16[16,3,16,128]{3,2,1,0:T(8,128)(2,1)}), bf16[16,3,16,128]{3,2,1,0:T(8,128)(2,1)S(1)}, u32[]{:S(2)}, u32[]{:S(2)}) async-start(bf16[16,3,16,128]{3,2,1,0:T(8,128)(2,1)} %get-tuple-element.104), calls=%async_computation.8 | async-start | bytes 393216 | tf_op jit(solution)/shard_map/all_to_all | solution.py:1236
  316.3 7.7 %all-to-all-done.5.grads = bf16[16,3,16,128]{3,2,1,0:T(8,128)(2,1)S(1)} async-done(((bf16[16,3,16,128]{3,2,1,0:T(8,128)(2,1)}), bf16[16,3,16,128]{3,2,1,0:T(8,128)(2,1)S(1)}, u32[]{:S(2)}, u32[]{:S(2)}) %all-to-all-start.5) | async-done | bytes 196640 | tf_op jit(solution)/shard_map/all_to_all | solution.py:1236
  324.7 4.3 %shard_map.315 = (f32[6,128,128]{2,1,0:T(8,128)}, f32[6,128,128]{2,1,0:T(8,128)}, bf16[16,3,16,128]{3,2,1,0:T(8,128)(2,1)}) custom-call(bf16[16,3,16,128]{3,2,1,0:T(8,128)(2,1)} %copy-done.10, f32[6,128,128]{2,1,0:T(8,128)} %bitcast.107, f32[6,128,128]{2,1,0:T(8,128)} %bitcast.108, f32[6,128,128]{2,1,0:T(8,128)} %bitcast.109, f32[6,128,128]{2,1,0:T(8,128)} %bitcast.110), custom_call_target="tpu_custom_call" | custom-call | bytes 2359296 | tf_op jit(solution)/shard_map/pallas_call | solution.py:987
  329.0 3.5 %all-to-all-start.6 = ((bf16[16,3,16,128]{3,2,1,0:T(8,128)(2,1)}), bf16[16,3,16,128]{3,2,1,0:T(8,128)(2,1)S(1)}, u32[]{:S(2)}, u32[]{:S(2)}) async-start(bf16[16,3,16,128]{3,2,1,0:T(8,128)(2,1)} %get-tuple-element.107), calls=%async_computation.9 | async-start | bytes 393216 | tf_op jit(solution)/shard_map/all_to_all | solution.py:1238
  333.8 7.0 %all-to-all-done.6.moved = bf16[16,3,16,128]{3,2,1,0:T(8,128)(2,1)S(1)} async-done(((bf16[16,3,16,128]{3,2,1,0:T(8,128)(2,1)}), bf16[16,3,16,128]{3,2,1,0:T(8,128)(2,1)S(1)}, u32[]{:S(2)}, u32[]{:S(2)}) %all-to-all-start.6) | async-done | bytes 196640 | tf_op jit(solution)/shard_map/all_to_all | solution.py:1238
  341.5 2.6 shard_map.316
  (156 shorter events, 54.7 us)
Async XLA Ops:
  7.2 109.1 %all-gather.2.cloned.1.call-start = ((), (), s32[]{:S(2)}) async-start(), calls=%async_computation.10 | async-start | bytes 16908288 | tf_op jit(solution)/shard_map/all_gather | solution.py:1073
  11.4 14.2 %collective-permute-start.4 = (bf16[8,2048]{1,0:T(8,128)(2,1)S(1)}, bf16[8,2048]{1,0:T(8,128)(2,1)S(1)}, u32[]{:S(2)}, u32[]{:S(2)}) collective-permute-start(bf16[8,2048]{1,0:T(8,128)(2,1)S(1)} %pad_maximum_fusion.2), channel_id=1, source_target_pairs={{0,96},{32,0},{64,32},{96,64},{1,97},{33,1},{65,33},{97,65},{2,98}... | collective-permute-start | bytes 98312 | tf_op jit(solution)/shard_map/ppermute | solution.py:1037
  14.3 11.3 %collective-permute-start.5 = (bf16[8,2048]{1,0:T(8,128)(2,1)S(1)}, bf16[8,2048]{1,0:T(8,128)(2,1)S(1)}, u32[]{:S(2)}, u32[]{:S(2)}) collective-permute-start(bf16[8,2048]{1,0:T(8,128)(2,1)S(1)} %pad_maximum_fusion.2), channel_id=1, source_target_pairs={{0,64},{32,96},{64,0},{96,32},{1,65},{33,97},{65,1},{97,33},{2,66}... | collective-permute-start | bytes 98312 | tf_op jit(solution)/shard_map/ppermute | solution.py:1037
  15.1 10.5 %collective-permute-start.6 = (bf16[8,2048]{1,0:T(8,128)(2,1)S(1)}, bf16[8,2048]{1,0:T(8,128)(2,1)S(1)}, u32[]{:S(2)}, u32[]{:S(2)}) collective-permute-start(bf16[8,2048]{1,0:T(8,128)(2,1)S(1)} %pad_maximum_fusion.2), channel_id=1, source_target_pairs={{0,32},{32,64},{64,96},{96,0},{1,33},{33,65},{65,97},{97,1},{2,34}... | collective-permute-start | bytes 98312 | tf_op jit(solution)/shard_map/ppermute | solution.py:1037
  17.6 20.1 %all-to-all-start = ((bf16[16,8,2176]{2,1,0:T(8,128)(2,1)}), bf16[16,8,2176]{2,1,0:T(8,128)(2,1)S(1)}, u32[]{:S(2)}, u32[]{:S(2)}) async-start(bf16[16,8,2176]{2,1,0:T(8,128)(2,1)} %broadcast_in_dim.41), calls=%async_computation | async-start | bytes 1114112 | tf_op jit(solution)/shard_map/all_to_all | solution.py:1090
  37.6 25.2 %collective-permute-start = (bf16[128,2176]{1,0:T(8,128)(2,1)S(1)}, bf16[128,2176]{1,0:T(8,128)(2,1)S(1)}, u32[]{:S(2)}, u32[]{:S(2)}) collective-permute-start(bf16[128,2176]{1,0:T(8,128)(2,1)S(1)} %bitcast.100), channel_id=1, source_target_pairs={{0,96},{32,0},{64,32},{96,64},{1,97},{33,1},{65,33},{97,65},{2,98}... | collective-permute-start | bytes 1671176 | tf_op jit(solution)/shard_map/ppermute | solution.py:1037
  41.6 37.2 %all-to-all-start.1 = ((bf16[16,4,8,2048]{3,2,1,0:T(8,128)(2,1)}), bf16[16,4,8,2048]{3,2,1,0:T(8,128)(2,1)S(1)}, u32[]{:S(2)}, u32[]{:S(2)}) async-start(bf16[16,4,8,2048]{3,2,1,0:T(8,128)(2,1)} %broadcast_in_dim.42), calls=%async_computation.1 | async-start | bytes 4194304 | tf_op jit(solution)/shard_map/all_to_all | solution.py:1090
  45.3 156.6 %reduce-scatter.4.cloned.1.call-start = ((), (), s32[]{:S(2)}) async-start(), calls=%async_computation.11 | async-start | bytes 9437184 | tf_op jit(solution)/shard_map/reduce_scatter | solution.py:1154
  45.4 20.4 %collective-permute-start.1 = (bf16[128,2176]{1,0:T(8,128)(2,1)S(1)}, bf16[128,2176]{1,0:T(8,128)(2,1)S(1)}, u32[]{:S(2)}, u32[]{:S(2)}) collective-permute-start(bf16[128,2176]{1,0:T(8,128)(2,1)S(1)} %bitcast.101), channel_id=1, source_target_pairs={{0,64},{32,96},{64,0},{96,32},{1,65},{33,97},{65,1},{97,33},{2,66}... | collective-permute-start | bytes 1671176 | tf_op jit(solution)/shard_map/ppermute | solution.py:1037
  47.0 29.9 %collective-permute-start.2 = (bf16[128,2176]{1,0:T(8,128)(2,1)S(1)}, bf16[128,2176]{1,0:T(8,128)(2,1)S(1)}, u32[]{:S(2)}, u32[]{:S(2)}) collective-permute-start(bf16[128,2176]{1,0:T(8,128)(2,1)S(1)} %bitcast.102), channel_id=1, source_target_pairs={{0,32},{32,64},{64,96},{96,0},{1,33},{33,65},{65,97},{97,1},{2,34}... | collective-permute-start | bytes 1671176 | tf_op jit(solution)/shard_map/ppermute | solution.py:1037
  78.8 6.6 %collective-permute-start.3 = (bf16[512,2176]{1,0:T(8,128)(2,1)}, bf16[512,2176]{1,0:T(8,128)(2,1)}, u32[]{:S(2)}, u32[]{:S(2)}) collective-permute-start(bf16[512,2176]{1,0:T(8,128)(2,1)} %bitcast.7.own_qk), channel_id=1, source_target_pairs={{0,16},{16,0},{1,17},{17,1},{2,18},{18,2},{3,19},{19,3},{4,20},{20... | collective-permute-start | bytes 6684680 | tf_op jit(solution)/shard_map/ppermute | solution.py:1028
  81.9 5.7 %collective-permute-start.7 = (bf16[512,2048]{1,0:T(8,128)(2,1)S(1)}, bf16[512,2048]{1,0:T(8,128)(2,1)}, u32[]{:S(2)}, u32[]{:S(2)}) collective-permute-start(bf16[512,2048]{1,0:T(8,128)(2,1)S(1)} %bitcast.94), channel_id=1, source_target_pairs={{0,16},{16,0},{1,17},{17,1},{2,18},{18,2},{3,19},{19,3},{4,20},{20... | collective-permute-start | bytes 6291464 | tf_op jit(solution)/shard_map/ppermute | solution.py:1028
  141.7 104.9 %reduce-scatter.6.cloned.1.call-start = ((), (), s32[]{:S(2)}) async-start(), calls=%async_computation.12 | async-start | bytes 3932160 | tf_op jit(solution)/shard_map/reduce_scatter | solution.py:1141
  167.8 15.8 %collective-permute-start.8 = (bf16[512,2048]{1,0:T(8,128)(2,1)}, bf16[512,2048]{1,0:T(8,128)(2,1)S(1)}, u32[]{:S(2)}, u32[]{:S(2)}) collective-permute-start(bf16[512,2048]{1,0:T(8,128)(2,1)} %get-tuple-element.81), channel_id=1, source_target_pairs={{0,16},{16,0},{1,17},{17,1},{2,18},{18,2},{3,19},{19,3},{4,20},{20... | collective-permute-start | bytes 6291464 | tf_op jit(solution)/shard_map/ppermute | solution.py:1028
  168.2 15.4 %collective-permute-start.9 = (bf16[16,32,2048]{2,1,0:T(8,128)(2,1)}, bf16[16,32,2048]{2,1,0:T(8,128)(2,1)}, u32[]{:S(2)}, u32[]{:S(2)}) collective-permute-start(bf16[16,32,2048]{2,1,0:T(8,128)(2,1)} %get-tuple-element.82), channel_id=1, source_target_pairs={{0,16},{16,0},{1,17},{17,1},{2,18},{18,2},{3,19},{19,3},{4,20},{20... | collective-permute-start | bytes 6291464 | tf_op jit(solution)/shard_map/ppermute | solution.py:1028
  180.6 3.0 collective-permute-start.10
  195.3 40.1 %all-to-all-start.2 = ((bf16[16,32,2048]{2,1,0:T(8,128)(2,1)}), bf16[16,32,2048]{2,1,0:T(8,128)(2,1)S(1)}, u32[]{:S(2)}, u32[]{:S(2)}) async-start(bf16[16,32,2048]{2,1,0:T(8,128)(2,1)} %get-tuple-element.86._), calls=%async_computation.3 | async-start | bytes 4194304 | tf_op jit(solution)/shard_map/all_to_all | solution.py:1151
  201.9 83.8 %reduce-scatter.8.cloned.1.call-start = ((), (), s32[]{:S(2)}) async-start(), calls=%async_computation.13 | async-start | bytes 3932160 | tf_op jit(solution)/shard_map/reduce_scatter | solution.py:1141
  218.7 19.5 %collective-permute-start.11 = (bf16[512,1024]{1,0:T(8,128)(2,1)}, bf16[512,1024]{1,0:T(8,128)(2,1)S(1)}, u32[]{:S(2)}, u32[]{:S(2)}) collective-permute-start(bf16[512,1024]{1,0:T(8,128)(2,1)} %get-tuple-element.94), channel_id=1, source_target_pairs={{0,16},{16,0},{1,17},{17,1},{2,18},{18,2},{3,19},{19,3},{4,20},{20... | collective-permute-start | bytes 3145736 | tf_op jit(solution)/shard_map/ppermute | solution.py:1028
  219.0 19.2 %collective-permute-start.12 = (bf16[512,1024]{1,0:T(8,128)(2,1)}, bf16[512,1024]{1,0:T(8,128)(2,1)}, u32[]{:S(2)}, u32[]{:S(2)}) collective-permute-start(bf16[512,1024]{1,0:T(8,128)(2,1)} %get-tuple-element.95), channel_id=1, source_target_pairs={{0,16},{16,0},{1,17},{17,1},{2,18},{18,2},{3,19},{19,3},{4,20},{20... | collective-permute-start | bytes 3145736 | tf_op jit(solution)/shard_map/ppermute | solution.py:1028
  219.5 18.7 %collective-permute-start.13 = (bf16[512,1024]{1,0:T(8,128)(2,1)}, bf16[512,1024]{1,0:T(8,128)(2,1)}, u32[]{:S(2)}, u32[]{:S(2)}) collective-permute-start(bf16[512,1024]{1,0:T(8,128)(2,1)} %get-tuple-element.96), channel_id=1, source_target_pairs={{0,16},{16,0},{1,17},{17,1},{2,18},{18,2},{3,19},{19,3},{4,20},{20... | collective-permute-start | bytes 3145736 | tf_op jit(solution)/shard_map/ppermute | solution.py:1028
  232.0 4.5 %collective-permute-start.14 = (f32[4,128,128]{2,1,0:T(8,128)S(1)}, f32[4,128,128]{2,1,0:T(8,128)}, u32[]{:S(2)}, u32[]{:S(2)}) collective-permute-start(f32[4,128,128]{2,1,0:T(8,128)S(1)} %dynamic-slice_bitcast_fusion), channel_id=1, source_target_pairs={{0,16},{16,0},{1,17},{17,1},{2,18},{18,2},{3,19},{19,3},{4,20},{20... | collective-permute-start | bytes 786440 | tf_op jit(solution)/shard_map/ppermute | solution.py:1028
  246.5 10.2 %collective-permute-start.15 = (f32[128,128]{1,0:T(8,128)S(1)}, f32[128,128]{1,0:T(8,128)S(1)}, u32[]{:S(2)}, u32[]{:S(2)}) collective-permute-start(f32[128,128]{1,0:T(8,128)S(1)} %get-tuple-element.120), channel_id=1, source_target_pairs={{0,96},{32,0},{64,32},{96,64},{1,97},{33,1},{65,33},{97,65},{2,98}... | collective-permute-start | bytes 196616 | tf_op jit(solution)/shard_map/ppermute | solution.py:1037
  250.1 34.5 %all-to-all-start.3 = ((bf16[16,8,7168]{2,1,0:T(8,128)(2,1)}), bf16[16,8,7168]{2,1,0:T(8,128)(2,1)S(1)}, u32[]{:S(2)}, u32[]{:S(2)}) async-start(bf16[16,8,7168]{2,1,0:T(8,128)(2,1)} %maximum_bitcast_fusion), calls=%async_computation.5 | async-start | bytes 3670016 | tf_op jit(solution)/shard_map/all_to_all | solution.py:1145
  254.7 7.9 %collective-permute-start.16 = (f32[128,128]{1,0:T(8,128)S(1)}, f32[128,128]{1,0:T(8,128)S(1)}, u32[]{:S(2)}, u32[]{:S(2)}) collective-permute-start(f32[128,128]{1,0:T(8,128)S(1)} %get-tuple-element.119), channel_id=1, source_target_pairs={{0,64},{32,96},{64,0},{96,32},{1,65},{33,97},{65,1},{97,33},{2,66}... | collective-permute-start | bytes 196616 | tf_op jit(solution)/shard_map/ppermute | solution.py:1037
  256.3 7.9 %collective-permute-start.17 = (f32[128,128]{1,0:T(8,128)S(1)}, f32[128,128]{1,0:T(8,128)S(1)}, u32[]{:S(2)}, u32[]{:S(2)}) collective-permute-start(f32[128,128]{1,0:T(8,128)S(1)} %get-tuple-element.118), channel_id=1, source_target_pairs={{0,32},{32,64},{64,96},{96,0},{1,33},{33,65},{65,97},{97,1},{2,34}... | collective-permute-start | bytes 196616 | tf_op jit(solution)/shard_map/ppermute | solution.py:1037
  287.8 21.1 %all-to-all-start.4 = ((bf16[16,8,3200]{2,1,0:T(8,128)(2,1)}), bf16[16,8,3200]{2,1,0:T(8,128)(2,1)S(1)}, u32[]{:S(2)}, u32[]{:S(2)}) async-start(bf16[16,8,3200]{2,1,0:T(8,128)(2,1)} %maximum_bitcast_fusion.1), calls=%async_computation.7 | async-start | bytes 1638400 | tf_op jit(solution)/shard_map/all_to_all | solution.py:1145
  294.0 4.0 %collective-permute-start.20 = (bf16[8,2048]{1,0:T(8,128)(2,1)S(1)}, bf16[8,2048]{1,0:T(8,128)(2,1)S(1)}, u32[]{:S(2)}, u32[]{:S(2)}) collective-permute-start(bf16[8,2048]{1,0:T(8,128)(2,1)S(1)} %get-tuple-element.123), channel_id=1, source_target_pairs={{0,96},{32,0},{64,32},{96,64},{1,97},{33,1},{65,33},{97,65},{2,98}... | collective-permute-start | bytes 98312 | tf_op jit(solution)/shard_map/ppermute | solution.py:1037
  294.9 5.7 %collective-permute-start.19 = (bf16[8,2048]{1,0:T(8,128)(2,1)S(1)}, bf16[8,2048]{1,0:T(8,128)(2,1)S(1)}, u32[]{:S(2)}, u32[]{:S(2)}) collective-permute-start(bf16[8,2048]{1,0:T(8,128)(2,1)S(1)} %get-tuple-element.122), channel_id=1, source_target_pairs={{0,64},{32,96},{64,0},{96,32},{1,65},{33,97},{65,1},{97,33},{2,66}... | collective-permute-start | bytes 98312 | tf_op jit(solution)/shard_map/ppermute | solution.py:1037
  295.4 5.4 %collective-permute-start.18 = (bf16[8,2048]{1,0:T(8,128)(2,1)S(1)}, bf16[8,2048]{1,0:T(8,128)(2,1)S(1)}, u32[]{:S(2)}, u32[]{:S(2)}) collective-permute-start(bf16[8,2048]{1,0:T(8,128)(2,1)S(1)} %get-tuple-element.121), channel_id=1, source_target_pairs={{0,32},{32,64},{64,96},{96,0},{1,33},{33,65},{65,97},{97,1},{2,34}... | collective-permute-start | bytes 98312 | tf_op jit(solution)/shard_map/ppermute | solution.py:1037
  312.2 11.8 %all-to-all-start.5 = ((bf16[16,3,16,128]{3,2,1,0:T(8,128)(2,1)}), bf16[16,3,16,128]{3,2,1,0:T(8,128)(2,1)S(1)}, u32[]{:S(2)}, u32[]{:S(2)}) async-start(bf16[16,3,16,128]{3,2,1,0:T(8,128)(2,1)} %get-tuple-element.104), calls=%async_computation.8 | async-start | bytes 393216 | tf_op jit(solution)/shard_map/all_to_all | solution.py:1236
  329.0 11.8 %all-to-all-start.6 = ((bf16[16,3,16,128]{3,2,1,0:T(8,128)(2,1)}), bf16[16,3,16,128]{3,2,1,0:T(8,128)(2,1)S(1)}, u32[]{:S(2)}, u32[]{:S(2)}) async-start(bf16[16,3,16,128]{3,2,1,0:T(8,128)(2,1)} %get-tuple-element.107), calls=%async_computation.9 | async-start | bytes 393216 | tf_op jit(solution)/shard_map/all_to_all | solution.py:1238
  (18 other events, 246.7 us)
Sparse Core Ops, SparseCore 0:
  11.7 100.5 all-gather.1
  141.8 52.0 reduce-scatter.3
  196.3 37.8 reduce-scatter.5
  246.5 38.3 reduce-scatter.7

commit v8 on v7

--- a/solution.py
+++ b/solution.py
@@ -66,7 +66,7 @@
         ),
         compiler_params=pltpu.CompilerParams(vmem_limit_bytes=VMEM_BYTES),
         cost_estimate=pl.CostEstimate(
-            flops=flops, bytes_accessed=bytes_accessed, transcendentals=0
+            flops=20 * flops, bytes_accessed=bytes_accessed, transcendentals=0
         ),
     )
 
@@ -231,11 +231,12 @@
 
 
 def attend_back_body(
-    core, queries, keys, values, mixed, grads, weights, normed, _, __, out, sent_q, sent_k, sent_v, turned
+    queries, keys, values, mixed, grads, weights, normed, _, __, out, local, turned
 ):
     @pl.when(pl.program_id(0) == 0)
     def _():
-        turn_rows(normed, turned, 1 - core[0])
+        for at in range(0, turned.shape[0], TILE):
+            turned[at : at + TILE, :] = jnp.transpose(normed[:, at : at + TILE])
 
     rows = queries.shape[0]
     head_dim = TILE // 2
@@ -271,15 +272,12 @@
     low_k = (jnp.concatenate(k_total, axis=0) * root).astype(BF16)
     low_v = jnp.concatenate(v_total, axis=0).astype(BF16)
     out[0], out[1], out[2] = low_q, low_k, low_v
-    values = dot_nn(turned[...], jnp.concatenate([low_q, low_k, low_v], axis=1)).astype(BF16)
-    for which, sent in enumerate((sent_q, sent_k, sent_v)):
-        sent[...] = values[:, which * TILE : (which + 1) * TILE]
-
-
-def attend_back(core, projected, mixed, grads, weights, normed, wait):
+    local[...] = dot_nn(turned[...], jnp.concatenate([low_q, low_k, low_v], axis=1)).astype(BF16)
+
+
+def attend_back(projected, mixed, grads, weights, normed, wait):
     rows, width3 = projected.shape
     width = width3 // 3
-    half = width // 2
     pairs = width // TILE
     block = rows // 2
     by_pair = pl.BlockSpec((rows, TILE), lambda pair, *_: (0, pair))
@@ -298,17 +296,16 @@
         ],
         [
             pl.BlockSpec((3, rows, TILE), lambda pair, *_: (0, 0, pair)),
-            *[pl.BlockSpec((half, TILE), lambda pair, *_: (0, pair)) for _ in range(3)],
+            pl.BlockSpec((width, 3 * TILE), lambda pair, *_: (0, pair)),
         ],
         [
             jax.ShapeDtypeStruct((3, rows, width), BF16),
-            *[jax.ShapeDtypeStruct((half, width), BF16) for _ in range(3)],
-        ],
-        scratch=[pltpu.VMEM((half, rows), BF16)],
+            jax.ShapeDtypeStruct((width, width3), BF16),
+        ],
+        scratch=[pltpu.VMEM((width, rows), BF16)],
         flops=10 * rows * rows * width,
         bytes_accessed=24 * rows * width,
-        scalars=1,
-    )(core, projected, projected, projected, mixed, grads, weights, normed, *wait)
+    )(projected, projected, projected, mixed, grads, weights, normed, *wait)
 
 
 def branch_body(core, scaled, own, other, tokens, vectors, branch, attended, normed, parts):
@@ -890,49 +887,16 @@
     )(core, left, right, add_first, add_second, *more, *wait)
 
 
-def outer_stack_body(core, left, right, *refs):
-    adds, (out, turned) = refs[:3], refs[-2:]
-    at = pl.program_id(0)
-
-    @pl.when(at == 0)
-    def _():
-        turn_rows(left, turned, core[0])
-
-    value = dot_nn(turned[...], right[...])
-    for which, add in enumerate(adds):
-
-        @pl.when(at == which)
-        def _(add=add):
-            out[...] = (value + add[...].astype(F32)).astype(BF16)
-
-
-def outer_stack(core, left, rights, adds, *wait):
-    count, rows, width = rights.shape
-    half = width // 2
-    return call(
-        outer_stack_body,
-        (count,),
-        [
-            whole((rows, width)),
-            pl.BlockSpec((None, rows, width), lambda at, *_: (at, 0, 0)),
-            *[whole((half, width)) for _ in adds],
-            *after(*wait),
-        ],
-        pl.BlockSpec((half, width), lambda at, *_: (0, at)),
-        jax.ShapeDtypeStruct((half, count * width), BF16),
-        scratch=[pltpu.VMEM((half, rows), BF16)],
-        flops=2 * rows * half * width * count,
-        bytes_accessed=6 * half * width * count,
-        scalars=1,
-    )(core, left, rights, *adds, *wait)
-
-
 def to_slots_body(perm, early, late, rest, *refs):
     grad_qkv, grad_out, grad_up, grad_down, slots, tiles = refs
     width = grad_out.shape[1]
     half = 2 * width
     grad_out[...] = early[:, half : half + width]
-    grad_qkv[...] = late[:, : 3 * width]
+    for pair in range(width // TILE):
+        for which in range(3):
+            at = (3 * pair + which) * TILE
+            to = which * width + pair * TILE
+            grad_qkv[:, to : to + TILE] = late[:, at : at + TILE]
     grad_down[...] = early[:, half + width :]
     grad_up[:, :half] = early[:, :half]
     grad_up[:, half:] = rest[...]
@@ -1186,8 +1150,7 @@
     )
     up_rest = plane_first(up_second)
     up_chips = over_x(up_first)
-    grads, *sent_attn = attend_back(
-        core_arg,
+    grads, attn_local = attend_back(
         projected,
         mixed,
         grad_mixed,
@@ -1203,23 +1166,20 @@
         grad_attended,
         vector_rows,
         (branch_sums, mid_sums, wide_sums),
-        up_second,
+        up_rest,
     )
 
     turned = turned.reshape(chips, 2, TILE, TILE)
     half_sums = take_core(turned, core) + swap_cores(take_core(turned, 1 - core))
-    attn_first = outer_stack(
-        core_arg, normed, grads, [swap_cores(part) for part in sent_attn], half_sums, up_rest
-    )
+    attn_chips = lax.psum_scatter(attn_local, ("x", "core"), scatter_dimension=0, tiled=True)
 
     early_parts = over_plane(jnp.concatenate([up_chips, down_chips], axis=1))
-    half_sums, _ = lax.optimization_barrier((half_sums, attn_first))
-    up_rest, early_parts = lax.optimization_barrier((up_rest, early_parts))
+    half_sums, up_rest, early_parts = lax.optimization_barrier((half_sums, up_rest, early_parts))
     small = jnp.sum(in_order(across_chips(half_sums)), axis=0)
     rest = up_rest.reshape(chips, shard, -1)
     rest = across_chips(rest.astype(BF16))
     rest = sum(part.astype(F32) for part in rest)
-    late_parts = over_plane(jnp.concatenate([over_x(attn_first), small.astype(BF16)], axis=1))
+    late_parts = over_plane(jnp.concatenate([attn_chips, small.astype(BF16)], axis=1))
     small = late_parts[:, 3 * width :]
     vector_grads = small.T[: vectors.shape[0]]
     head_total = small[0, HEAD_AT : HEAD_AT + heads]

time: 357 us -> 355 us (level)
  Pallas kernels: 146 us -> 142 us
    all_to_all x1, waiting for transfers between devices: 2.9 us -> 13.9 us  [plane_first(): lax.all_to_all(part, 'fsdp', split_axis=0, concat_axis=0, tiled=True)]
    all_to_all x2, waiting for transfers between devices: 27.7 us -> 19.2 us  [over_plane(): lax.all_to_all(part.reshape(plane, shard, -1), 'fsdp', split_axis=0, conc...]
    pallas_call x1 -> x0, Pallas kernels: 7.1 us -> none  [outer_stack(): call(outer_stack_body, (count,), [whole((rows, width)), pl.BlockSpec((Non...]
    unnamed x56 -> x54, local copies, waits for them, and re-layouts: 7.48 us -> 6.19 us
  transfers between devices with their start and end apart: 32 -> 29, of which waited for: 15 -> 17; matrix products, arithmetic and copies ran while one was open for 7% -> 7% of each run, Pallas kernels for 32% -> 31%
where the time goes in v8:
time: 355 us; the launch traced here: 349 us
  Pallas kernels  142 us (40%)
  waiting for transfers between devices  103 us (29%)
  starting transfers between devices  53.1 us (15%)
  other arithmetic  17.7 us (5%)
  local copies, waits for them, and re-layouts  17.1 us (5%)
  between operations  15.4 us (4%)
    ppermute x12, waiting for transfers between devices, turn_chips(): lax.ppermute(values, 'x', [(at, (at + step) % count) for at in range(coun...  39 us
    pallas_call x1, Pallas kernels, backward_ffn(): call(functools.partial(backward_ffn_body, steps), (2 * steps,), [whole((r...  25.9 us
    pallas_call x1, Pallas kernels, forward_ffn(): call(functools.partial(forward_ffn_body, steps), (2 * steps,), [whole((ro...  25.3 us
    pallas_call x1, Pallas kernels, attend_back(): call(attend_back_body, (pairs,), [by_pair, pl.BlockSpec((rows, TILE), lam...  19.3 us
    all_to_all x2, waiting for transfers between devices, over_plane(): lax.all_to_all(part.reshape(plane, shard, -1), 'fsdp', split_axis=0, conc...  19.2 us
    all_to_all x1, waiting for transfers between devices, plane_first(): lax.all_to_all(part, 'fsdp', split_axis=0, concat_axis=0, tiled=True)  13.9 us
    ppermute x12, starting transfers between devices, turn_chips(): lax.ppermute(values, 'x', [(at, (at + step) % count) for at in range(coun...  13.8 us
    pallas_call x1, Pallas kernels, attend(): call(attend_body, (pairs,), [pl.BlockSpec((rows, TILE), lambda pair, *_:...  13.4 us
  transfers between devices with their start and end apart: 29, of which 17 were waited for; matrix products, arithmetic and copies ran while one was open for 7% of the time, Pallas kernels for 31%

profile of v8, /device:TPU:0, one launch (start us, length us, event | category | flops | bytes accessed | tf_op | source)
XLA Modules:
  0.0 348.6 jit_solution(8065103435078281282)
XLA Ops:
  11.4 2.9 collective-permute-start.4
  17.6 8.0 %all-to-all-start = ((bf16[16,8,2176]{2,1,0:T(8,128)(2,1)}), bf16[16,8,2176]{2,1,0:T(8,128)(2,1)S(1)}, u32[]{:S(2)}, u32[]{:S(2)}) async-start(bf16[16,8,2176]{2,1,0:T(8,128)(2,1)} %broadcast_in_dim.41), calls=%async_computation | async-start | bytes 1114112 | tf_op jit(solution)/shard_map/all_to_all | solution.py:1054
  25.7 11.9 %all-to-all-done = bf16[16,8,2176]{2,1,0:T(8,128)(2,1)S(1)} async-done(((bf16[16,8,2176]{2,1,0:T(8,128)(2,1)}), bf16[16,8,2176]{2,1,0:T(8,128)(2,1)S(1)}, u32[]{:S(2)}, u32[]{:S(2)}) %all-to-all-start) | async-done | bytes 557088 | tf_op jit(solution)/shard_map/all_to_all | solution.py:1054
  41.6 3.7 %all-to-all-start.1 = ((bf16[16,4,8,2048]{3,2,1,0:T(8,128)(2,1)}), bf16[16,4,8,2048]{3,2,1,0:T(8,128)(2,1)S(1)}, u32[]{:S(2)}, u32[]{:S(2)}) async-start(bf16[16,4,8,2048]{3,2,1,0:T(8,128)(2,1)} %broadcast_in_dim.42), calls=%async_computation.1 | async-start | bytes 4194304 | tf_op jit(solution)/shard_map/all_to_all | solution.py:1054
  47.0 15.8 %collective-permute-done = bf16[128,2176]{1,0:T(8,128)(2,1)S(1)} collective-permute-done((bf16[128,2176]{1,0:T(8,128)(2,1)S(1)}, bf16[128,2176]{1,0:T(8,128)(2,1)S(1)}, u32[]{:S(2)}, u32[]{:S(2)}) %collective-permute-start) | collective-permute-done | bytes 557088 | tf_op jit(solution)/shard_map/ppermute | solution.py:1001
  62.8 3.0 collective-permute-done.1
  65.9 11.0 %collective-permute-done.2 = bf16[128,2176]{1,0:T(8,128)(2,1)S(1)} collective-permute-done((bf16[128,2176]{1,0:T(8,128)(2,1)S(1)}, bf16[128,2176]{1,0:T(8,128)(2,1)S(1)}, u32[]{:S(2)}, u32[]{:S(2)}) %collective-permute-start.2) | collective-permute-done | bytes 557088 | tf_op jit(solution)/shard_map/ppermute | solution.py:1001
  89.2 9.0 %shard_map.304 = (bf16[512,1024]{1,0:T(8,128)(2,1)}, bf16[512,3072]{1,0:T(8,128)(2,1)}) custom-call(s32[1]{0:T(128)} %bitcast.core, bf16[512,1024]{1,0:T(8,128)(2,1)} %tokens.5, f32[24,1024]{1,0:T(8,128)} %copy-done.5, bf16[512,2176]{1,0:T(8,128)(2,1)} %bitcast.7.own_qk, bf16[512,2176]{1,0:T(8,128)(2,1)} %collective-permute-done.3.other_qk, ...), custom_call_target="tpu_custom_call" | custom-call | flops 64424509440 | bytes 6291456 | tf_op jit(solution)/shard_map/pallas_call | solution.py:142
  98.1 13.4 %shard_map.305 = (f32[512,1024]{1,0:T(8,128)}, bf16[512,1024]{1,0:T(8,128)(2,1)}, bf16[16,256,768]{2,1,0:T(8,128)(2,1)}) custom-call(s32[1]{0:T(128)S(6)} %copy.59.length, f32[16]{0:T(128)} %scales.1, bf16[512,3072]{1,0:T(8,128)(2,1)} %get-tuple-element.63.queries.keys.values, bf16[512,3072]{1,0:T(8,128)(2,1)} %get-tuple-element.63.queries.keys.values, ...), custom_call_target="tpu_custom_call" | custom-call | flops 21474836480 | bytes 10485760 | tf_op jit(solution)/shard_map/pallas_call | solution.py:209
  111.6 6.3 %shard_map.306 = (f32[512,1024]{1,0:T(8,128)}, f32[512,1024]{1,0:T(8,128)}, bf16[512,1024]{1,0:T(8,128)(2,1)}) custom-call(s32[1]{0:T(128)} %bitcast.core, bf16[512,1024]{1,0:T(8,128)(2,1)} %get-tuple-element.64.scaled, bf16[512,2048]{1,0:T(8,128)(2,1)} %bitcast.19.own_vo.own, bf16[512,2048]{1,0:T(8,128)(2,1)} %copy-done.13, bf16[512,1024]{1,0:T(8,128)(2,1)} %tokens.5, ...), custom_call_target="tpu_custom_call" | custom-call | flops 21474836480 | bytes 9437184 | tf_op jit(solution)/shard_map/pallas_call | solution.py:328
  117.9 25.3 %shard_map.307 = (bf16[512,1024]{1,0:T(8,128)(2,1)}, bf16[512,4096]{1,0:T(8,128)(2,1)}, bf16[512,4096]{1,0:T(8,128)(2,1)}, f32[512,256]{1,0:T(8,128)}, bf16[1024,4096]{1,0:T(8,128)(2,1)}) custom-call(bf16[512,1024]{1,0:T(8,128)(2,1)} %get-tuple-element.65.normed.left, f32[512,1024]{1,0:T(8,128)} %get-tuple-element.66.attended, f32[24,1024]{1,0:T(8,128)} %copy-done.5, ...), custom_call_target="tpu_custom_call" | custom-call | flops 257698037760 | bytes 29360128 | tf_op jit(solution)/shard_map/pallas_call | solution.py:536
  143.5 25.9 %shard_map.308 = (f32[512,1024]{1,0:T(8,128)}, bf16[512,4096]{1,0:T(8,128)(2,1)}, f32[4,8,1024]{2,1,0:T(8,128)}, f32[8,1024]{1,0:T(8,128)}, bf16[512,2048]{1,0:T(8,128)(2,1)}, /*index=5*/bf16[16,32,2048]{2,1,0:T(8,128)(2,1)}) custom-call(s32[1]{0:T(128)} %bitcast.core, bf16[512,1024]{1,0:T(8,128)(2,1)} %broadcast_select_fusion.upstream, ...), custom_call_target="tpu_custom_call" | custom-call | flops 214748364800 | bytes 33554432 | tf_op jit(solution)/shard_map/pallas_call | solution.py:673
  170.6 11.4 %shard_map.309 = (bf16[512,1024]{1,0:T(8,128)(2,1)}, bf16[512,1024]{1,0:T(8,128)(2,1)}, f32[8,1024]{1,0:T(8,128)}, bf16[512,1024]{1,0:T(8,128)(2,1)}, f32[512,1024]{1,0:T(8,128)}) custom-call(s32[1]{0:T(128)} %bitcast.core, f32[512,1024]{1,0:T(8,128)} %get-tuple-element.73.grad_attended, f32[512,1024]{1,0:T(8,128)} %get-tuple-element.74.branch, ...), custom_call_target="tpu_custom_call" | custom-call | flops 42949672960 | bytes 10485760 | tf_op jit(solution)/shard_map/pallas_call | solution.py:400
  182.2 2.9 collective-permute-done.10.refs_1_
  187.6 9.9 %shard_map.310 = (bf16[512,3072]{1,0:T(8,128)(2,1)}, bf16[16,32,2048]{2,1,0:T(8,128)(2,1)}) custom-call(s32[1]{0:T(128)} %bitcast.core, bf16[512,1024]{1,0:T(8,128)(2,1)} %get-tuple-element.65.normed.left, bf16[512,4096]{1,0:T(8,128)(2,1)} %get-tuple-element.78.right, bf16[512,2048]{1,0:T(8,128)(2,1)} %copy-done.14, bf16[16,32,2048]{2,1,0:T(8,128)(2,1)} %copy-done.15, ...), custom_call_target="tpu_custom_call" | custom-call | flops 42949672960 | bytes 12582912 | tf_op jit(solution)/shard_map/pallas_call | solution.py:870
  197.5 6.5 %all-to-all-start.2 = ((bf16[16,32,2048]{2,1,0:T(8,128)(2,1)}), bf16[16,32,2048]{2,1,0:T(8,128)(2,1)S(1)}, u32[]{:S(2)}, u32[]{:S(2)}) async-start(bf16[16,32,2048]{2,1,0:T(8,128)(2,1)} %get-tuple-element.84._), calls=%async_computation.3 | async-start | bytes 4194304 | tf_op jit(solution)/shard_map/all_to_all | solution.py:1115
  204.4 19.3 %shard_map.311 = (bf16[3,512,1024]{2,1,0:T(8,128)(2,1)}, bf16[1024,3072]{1,0:T(8,128)(2,1)}) custom-call(bf16[512,3072]{1,0:T(8,128)(2,1)} %get-tuple-element.63.queries.keys.values, bf16[512,3072]{1,0:T(8,128)(2,1)} %get-tuple-element.63.queries.keys.values, bf16[512,3072]{1,0:T(8,128)(2,1)} %get-tuple-element.63.queries.keys.values, ...), custom_call_target="tpu_custom_call" | custom-call | flops 53687091200 | bytes 12582912 | tf_op jit(solution)/shard_map/pallas_call | solution.py:284
  223.7 13.9 %all-to-all-done.2 = bf16[16,32,2048]{2,1,0:T(8,128)(2,1)S(1)} async-done(((bf16[16,32,2048]{2,1,0:T(8,128)(2,1)}), bf16[16,32,2048]{2,1,0:T(8,128)(2,1)S(1)}, u32[]{:S(2)}, u32[]{:S(2)}) %all-to-all-start.2) | async-done | bytes 2097184 | tf_op jit(solution)/shard_map/all_to_all | solution.py:1115
  238.7 2.5 maximum_bitcast_fusion
  241.2 4.1 %all-to-all-start.3 = ((bf16[16,8,7168]{2,1,0:T(8,128)(2,1)}), bf16[16,8,7168]{2,1,0:T(8,128)(2,1)S(1)}, u32[]{:S(2)}, u32[]{:S(2)}) async-start(bf16[16,8,7168]{2,1,0:T(8,128)(2,1)} %maximum_bitcast_fusion), calls=%async_computation.5 | async-start | bytes 3670016 | tf_op jit(solution)/shard_map/all_to_all | solution.py:1109
  245.3 11.8 %shard_map.312 = (f32[512,1024]{1,0:T(8,128)}, f32[8,128,128]{2,1,0:T(8,128)}) custom-call(s32[1]{0:T(128)} %bitcast.core, bf16[3,512,1024]{2,1,0:T(8,128)(2,1)} %get-tuple-element.85.grads, bf16[512,2176]{1,0:T(8,128)(2,1)} %bitcast.7.own_qk, bf16[512,2176]{1,0:T(8,128)(2,1)} %collective-permute-done.3.other_qk, bf16[512,2048]{1,0:T(8,128)(2,1)} %bitcast.19.own_vo.own, ...), custom_call_target="tpu_custom_call" | custom-call | flops 64424509440 | bytes 14680064 | tf_op jit(solution)/shard_map/pallas_call | solution.py:794
  260.8 12.6 %all-to-all-done.3 = bf16[16,8,7168]{2,1,0:T(8,128)(2,1)S(1)} async-done(((bf16[16,8,7168]{2,1,0:T(8,128)(2,1)}), bf16[16,8,7168]{2,1,0:T(8,128)(2,1)S(1)}, u32[]{:S(2)}, u32[]{:S(2)}) %all-to-all-start.3) | async-done | bytes 1835040 | tf_op jit(solution)/shard_map/all_to_all | solution.py:1109
  284.5 7.7 %all-to-all-start.4 = ((bf16[16,8,3200]{2,1,0:T(8,128)(2,1)}), bf16[16,8,3200]{2,1,0:T(8,128)(2,1)S(1)}, u32[]{:S(2)}, u32[]{:S(2)}) async-start(bf16[16,8,3200]{2,1,0:T(8,128)(2,1)} %maximum_bitcast_fusion.1), calls=%async_computation.7 | async-start | bytes 1638400 | tf_op jit(solution)/shard_map/all_to_all | solution.py:1109
  296.2 2.5 collective-permute-done.16
  299.7 6.6 %all-to-all-done.4 = bf16[16,8,3200]{2,1,0:T(8,128)(2,1)S(1)} async-done(((bf16[16,8,3200]{2,1,0:T(8,128)(2,1)}), bf16[16,8,3200]{2,1,0:T(8,128)(2,1)S(1)}, u32[]{:S(2)}, u32[]{:S(2)}) %all-to-all-start.4) | async-done | bytes 819232 | tf_op jit(solution)/shard_map/all_to_all | solution.py:1109
  307.1 2.5 shard_map.313
  309.6 3.5 %all-to-all-start.5 = ((bf16[16,3,16,128]{3,2,1,0:T(8,128)(2,1)}), bf16[16,3,16,128]{3,2,1,0:T(8,128)(2,1)S(1)}, u32[]{:S(2)}, u32[]{:S(2)}) async-start(bf16[16,3,16,128]{3,2,1,0:T(8,128)(2,1)} %get-tuple-element.100), calls=%async_computation.8 | async-start | bytes 393216 | tf_op jit(solution)/shard_map/all_to_all | solution.py:1196
  313.8 7.7 %all-to-all-done.5.grads = bf16[16,3,16,128]{3,2,1,0:T(8,128)(2,1)S(1)} async-done(((bf16[16,3,16,128]{3,2,1,0:T(8,128)(2,1)}), bf16[16,3,16,128]{3,2,1,0:T(8,128)(2,1)S(1)}, u32[]{:S(2)}, u32[]{:S(2)}) %all-to-all-start.5) | async-done | bytes 196640 | tf_op jit(solution)/shard_map/all_to_all | solution.py:1196
  322.2 4.3 %shard_map.314 = (f32[6,128,128]{2,1,0:T(8,128)}, f32[6,128,128]{2,1,0:T(8,128)}, bf16[16,3,16,128]{3,2,1,0:T(8,128)(2,1)}) custom-call(bf16[16,3,16,128]{3,2,1,0:T(8,128)(2,1)} %copy-done.2, f32[6,128,128]{2,1,0:T(8,128)} %bitcast.98, f32[6,128,128]{2,1,0:T(8,128)} %bitcast.99, f32[6,128,128]{2,1,0:T(8,128)} %bitcast.100, f32[6,128,128]{2,1,0:T(8,128)} %bitcast.101), custom_call_target="tpu_custom_call" | custom-call | bytes 2359296 | tf_op jit(solution)/shard_map/pallas_call | solution.py:951
  326.5 3.5 %all-to-all-start.6 = ((bf16[16,3,16,128]{3,2,1,0:T(8,128)(2,1)}), bf16[16,3,16,128]{3,2,1,0:T(8,128)(2,1)S(1)}, u32[]{:S(2)}, u32[]{:S(2)}) async-start(bf16[16,3,16,128]{3,2,1,0:T(8,128)(2,1)} %get-tuple-element.103), calls=%async_computation.9 | async-start | bytes 393216 | tf_op jit(solution)/shard_map/all_to_all | solution.py:1198
  331.3 7.0 %all-to-all-done.6.moved = bf16[16,3,16,128]{3,2,1,0:T(8,128)(2,1)S(1)} async-done(((bf16[16,3,16,128]{3,2,1,0:T(8,128)(2,1)}), bf16[16,3,16,128]{3,2,1,0:T(8,128)(2,1)S(1)}, u32[]{:S(2)}, u32[]{:S(2)}) %all-to-all-start.6) | async-done | bytes 196640 | tf_op jit(solution)/shard_map/all_to_all | solution.py:1198
  339.0 2.6 shard_map.315
  (147 shorter events, 54.0 us)
Async XLA Ops:
  7.2 110.7 %all-gather.2.cloned.1.call-start = ((), (), s32[]{:S(2)}) async-start(), calls=%async_computation.10 | async-start | bytes 16908288 | tf_op jit(solution)/shard_map/all_gather | solution.py:1037
  11.4 14.2 %collective-permute-start.4 = (bf16[8,2048]{1,0:T(8,128)(2,1)S(1)}, bf16[8,2048]{1,0:T(8,128)(2,1)S(1)}, u32[]{:S(2)}, u32[]{:S(2)}) collective-permute-start(bf16[8,2048]{1,0:T(8,128)(2,1)S(1)} %pad_maximum_fusion.2), channel_id=1, source_target_pairs={{0,96},{32,0},{64,32},{96,64},{1,97},{33,1},{65,33},{97,65},{2,98}... | collective-permute-start | bytes 98312 | tf_op jit(solution)/shard_map/ppermute | solution.py:1001
  14.3 11.3 %collective-permute-start.5 = (bf16[8,2048]{1,0:T(8,128)(2,1)S(1)}, bf16[8,2048]{1,0:T(8,128)(2,1)S(1)}, u32[]{:S(2)}, u32[]{:S(2)}) collective-permute-start(bf16[8,2048]{1,0:T(8,128)(2,1)S(1)} %pad_maximum_fusion.2), channel_id=1, source_target_pairs={{0,64},{32,96},{64,0},{96,32},{1,65},{33,97},{65,1},{97,33},{2,66}... | collective-permute-start | bytes 98312 | tf_op jit(solution)/shard_map/ppermute | solution.py:1001
  15.1 10.5 %collective-permute-start.6 = (bf16[8,2048]{1,0:T(8,128)(2,1)S(1)}, bf16[8,2048]{1,0:T(8,128)(2,1)S(1)}, u32[]{:S(2)}, u32[]{:S(2)}) collective-permute-start(bf16[8,2048]{1,0:T(8,128)(2,1)S(1)} %pad_maximum_fusion.2), channel_id=1, source_target_pairs={{0,32},{32,64},{64,96},{96,0},{1,33},{33,65},{65,97},{97,1},{2,34}... | collective-permute-start | bytes 98312 | tf_op jit(solution)/shard_map/ppermute | solution.py:1001
  17.6 20.1 %all-to-all-start = ((bf16[16,8,2176]{2,1,0:T(8,128)(2,1)}), bf16[16,8,2176]{2,1,0:T(8,128)(2,1)S(1)}, u32[]{:S(2)}, u32[]{:S(2)}) async-start(bf16[16,8,2176]{2,1,0:T(8,128)(2,1)} %broadcast_in_dim.41), calls=%async_computation | async-start | bytes 1114112 | tf_op jit(solution)/shard_map/all_to_all | solution.py:1054
  37.6 25.2 %collective-permute-start = (bf16[128,2176]{1,0:T(8,128)(2,1)S(1)}, bf16[128,2176]{1,0:T(8,128)(2,1)S(1)}, u32[]{:S(2)}, u32[]{:S(2)}) collective-permute-start(bf16[128,2176]{1,0:T(8,128)(2,1)S(1)} %bitcast.91), channel_id=1, source_target_pairs={{0,96},{32,0},{64,32},{96,64},{1,97},{33,1},{65,33},{97,65},{2,98}... | collective-permute-start | bytes 1671176 | tf_op jit(solution)/shard_map/ppermute | solution.py:1001
  41.6 37.2 %all-to-all-start.1 = ((bf16[16,4,8,2048]{3,2,1,0:T(8,128)(2,1)}), bf16[16,4,8,2048]{3,2,1,0:T(8,128)(2,1)S(1)}, u32[]{:S(2)}, u32[]{:S(2)}) async-start(bf16[16,4,8,2048]{3,2,1,0:T(8,128)(2,1)} %broadcast_in_dim.42), calls=%async_computation.1 | async-start | bytes 4194304 | tf_op jit(solution)/shard_map/all_to_all | solution.py:1054
  45.3 159.0 %reduce-scatter.4.cloned.1.call-start = ((), (), s32[]{:S(2)}) async-start(), calls=%async_computation.11 | async-start | bytes 9437184 | tf_op jit(solution)/shard_map/reduce_scatter | solution.py:1118
  45.4 20.4 %collective-permute-start.1 = (bf16[128,2176]{1,0:T(8,128)(2,1)S(1)}, bf16[128,2176]{1,0:T(8,128)(2,1)S(1)}, u32[]{:S(2)}, u32[]{:S(2)}) collective-permute-start(bf16[128,2176]{1,0:T(8,128)(2,1)S(1)} %bitcast.92), channel_id=1, source_target_pairs={{0,64},{32,96},{64,0},{96,32},{1,65},{33,97},{65,1},{97,33},{2,66}... | collective-permute-start | bytes 1671176 | tf_op jit(solution)/shard_map/ppermute | solution.py:1001
  47.0 29.9 %collective-permute-start.2 = (bf16[128,2176]{1,0:T(8,128)(2,1)S(1)}, bf16[128,2176]{1,0:T(8,128)(2,1)S(1)}, u32[]{:S(2)}, u32[]{:S(2)}) collective-permute-start(bf16[128,2176]{1,0:T(8,128)(2,1)S(1)} %bitcast.93), channel_id=1, source_target_pairs={{0,32},{32,64},{64,96},{96,0},{1,33},{33,65},{65,97},{97,1},{2,34}... | collective-permute-start | bytes 1671176 | tf_op jit(solution)/shard_map/ppermute | solution.py:1001
  78.8 6.9 %collective-permute-start.3 = (bf16[512,2176]{1,0:T(8,128)(2,1)}, bf16[512,2176]{1,0:T(8,128)(2,1)}, u32[]{:S(2)}, u32[]{:S(2)}) collective-permute-start(bf16[512,2176]{1,0:T(8,128)(2,1)} %bitcast.7.own_qk), channel_id=1, source_target_pairs={{0,16},{16,0},{1,17},{17,1},{2,18},{18,2},{3,19},{19,3},{4,20},{20... | collective-permute-start | bytes 6684680 | tf_op jit(solution)/shard_map/ppermute | solution.py:992
  80.4 7.5 %collective-permute-start.7 = (bf16[512,2048]{1,0:T(8,128)(2,1)}, bf16[512,2048]{1,0:T(8,128)(2,1)S(1)}, u32[]{:S(2)}, u32[]{:S(2)}) collective-permute-start(bf16[512,2048]{1,0:T(8,128)(2,1)} %bitcast.19.own_vo.own), channel_id=1, source_target_pairs={{0,16},{16,0},{1,17},{17,1},{2,18},{18,2},{3,19},{19,3},{4,20},{20... | collective-permute-start | bytes 6291464 | tf_op jit(solution)/shard_map/ppermute | solution.py:992
  143.3 95.5 %reduce-scatter.6.cloned.1.call-start = ((), (), s32[]{:S(2)}) async-start(), calls=%async_computation.12 | async-start | bytes 3932160 | tf_op jit(solution)/shard_map/reduce_scatter | solution.py:1105
  169.4 15.7 %collective-permute-start.8 = (bf16[512,2048]{1,0:T(8,128)(2,1)}, bf16[512,2048]{1,0:T(8,128)(2,1)S(1)}, u32[]{:S(2)}, u32[]{:S(2)}) collective-permute-start(bf16[512,2048]{1,0:T(8,128)(2,1)} %get-tuple-element.79), channel_id=1, source_target_pairs={{0,16},{16,0},{1,17},{17,1},{2,18},{18,2},{3,19},{19,3},{4,20},{20... | collective-permute-start | bytes 6291464 | tf_op jit(solution)/shard_map/ppermute | solution.py:992
  169.5 15.7 %collective-permute-start.9 = (bf16[16,32,2048]{2,1,0:T(8,128)(2,1)}, bf16[16,32,2048]{2,1,0:T(8,128)(2,1)S(1)}, u32[]{:S(2)}, u32[]{:S(2)}) collective-permute-start(bf16[16,32,2048]{2,1,0:T(8,128)(2,1)} %get-tuple-element.80), channel_id=1, source_target_pairs={{0,16},{16,0},{1,17},{17,1},{2,18},{18,2},{3,19},{19,3},{4,20},{20... | collective-permute-start | bytes 6291464 | tf_op jit(solution)/shard_map/ppermute | solution.py:992
  182.0 3.1 collective-permute-start.10
  197.5 40.1 %all-to-all-start.2 = ((bf16[16,32,2048]{2,1,0:T(8,128)(2,1)}), bf16[16,32,2048]{2,1,0:T(8,128)(2,1)S(1)}, u32[]{:S(2)}, u32[]{:S(2)}) async-start(bf16[16,32,2048]{2,1,0:T(8,128)(2,1)} %get-tuple-element.84._), calls=%async_computation.3 | async-start | bytes 4194304 | tf_op jit(solution)/shard_map/all_to_all | solution.py:1115
  204.1 78.3 %reduce-scatter.8.cloned.1.call-start = ((), (), s32[]{:S(2)}) async-start(), calls=%async_computation.13 | async-start | bytes 7077888 | tf_op jit(solution)/shard_map/reduce_scatter | solution.py:1174
  241.2 32.1 %all-to-all-start.3 = ((bf16[16,8,7168]{2,1,0:T(8,128)(2,1)}), bf16[16,8,7168]{2,1,0:T(8,128)(2,1)S(1)}, u32[]{:S(2)}, u32[]{:S(2)}) async-start(bf16[16,8,7168]{2,1,0:T(8,128)(2,1)} %maximum_bitcast_fusion), calls=%async_computation.5 | async-start | bytes 3670016 | tf_op jit(solution)/shard_map/all_to_all | solution.py:1109
  258.1 1.7 collective-permute-start.11
  274.4 5.3 %collective-permute-start.12 = (f32[128,128]{1,0:T(8,128)S(1)}, f32[128,128]{1,0:T(8,128)S(1)}, u32[]{:S(2)}, u32[]{:S(2)}) collective-permute-start(f32[128,128]{1,0:T(8,128)S(1)} %get-tuple-element.116), channel_id=1, source_target_pairs={{0,96},{32,0},{64,32},{96,64},{1,97},{33,1},{65,33},{97,65},{2,98}... | collective-permute-start | bytes 196616 | tf_op jit(solution)/shard_map/ppermute | solution.py:1001
  275.2 6.2 %collective-permute-start.13 = (f32[128,128]{1,0:T(8,128)S(1)}, f32[128,128]{1,0:T(8,128)S(1)}, u32[]{:S(2)}, u32[]{:S(2)}) collective-permute-start(f32[128,128]{1,0:T(8,128)S(1)} %get-tuple-element.115), channel_id=1, source_target_pairs={{0,64},{32,96},{64,0},{96,32},{1,65},{33,97},{65,1},{97,33},{2,66}... | collective-permute-start | bytes 196616 | tf_op jit(solution)/shard_map/ppermute | solution.py:1001
  276.7 36.4 %copy-start.8 = (f32[22,8]{0,1:T(8,128)S(1)}, f32[22,8]{0,1:T(8,128)}, u32[]{:S(2)}) copy-start(f32[22,8]{0,1:T(8,128)} %param.32) | copy-start | bytes 2116
  276.7 5.5 %collective-permute-start.14 = (f32[128,128]{1,0:T(8,128)S(1)}, f32[128,128]{1,0:T(8,128)S(1)}, u32[]{:S(2)}, u32[]{:S(2)}) collective-permute-start(f32[128,128]{1,0:T(8,128)S(1)} %get-tuple-element.114), channel_id=1, source_target_pairs={{0,32},{32,64},{64,96},{96,0},{1,33},{33,65},{65,97},{97,1},{2,34}... | collective-permute-start | bytes 196616 | tf_op jit(solution)/shard_map/ppermute | solution.py:1001
  282.3 47.7 %copy-start.11 = (f32[16]{0:T(128)S(1)}, f32[16]{0:T(128)}, u32[]{:S(2)}) copy-start(f32[16]{0:T(128)} %scales.1) | copy-start | bytes 196
  282.3 47.7 %copy-start.12 = (f32[16]{0:T(128)S(1)}, f32[16]{0:T(128)}, u32[]{:S(2)}) copy-start(f32[16]{0:T(128)} %param.33) | copy-start | bytes 196
  284.5 21.9 %all-to-all-start.4 = ((bf16[16,8,3200]{2,1,0:T(8,128)(2,1)}), bf16[16,8,3200]{2,1,0:T(8,128)(2,1)S(1)}, u32[]{:S(2)}, u32[]{:S(2)}) async-start(bf16[16,8,3200]{2,1,0:T(8,128)(2,1)} %maximum_bitcast_fusion.1), calls=%async_computation.7 | async-start | bytes 1638400 | tf_op jit(solution)/shard_map/all_to_all | solution.py:1109
  292.3 4.0 %collective-permute-start.17 = (bf16[8,2048]{1,0:T(8,128)(2,1)S(1)}, bf16[8,2048]{1,0:T(8,128)(2,1)S(1)}, u32[]{:S(2)}, u32[]{:S(2)}) collective-permute-start(bf16[8,2048]{1,0:T(8,128)(2,1)S(1)} %get-tuple-element.119), channel_id=1, source_target_pairs={{0,96},{32,0},{64,32},{96,64},{1,97},{33,1},{65,33},{97,65},{2,98}... | collective-permute-start | bytes 98312 | tf_op jit(solution)/shard_map/ppermute | solution.py:1001
  293.1 5.6 %collective-permute-start.16 = (bf16[8,2048]{1,0:T(8,128)(2,1)S(1)}, bf16[8,2048]{1,0:T(8,128)(2,1)S(1)}, u32[]{:S(2)}, u32[]{:S(2)}) collective-permute-start(bf16[8,2048]{1,0:T(8,128)(2,1)S(1)} %get-tuple-element.118), channel_id=1, source_target_pairs={{0,64},{32,96},{64,0},{96,32},{1,65},{33,97},{65,1},{97,33},{2,66}... | collective-permute-start | bytes 98312 | tf_op jit(solution)/shard_map/ppermute | solution.py:1001
  293.8 5.3 %collective-permute-start.15 = (bf16[8,2048]{1,0:T(8,128)(2,1)S(1)}, bf16[8,2048]{1,0:T(8,128)(2,1)S(1)}, u32[]{:S(2)}, u32[]{:S(2)}) collective-permute-start(bf16[8,2048]{1,0:T(8,128)(2,1)S(1)} %get-tuple-element.117), channel_id=1, source_target_pairs={{0,32},{32,64},{64,96},{96,0},{1,33},{33,65},{65,97},{97,1},{2,34}... | collective-permute-start | bytes 98312 | tf_op jit(solution)/shard_map/ppermute | solution.py:1001
  309.6 11.8 %all-to-all-start.5 = ((bf16[16,3,16,128]{3,2,1,0:T(8,128)(2,1)}), bf16[16,3,16,128]{3,2,1,0:T(8,128)(2,1)S(1)}, u32[]{:S(2)}, u32[]{:S(2)}) async-start(bf16[16,3,16,128]{3,2,1,0:T(8,128)(2,1)} %get-tuple-element.100), calls=%async_computation.8 | async-start | bytes 393216 | tf_op jit(solution)/shard_map/all_to_all | solution.py:1196
  326.5 11.8 %all-to-all-start.6 = ((bf16[16,3,16,128]{3,2,1,0:T(8,128)(2,1)}), bf16[16,3,16,128]{3,2,1,0:T(8,128)(2,1)S(1)}, u32[]{:S(2)}, u32[]{:S(2)}) async-start(bf16[16,3,16,128]{3,2,1,0:T(8,128)(2,1)} %get-tuple-element.103), calls=%async_computation.9 | async-start | bytes 393216 | tf_op jit(solution)/shard_map/all_to_all | solution.py:1198
  (14 other events, 117.0 us)
Sparse Core Ops, SparseCore 0:
  11.7 100.5 all-gather.1
  143.4 52.1 reduce-scatter.3
  197.9 37.8 reduce-scatter.5
  238.1 43.7 reduce-scatter.7

commit v9 on v8

--- a/solution.py
+++ b/solution.py
@@ -887,7 +887,7 @@
     )(core, left, right, add_first, add_second, *more, *wait)
 
 
-def to_slots_body(perm, early, late, rest, *refs):
+def to_slots_body(perm, early, late, rest, small, *refs):
     grad_qkv, grad_out, grad_up, grad_down, slots, tiles = refs
     width = grad_out.shape[1]
     half = 2 * width
@@ -905,17 +905,19 @@
         for at in range(0, result.shape[1], TILE):
             tiles[column] = result[:, at : at + TILE]
             column += 1
-    planes, pairs = slots.shape[:2]
+    planes, pairs = slots.shape[0], slots.shape[1] - 1
     for slot in range(planes * pairs):
         pair = [tiles[perm[2 * slot + which]] for which in range(2)]
         slots[slot // pairs, slot % pairs] = jnp.concatenate(pair, axis=0).astype(BF16)
-
-
-def to_slots(perm, early, late, rest, plane, widths):
-    arrays = [early, late, rest]
+    rounded = small[...].astype(BF16).astype(F32)
+    slots[:, pairs] = jnp.concatenate([rounded, small[...] - rounded], axis=1).astype(BF16)
+
+
+def to_slots(perm, early, late, rest, small, plane, widths):
+    arrays = [early, late, rest, small]
     pairs = perm.shape[0] // (2 * plane)
     shapes = [jax.ShapeDtypeStruct((8, columns), F32) for columns in widths]
-    shapes.append(jax.ShapeDtypeStruct((plane, pairs, 16, TILE), BF16))
+    shapes.append(jax.ShapeDtypeStruct((plane, pairs + 1, 16, TILE), BF16))
     return call(
         to_slots_body,
         (1,),
@@ -929,7 +931,7 @@
 
 
 def update_body(grads, left_stats, right_stats, left_roots, right_roots, left_new, right_new, back):
-    planes, pairs = grads.shape[:2]
+    planes, pairs = back.shape[:2]
     for pair in range(pairs):
         block = grads[:, pair].astype(F32)
         moved = []
@@ -948,12 +950,13 @@
 def update(grads, left_stats, right_stats, left_roots, right_roots):
     arrays = [item[0] for item in (left_stats, right_stats, left_roots, right_roots)]
     stats = jax.ShapeDtypeStruct(arrays[0].shape, F32)
+    moved = (grads.shape[0], arrays[0].shape[0] // 2, 16, TILE)
     left_new, right_new, back = call(
         update_body,
         (1,),
         [whole(grads.shape)] + [whole(item.shape) for item in arrays],
-        [whole(stats.shape), whole(stats.shape), whole(grads.shape)],
-        [stats, stats, jax.ShapeDtypeStruct(grads.shape, BF16)],
+        [whole(stats.shape), whole(stats.shape), whole(moved)],
+        [stats, stats, jax.ShapeDtypeStruct(moved, BF16)],
         bytes_accessed=24 * arrays[0].size,
     )(grads, *arrays)
     return left_new[None], right_new[None], back
@@ -1179,10 +1182,7 @@
     rest = up_rest.reshape(chips, shard, -1)
     rest = across_chips(rest.astype(BF16))
     rest = sum(part.astype(F32) for part in rest)
-    late_parts = over_plane(jnp.concatenate([attn_chips, small.astype(BF16)], axis=1))
-    small = late_parts[:, 3 * width :]
-    vector_grads = small.T[: vectors.shape[0]]
-    head_total = small[0, HEAD_AT : HEAD_AT + heads]
+    late_parts = over_plane(attn_chips)
 
     masters = (w_qkv, w_out, w_up, w_down)
     grad_qkv, grad_out, grad_up, grad_down, slots = to_slots(
@@ -1190,10 +1190,15 @@
         early_parts,
         late_parts,
         rest,
+        small.reshape(plane, shard, TILE),
         plane,
         [item.shape[1] for item in masters],
     )
     slots = lax.all_to_all(slots, "fsdp", split_axis=0, concat_axis=0, tiled=True)
+    small = sum_parts(slots[:, -1])
+    small = small[:shard] + small[shard:]
+    vector_grads = small.T[: vectors.shape[0]]
+    head_total = small[0, HEAD_AT : HEAD_AT + heads]
     left_new, right_new, back = update(slots, left_stats, right_stats, left_roots, right_roots)
     back = lax.all_to_all(back, "fsdp", split_axis=0, concat_axis=0, tiled=True)
     new_qkv, new_out, new_up, new_down = apply_steps(owner_perm, back, masters)

time: 355 us -> 354 us (level)
  blocking collectives: 0 us -> 12.2 us
  waiting for transfers between devices: 103 us -> 97.2 us
  starting transfers between devices: 53.1 us -> 48.8 us
    all_to_all x0 -> x1, blocking collectives: none -> 12.2 us  [shards(): lax.all_to_all(slots, 'fsdp', split_axis=0, concat_axis=0, tiled=True)]
    all_to_all x1 -> x0, waiting for transfers between devices: 7.68 us -> none  [shards(): lax.all_to_all(slots, 'fsdp', split_axis=0, concat_axis=0, tiled=True)]
    all_to_all x2, waiting for transfers between devices: 19.2 us -> 26.3 us  [over_plane(): lax.all_to_all(part.reshape(plane, shard, -1), 'fsdp', split_axis=0, conc...]
    ppermute x12, waiting for transfers between devices: 39 us -> 33.4 us  [turn_chips(): lax.ppermute(values, 'x', [(at, (at + step) % count) for at in range(coun...]
  transfers between devices with their start and end apart: 29 -> 28, of which waited for: 17 -> 13; matrix products, arithmetic and copies ran while one was open for 7% -> 7% of each run, Pallas kernels for 31% -> 31%
where the time goes in v9:
time: 354 us; the launch traced here: 348 us
  Pallas kernels  142 us (40%)
  waiting for transfers between devices  97.2 us (27%)
  starting transfers between devices  48.8 us (14%)
  local copies, waits for them, and re-layouts  16.4 us (5%)
  other arithmetic  16.2 us (5%)
  between operations  15.4 us (4%)
  blocking collectives  12.2 us (3%)
    ppermute x12, waiting for transfers between devices, turn_chips(): lax.ppermute(values, 'x', [(at, (at + step) % count) for at in range(coun...  33.4 us
    all_to_all x2, waiting for transfers between devices, over_plane(): lax.all_to_all(part.reshape(plane, shard, -1), 'fsdp', split_axis=0, conc...  26.3 us
    pallas_call x1, Pallas kernels, backward_ffn(): call(functools.partial(backward_ffn_body, steps), (2 * steps,), [whole((r...  25.9 us
    pallas_call x1, Pallas kernels, forward_ffn(): call(functools.partial(forward_ffn_body, steps), (2 * steps,), [whole((ro...  25.3 us
    pallas_call x1, Pallas kernels, attend_back(): call(attend_back_body, (pairs,), [by_pair, pl.BlockSpec((rows, TILE), lam...  19.3 us
    ppermute x12, starting transfers between devices, turn_chips(): lax.ppermute(values, 'x', [(at, (at + step) % count) for at in range(coun...  16.4 us
    all_to_all x1, waiting for transfers between devices, plane_first(): lax.all_to_all(part, 'fsdp', split_axis=0, concat_axis=0, tiled=True)  13.9 us
    pallas_call x1, Pallas kernels, attend(): call(attend_body, (pairs,), [pl.BlockSpec((rows, TILE), lambda pair, *_:...  13.5 us
  transfers between devices with their start and end apart: 28, of which 13 were waited for; matrix products, arithmetic and copies ran while one was open for 7% of the time, Pallas kernels for 31%

profile of v9, /device:TPU:0, one launch (start us, length us, event | category | flops | bytes accessed | tf_op | source)
XLA Modules:
  0.0 348.0 jit_solution(17487939923705127700)
XLA Ops:
  11.4 2.9 collective-permute-start.4
  17.6 8.0 %all-to-all-start = ((bf16[16,8,2176]{2,1,0:T(8,128)(2,1)}), bf16[16,8,2176]{2,1,0:T(8,128)(2,1)S(1)}, u32[]{:S(2)}, u32[]{:S(2)}) async-start(bf16[16,8,2176]{2,1,0:T(8,128)(2,1)} %broadcast_in_dim.41), calls=%async_computation | async-start | bytes 1114112 | tf_op jit(solution)/shard_map/all_to_all | solution.py:1057
  25.7 11.9 %all-to-all-done = bf16[16,8,2176]{2,1,0:T(8,128)(2,1)S(1)} async-done(((bf16[16,8,2176]{2,1,0:T(8,128)(2,1)}), bf16[16,8,2176]{2,1,0:T(8,128)(2,1)S(1)}, u32[]{:S(2)}, u32[]{:S(2)}) %all-to-all-start) | async-done | bytes 557088 | tf_op jit(solution)/shard_map/all_to_all | solution.py:1057
  41.6 3.7 %all-to-all-start.1 = ((bf16[16,4,8,2048]{3,2,1,0:T(8,128)(2,1)}), bf16[16,4,8,2048]{3,2,1,0:T(8,128)(2,1)S(1)}, u32[]{:S(2)}, u32[]{:S(2)}) async-start(bf16[16,4,8,2048]{3,2,1,0:T(8,128)(2,1)} %broadcast_in_dim.42), calls=%async_computation.1 | async-start | bytes 4194304 | tf_op jit(solution)/shard_map/all_to_all | solution.py:1057
  47.0 15.8 %collective-permute-done = bf16[128,2176]{1,0:T(8,128)(2,1)S(1)} collective-permute-done((bf16[128,2176]{1,0:T(8,128)(2,1)S(1)}, bf16[128,2176]{1,0:T(8,128)(2,1)S(1)}, u32[]{:S(2)}, u32[]{:S(2)}) %collective-permute-start) | collective-permute-done | bytes 557088 | tf_op jit(solution)/shard_map/ppermute | solution.py:1004
  62.8 3.0 collective-permute-done.1
  65.9 11.0 %collective-permute-done.2 = bf16[128,2176]{1,0:T(8,128)(2,1)S(1)} collective-permute-done((bf16[128,2176]{1,0:T(8,128)(2,1)S(1)}, bf16[128,2176]{1,0:T(8,128)(2,1)S(1)}, u32[]{:S(2)}, u32[]{:S(2)}) %collective-permute-start.2) | collective-permute-done | bytes 557088 | tf_op jit(solution)/shard_map/ppermute | solution.py:1004
  89.2 9.0 %shard_map.304 = (bf16[512,1024]{1,0:T(8,128)(2,1)}, bf16[512,3072]{1,0:T(8,128)(2,1)}) custom-call(s32[1]{0:T(128)} %bitcast.core, bf16[512,1024]{1,0:T(8,128)(2,1)} %tokens.5, f32[24,1024]{1,0:T(8,128)} %copy-done.4, bf16[512,2176]{1,0:T(8,128)(2,1)} %bitcast.7.own_qk, bf16[512,2176]{1,0:T(8,128)(2,1)} %collective-permute-done.3.other_qk, ...), custom_call_target="tpu_custom_call" | custom-call | flops 64424509440 | bytes 6291456 | tf_op jit(solution)/shard_map/pallas_call | solution.py:142
  98.2 13.5 %shard_map.305 = (f32[512,1024]{1,0:T(8,128)}, bf16[512,1024]{1,0:T(8,128)(2,1)}, bf16[16,256,768]{2,1,0:T(8,128)(2,1)}) custom-call(s32[1]{0:T(128)S(6)} %copy.59.length, f32[16]{0:T(128)} %scales.1, bf16[512,3072]{1,0:T(8,128)(2,1)} %get-tuple-element.63.queries.keys.values, bf16[512,3072]{1,0:T(8,128)(2,1)} %get-tuple-element.63.queries.keys.values, ...), custom_call_target="tpu_custom_call" | custom-call | flops 21474836480 | bytes 10485760 | tf_op jit(solution)/shard_map/pallas_call | solution.py:209
  111.6 6.3 %shard_map.306 = (f32[512,1024]{1,0:T(8,128)}, f32[512,1024]{1,0:T(8,128)}, bf16[512,1024]{1,0:T(8,128)(2,1)}) custom-call(s32[1]{0:T(128)} %bitcast.core, bf16[512,1024]{1,0:T(8,128)(2,1)} %get-tuple-element.64.scaled, bf16[512,2048]{1,0:T(8,128)(2,1)} %bitcast.19.own_vo.own, bf16[512,2048]{1,0:T(8,128)(2,1)} %copy-done.12, bf16[512,1024]{1,0:T(8,128)(2,1)} %tokens.5, ...), custom_call_target="tpu_custom_call" | custom-call | flops 21474836480 | bytes 9437184 | tf_op jit(solution)/shard_map/pallas_call | solution.py:328
  118.0 25.3 %shard_map.307 = (bf16[512,1024]{1,0:T(8,128)(2,1)}, bf16[512,4096]{1,0:T(8,128)(2,1)}, bf16[512,4096]{1,0:T(8,128)(2,1)}, f32[512,256]{1,0:T(8,128)}, bf16[1024,4096]{1,0:T(8,128)(2,1)}) custom-call(bf16[512,1024]{1,0:T(8,128)(2,1)} %get-tuple-element.65.normed.left, f32[512,1024]{1,0:T(8,128)} %get-tuple-element.66.attended, f32[24,1024]{1,0:T(8,128)} %copy-done.4, ...), custom_call_target="tpu_custom_call" | custom-call | flops 257698037760 | bytes 29360128 | tf_op jit(solution)/shard_map/pallas_call | solution.py:536
  143.6 25.9 %shard_map.308 = (f32[512,1024]{1,0:T(8,128)}, bf16[512,4096]{1,0:T(8,128)(2,1)}, f32[4,8,1024]{2,1,0:T(8,128)}, f32[8,1024]{1,0:T(8,128)}, bf16[512,2048]{1,0:T(8,128)(2,1)}, /*index=5*/bf16[16,32,2048]{2,1,0:T(8,128)(2,1)}) custom-call(s32[1]{0:T(128)} %bitcast.core, bf16[512,1024]{1,0:T(8,128)(2,1)} %broadcast_select_fusion.upstream, ...), custom_call_target="tpu_custom_call" | custom-call | flops 214748364800 | bytes 33554432 | tf_op jit(solution)/shard_map/pallas_call | solution.py:673
  170.6 11.4 %shard_map.309 = (bf16[512,1024]{1,0:T(8,128)(2,1)}, bf16[512,1024]{1,0:T(8,128)(2,1)}, f32[8,1024]{1,0:T(8,128)}, bf16[512,1024]{1,0:T(8,128)(2,1)}, f32[512,1024]{1,0:T(8,128)}) custom-call(s32[1]{0:T(128)} %bitcast.core, f32[512,1024]{1,0:T(8,128)} %get-tuple-element.73.grad_attended, f32[512,1024]{1,0:T(8,128)} %get-tuple-element.74.branch, ...), custom_call_target="tpu_custom_call" | custom-call | flops 42949672960 | bytes 10485760 | tf_op jit(solution)/shard_map/pallas_call | solution.py:400
  182.2 2.9 collective-permute-done.10.refs_1_
  187.6 9.9 %shard_map.310 = (bf16[512,3072]{1,0:T(8,128)(2,1)}, bf16[16,32,2048]{2,1,0:T(8,128)(2,1)}) custom-call(s32[1]{0:T(128)} %bitcast.core, bf16[512,1024]{1,0:T(8,128)(2,1)} %get-tuple-element.65.normed.left, bf16[512,4096]{1,0:T(8,128)(2,1)} %get-tuple-element.78.right, bf16[512,2048]{1,0:T(8,128)(2,1)} %copy-done.13, bf16[16,32,2048]{2,1,0:T(8,128)(2,1)} %copy-done.14, ...), custom_call_target="tpu_custom_call" | custom-call | flops 42949672960 | bytes 12582912 | tf_op jit(solution)/shard_map/pallas_call | solution.py:870
  197.5 6.5 %all-to-all-start.2 = ((bf16[16,32,2048]{2,1,0:T(8,128)(2,1)}), bf16[16,32,2048]{2,1,0:T(8,128)(2,1)S(1)}, u32[]{:S(2)}, u32[]{:S(2)}) async-start(bf16[16,32,2048]{2,1,0:T(8,128)(2,1)} %get-tuple-element.84._), calls=%async_computation.3 | async-start | bytes 4194304 | tf_op jit(solution)/shard_map/all_to_all | solution.py:1118
  204.3 19.3 %shard_map.311 = (bf16[3,512,1024]{2,1,0:T(8,128)(2,1)}, bf16[1024,3072]{1,0:T(8,128)(2,1)}) custom-call(bf16[512,3072]{1,0:T(8,128)(2,1)} %get-tuple-element.63.queries.keys.values, bf16[512,3072]{1,0:T(8,128)(2,1)} %get-tuple-element.63.queries.keys.values, bf16[512,3072]{1,0:T(8,128)(2,1)} %get-tuple-element.63.queries.keys.values, ...), custom_call_target="tpu_custom_call" | custom-call | flops 53687091200 | bytes 12582912 | tf_op jit(solution)/shard_map/pallas_call | solution.py:284
  223.6 13.9 %all-to-all-done.2 = bf16[16,32,2048]{2,1,0:T(8,128)(2,1)S(1)} async-done(((bf16[16,32,2048]{2,1,0:T(8,128)(2,1)}), bf16[16,32,2048]{2,1,0:T(8,128)(2,1)S(1)}, u32[]{:S(2)}, u32[]{:S(2)}) %all-to-all-start.2) | async-done | bytes 2097184 | tf_op jit(solution)/shard_map/all_to_all | solution.py:1118
  238.6 2.5 maximum_bitcast_fusion
  241.0 4.2 %all-to-all-start.3 = ((bf16[16,8,7168]{2,1,0:T(8,128)(2,1)}), bf16[16,8,7168]{2,1,0:T(8,128)(2,1)S(1)}, u32[]{:S(2)}, u32[]{:S(2)}) async-start(bf16[16,8,7168]{2,1,0:T(8,128)(2,1)} %maximum_bitcast_fusion), calls=%async_computation.5 | async-start | bytes 3670016 | tf_op jit(solution)/shard_map/all_to_all | solution.py:1112
  245.3 11.8 %shard_map.312 = (f32[512,1024]{1,0:T(8,128)}, f32[8,128,128]{2,1,0:T(8,128)}) custom-call(s32[1]{0:T(128)} %bitcast.core, bf16[3,512,1024]{2,1,0:T(8,128)(2,1)} %get-tuple-element.85.grads, bf16[512,2176]{1,0:T(8,128)(2,1)} %bitcast.7.own_qk, bf16[512,2176]{1,0:T(8,128)(2,1)} %collective-permute-done.3.other_qk, bf16[512,2048]{1,0:T(8,128)(2,1)} %bitcast.19.own_vo.own, ...), custom_call_target="tpu_custom_call" | custom-call | flops 64424509440 | bytes 14680064 | tf_op jit(solution)/shard_map/pallas_call | solution.py:794
  260.6 12.7 %all-to-all-done.3 = bf16[16,8,7168]{2,1,0:T(8,128)(2,1)S(1)} async-done(((bf16[16,8,7168]{2,1,0:T(8,128)(2,1)}), bf16[16,8,7168]{2,1,0:T(8,128)(2,1)S(1)}, u32[]{:S(2)}, u32[]{:S(2)}) %all-to-all-start.3) | async-done | bytes 1835040 | tf_op jit(solution)/shard_map/all_to_all | solution.py:1112
  277.4 2.8 collective-permute-start.15
  283.5 2.5 collective-permute-done.16
  286.7 4.2 %all-to-all-start.4 = ((bf16[16,8,3072]{2,1,0:T(8,128)(2,1)}), bf16[16,8,3072]{2,1,0:T(8,128)(2,1)S(1)}, u32[]{:S(2)}, u32[]{:S(2)}) async-start(bf16[16,8,3072]{2,1,0:T(8,128)(2,1)} %bitcast.96), calls=%async_computation.7 | async-start | bytes 1572864 | tf_op jit(solution)/shard_map/all_to_all | solution.py:1112
  291.7 13.6 %all-to-all-done.4 = bf16[16,8,3072]{2,1,0:T(8,128)(2,1)S(1)} async-done(((bf16[16,8,3072]{2,1,0:T(8,128)(2,1)}), bf16[16,8,3072]{2,1,0:T(8,128)(2,1)S(1)}, u32[]{:S(2)}, u32[]{:S(2)}) %all-to-all-start.4) | async-done | bytes 786464 | tf_op jit(solution)/shard_map/all_to_all | solution.py:1112
  306.0 2.6 shard_map.313
  308.6 12.2 %all_to_all.45.grads = bf16[16,4,16,128]{3,2,1,0:T(8,128)(2,1)S(1)} all-to-all(bf16[16,4,16,128]{3,2,1,0:T(8,128)(2,1)} %get-tuple-element.100), channel_id=1, replica_groups=mesh['x'=4,'core'=2,'fsdp'=16] {'fsdp'}, dimensions={0} | all-to-all | bytes 524288 | tf_op jit(solution)/shard_map/all_to_all | solution.py:1197
  321.5 4.4 %shard_map.314 = (f32[6,128,128]{2,1,0:T(8,128)}, f32[6,128,128]{2,1,0:T(8,128)}, bf16[16,3,16,128]{3,2,1,0:T(8,128)(2,1)}) custom-call(bf16[16,4,16,128]{3,2,1,0:T(8,128)(2,1)} %copy-done, f32[6,128,128]{2,1,0:T(8,128)} %bitcast.99, f32[6,128,128]{2,1,0:T(8,128)} %bitcast.100, f32[6,128,128]{2,1,0:T(8,128)} %bitcast.101, f32[6,128,128]{2,1,0:T(8,128)} %bitcast.102), custom_call_target="tpu_custom_call" | custom-call | bytes 2359296 | tf_op jit(solution)/shard_map/pallas_call | solution.py:954
  325.8 3.5 %all-to-all-start.6 = ((bf16[16,3,16,128]{3,2,1,0:T(8,128)(2,1)}), bf16[16,3,16,128]{3,2,1,0:T(8,128)(2,1)S(1)}, u32[]{:S(2)}, u32[]{:S(2)}) async-start(bf16[16,3,16,128]{3,2,1,0:T(8,128)(2,1)} %get-tuple-element.103), calls=%async_computation.9 | async-start | bytes 393216 | tf_op jit(solution)/shard_map/all_to_all | solution.py:1203
  330.6 7.1 %all-to-all-done.6.moved = bf16[16,3,16,128]{3,2,1,0:T(8,128)(2,1)S(1)} async-done(((bf16[16,3,16,128]{3,2,1,0:T(8,128)(2,1)}), bf16[16,3,16,128]{3,2,1,0:T(8,128)(2,1)S(1)}, u32[]{:S(2)}, u32[]{:S(2)}) %all-to-all-start.6) | async-done | bytes 196640 | tf_op jit(solution)/shard_map/all_to_all | solution.py:1203
  338.4 2.6 shard_map.315
  (145 shorter events, 45.8 us)
Async XLA Ops:
  7.2 110.8 %all-gather.2.cloned.1.call-start = ((), (), s32[]{:S(2)}) async-start(), calls=%async_computation.10 | async-start | bytes 16908288 | tf_op jit(solution)/shard_map/all_gather | solution.py:1040
  11.4 14.2 %collective-permute-start.4 = (bf16[8,2048]{1,0:T(8,128)(2,1)S(1)}, bf16[8,2048]{1,0:T(8,128)(2,1)S(1)}, u32[]{:S(2)}, u32[]{:S(2)}) collective-permute-start(bf16[8,2048]{1,0:T(8,128)(2,1)S(1)} %pad_maximum_fusion.2), channel_id=1, source_target_pairs={{0,96},{32,0},{64,32},{96,64},{1,97},{33,1},{65,33},{97,65},{2,98}... | collective-permute-start | bytes 98312 | tf_op jit(solution)/shard_map/ppermute | solution.py:1004
  14.3 11.3 %collective-permute-start.5 = (bf16[8,2048]{1,0:T(8,128)(2,1)S(1)}, bf16[8,2048]{1,0:T(8,128)(2,1)S(1)}, u32[]{:S(2)}, u32[]{:S(2)}) collective-permute-start(bf16[8,2048]{1,0:T(8,128)(2,1)S(1)} %pad_maximum_fusion.2), channel_id=1, source_target_pairs={{0,64},{32,96},{64,0},{96,32},{1,65},{33,97},{65,1},{97,33},{2,66}... | collective-permute-start | bytes 98312 | tf_op jit(solution)/shard_map/ppermute | solution.py:1004
  15.1 10.5 %collective-permute-start.6 = (bf16[8,2048]{1,0:T(8,128)(2,1)S(1)}, bf16[8,2048]{1,0:T(8,128)(2,1)S(1)}, u32[]{:S(2)}, u32[]{:S(2)}) collective-permute-start(bf16[8,2048]{1,0:T(8,128)(2,1)S(1)} %pad_maximum_fusion.2), channel_id=1, source_target_pairs={{0,32},{32,64},{64,96},{96,0},{1,33},{33,65},{65,97},{97,1},{2,34}... | collective-permute-start | bytes 98312 | tf_op jit(solution)/shard_map/ppermute | solution.py:1004
  17.6 20.1 %all-to-all-start = ((bf16[16,8,2176]{2,1,0:T(8,128)(2,1)}), bf16[16,8,2176]{2,1,0:T(8,128)(2,1)S(1)}, u32[]{:S(2)}, u32[]{:S(2)}) async-start(bf16[16,8,2176]{2,1,0:T(8,128)(2,1)} %broadcast_in_dim.41), calls=%async_computation | async-start | bytes 1114112 | tf_op jit(solution)/shard_map/all_to_all | solution.py:1057
  37.6 25.2 %collective-permute-start = (bf16[128,2176]{1,0:T(8,128)(2,1)S(1)}, bf16[128,2176]{1,0:T(8,128)(2,1)S(1)}, u32[]{:S(2)}, u32[]{:S(2)}) collective-permute-start(bf16[128,2176]{1,0:T(8,128)(2,1)S(1)} %bitcast.91), channel_id=1, source_target_pairs={{0,96},{32,0},{64,32},{96,64},{1,97},{33,1},{65,33},{97,65},{2,98}... | collective-permute-start | bytes 1671176 | tf_op jit(solution)/shard_map/ppermute | solution.py:1004
  41.6 37.2 %all-to-all-start.1 = ((bf16[16,4,8,2048]{3,2,1,0:T(8,128)(2,1)}), bf16[16,4,8,2048]{3,2,1,0:T(8,128)(2,1)S(1)}, u32[]{:S(2)}, u32[]{:S(2)}) async-start(bf16[16,4,8,2048]{3,2,1,0:T(8,128)(2,1)} %broadcast_in_dim.42), calls=%async_computation.1 | async-start | bytes 4194304 | tf_op jit(solution)/shard_map/all_to_all | solution.py:1057
  45.3 159.0 %reduce-scatter.4.cloned.1.call-start = ((), (), s32[]{:S(2)}) async-start(), calls=%async_computation.11 | async-start | bytes 9437184 | tf_op jit(solution)/shard_map/reduce_scatter | solution.py:1121
  45.4 20.4 %collective-permute-start.1 = (bf16[128,2176]{1,0:T(8,128)(2,1)S(1)}, bf16[128,2176]{1,0:T(8,128)(2,1)S(1)}, u32[]{:S(2)}, u32[]{:S(2)}) collective-permute-start(bf16[128,2176]{1,0:T(8,128)(2,1)S(1)} %bitcast.92), channel_id=1, source_target_pairs={{0,64},{32,96},{64,0},{96,32},{1,65},{33,97},{65,1},{97,33},{2,66}... | collective-permute-start | bytes 1671176 | tf_op jit(solution)/shard_map/ppermute | solution.py:1004
  47.0 29.9 %collective-permute-start.2 = (bf16[128,2176]{1,0:T(8,128)(2,1)S(1)}, bf16[128,2176]{1,0:T(8,128)(2,1)S(1)}, u32[]{:S(2)}, u32[]{:S(2)}) collective-permute-start(bf16[128,2176]{1,0:T(8,128)(2,1)S(1)} %bitcast.93), channel_id=1, source_target_pairs={{0,32},{32,64},{64,96},{96,0},{1,33},{33,65},{65,97},{97,1},{2,34}... | collective-permute-start | bytes 1671176 | tf_op jit(solution)/shard_map/ppermute | solution.py:1004
  78.8 6.9 %collective-permute-start.3 = (bf16[512,2176]{1,0:T(8,128)(2,1)}, bf16[512,2176]{1,0:T(8,128)(2,1)}, u32[]{:S(2)}, u32[]{:S(2)}) collective-permute-start(bf16[512,2176]{1,0:T(8,128)(2,1)} %bitcast.7.own_qk), channel_id=1, source_target_pairs={{0,16},{16,0},{1,17},{17,1},{2,18},{18,2},{3,19},{19,3},{4,20},{20... | collective-permute-start | bytes 6684680 | tf_op jit(solution)/shard_map/ppermute | solution.py:995
  80.3 7.5 %collective-permute-start.7 = (bf16[512,2048]{1,0:T(8,128)(2,1)}, bf16[512,2048]{1,0:T(8,128)(2,1)S(1)}, u32[]{:S(2)}, u32[]{:S(2)}) collective-permute-start(bf16[512,2048]{1,0:T(8,128)(2,1)} %bitcast.19.own_vo.own), channel_id=1, source_target_pairs={{0,16},{16,0},{1,17},{17,1},{2,18},{18,2},{3,19},{19,3},{4,20},{20... | collective-permute-start | bytes 6291464 | tf_op jit(solution)/shard_map/ppermute | solution.py:995
  143.3 95.3 %reduce-scatter.6.cloned.1.call-start = ((), (), s32[]{:S(2)}) async-start(), calls=%async_computation.12 | async-start | bytes 3932160 | tf_op jit(solution)/shard_map/reduce_scatter | solution.py:1108
  169.4 15.8 %collective-permute-start.8 = (bf16[512,2048]{1,0:T(8,128)(2,1)}, bf16[512,2048]{1,0:T(8,128)(2,1)S(1)}, u32[]{:S(2)}, u32[]{:S(2)}) collective-permute-start(bf16[512,2048]{1,0:T(8,128)(2,1)} %get-tuple-element.79), channel_id=1, source_target_pairs={{0,16},{16,0},{1,17},{17,1},{2,18},{18,2},{3,19},{19,3},{4,20},{20... | collective-permute-start | bytes 6291464 | tf_op jit(solution)/shard_map/ppermute | solution.py:995
  169.5 15.7 %collective-permute-start.9 = (bf16[16,32,2048]{2,1,0:T(8,128)(2,1)}, bf16[16,32,2048]{2,1,0:T(8,128)(2,1)S(1)}, u32[]{:S(2)}, u32[]{:S(2)}) collective-permute-start(bf16[16,32,2048]{2,1,0:T(8,128)(2,1)} %get-tuple-element.80), channel_id=1, source_target_pairs={{0,16},{16,0},{1,17},{17,1},{2,18},{18,2},{3,19},{19,3},{4,20},{20... | collective-permute-start | bytes 6291464 | tf_op jit(solution)/shard_map/ppermute | solution.py:995
  182.0 3.1 collective-permute-start.10
  197.5 40.0 %all-to-all-start.2 = ((bf16[16,32,2048]{2,1,0:T(8,128)(2,1)}), bf16[16,32,2048]{2,1,0:T(8,128)(2,1)S(1)}, u32[]{:S(2)}, u32[]{:S(2)}) async-start(bf16[16,32,2048]{2,1,0:T(8,128)(2,1)} %get-tuple-element.84._), calls=%async_computation.3 | async-start | bytes 4194304 | tf_op jit(solution)/shard_map/all_to_all | solution.py:1118
  204.0 82.7 %reduce-scatter.8.cloned.1.call-start = ((), (), s32[]{:S(2)}) async-start(), calls=%async_computation.13 | async-start | bytes 7077888 | tf_op jit(solution)/shard_map/reduce_scatter | solution.py:1177
  241.0 32.3 %all-to-all-start.3 = ((bf16[16,8,7168]{2,1,0:T(8,128)(2,1)}), bf16[16,8,7168]{2,1,0:T(8,128)(2,1)S(1)}, u32[]{:S(2)}, u32[]{:S(2)}) async-start(bf16[16,8,7168]{2,1,0:T(8,128)(2,1)} %maximum_bitcast_fusion), calls=%async_computation.5 | async-start | bytes 3670016 | tf_op jit(solution)/shard_map/all_to_all | solution.py:1112
  258.0 1.6 collective-permute-start.11
  274.4 6.6 %collective-permute-start.14 = (bf16[8,2048]{1,0:T(8,128)(2,1)S(1)}, bf16[8,2048]{1,0:T(8,128)(2,1)S(1)}, u32[]{:S(2)}, u32[]{:S(2)}) collective-permute-start(bf16[8,2048]{1,0:T(8,128)(2,1)S(1)} %get-tuple-element.119), channel_id=1, source_target_pairs={{0,96},{32,0},{64,32},{96,64},{1,97},{33,1},{65,33},{97,65},{2,98}... | collective-permute-start | bytes 98312 | tf_op jit(solution)/shard_map/ppermute | solution.py:1004
  275.3 7.0 %collective-permute-start.13 = (bf16[8,2048]{1,0:T(8,128)(2,1)S(1)}, bf16[8,2048]{1,0:T(8,128)(2,1)S(1)}, u32[]{:S(2)}, u32[]{:S(2)}) collective-permute-start(bf16[8,2048]{1,0:T(8,128)(2,1)S(1)} %get-tuple-element.118), channel_id=1, source_target_pairs={{0,64},{32,96},{64,0},{96,32},{1,65},{33,97},{65,1},{97,33},{2,66}... | collective-permute-start | bytes 98312 | tf_op jit(solution)/shard_map/ppermute | solution.py:1004
  276.8 6.0 %collective-permute-start.12 = (bf16[8,2048]{1,0:T(8,128)(2,1)S(1)}, bf16[8,2048]{1,0:T(8,128)(2,1)S(1)}, u32[]{:S(2)}, u32[]{:S(2)}) collective-permute-start(bf16[8,2048]{1,0:T(8,128)(2,1)S(1)} %get-tuple-element.117), channel_id=1, source_target_pairs={{0,32},{32,64},{64,96},{96,0},{1,33},{33,65},{65,97},{97,1},{2,34}... | collective-permute-start | bytes 98312 | tf_op jit(solution)/shard_map/ppermute | solution.py:1004
  277.4 6.1 %collective-permute-start.15 = (f32[128,128]{1,0:T(8,128)S(1)}, f32[128,128]{1,0:T(8,128)S(1)}, u32[]{:S(2)}, u32[]{:S(2)}) collective-permute-start(f32[128,128]{1,0:T(8,128)S(1)} %get-tuple-element.116), channel_id=1, source_target_pairs={{0,96},{32,0},{64,32},{96,64},{1,97},{33,1},{65,33},{97,65},{2,98}... | collective-permute-start | bytes 196616 | tf_op jit(solution)/shard_map/ppermute | solution.py:1004
  280.2 5.8 %collective-permute-start.16 = (f32[128,128]{1,0:T(8,128)S(1)}, f32[128,128]{1,0:T(8,128)S(1)}, u32[]{:S(2)}, u32[]{:S(2)}) collective-permute-start(f32[128,128]{1,0:T(8,128)S(1)} %get-tuple-element.115), channel_id=1, source_target_pairs={{0,64},{32,96},{64,0},{96,32},{1,65},{33,97},{65,1},{97,33},{2,66}... | collective-permute-start | bytes 196616 | tf_op jit(solution)/shard_map/ppermute | solution.py:1004
  281.0 48.3 %copy-start.6 = (f32[22,8]{0,1:T(8,128)S(1)}, f32[22,8]{0,1:T(8,128)}, u32[]{:S(2)}) copy-start(f32[22,8]{0,1:T(8,128)} %param.26) | copy-start | bytes 2116
  281.0 48.3 %copy-start.7 = (f32[22,8]{0,1:T(8,128)S(1)}, f32[22,8]{0,1:T(8,128)}, u32[]{:S(2)}) copy-start(f32[22,8]{0,1:T(8,128)} %param.32) | copy-start | bytes 2116
  281.0 49.0 %copy-start.10 = (f32[16]{0:T(128)S(1)}, f32[16]{0:T(128)}, u32[]{:S(2)}) copy-start(f32[16]{0:T(128)} %scales.1) | copy-start | bytes 196
  281.0 49.0 %copy-start.11 = (f32[16]{0:T(128)S(1)}, f32[16]{0:T(128)}, u32[]{:S(2)}) copy-start(f32[16]{0:T(128)} %param.33) | copy-start | bytes 196
  281.0 5.6 %collective-permute-start.17 = (f32[128,128]{1,0:T(8,128)S(1)}, f32[128,128]{1,0:T(8,128)S(1)}, u32[]{:S(2)}, u32[]{:S(2)}) collective-permute-start(f32[128,128]{1,0:T(8,128)S(1)} %get-tuple-element.114), channel_id=1, source_target_pairs={{0,32},{32,64},{64,96},{96,0},{1,33},{33,65},{65,97},{97,1},{2,34}... | collective-permute-start | bytes 196616 | tf_op jit(solution)/shard_map/ppermute | solution.py:1004
  286.7 18.6 %all-to-all-start.4 = ((bf16[16,8,3072]{2,1,0:T(8,128)(2,1)}), bf16[16,8,3072]{2,1,0:T(8,128)(2,1)S(1)}, u32[]{:S(2)}, u32[]{:S(2)}) async-start(bf16[16,8,3072]{2,1,0:T(8,128)(2,1)} %bitcast.96), calls=%async_computation.7 | async-start | bytes 1572864 | tf_op jit(solution)/shard_map/all_to_all | solution.py:1112
  325.8 11.8 %all-to-all-start.6 = ((bf16[16,3,16,128]{3,2,1,0:T(8,128)(2,1)}), bf16[16,3,16,128]{3,2,1,0:T(8,128)(2,1)S(1)}, u32[]{:S(2)}, u32[]{:S(2)}) async-start(bf16[16,3,16,128]{3,2,1,0:T(8,128)(2,1)} %get-tuple-element.103), calls=%async_computation.9 | async-start | bytes 393216 | tf_op jit(solution)/shard_map/all_to_all | solution.py:1203
  (12 other events, 88.6 us)
Sparse Core Ops, SparseCore 0:
  11.7 100.5 all-gather.1
  143.4 52.0 reduce-scatter.3
  197.9 37.8 reduce-scatter.5
  238.1 42.9 reduce-scatter.7
